TPU v7x, 32 devices: a whole 2x2x4 slice. The times are simulated.
32 devices in a mesh: dp: 8 (over z, core), mp: 4 (over y, x).
Axes of the slice: x: 2, y: 2, z: 4, core: 2. Of those that a mesh axis runs over, the one named last changes fastest.
Arguments:
- inputs: bfloat16 [8192, 2048], P('dp'), may hold values from -6 to 6
- counts: int32 [8], P('dp'), may hold values from 1 to 1024, 4096 in all
- cotangent: bfloat16 [8192, 2048], P('dp'), may hold values from -6 to 6
- gain_attn: float32 [2048], P('dp'), may hold values from 0.5 to 1.5
- w_query: float32 [2048, 2048], P('dp', 'mp'), may hold values from -0.125 to 0.125
- w_key: float32 [2048, 2048], P('dp', 'mp'), may hold values from -0.125 to 0.125
- w_value: float32 [2048, 2048], P('dp', 'mp'), may hold values from -0.125 to 0.125
- w_output: float32 [2048, 2048], P('mp', 'dp'), may hold values from -0.5 to 0.5
- gain_ffn: float32 [2048], P('dp'), may hold values from 0.5 to 1.5
- w_gate: float32 [2048, 8192], P('dp', 'mp'), may hold values from -0.125 to 0.125
- w_up: float32 [2048, 8192], P('dp', 'mp'), may hold values from -0.125 to 0.125
- w_down: float32 [8192, 2048], P('mp', 'dp'), may hold values from -0.0625 to 0.0625
Outputs:
- layer_out: bfloat16 [8192, 2048], P('dp')
- input_grad: float32 [8192, 2048], P('dp')
- grad_gain_attn: float32 [2048], P('dp')
- grad_w_query: float32 [2048, 2048], P('dp', 'mp')
- grad_w_key: float32 [2048, 2048], P('dp', 'mp')
- grad_w_value: float32 [2048, 2048], P('dp', 'mp')
- grad_w_output: float32 [2048, 2048], P('mp', 'dp')
- grad_gain_ffn: float32 [2048], P('dp')
- grad_w_gate: float32 [2048, 8192], P('dp', 'mp')
- grad_w_up: float32 [2048, 8192], P('dp', 'mp')
- grad_w_down: float32 [8192, 2048], P('mp', 'dp')
Inputs may be any that keep to these rules, and one draw needn't show every extreme that they name: `counts`: valid tokens of each sequence, the first ones of its row; one sequence has exactly 1024, and all together make half of the 8192 slots.
All inputs are finite; a program needn't handle non-finite values. No bound on the sum of `counts` on one device may be relied on, other than what follows from the above.
Results may differ from a plain program's by a relative error of at most 0.02.
Values may be sent and summed in bfloat16 or wider, within the bound.
A program may use at most 192 MiB of HBM per device.

v0:
```python
import math

import jax
import jax.numpy as jnp
from jax import lax
from jax.sharding import PartitionSpec as P

HD = 128


EPS = 1e-06


def score_block(query_block, start, keys_three, count):
    head_size = query_block.shape[2]
    raw = jnp.einsum("qhd,khd->hqk", query_block, keys_three, preferred_element_type=jnp.float32)
    logistic = jax.nn.sigmoid(raw * head_size ** (-0.5) - math.log(keys_three.shape[0]))
    rows_at = start + jnp.arange(query_block.shape[0])[:, None]
    columns = jnp.arange(keys_three.shape[0])[None, :]
    allowed = ((columns <= rows_at) & (columns < count)).astype(jnp.float32)
    return (logistic, allowed[None])


def attend_forward(queries_three, keys_three, values_three, count, block_rows):
    length = queries_three.shape[0]

    def one_block(index):
        start = index * block_rows
        query_block = lax.dynamic_slice_in_dim(queries_three, start, block_rows, 0)
        logistic, allowed = score_block(query_block, start, keys_three, count)
        attn_weight = (logistic * allowed).astype(jnp.bfloat16)
        return jnp.einsum(
            "hqk,khd->qhd", attn_weight, values_three, preferred_element_type=jnp.float32
        )

    stacked = lax.map(one_block, jnp.arange(length // block_rows))
    return stacked.reshape(length, -1).astype(jnp.bfloat16)


def attend_backward(queries_three, keys_three, values_three, grad_three, count, block_rows):
    length = queries_three.shape[0]
    head_scale = queries_three.shape[2] ** (-0.5)

    def one_block(carry, index):
        grad_keys, grad_values = carry
        start = index * block_rows
        query_block = lax.dynamic_slice_in_dim(queries_three, start, block_rows, 0)
        grad_block = lax.dynamic_slice_in_dim(grad_three, start, block_rows, 0)
        logistic, allowed = score_block(query_block, start, keys_three, count)
        attn_weight = (logistic * allowed).astype(jnp.bfloat16)
        grad_weight = jnp.einsum(
            "qhd,khd->hqk", grad_block, values_three, preferred_element_type=jnp.float32
        )
        grad_score = (grad_weight * logistic * (1.0 - logistic) * allowed * head_scale).astype(
            jnp.bfloat16
        )
        grad_query_block = jnp.einsum(
            "hqk,khd->qhd", grad_score, keys_three, preferred_element_type=jnp.float32
        )
        grad_keys = grad_keys + jnp.einsum(
            "hqk,qhd->khd", grad_score, query_block, preferred_element_type=jnp.float32
        )
        grad_values = grad_values + jnp.einsum(
            "hqk,qhd->khd", attn_weight, grad_block, preferred_element_type=jnp.float32
        )
        return ((grad_keys, grad_values), grad_query_block)

    zeros = jnp.zeros(keys_three.shape, jnp.float32)
    (grad_keys, grad_values), grad_queries = lax.scan(
        one_block, (zeros, zeros), jnp.arange(length // block_rows)
    )
    return (
        grad_queries.reshape(length, -1).astype(jnp.bfloat16),
        grad_keys.reshape(length, -1).astype(jnp.bfloat16),
        grad_values.reshape(length, -1).astype(jnp.bfloat16),
    )


def norm_backward(grad_normed, field, scale, gain):
    unit = field * scale
    weighted = grad_normed * gain
    grad_field = scale * (weighted - unit * jnp.mean(weighted * unit, axis=1, keepdims=True))
    return (grad_field, jnp.sum(grad_normed * unit, axis=0))


def on_device(
    inputs,
    counts,
    cotangent,
    gain_attn,
    w_query,
    w_key,
    w_value,
    w_output,
    gain_ffn,
    w_gate,
    w_up,
    w_down,
):
    attn_set = (
        lax.all_gather(gain_attn.astype(jnp.bfloat16), "dp", axis=0, tiled=True),
        lax.all_gather(w_query.astype(jnp.bfloat16), "dp", axis=0, tiled=True),
        lax.all_gather(w_key.astype(jnp.bfloat16), "dp", axis=0, tiled=True),
        lax.all_gather(w_value.astype(jnp.bfloat16), "dp", axis=0, tiled=True),
        lax.all_gather(w_output.astype(jnp.bfloat16), "dp", axis=1, tiled=True),
    )
    ffn_set = (
        lax.all_gather(gain_ffn.astype(jnp.bfloat16), "dp", axis=0, tiled=True),
        lax.all_gather(w_gate.astype(jnp.bfloat16), "dp", axis=0, tiled=True),
        lax.all_gather(w_up.astype(jnp.bfloat16), "dp", axis=0, tiled=True),
        lax.all_gather(w_down.astype(jnp.bfloat16), "dp", axis=1, tiled=True),
    )
    length = inputs.shape[0]
    block_rows = min(512, length)
    count = counts[0]
    valid = (jnp.arange(length) < count).astype(jnp.float32)[:, None]
    source = inputs.astype(jnp.float32)
    gain_in, query_w, key_w, value_w, output_w = attn_set
    gain_in_f = gain_in.astype(jnp.float32)
    scale_in = lax.rsqrt(jnp.mean(source * source, axis=1, keepdims=True) + EPS)
    normed_in = (source * scale_in * gain_in_f).astype(jnp.bfloat16)
    queries = jnp.dot(normed_in, query_w, preferred_element_type=jnp.float32).astype(jnp.bfloat16)
    keys = jnp.dot(normed_in, key_w, preferred_element_type=jnp.float32).astype(jnp.bfloat16)
    values = jnp.dot(normed_in, value_w, preferred_element_type=jnp.float32).astype(jnp.bfloat16)
    shape_three = (length, -1, HD)
    queries_three = queries.reshape(shape_three)
    keys_three = keys.reshape(shape_three)
    values_three = values.reshape(shape_three)
    attended = attend_forward(queries_three, keys_three, values_three, count, block_rows)
    attn_terms = jnp.dot(attended, output_w, preferred_element_type=jnp.float32)
    gain_mid, gate_w, up_w, down_w = ffn_set
    gain_mid_f = gain_mid.astype(jnp.float32)
    hidden_state = source + lax.psum(attn_terms, "mp")
    scale_mid = lax.rsqrt(jnp.mean(hidden_state * hidden_state, axis=1, keepdims=True) + EPS)
    normed_mid = (hidden_state * scale_mid * gain_mid_f).astype(jnp.bfloat16)
    gate_value = jnp.dot(normed_mid, gate_w, preferred_element_type=jnp.float32).astype(
        jnp.bfloat16
    )
    up_value = jnp.dot(normed_mid, up_w, preferred_element_type=jnp.float32).astype(jnp.bfloat16)
    gate_float = gate_value.astype(jnp.float32)
    up_float = up_value.astype(jnp.float32)
    gate_logistic = jax.nn.sigmoid(gate_float)
    silu_value = gate_float * gate_logistic
    inner = (silu_value * up_float).astype(jnp.bfloat16)
    ffn_terms = jnp.dot(inner, down_w, preferred_element_type=jnp.float32)
    layer_out = (
        hidden_state + lax.psum(ffn_terms.astype(jnp.bfloat16), "mp").astype(jnp.float32)
    ).astype(jnp.bfloat16)
    grad_ffn = cotangent.astype(jnp.float32) * valid
    grad_ffn_low = grad_ffn.astype(jnp.bfloat16)
    grad_down = jnp.einsum("tf,td->fd", inner, grad_ffn_low, preferred_element_type=jnp.float32)
    grad_inner = jnp.einsum("td,fd->tf", grad_ffn_low, down_w, preferred_element_type=jnp.float32)
    grad_gate = (
        grad_inner * up_float * gate_logistic * (1.0 + gate_float * (1.0 - gate_logistic))
    ).astype(jnp.bfloat16)
    grad_up = (grad_inner * silu_value).astype(jnp.bfloat16)
    grad_gate_w = jnp.einsum("td,tf->df", normed_mid, grad_gate, preferred_element_type=jnp.float32)
    grad_up_w = jnp.einsum("td,tf->df", normed_mid, grad_up, preferred_element_type=jnp.float32)
    mid_terms = jnp.einsum(
        "tf,df->td", grad_gate, gate_w, preferred_element_type=jnp.float32
    ) + jnp.einsum("tf,df->td", grad_up, up_w, preferred_element_type=jnp.float32)
    grad_mid = lax.psum(mid_terms, "mp")
    grad_hidden_norm, grad_gain_mid = norm_backward(grad_mid, hidden_state, scale_mid, gain_mid_f)
    grad_hidden = grad_ffn + grad_hidden_norm
    grad_attn_low = grad_hidden.astype(jnp.bfloat16)
    grad_output_w = jnp.einsum(
        "tc,td->cd", attended, grad_attn_low, preferred_element_type=jnp.float32
    )
    grad_attended = jnp.einsum(
        "td,cd->tc", grad_attn_low, output_w, preferred_element_type=jnp.float32
    ).astype(jnp.bfloat16)
    grad_queries, grad_keys, grad_values = attend_backward(
        queries_three,
        keys_three,
        values_three,
        grad_attended.reshape(shape_three),
        count,
        block_rows,
    )
    grad_query_w = jnp.einsum(
        "td,tc->dc", normed_in, grad_queries, preferred_element_type=jnp.float32
    )
    grad_key_w = jnp.einsum("td,tc->dc", normed_in, grad_keys, preferred_element_type=jnp.float32)
    grad_value_w = jnp.einsum(
        "td,tc->dc", normed_in, grad_values, preferred_element_type=jnp.float32
    )
    in_terms = (
        jnp.einsum("tc,dc->td", grad_queries, query_w, preferred_element_type=jnp.float32)
        + jnp.einsum("tc,dc->td", grad_keys, key_w, preferred_element_type=jnp.float32)
        + jnp.einsum("tc,dc->td", grad_values, value_w, preferred_element_type=jnp.float32)
    )
    grad_in = lax.psum(in_terms.astype(jnp.bfloat16), "mp").astype(jnp.float32)
    grad_source, grad_gain_in = norm_backward(grad_in, source, scale_in, gain_in_f)
    input_grad = grad_hidden + grad_source
    every_shard = (
        lax.psum_scatter(
            grad_gain_in.astype(jnp.bfloat16), "dp", scatter_dimension=0, tiled=True
        ).astype(jnp.float32),
        lax.psum_scatter(
            grad_query_w.astype(jnp.bfloat16), "dp", scatter_dimension=0, tiled=True
        ).astype(jnp.float32),
        lax.psum_scatter(
            grad_key_w.astype(jnp.bfloat16), "dp", scatter_dimension=0, tiled=True
        ).astype(jnp.float32),
        lax.psum_scatter(
            grad_value_w.astype(jnp.bfloat16), "dp", scatter_dimension=0, tiled=True
        ).astype(jnp.float32),
        lax.psum_scatter(
            grad_output_w.astype(jnp.bfloat16), "dp", scatter_dimension=1, tiled=True
        ).astype(jnp.float32),
        lax.psum_scatter(
            grad_gain_mid.astype(jnp.bfloat16), "dp", scatter_dimension=0, tiled=True
        ).astype(jnp.float32),
        lax.psum_scatter(
            grad_gate_w.astype(jnp.bfloat16), "dp", scatter_dimension=0, tiled=True
        ).astype(jnp.float32),
        lax.psum_scatter(
            grad_up_w.astype(jnp.bfloat16), "dp", scatter_dimension=0, tiled=True
        ).astype(jnp.float32),
        lax.psum_scatter(
            grad_down.astype(jnp.bfloat16), "dp", scatter_dimension=1, tiled=True
        ).astype(jnp.float32),
    )
    return (
        layer_out,
        input_grad,
        every_shard[0],
        every_shard[1],
        every_shard[2],
        every_shard[3],
        every_shard[4],
        every_shard[5],
        every_shard[6],
        every_shard[7],
        every_shard[8],
    )


def solution(mesh):
    placed = (
        P("dp", None),
        P("dp"),
        P("dp", None),
        P("dp"),
        P("dp", "mp"),
        P("dp", "mp"),
        P("dp", "mp"),
        P("mp", "dp"),
        P("dp"),
        P("dp", "mp"),
        P("dp", "mp"),
        P("mp", "dp"),
    )
    return jax.shard_map(
        on_device,
        mesh=mesh,
        in_specs=placed,
        out_specs=(
            P("dp", None),
            P("dp", None),
            P("dp"),
            P("dp", "mp"),
            P("dp", "mp"),
            P("dp", "mp"),
            P("mp", "dp"),
            P("dp"),
            P("dp", "mp"),
            P("dp", "mp"),
            P("mp", "dp"),
        ),
        check_vma=False,
    )
```

profile of v0, /device:TPU:0, one launch (start us, length us, event | category | flops | bytes accessed | tf_op | source)
XLA Modules:
  0.0 1476.3 jit_solution(4266643782011365877)
XLA Ops:
  15.3 13.5 all-gather
  32.0 10.0 all-gather.10.cloned.1.call-done
  49.2 23.6 %all-gather.12.cloned.1.call-done = bf16[2048,512]{1,0:T(8,128)(2,1)} async-done(((bf16[256,512]{1,0:T(8,128)(2,1)}), bf16[2048,512]{1,0:T(8,128)(2,1)}) %all-gather.12.cloned.1.call-update) | async-done | bytes 2097168 | tf_op jit(solution)/shard_map/all_gather | solution.py:103
  79.5 24.1 %all-gather.14.cloned.1.call-done = bf16[2048,512]{1,0:T(8,128)(2,1)} async-done(((bf16[256,512]{1,0:T(8,128)(2,1)}), bf16[2048,512]{1,0:T(8,128)(2,1)}) %all-gather.14.cloned.1.call-update) | async-done | bytes 2097168 | tf_op jit(solution)/shard_map/all_gather | solution.py:104
  110.8 16.5 %while.29 = (s32[]{:T(128)}, bf16[2,512,4,128]{3,1,2,0:T(8,128)(2,1)}, s32[2]{0:T(128)S(1)}, bf16[1024,4,128]{2,0,1:T(8,128)(2,1)}, bf16[1024,4,128]{2,0,1:T(8,1...) while((s32[]{:T(128)}, ...), condition=%wide.region_2.3_spmd, body=%wide.region_1.2_spmd.sunk | while | flops 1089996288 | bytes 7870655 | solution.py:36
  136.0 7.3 fusion.60
  151.1 11.9 all-gather.1
  163.0 151.7 %all-reduce.8.cloned.1.call-done = f32[1024,2048]{1,0:T(8,128)} async-done(((f32[1024,2048]{1,0:T(8,128)}), f32[1024,2048]{1,0:T(8,128)}) %all-reduce.8.cloned.1.call-update) | async-done | bytes 8388624 | tf_op jit(solution)/shard_map/psum | solution.py:133
  326.5 73.1 %all-gather.20.cloned.1.call-done = bf16[2048,2048]{1,0:T(8,128)(2,1)} async-done(((bf16[256,2048]{1,0:T(8,128)(2,1)}), bf16[2048,2048]{1,0:T(8,128)(2,1)}) %all-gather.20.cloned.1.call-update) | async-done | bytes 8388624 | tf_op jit(solution)/shard_map/all_gather | solution.py:110
  399.6 13.9 convolution_convert_fusion.4
  413.5 69.0 %all-gather.18.cloned.1.call-done = bf16[2048,2048]{1,0:T(8,128)(2,1)} async-done(((bf16[256,2048]{1,0:T(8,128)(2,1)}), bf16[2048,2048]{1,0:T(8,128)(2,1)}) %all-gather.18.cloned.1.call-update) | async-done | bytes 8388624 | tf_op jit(solution)/shard_map/all_gather | solution.py:109
  482.5 13.9 convolution_convert_fusion.5
  496.3 68.9 %all-gather.22.cloned.1.call-done = bf16[2048,2048]{1,0:T(8,128)(2,1)} async-done(((bf16[2048,256]{1,0:T(8,128)(2,1)}), bf16[2048,2048]{1,0:T(8,128)(2,1)}) %all-gather.22.cloned.1.call-update) | async-done | bytes 8388624 | tf_op jit(solution)/shard_map/all_gather | solution.py:111
  565.2 19.7 %fusion.37 = (bf16[1024,2048]{1,0:T(8,128)(2,1)S(1)}, f32[1024,2048]{1,0:T(8,128)}) fusion(bf16[1024,2048]{1,0:T(8,128)(2,1)} %convolution_convert_fusion.4, bf16[1024,2048]{1,0:T(8,128)(2,1)} %convolution_convert_fusion.5, bf16[2048,2048]{1,0:T(8,128)(2,1)} %all-gather.22.cloned.1.call-done, bf16[1024,2048]{1,0:T(8,128)(2,1)} %param.18, f32[1024]{0:T(1024)S(1)} %fusion.66), kind=kOutput, calls=%fused_computation.56 | convolution fusion | flops 8621391872 | bytes 33558528 | tf_op jit(solution)/shard_map/td,fd->tf/dot_general | solution.py:152
  584.9 14.7 fusion.75
  599.6 18.6 %convolution_add_fusion = f32[1024,2048]{1,0:T(8,128)} fusion(f32[1024,2048]{1,0:T(8,128)} %fusion.75, bf16[2048,2048]{1,0:T(8,128)(2,1)} %all-gather.20.cloned.1.call-done, f32[1024,2048]{1,0:T(8,128)} %get-tuple-element.360, bf16[1024,2048]{1,0:T(8,128)(2,1)} %convolution_convert_fusion.5), kind=kOutput, calls=%fused_computation.78 | convolution fusion | flops 8606711808 | bytes 37748736 | tf_op jit(solution)/shard_map/tf,df->td/dot_general | solution.py:161
  618.3 170.4 %all-reduce.10.cloned.1.call-done = f32[1024,2048]{1,0:T(8,128)} async-done(((f32[1024,2048]{1,0:T(8,128)}), f32[1024,2048]{1,0:T(8,128)}) %all-reduce.10.cloned.1.call-update) | async-done | bytes 8388624 | tf_op jit(solution)/shard_map/psum | solution.py:162
  788.7 8.0 multiply_reduce_fusion
  811.3 49.5 %while.30 = (s32[]{:T(128)}, f32[1024,4,128]{0,2,1:T(8,128)}, f32[1024,4,128]{0,2,1:T(8,128)}, bf16[2,512,4,128]{3,1,2,0:T(8,128)(2,1)}, s32[2]{0:T(128)S(1)}, /...) while((s32[]{:T(128)}, f32[1024,4,128]{0,2,1:T(8,128)}, ...), condition=%wide.region_9.10_spmd.clone, body=%wide.region_8.9_spmd.clone.sunk | while | flops 2715289088 | bytes 176167424 | solution.py:69
  884.7 7.2 convolution_convert_fusion.6
  892.0 14.3 convolution_convert_fusion.2
  906.4 15.6 %convolution_convert_fusion.1 = bf16[2048,2048]{1,0:T(8,128)(2,1)} fusion(bf16[1024,2048]{1,0:T(8,128)(2,1)} %multiply_convert_fusion.12, f32[1024,2048]{1,0:T(8,128)} %get-tuple-element.360, bf16[1024,2048]{1,0:T(8,128)(2,1)} %convolution_convert_fusion.5), kind=kOutput, calls=%fused_computation.76 | convolution fusion | flops 8608808960 | bytes 25165824 | tf_op jit(solution)/shard_map/td,tf->df/dot_general | solution.py:158
  922.1 16.4 %convolution_convert_fusion.3 = bf16[1024,2048]{1,0:T(8,128)(2,1)} fusion(bf16[2048,2048]{1,0:T(8,128)(2,1)} %all-gather.22.cloned.1.call-done, bf16[1024,2048]{1,0:T(8,128)(2,1)} %convolution_convert_fusion.4, bf16[1024,2048]{1,0:T(8,128)(2,1)} %convolution_convert_fusion.5), kind=kOutput, calls=%fused_computation.79 | convolution fusion | flops 8608808960 | bytes 20971520 | tf_op jit(solution)/shard_map/dot_general | solution.py:145
  950.1 19.0 %convolution_convert_fusion = bf16[2048,2048]{1,0:T(8,128)(2,1)} fusion(bf16[1024,2048]{1,0:T(8,128)(2,1)} %param.18, f32[1024]{0:T(1024)S(1)} %copy-done.27, bf16[1024,2048]{1,0:T(8,128)(2,1)} %convolution_convert_fusion.4, bf16[1024,2048]{1,0:T(8,128)(2,1)} %convolution_convert_fusion.5), kind=kOutput, calls=%fused_computation.75 | convolution fusion | flops 8617197568 | bytes 20975616 | tf_op jit(solution)/shard_map/tf,td->fd/dot_general | solution.py:151
  974.6 6.7 reduce-scatter.12.cloned.1.call-done
  983.1 35.0 %reduce-scatter.14.cloned.1.call-done = bf16[512,256]{1,0:T(8,128)(2,1)} async-done(((bf16[512,2048]{1,0:T(8,128)(2,1)}), bf16[512,256]{1,0:T(8,128)(2,1)}) %reduce-scatter.14.cloned.1.call-update) | async-done | bytes 262160 | tf_op jit(solution)/shard_map/reduce_scatter | solution.py:208
  1019.9 88.6 %reduce-scatter.16.cloned.1.call-done = bf16[256,2048]{1,0:T(8,128)(2,1)} async-done(((bf16[2048,2048]{1,0:T(8,128)(2,1)}), bf16[256,2048]{1,0:T(8,128)(2,1)}) %reduce-scatter.16.cloned.1.call-update) | async-done | bytes 1048592 | tf_op jit(solution)/shard_map/reduce_scatter | solution.py:214
  1111.3 87.4 %reduce-scatter.18.cloned.1.call-done = bf16[256,2048]{1,0:T(8,128)(2,1)} async-done(((bf16[2048,2048]{1,0:T(8,128)(2,1)}), bf16[256,2048]{1,0:T(8,128)(2,1)}) %reduce-scatter.18.cloned.1.call-update) | async-done | bytes 1048592 | tf_op jit(solution)/shard_map/reduce_scatter | solution.py:217
  1201.5 172.4 %all-reduce.12.cloned.1.call-done = (bf16[1024,2048]{1,0:T(8,128)(2,1)}, bf16[1024,2048]{1,0:T(8,128)(2,1)}) async-done(((bf16[1024,2048]{1,0:T(8,128)(2,1)}, bf16[1024,2048]{1,0:T(8,128)(2,1)}), (bf16[1024,2048]{1,0:T(8,128)(2,1)}, bf16[1024,2048]{1,0:T(8,128)(2,1)})) %all-reduce.12.cloned.1.call-update) | async-done | bytes 8388624 | tf_op jit(solution)/shard_map/psum | solution.py:147
  1378.8 17.1 %all-reduce.2 = (bf16[2048]{0:T(1024)(128)(2,1)S(1)}, bf16[2048]{0:T(1024)(128)(2,1)S(1)}) all-reduce(bf16[2048]{0:T(1024)(128)(2,1)S(1)} %get-tuple-element.317, bf16[2048]{0:T(1024)(128)(2,1)S(1)} %copy-done.28), channel_id=2, replica_groups=mesh['dp'=8,'mp'=4] {'dp'}, use_global_device_ids=true, to_apply=%region_13.14.clone | all-reduce | flops 4096 | bytes 16384
  1396.6 16.8 %fusion.33 = (f32[1024,2048]{1,0:T(8,128)}, bf16[1024,2048]{1,0:T(8,128)(2,1)}) fusion(f32[1024,2048]{1,0:T(8,128)} %copy-done.5, bf16[1024,2048]{1,0:T(8,128)(2,1)} %get-tuple-element.356, bf16[1024,2048]{1,0:T(8,128)(2,1)} %param.16, f32[1024]{0:T(1024)S(1)} %broadcast_multiply_fusion, f32[2048]{0:T(1024)S(1)} %bitcast.122, f32[1024]{0:T(1024)S(1)} %copy-done.25, ...), kind=kLoop, calls=%fused_computation.52 | loop fusion | flops 23068672 | bytes 41959424 | tf_op jit(solution)/shard_map/add | solution.py:194
  1413.4 53.5 %reduce-scatter.20.cloned.1.call-done = bf16[2048,256]{1,0:T(8,128)(2,1)} async-done(((bf16[2048,2048]{1,0:T(8,128)(2,1)}), bf16[2048,256]{1,0:T(8,128)(2,1)}) %reduce-scatter.20.cloned.1.call-update) | async-done | bytes 1048592 | tf_op jit(solution)/shard_map/reduce_scatter | solution.py:220
  (206 shorter events, 195.0 us)
Async XLA Ops:
  7.2 34.9 %all-gather.10.cloned.1.call-start = ((), (), s32[]{:S(2)}) async-start(), calls=%async_computation.7 | async-start | bytes 2359296 | tf_op jit(solution)/shard_map/all_gather | solution.py:102
  9.0 63.8 %all-gather.12.cloned.1.call-start = ((), (), s32[]{:S(2)}) async-start(), calls=%async_computation.8 | async-start | bytes 2359296 | tf_op jit(solution)/shard_map/all_gather | solution.py:103
  10.9 92.8 %all-gather.14.cloned.1.call-start = ((), (), s32[]{:S(2)}) async-start(), calls=%async_computation.9 | async-start | bytes 2359296 | tf_op jit(solution)/shard_map/all_gather | solution.py:104
  12.7 123.3 %all-gather.16.cloned.1.call-start = ((), (), s32[]{:S(2)}) async-start(), calls=%async_computation.10 | async-start | bytes 2359296 | tf_op jit(solution)/shard_map/all_gather | solution.py:105
  14.6 300.1 %all-reduce.8.cloned.1.call-start = ((), (), s32[]{:S(2)}) async-start(), calls=%async_computation.11 | async-start | bytes 16777216 | tf_op jit(solution)/shard_map/psum | solution.py:133
  28.9 74.8 %copy-start.22 = (f32[8,1,256]{2,1,0:T(1,128)}, f32[8,1,256]{2,1,0:T(1,128)S(1)}, u32[]{:S(2)}) copy-start(f32[8,1,256]{2,1,0:T(1,128)S(1)} %convert_element_type.282) | copy-start | bytes 24580
  32.0 71.7 %copy-start.24 = (f32[1024]{0:T(1024)}, f32[1024]{0:T(1024)S(1)}, u32[]{:S(2)}) copy-start(f32[1024]{0:T(1024)S(1)} %add_rsqrt_fusion.1) | copy-start | bytes 12292
  129.4 14.0 copy-start.15
  143.4 7.7 copy-start.31
  143.4 256.2 %all-gather.20.cloned.1.call-start = ((), (), s32[]{:S(2)}) async-start(), calls=%async_computation.13 | async-start | bytes 9437184 | tf_op jit(solution)/shard_map/all_gather | solution.py:110
  146.4 336.1 %all-gather.18.cloned.1.call-start = ((), (), s32[]{:S(2)}) async-start(), calls=%async_computation.12 | async-start | bytes 9437184 | tf_op jit(solution)/shard_map/all_gather | solution.py:109
  149.2 416.0 %all-gather.22.cloned.1.call-start = ((), (), s32[]{:S(2)}) async-start(), calls=%async_computation.14 | async-start | bytes 9437184 | tf_op jit(solution)/shard_map/all_gather | solution.py:111
  150.4 638.3 %all-reduce.10.cloned.1.call-start = ((), (), s32[]{:S(2)}) async-start(), calls=%async_computation.15 | async-start | bytes 16777216 | tf_op jit(solution)/shard_map/psum | solution.py:162
  163.0 633.7 %copy-start.26 = (f32[1024]{0:T(1024)}, f32[1024]{0:T(1024)S(1)}, u32[]{:S(2)}) copy-start(f32[1024]{0:T(1024)S(1)} %fusion.66) | copy-start | bytes 12292
  584.9 14.7 copy-start.33
  618.2 352.8 %reduce-scatter.8.cloned.1.call-start = ((), (), s32[]{:S(2)}) async-start(), calls=%async_computation.16 | async-start | bytes 2359296 | tf_op jit(solution)/shard_map/reduce_scatter | solution.py:199
  788.7 8.2 copy-start.9
  788.7 9.4 copy-start.12
  811.3 52.6 %copy-start.23 = (f32[8,1,256]{2,1,0:T(1,128)S(1)}, f32[8,1,256]{2,1,0:T(1,128)}, u32[]{:S(2)}) copy-start(f32[8,1,256]{2,1,0:T(1,128)} %copy-done.22) | copy-start | bytes 24580
  811.3 52.6 %copy-start.25 = (f32[1024]{0:T(1024)S(1)}, f32[1024]{0:T(1024)}, u32[]{:S(2)}) copy-start(f32[1024]{0:T(1024)} %copy-done.24) | copy-start | bytes 12292
  812.6 7.2 copy-start.10
  836.9 7.2 copy-start.10
  870.3 102.6 %reduce-scatter.10.cloned.1.call-start = ((), (), s32[]{:S(2)}) async-start(), calls=%async_computation.17 | async-start | bytes 2359296 | tf_op jit(solution)/shard_map/reduce_scatter | solution.py:202
  878.0 103.4 %reduce-scatter.12.cloned.1.call-start = ((), (), s32[]{:S(2)}) async-start(), calls=%async_computation.18 | async-start | bytes 2359296 | tf_op jit(solution)/shard_map/reduce_scatter | solution.py:205
  884.7 133.4 %reduce-scatter.14.cloned.1.call-start = ((), (), s32[]{:S(2)}) async-start(), calls=%async_computation.19 | async-start | bytes 2359296 | tf_op jit(solution)/shard_map/reduce_scatter | solution.py:208
  892.0 216.5 %reduce-scatter.16.cloned.1.call-start = ((), (), s32[]{:S(2)}) async-start(), calls=%async_computation.20 | async-start | bytes 9437184 | tf_op jit(solution)/shard_map/reduce_scatter | solution.py:214
  906.4 292.3 %reduce-scatter.18.cloned.1.call-start = ((), (), s32[]{:S(2)}) async-start(), calls=%async_computation.21 | async-start | bytes 9437184 | tf_op jit(solution)/shard_map/reduce_scatter | solution.py:217
  922.0 451.8 %all-reduce.12.cloned.1.call-start = ((), (), s32[]{:S(2)}) async-start(), calls=%async_computation.23 | async-start | bytes 16777216 | tf_op jit(solution)/shard_map/psum | solution.py:147
  922.1 16.4 %copy-start.21 = (bf16[2,512,4,128]{3,2,1,0:T(4,128)(2,1)S(1)}, bf16[2,512,4,128]{3,2,1,0:T(4,128)(2,1)}, u32[]{:S(2)}) copy-start(bf16[2,512,4,128]{3,2,1,0:T(4,128)(2,1)} %copy-done.20) | copy-start | bytes 3145732
  922.1 16.4 %copy-start.29 = (bf16[2048,512]{1,0:T(8,128)(2,1)S(1)}, bf16[2048,512]{1,0:T(8,128)(2,1)}, u32[]{:S(2)}) copy-start(bf16[2048,512]{1,0:T(8,128)(2,1)} %all-gather.10.cloned.1.call-done) | copy-start | bytes 6291460
  949.4 517.4 %reduce-scatter.20.cloned.1.call-start = ((), (), s32[]{:S(2)}) async-start(), calls=%async_computation.22 | async-start | bytes 9437184 | tf_op jit(solution)/shard_map/reduce_scatter | solution.py:220
  972.8 406.0 %copy-start.28 = (bf16[2048]{0:T(1024)(128)(2,1)S(1)}, bf16[2048]{0:T(1024)(128)(2,1)}, u32[]{:S(2)}) copy-start(bf16[2048]{0:T(1024)(128)(2,1)} %get-tuple-element.315) | copy-start | bytes 12292
  (28 other events, 110.0 us)
Sparse Core Ops, SparseCore 0:
  10.2 31.8 all-gather.9
  44.2 28.5 all-gather.11
  75.0 28.5 all-gather.13
  105.7 30.3 all-gather.15
  143.5 171.1 all-reduce.7
  316.8 82.7 all-gather.19
  401.9 80.5 all-gather.17
  484.1 81.0 all-gather.21
  618.4 170.2 all-reduce.9
  870.4 36.4 reduce-scatter.7
  909.7 34.3 reduce-scatter.9
  946.8 34.4 reduce-scatter.11
  983.6 34.4 reduce-scatter.13
  1020.3 88.2 reduce-scatter.15
  1110.7 87.9 reduce-scatter.17
  1202.9 170.9 all-reduce.11
  1376.1 90.7 reduce-scatter.19
where the time goes:
time: 1480 us
  waiting for transfers between devices  1040 us (70%)
  matrix products  260 us (18%)
  other arithmetic  82.1 us (6%)
  blocking collectives  42.5 us (3%)
  local copies, waits for them, and re-layouts  30.6 us (2%)
  between operations  15.8 us (1%)
    psum x1, waiting for transfers between devices, on_device(): lax.psum(ffn_terms.astype(jnp.bfloat16), 'mp').astype(jnp.float32)  172 us
    psum x1, waiting for transfers between devices, on_device(): grad_mid = lax.psum(mid_terms, 'mp')  170 us
    psum x1, waiting for transfers between devices, on_device(): hidden_state = source + lax.psum(attn_terms, 'mp')  152 us
    reduce_scatter x1, waiting for transfers between devices, on_device(): lax.psum_scatter(grad_gate_w.astype(jnp.bfloat16), 'dp', scatter_dimensio...  88.6 us
    reduce_scatter x1, waiting for transfers between devices, on_device(): lax.psum_scatter(grad_up_w.astype(jnp.bfloat16), 'dp', scatter_dimension=...  87.4 us
    all_gather x1, waiting for transfers between devices, on_device(): lax.all_gather(w_up.astype(jnp.bfloat16), 'dp', axis=0, tiled=True)  73.1 us
    all_gather x1, waiting for transfers between devices, on_device(): lax.all_gather(w_gate.astype(jnp.bfloat16), 'dp', axis=0, tiled=True)  69 us
    all_gather x1, waiting for transfers between devices, on_device(): lax.all_gather(w_down.astype(jnp.bfloat16), 'dp', axis=1, tiled=True)  68.9 us
  transfers between devices with their start and end apart: 17, of which 15 were waited for; matrix products, arithmetic and copies ran while one was open for 15% of the time, Pallas kernels for 0%

commit v1 on v0

v1 whole, which is shorter than its diff:
```python
import functools
import math

import jax
import jax.numpy as jnp
from jax import lax
from jax.experimental import pallas as pl
from jax.experimental.pallas import tpu as pltpu
from jax.sharding import PartitionSpec as P

HD = 128
EPS = 1e-06
BF = jnp.bfloat16
F32 = jnp.float32
NT = (((1,), (1,)), ((), ()))
TN = (((0,), (0,)), ((), ()))
NN = (((1,), (0,)), ((), ()))


def dot(a, b, dims=NN):
    return lax.dot_general(a, b, dims, preferred_element_type=F32)


def logistic_block(q, k, seq):
    raw = dot(q, k, NT)
    shifted = math.log(seq) - raw * HD ** (-0.5)
    return 1.0 / (1.0 + jnp.exp(shifted))


def allowed_block(row0, rows, col0, cols, count):
    ri = row0 + lax.broadcasted_iota(jnp.int32, (rows, cols), 0)
    ci = col0 + lax.broadcasted_iota(jnp.int32, (rows, cols), 1)
    return (ci <= ri) & (ci < count)


def attn_fwd_kernel(seq, blk, count_ref, q_ref, k_ref, v_ref, o_ref):
    count = count_ref[0]
    for i in range(seq // blk):
        rows = pl.ds(i * blk, blk)
        width = (i + 1) * blk
        lg = logistic_block(q_ref[rows, :], k_ref[pl.ds(0, width), :], seq)
        w = jnp.where(allowed_block(i * blk, blk, 0, width, count), lg, 0.0).astype(BF)
        o_ref[rows, :] = dot(w, v_ref[pl.ds(0, width), :]).astype(BF)


def attn_fwd(qkv, count, seq):
    heads = qkv.shape[1] // (3 * HD)
    blk = min(256, seq)
    spec = lambda part: pl.BlockSpec((seq, HD), lambda h, c: (0, part * heads + h))
    return pl.pallas_call(
        functools.partial(attn_fwd_kernel, seq, blk),
        grid_spec=pltpu.PrefetchScalarGridSpec(
            num_scalar_prefetch=1,
            grid=(heads,),
            in_specs=[spec(0), spec(1), spec(2)],
            out_specs=pl.BlockSpec((seq, HD), lambda h, c: (0, h)),
        ),
        out_shape=jax.ShapeDtypeStruct((seq, heads * HD), BF),
        compiler_params=pltpu.CompilerParams(vmem_limit_bytes=48 * 1024 * 1024),
        name="attn_fwd",
    )(count, qkv, qkv, qkv)


def attn_bwd_kernel(seq, blk, count_ref, q_ref, k_ref, v_ref, g_ref, dq_ref, dk_ref, dv_ref, dka, dva):
    count = count_ref[0]
    n = seq // blk
    for i in range(n - 1, -1, -1):
        rows = pl.ds(i * blk, blk)
        width = (i + 1) * blk
        keys = pl.ds(0, width)
        q = q_ref[rows, :]
        g = g_ref[rows, :]
        k = k_ref[keys, :]
        lg = jnp.where(
            allowed_block(i * blk, blk, 0, width, count), logistic_block(q, k, seq), 0.0
        )
        w = lg.astype(BF)
        gw = dot(g, v_ref[keys, :], NT)
        gs = (gw * lg * (1.0 - lg) * HD ** (-0.5)).astype(BF)
        dq_ref[rows, :] = dot(gs, k).astype(BF)
        dk = dot(gs, q, TN)
        dv = dot(w, g, TN)
        if i == n - 1:
            dka[...] = dk
            dva[...] = dv
        else:
            dka[keys, :] += dk
            dva[keys, :] += dv
    dk_ref[...] = dka[...].astype(BF)
    dv_ref[...] = dva[...].astype(BF)


def attn_bwd(qkv, grad, count, seq):
    heads = qkv.shape[1] // (3 * HD)
    blk = min(256, seq)
    spec = lambda part: pl.BlockSpec((seq, HD), lambda h, c: (0, part * heads + h))
    out = jax.ShapeDtypeStruct((seq, heads * HD), BF)
    return pl.pallas_call(
        functools.partial(attn_bwd_kernel, seq, blk),
        grid_spec=pltpu.PrefetchScalarGridSpec(
            num_scalar_prefetch=1,
            grid=(heads,),
            in_specs=[spec(0), spec(1), spec(2), spec(0)],
            out_specs=[spec(0)] * 3,
            scratch_shapes=[pltpu.VMEM((seq, HD), F32), pltpu.VMEM((seq, HD), F32)],
        ),
        out_shape=[out, out, out],
        compiler_params=pltpu.CompilerParams(vmem_limit_bytes=48 * 1024 * 1024),
        name="attn_bwd",
    )(count, qkv, qkv, qkv, grad)


def norm_backward(grad_normed, field, scale, gain):
    unit = field * scale
    weighted = grad_normed * gain
    grad_field = scale * (weighted - unit * jnp.mean(weighted * unit, axis=1, keepdims=True))
    return (grad_field, jnp.sum(grad_normed * unit, axis=0))


def after(value, *deps):
    return lax.optimization_barrier((value,) + deps)[0]


def on_device(
    inputs,
    counts,
    cotangent,
    gain_attn,
    w_query,
    w_key,
    w_value,
    w_output,
    gain_ffn,
    w_gate,
    w_up,
    w_down,
):
    seq = inputs.shape[0]
    hh = w_query.shape[1]
    ff = w_gate.shape[1]
    mp = lax.axis_size("mp")
    me = lax.axis_index("mp")
    part = seq // mp
    gather = lambda x: lax.all_gather(x, "dp", axis=0, tiled=True)
    scatter = lambda x: lax.psum_scatter(x, "dp", scatter_dimension=0, tiled=True)
    mp_gather = lambda x: lax.all_gather(x, "mp", axis=0, tiled=True)
    mp_scatter = lambda x: lax.psum_scatter(x.astype(BF), "mp", scatter_dimension=0, tiled=True)
    mine = lambda x: lax.dynamic_slice_in_dim(x, me * part, part, 0)

    attn_shard = jnp.concatenate([w_query, w_key, w_value, w_output.T], axis=1).astype(BF)
    attn_w = gather(attn_shard)
    gu_shard = jnp.concatenate([w_gate, w_up], axis=1).astype(BF)
    gu_w = gather(after(gu_shard, attn_w))
    down_shard = w_down.T.astype(BF)
    down_w = gather(after(down_shard, gu_w))
    gains = lax.all_gather(jnp.stack([gain_attn, gain_ffn]).astype(BF), "dp", axis=1, tiled=True)
    gains = gains.astype(F32)
    gain_in, gain_mid = gains[0:1], gains[1:2]

    count = counts[0]
    valid = (jnp.arange(seq) < count)[:, None]
    source = inputs.astype(F32)
    scale_in = lax.rsqrt(jnp.mean(source * source, axis=1, keepdims=True) + EPS)
    normed_in = (source * scale_in * gain_in).astype(BF)
    qkv = dot(normed_in, attn_w[:, : 3 * hh]).astype(BF)
    attended = attn_fwd(qkv, counts, seq)
    out_wt = attn_w[:, 3 * hh :]
    attn_sum = mp_scatter(dot(attended, out_wt, NT))
    my_source = mine(inputs).astype(F32)
    hidden = my_source + attn_sum.astype(F32)
    scale_mid = lax.rsqrt(jnp.mean(hidden * hidden, axis=1, keepdims=True) + EPS)
    normed_mid = mp_gather((hidden * scale_mid * gain_mid).astype(BF))
    gate_w, up_w = gu_w[:, :ff], gu_w[:, ff:]
    gate = dot(normed_mid, gate_w).astype(BF)
    up = dot(normed_mid, up_w).astype(BF)
    gate_f = gate.astype(F32)
    up_f = up.astype(F32)
    sg = jax.nn.sigmoid(gate_f)
    silu = gate_f * sg
    inner = (silu * up_f).astype(BF)
    grad_ffn = jnp.where(valid, cotangent, jnp.zeros_like(cotangent))
    grad_down_t = dot(grad_ffn, inner, TN).astype(BF)
    grad_inner = dot(grad_ffn, down_w)
    grad_gate = (grad_inner * up_f * sg * (1.0 + gate_f * (1.0 - sg))).astype(BF)
    grad_up = (grad_inner * silu).astype(BF)
    mid_terms = dot(grad_gate, gate_w, NT) + dot(grad_up, up_w, NT)
    grad_mid = mp_scatter(mid_terms).astype(F32)
    rs_down = scatter(grad_down_t)
    grad_gu = jnp.concatenate(
        [dot(normed_mid, grad_gate, TN).astype(BF), dot(normed_mid, grad_up, TN).astype(BF)], axis=1
    )
    rs_gu = scatter(after(grad_gu, rs_down))
    ffn_sum = mp_scatter(dot(inner, down_w, NT))
    layer_out = mp_gather((hidden + ffn_sum.astype(F32)).astype(BF))

    g_norm, g_gain_mid = norm_backward(grad_mid, hidden, scale_mid, gain_mid)
    grad_hidden = mine(grad_ffn).astype(F32) + g_norm
    grad_low = mp_gather(grad_hidden.astype(BF))
    grad_attended = dot(grad_low, out_wt).astype(BF)
    dq, dk, dv = attn_bwd(qkv, grad_attended, counts, seq)
    grads = [dq, dk, dv]
    grad_attn = jnp.concatenate(
        [dot(normed_in, g, TN).astype(BF) for g in grads] + [dot(grad_low, attended, TN).astype(BF)],
        axis=1,
    )
    rs_attn = scatter(after(grad_attn, rs_gu))
    in_terms = sum(dot(g, attn_w[:, i * hh : (i + 1) * hh], NT) for i, g in enumerate(grads))
    grad_in = mp_scatter(in_terms).astype(F32)
    g_source, g_gain_in = norm_backward(grad_in, my_source, mine(scale_in), gain_in)
    input_grad = mp_gather((grad_hidden + g_source).astype(BF)).astype(F32)
    g_gains = lax.psum(jnp.stack([g_gain_in, g_gain_mid]), ("dp", "mp"))
    width = g_gains.shape[1] // lax.axis_size("dp")
    g_gains = lax.dynamic_slice_in_dim(g_gains, lax.axis_index("dp") * width, width, 1)
    rs_attn = rs_attn.astype(F32)
    rs_gu = rs_gu.astype(F32)
    return (
        layer_out,
        input_grad,
        g_gains[0],
        rs_attn[:, :hh],
        rs_attn[:, hh : 2 * hh],
        rs_attn[:, 2 * hh : 3 * hh],
        rs_attn[:, 3 * hh :].T,
        g_gains[1],
        rs_gu[:, :ff],
        rs_gu[:, ff:],
        rs_down.astype(F32).T,
    )


def solution(mesh):
    row, both, swapped = P("dp", None), P("dp", "mp"), P("mp", "dp")
    weights = (both, both, both, swapped)
    ffn = (both, both, swapped)
    return jax.shard_map(
        on_device,
        mesh=mesh,
        in_specs=(row, P("dp"), row, P("dp")) + weights + (P("dp"),) + ffn,
        out_specs=(row, row, P("dp")) + weights + (P("dp"),) + ffn,
        check_vma=False,
    )
```

time: 1480 us -> 1230 us (0.83)
  waiting for transfers between devices: 1040 us -> 852 us
  matrix products: 260 us -> 195 us
  other arithmetic: 82.1 us -> 54.6 us
  Pallas kernels: 0 us -> 18.2 us
    psum x3 -> x0, waiting for transfers between devices: 494 us -> none  [the longest x1 172 us: on_device(): lax.psum(ffn_terms.astype(jnp.bfloat16), 'mp').astype(jnp.float32)]
    reduce_scatter x7, waiting for transfers between devices: 271 us -> 424 us  [the longest x3 223 us: on_device(): lax.psum_scatter(x, 'dp', scatter_dimension=0, tiled=True)]
    all_gather x7, waiting for transfers between devices: 275 us -> 427 us  [the longest x3 273 us: on_device(): gather = lambda x: lax.all_gather(x, 'dp', axis=0, tiled=True)]
    dot_general x33 -> x19, matrix products: 260 us -> 195 us  [dot(): return lax.dot_general(a, b, dims, preferred_element_type=F32)]
    psum x0 -> x1, blocking collectives: none -> 38.5 us  [on_device(): g_gains = lax.psum(jnp.stack([g_gain_in, g_gain_mid]), ('dp', 'mp'))]
    add x6 -> x0, other arithmetic: 22.4 us -> none  [the longest x1 16.8 us: on_device(): input_grad = grad_hidden + grad_source]
    pallas_call x0 -> x2, Pallas kernels: none -> 18.2 us  [the longest x1 12.4 us: attn_bwd(): pl.pallas_call(functools.partial(attn_bwd_kernel, seq, blk), grid_spec=pl...]
    concatenate x0 -> x4, other arithmetic: none -> 17.4 us  [the longest x1 10.8 us: on_device(): jnp.concatenate([dot(normed_mid, grad_gate, TN).astype(BF), dot(normed_mi...]
  transfers between devices with their start and end apart: 17 -> 14, of which waited for: 15 -> 13; matrix products, arithmetic and copies ran while one was open for 15% -> 15% of each run, Pallas kernels for 0% -> 1%
where the time goes in v1:
time: 1230 us; the launch traced here: 1210 us
  waiting for transfers between devices  852 us (69%)
  matrix products  195 us (16%)
  other arithmetic  54.6 us (4%)
  blocking collectives  51.9 us (4%)
  local copies, waits for them, and re-layouts  26.6 us (2%)
  Pallas kernels  18.2 us (1%)
  between operations  15.2 us (1%)
    all_gather x3, waiting for transfers between devices, on_device(): gather = lambda x: lax.all_gather(x, 'dp', axis=0, tiled=True)  273 us
    reduce_scatter x3, waiting for transfers between devices, on_device(): lax.psum_scatter(x, 'dp', scatter_dimension=0, tiled=True)  223 us
    reduce_scatter x4, waiting for transfers between devices, on_device(): lax.psum_scatter(x.astype(BF), 'mp', scatter_dimension=0, tiled=True)  201 us
    dot_general x19, matrix products, dot(): return lax.dot_general(a, b, dims, preferred_element_type=F32)  195 us
    all_gather x4, waiting for transfers between devices, on_device(): mp_gather = lambda x: lax.all_gather(x, 'mp', axis=0, tiled=True)  154 us
    psum x1, blocking collectives, on_device(): g_gains = lax.psum(jnp.stack([g_gain_in, g_gain_mid]), ('dp', 'mp'))  38.5 us
  transfers between devices with their start and end apart: 14, of which 13 were waited for; matrix products, arithmetic and copies ran while one was open for 15% of the time, Pallas kernels for 1%

profile of v1, /device:TPU:0, one launch (start us, length us, event | category | flops | bytes accessed | tf_op | source)
XLA Modules:
  0.0 1214.6 jit_solution(15089854074333892800)
XLA Ops:
  13.7 13.4 %all_gather.24 = bf16[2,2048]{1,0:T(2,128)(2,1)S(1)} all-gather(bf16[2,256]{1,0:T(2,128)(2,1)S(1)} %pad_maximum_fusion.5), channel_id=1, replica_groups=mesh['dp'=8,'mp'=4] {'dp'}, dimensions={1}, use_global_device_ids=true | all-gather | bytes 9216 | tf_op jit(solution)/shard_map/all_gather | solution.py:156
  30.4 67.9 %all-gather.8.cloned.1.call-done = bf16[2048,2048]{0,1:T(8,128)(2,1)} async-done(((bf16[256,2048]{0,1:T(8,128)(2,1)}), bf16[2048,2048]{0,1:T(8,128)(2,1)}) %all-gather.8.cloned.1.call-update) | async-done | bytes 8388624 | tf_op jit(solution)/shard_map/all_gather | solution.py:144
  98.3 10.1 fusion.23.q_ref.k_ref.v_ref
  108.4 5.9 attn_fwd.1
  115.3 5.9 convolution_convert_fusion.4
  126.2 46.1 %reduce-scatter.8.cloned.1.call-done = bf16[256,2048]{1,0:T(8,128)(2,1)} async-done(((bf16[1024,2048]{1,0:T(8,128)(2,1)}), bf16[256,2048]{1,0:T(8,128)(2,1)}) %reduce-scatter.8.cloned.1.call-update) | async-done | bytes 1048592 | tf_op jit(solution)/shard_map/reduce_scatter | solution.py:147
  178.4 147.4 %all-gather.12.cloned.1.call-done = bf16[2048,4096]{1,0:T(8,128)(2,1)} async-done(((bf16[256,4096]{1,0:T(8,128)(2,1)}), bf16[2048,4096]{1,0:T(8,128)(2,1)}) %all-gather.12.cloned.1.call-update) | async-done | bytes 16777232 | tf_op jit(solution)/shard_map/all_gather | solution.py:144
  330.6 48.5 %all-gather.10.cloned.1.call-done = bf16[1024,2048]{1,0:T(8,128)(2,1)} async-done(((bf16[256,2048]{1,0:T(8,128)(2,1)}), bf16[1024,2048]{1,0:T(8,128)(2,1)}) %all-gather.10.cloned.1.call-update) | async-done | bytes 4194320 | tf_op jit(solution)/shard_map/all_gather | solution.py:146
  379.1 14.6 %fusion.29 = bf16[1024,2048]{1,0:T(8,128)(2,1)} fusion(bf16[1024,2048]{1,0:T(8,128)(2,1)} %all-gather.10.cloned.1.call-done, bf16[2048,4096]{1,0:T(8,128)(2,1)} %all-gather.12.cloned.1.call-done), kind=kOutput, calls=%fused_computation.39 | convolution fusion | flops 8592031744 | bytes 16777216 | tf_op jit(solution)/shard_map/dot_general | solution.py:21
  393.7 12.7 %fusion.26 = bf16[1024,2048]{1,0:T(8,128)(2,1)} fusion(bf16[1024,2048]{1,0:T(8,128)(2,1)S(1)} %copy-done.20, bf16[2048,4096]{1,0:T(8,128)(2,1)} %all-gather.12.cloned.1.call-done), kind=kOutput, calls=%fused_computation.38 | convolution fusion | flops 8592031744 | bytes 16777216 | tf_op jit(solution)/shard_map/dot_general | solution.py:21
  406.4 57.3 %all-gather.14.cloned.1.call-done = bf16[2048,2048]{0,1:T(8,128)(2,1)} async-done(((bf16[256,2048]{0,1:T(8,128)(2,1)}), bf16[2048,2048]{0,1:T(8,128)(2,1)}) %all-gather.14.cloned.1.call-update) | async-done | bytes 8388624 | tf_op jit(solution)/shard_map/all_gather | solution.py:144
  463.7 18.3 %fusion.6 = (bf16[1024,2048]{1,0:T(8,128)(2,1)S(1)}, f32[1024,2048]{1,0:T(8,128)}) fusion(bf16[1024,2048]{1,0:T(8,128)(2,1)} %fusion.29, bf16[1024,2048]{1,0:T(8,128)(2,1)} %fusion.26, bf16[1024,2048]{1,0:T(8,128)(2,1)} %broadcast_select_fusion, bf16[2048,2048]{0,1:T(8,128)(2,1)} %all-gather.14.cloned.1.call-done), kind=kOutput, calls=%fused_computation.14 | convolution fusion | flops 8615100416 | bytes 33554432 | tf_op jit(solution)/shard_map/dot_general | solution.py:21
  482.1 18.2 %fusion.11 = f32[1024,2048]{1,0:T(8,128)} fusion(bf16[2048,4096]{1,0:T(8,128)(2,1)} %all-gather.12.cloned.1.call-done, f32[1024,2048]{1,0:T(8,128)} %get-tuple-element.52, bf16[1024,2048]{1,0:T(8,128)(2,1)} %fusion.26), kind=kOutput, calls=%fused_computation.26 | convolution fusion | flops 8604614656 | bytes 29360128 | tf_op jit(solution)/shard_map/dot_general | solution.py:21
  500.2 14.5 %add_convert_fusion.1 = bf16[1024,2048]{1,0:T(8,128)(2,1)} fusion(f32[1024,2048]{1,0:T(8,128)} %fusion.11, bf16[1024,2048]{1,0:T(8,128)(2,1)S(1)} %get-tuple-element.51, bf16[2048,4096]{1,0:T(8,128)(2,1)} %all-gather.12.cloned.1.call-done), kind=kOutput, calls=%fused_computation.21 | convolution fusion | flops 8594128896 | bytes 25165824 | tf_op jit(solution)/shard_map/dot_general | solution.py:21
  514.9 51.0 %reduce-scatter.12.cloned.1.call-done = bf16[256,2048]{1,0:T(8,128)(2,1)} async-done(((bf16[1024,2048]{1,0:T(8,128)(2,1)}), bf16[256,2048]{1,0:T(8,128)(2,1)}) %reduce-scatter.12.cloned.1.call-update) | async-done | bytes 1048592 | tf_op jit(solution)/shard_map/reduce_scatter | solution.py:147
  572.8 14.9 %convolution_convert_fusion = bf16[2048,2048]{1,0:T(8,128)(2,1)} fusion(bf16[1024,2048]{1,0:T(8,128)(2,1)} %broadcast_select_fusion, bf16[1024,2048]{1,0:T(8,128)(2,1)} %fusion.29, bf16[1024,2048]{1,0:T(8,128)(2,1)} %fusion.26), kind=kOutput, calls=%fused_computation.23 | convolution fusion | flops 8610906112 | bytes 20971520 | tf_op jit(solution)/shard_map/dot_general | solution.py:21
  587.8 37.8 %all-gather.18.cloned.1.call-done = bf16[1024,2048]{1,0:T(8,128)(2,1)} async-done(((bf16[256,2048]{1,0:T(8,128)(2,1)}), bf16[1024,2048]{1,0:T(8,128)(2,1)}) %all-gather.18.cloned.1.call-update) | async-done | bytes 4194320 | tf_op jit(solution)/shard_map/all_gather | solution.py:146
  630.9 12.4 %attn_bwd.1 = (bf16[1024,512]{1,0:T(8,128)(2,1)S(1)}, bf16[1024,512]{1,0:T(8,128)(2,1)S(1)}, bf16[1024,512]{1,0:T(8,128)(2,1)S(1)}) custom-call(s32[1]{0:T(128)} %copy.33.count_ref, bf16[1024,1536]{1,0:T(8,128)(2,1)} %copy-done, bf16[1024,1536]{1,0:T(8,128)(2,1)} %copy-done, bf16[1024,1536]{1,0:T(8,128)(2,1)} %copy-done, bf16[1024,512]{1,0:T(8,128)(2,1)S(1)} %fusion.55.g_ref), custom_call_target="tpu_custom_call" | custom-call | tf_op jit(solution)/shard_map/attn_bwd/pallas_call | solution.py:98
  647.6 7.2 fusion.47
  654.8 8.4 add_convert_fusion
  663.3 15.8 %convolution_convert_fusion.3 = bf16[1024,2048]{1,0:T(8,128)(2,1)} fusion(bf16[2048,2048]{0,1:T(8,128)(2,1)} %all-gather.14.cloned.1.call-done, bf16[1024,2048]{1,0:T(8,128)(2,1)} %fusion.29, bf16[1024,2048]{1,0:T(8,128)(2,1)} %fusion.26), kind=kOutput, calls=%fused_computation.40 | convolution fusion | flops 8608808960 | bytes 20971520 | tf_op jit(solution)/shard_map/dot_general | solution.py:21
  679.2 12.7 %convolution_convert_fusion.2 = bf16[2048,2048]{0,1:T(8,128)(2,1)S(1)} fusion(bf16[1024,2048]{1,0:T(8,128)(2,1)} %all-gather.10.cloned.1.call-done, bf16[1024,2048]{1,0:T(8,128)(2,1)} %copy-done.24), kind=kOutput, calls=%fused_computation.25 | convolution fusion | flops 8594128896 | bytes 16777216 | tf_op jit(solution)/shard_map/dot_general | solution.py:21
  691.9 17.9 %convolution_convert_fusion.1 = bf16[2048,2048]{0,1:T(8,128)(2,1)} fusion(bf16[1024,2048]{1,0:T(8,128)(2,1)S(1)} %copy-done.21, f32[1024,2048]{1,0:T(8,128)} %get-tuple-element.52, bf16[1024,2048]{1,0:T(8,128)(2,1)} %fusion.26), kind=kOutput, calls=%fused_computation.24 | convolution fusion | flops 8608808960 | bytes 25165824 | tf_op jit(solution)/shard_map/dot_general | solution.py:21
  709.8 10.8 pad_maximum_fusion
  721.3 50.3 %reduce-scatter.14.cloned.1.call-done = bf16[256,2048]{1,0:T(8,128)(2,1)} async-done(((bf16[1024,2048]{1,0:T(8,128)(2,1)}), bf16[256,2048]{1,0:T(8,128)(2,1)}) %reduce-scatter.14.cloned.1.call-update) | async-done | bytes 1048592 | tf_op jit(solution)/shard_map/reduce_scatter | solution.py:147
  774.1 53.4 %reduce-scatter.10.cloned.1.call-done = bf16[256,2048]{1,0:T(8,128)(2,1)} async-done(((bf16[1024,2048]{1,0:T(8,128)(2,1)}), bf16[256,2048]{1,0:T(8,128)(2,1)}) %reduce-scatter.10.cloned.1.call-update) | async-done | bytes 1048592 | tf_op jit(solution)/shard_map/reduce_scatter | solution.py:147
  852.4 145.7 %reduce-scatter.18.cloned.1.call-done = bf16[256,4096]{0,1:T(8,128)(2,1)} async-done(((bf16[2048,4096]{0,1:T(8,128)(2,1)}), bf16[256,4096]{0,1:T(8,128)(2,1)}) %reduce-scatter.18.cloned.1.call-update) | async-done | bytes 2097168 | tf_op jit(solution)/shard_map/reduce_scatter | solution.py:145
  1000.3 38.5 %psum.7 = f32[2,2048]{1,0:T(2,128)S(1)} all-reduce(f32[2,2048]{1,0:T(2,128)S(1)} %pad_maximum_fusion.4), channel_id=1, replica_groups=mesh['dp'=8,'mp'=4] {'dp','mp'}, use_global_device_ids=true, to_apply=%region_10.11 | all-reduce | flops 4096 | bytes 32768 | tf_op jit(solution)/shard_map/psum | solution.py:211
  1039.4 12.9 %all-gather.16.cloned.1.call-done = bf16[1024,2048]{1,0:T(8,128)(2,1)} async-done(((bf16[256,2048]{1,0:T(8,128)(2,1)}), bf16[1024,2048]{1,0:T(8,128)(2,1)}) %all-gather.16.cloned.1.call-update) | async-done | bytes 4194320 | tf_op jit(solution)/shard_map/all_gather | solution.py:146
  1052.3 55.2 %all-gather.20.cloned.1.call-done = bf16[1024,2048]{1,0:T(8,128)(2,1)} async-done(((bf16[256,2048]{1,0:T(8,128)(2,1)}), bf16[1024,2048]{1,0:T(8,128)(2,1)}) %all-gather.20.cloned.1.call-update) | async-done | bytes 4194320 | tf_op jit(solution)/shard_map/all_gather | solution.py:146
  1107.4 6.7 convert_element_type.146
  1121.4 77.8 %reduce-scatter.20.cloned.1.call-done = bf16[256,2048]{0,1:T(8,128)(2,1)} async-done(((bf16[2048,2048]{0,1:T(8,128)(2,1)}), bf16[256,2048]{0,1:T(8,128)(2,1)}) %reduce-scatter.20.cloned.1.call-update) | async-done | bytes 1048592 | tf_op jit(solution)/shard_map/reduce_scatter | solution.py:145
  (129 shorter events, 89.3 us)
Async XLA Ops:
  7.2 6.4 copy-start.22
  7.2 6.5 copy-start.23
  7.2 91.1 %all-gather.8.cloned.1.call-start = ((), (), s32[]{:S(2)}) async-start(), calls=%async_computation.7 | async-start | bytes 9437184 | tf_op jit(solution)/shard_map/all_gather | solution.py:144
  12.9 159.4 %reduce-scatter.8.cloned.1.call-start = ((), (), s32[]{:S(2)}) async-start(), calls=%async_computation.8 | async-start | bytes 5242880 | tf_op jit(solution)/shard_map/reduce_scatter | solution.py:147
  30.3 78.1 %copy-start.18 = (f32[1024]{0:T(1024)}, f32[1024]{0:T(1024)S(1)}, u32[]{:S(2)}) copy-start(f32[1024]{0:T(1024)S(1)} %add_rsqrt_fusion) | copy-start | bytes 12292
  30.3 78.1 %copy-start.15 = (f32[1,2048]{1,0:T(1,128)}, f32[1,2048]{1,0:T(1,128)S(1)}, u32[]{:S(2)}) copy-start(f32[1,2048]{1,0:T(1,128)S(1)} %get-tuple-element.50) | copy-start | bytes 24580
  108.4 5.9 copy-start
  121.3 204.4 %all-gather.12.cloned.1.call-start = ((), (), s32[]{:S(2)}) async-start(), calls=%async_computation.10 | async-start | bytes 18874368 | tf_op jit(solution)/shard_map/all_gather | solution.py:144
  126.1 51.2 %copy-start.13 = (f32[2048,256]{1,0:T(8,128)S(1)}, f32[2048,256]{1,0:T(8,128)}, u32[]{:S(2)}) copy-start(f32[2048,256]{1,0:T(8,128)} %param.23) | copy-start | bytes 6291460
  126.2 253.0 %all-gather.10.cloned.1.call-start = ((), (), s32[]{:S(2)}) async-start(), calls=%async_computation.9 | async-start | bytes 5242880 | tf_op jit(solution)/shard_map/all_gather | solution.py:146
  177.2 286.5 %all-gather.14.cloned.1.call-start = ((), (), s32[]{:S(2)}) async-start(), calls=%async_computation.11 | async-start | bytes 9437184 | tf_op jit(solution)/shard_map/all_gather | solution.py:144
  325.7 240.1 %reduce-scatter.12.cloned.1.call-start = ((), (), s32[]{:S(2)}) async-start(), calls=%async_computation.14 | async-start | bytes 5242880 | tf_op jit(solution)/shard_map/reduce_scatter | solution.py:147
  379.1 14.6 %copy-start.20 = (bf16[1024,2048]{1,0:T(8,128)(2,1)S(1)}, bf16[1024,2048]{1,0:T(8,128)(2,1)}, u32[]{:S(2)}) copy-start(bf16[1024,2048]{1,0:T(8,128)(2,1)} %all-gather.10.cloned.1.call-done) | copy-start | bytes 12582916
  482.1 18.2 %copy-start.24 = (bf16[1024,2048]{1,0:T(8,128)(2,1)}, bf16[1024,2048]{1,0:T(8,128)(2,1)S(1)}, u32[]{:S(2)}) copy-start(bf16[1024,2048]{1,0:T(8,128)(2,1)S(1)} %get-tuple-element.51) | copy-start | bytes 12582916
  514.8 51.1 %copy-start.6 = (bf16[256,2048]{1,0:T(8,128)(2,1)S(1)}, bf16[256,2048]{1,0:T(8,128)(2,1)}, u32[]{:S(2)}) copy-start(bf16[256,2048]{1,0:T(8,128)(2,1)} %reduce-scatter.8.cloned.1.call-done) | copy-start | bytes 3145732
  514.8 110.8 %all-gather.18.cloned.1.call-start = ((), (), s32[]{:S(2)}) async-start(), calls=%async_computation.15 | async-start | bytes 5242880 | tf_op jit(solution)/shard_map/all_gather | solution.py:146
  572.8 147.8 %reduce-scatter.16.cloned.1.call-start = ((), (), s32[]{:S(2)}) async-start(), calls=%async_computation.18 | async-start | bytes 9437184 | tf_op jit(solution)/shard_map/reduce_scatter | solution.py:145
  587.8 183.9 %reduce-scatter.14.cloned.1.call-start = ((), (), s32[]{:S(2)}) async-start(), calls=%async_computation.16 | async-start | bytes 5242880 | tf_op jit(solution)/shard_map/reduce_scatter | solution.py:147
  643.3 4.4 copy-start.3
  663.3 164.2 %reduce-scatter.10.cloned.1.call-start = ((), (), s32[]{:S(2)}) async-start(), calls=%async_computation.12 | async-start | bytes 5242880 | tf_op jit(solution)/shard_map/reduce_scatter | solution.py:147
  679.1 319.0 %reduce-scatter.18.cloned.1.call-start = ((), (), s32[]{:S(2)}) async-start(), calls=%async_computation.19 | async-start | bytes 18874368 | tf_op jit(solution)/shard_map/reduce_scatter | solution.py:145
  679.2 12.7 %copy-start.21 = (bf16[1024,2048]{1,0:T(8,128)(2,1)S(1)}, bf16[1024,2048]{1,0:T(8,128)(2,1)}, u32[]{:S(2)}) copy-start(bf16[1024,2048]{1,0:T(8,128)(2,1)} %all-gather.10.cloned.1.call-done) | copy-start | bytes 12582916
  720.6 51.1 %copy-start.16 = (f32[1,2048]{1,0:T(1,128)S(1)}, f32[1,2048]{1,0:T(1,128)}, u32[]{:S(2)}) copy-start(f32[1,2048]{1,0:T(1,128)} %copy-done.15) | copy-start | bytes 24580
  720.6 331.7 %all-gather.16.cloned.1.call-start = ((), (), s32[]{:S(2)}) async-start(), calls=%async_computation.13 | async-start | bytes 5242880 | tf_op jit(solution)/shard_map/all_gather | solution.py:146
  774.0 60.5 %copy-start.2 = (bf16[1024,512]{1,0:T(8,128)(2,1)S(1)}, bf16[1024,512]{1,0:T(8,128)(2,1)}, u32[]{:S(2)}) copy-start(bf16[1024,512]{1,0:T(8,128)(2,1)} %copy-done.1) | copy-start | bytes 3145732
  833.3 274.1 %all-gather.20.cloned.1.call-start = ((), (), s32[]{:S(2)}) async-start(), calls=%async_computation.17 | async-start | bytes 5242880 | tf_op jit(solution)/shard_map/all_gather | solution.py:146
  834.1 365.1 %reduce-scatter.20.cloned.1.call-start = ((), (), s32[]{:S(2)}) async-start(), calls=%async_computation.20 | async-start | bytes 9437184 | tf_op jit(solution)/shard_map/reduce_scatter | solution.py:145
  834.5 5.5 copy-start.5
  852.4 145.7 %copy-start.14 = (bf16[256,2048]{1,0:T(8,128)(2,1)S(1)}, bf16[256,2048]{1,0:T(8,128)(2,1)}, u32[]{:S(2)}) copy-start(bf16[256,2048]{1,0:T(8,128)(2,1)} %reduce-scatter.16.cloned.1.call-done) | copy-start | bytes 3145732
  1039.4 74.7 %copy-start.7 = (bf16[256,4096]{0,1:T(8,128)(2,1)S(1)}, bf16[256,4096]{0,1:T(8,128)(2,1)}, u32[]{:S(2)}) copy-start(bf16[256,4096]{0,1:T(8,128)(2,1)} %reduce-scatter.18.cloned.1.call-done) | copy-start | bytes 6291460
  1116.6 3.0 copy-start.8
  1199.2 4.3 copy-start.9
  (7 other events, 12.1 us)
Sparse Core Ops, SparseCore 0:
  13.0 85.1 all-gather.7
  121.4 50.8 reduce-scatter.7
  174.6 151.0 all-gather.11
  328.1 50.9 all-gather.9
  381.2 82.4 all-gather.13
  514.9 50.8 reduce-scatter.11
  572.9 52.6 all-gather.17
  627.9 89.5 reduce-scatter.15
  720.6 51.0 reduce-scatter.13
  774.7 52.6 reduce-scatter.9
  829.8 168.2 reduce-scatter.17
  1000.4 51.8 all-gather.15
  1054.7 52.6 all-gather.19
  1109.6 89.5 reduce-scatter.19

commit v2 on v1

--- a/solution.py
+++ b/solution.py
@@ -108,6 +108,553 @@
         compiler_params=pltpu.CompilerParams(vmem_limit_bytes=48 * 1024 * 1024),
         name="attn_bwd",
     )(count, qkv, qkv, qkv, grad)
+
+
+MESH = pl.DeviceIdType.MESH
+VMEM_LIMIT = 60 * 1024 * 1024
+
+
+class Place:
+    def __init__(self, n_dp):
+        self.n = n_dp // 2
+        self.dp = lax.axis_index("dp")
+        self.m = lax.axis_index("mp")
+        self.p = lax.div(self.dp, 2)
+        self.c = lax.rem(self.dp, 2)
+        self.above = (self.dp + 2, self.m)
+        self.below = (self.dp - 2, self.m)
+        self.core = (self.dp + 1 - 2 * self.c, self.m)
+        x = lax.rem(self.m, 2)
+        y = lax.div(self.m, 2)
+        self.qx = self.m + 1 - 2 * x
+        self.qy = self.m + 2 - 4 * y
+        self.qd = 3 - self.m
+        self.xdev = (self.dp, self.qx)
+        self.ydev = (self.dp, self.qy)
+        self.has_above = self.p < self.n - 1
+        self.has_below = self.p > 0
+
+    def fold(self, bit):
+        return (self.dp + bit - 2 * bit * lax.rem(lax.div(self.dp, bit), 2), self.m)
+
+
+def signal(dev):
+    pl.semaphore_signal(pltpu.get_barrier_semaphore(), inc=1, device_id=dev, device_id_type=MESH)
+
+
+def enter(at, extra=()):
+    always = [at.core, at.xdev, at.ydev] + list(extra)
+    for dev in always:
+        signal(dev)
+
+    @pl.when(at.has_above)
+    def _():
+        signal(at.above)
+
+    @pl.when(at.has_below)
+    def _():
+        signal(at.below)
+
+    ends = at.has_above.astype(jnp.int32) + at.has_below.astype(jnp.int32)
+    pl.semaphore_wait(pltpu.get_barrier_semaphore(), len(always) + ends)
+
+
+def remote(src, dst, send, recv, dev):
+    return pltpu.make_async_remote_copy(
+        src_ref=src, dst_ref=dst, send_sem=send, recv_sem=recv, device_id=dev, device_id_type=MESH
+    )
+
+
+def order_of(k, at):
+    n, p = at.n, at.p
+    if k == n - 1:
+        return p
+    high = jnp.where(k < p, k, n - 1 - k + p)
+    low = jnp.where(k < n - 1 - p, n - 1 - k, k - (n - 1 - p))
+    return jnp.where(2 * p >= n, high, low)
+
+
+class LineSum:
+    def __init__(self, at, pout, own, din, uin, sems):
+        self.at, self.pout, self.own, self.din, self.uin = at, pout, own, din, uin
+        self.po_s, self.po_r, self.d_s, self.d_r, self.u_s, self.u_r = sems
+        self.pieces = own.shape[1]
+
+    def core_copy(self, k):
+        j = order_of(k, self.at)
+        return remote(
+            self.pout.at[k % 2], self.own.at[j], self.po_s.at[k % 2], self.po_r.at[k], self.at.core
+        )
+
+    def down_copy(self, s, i):
+        return remote(
+            self.own.at[s, i], self.din.at[s, i], self.d_s.at[s, i], self.d_r.at[s, i], self.at.below
+        )
+
+    def up_copy(self, s, i):
+        n = self.at.n
+        return remote(
+            self.own.at[n - 1 - s, i],
+            self.uin.at[s, i],
+            self.u_s.at[s, i],
+            self.u_r.at[s, i],
+            self.at.above,
+        )
+
+    def other(self, k, tile):
+        if k >= 2:
+            self.core_copy(k - 2).wait_send()
+        j = order_of(k, self.at)
+        tile(2 * j + 1 - self.at.c, lambda i, v: self.store(self.pout, (k % 2,), i, v, False))
+        self.core_copy(k).start()
+
+    def store(self, ref, lead, i, value, add):
+        at = lead + (i,)
+        if add:
+            value = value + ref[at].astype(F32)
+        ref[at] = value.astype(BF)
+
+    def mine(self, k, tile):
+        at = self.at
+        j = order_of(k, at)
+        self.core_copy(k).wait_recv()
+        tile(2 * j + at.c, lambda i, v: self.store(self.own, (j,), i, v, True))
+        if k < at.n - 1:
+
+            @pl.when(at.p == at.n - 1)
+            def _():
+                for i in range(self.pieces):
+                    self.down_copy(k, i).start()
+
+            @pl.when(at.p == 0)
+            def _():
+                for i in range(self.pieces):
+                    self.up_copy(k, i).start()
+
+    def add(self, dst, src, i):
+        rows = dst.shape[0]
+        step = 64
+        for r in range(0, rows, step):
+            rs = pl.ds(r, step)
+            dst[rs, :] = (dst[rs, :].astype(F32) + src[rs, :].astype(F32)).astype(BF)
+
+    def slot(self, t):
+        at = self.at
+        n, p = at.n, at.p
+        sd = t - (n - 2 - p)
+        su = t - (p - 1)
+
+        @pl.loop(0, self.pieces)
+        def _(i):
+            @pl.when((sd >= 0) & (sd < p) & at.has_above)
+            def _():
+                self.down_copy(sd, i).wait_recv()
+                self.add(self.own.at[sd, i], self.din.at[sd, i], i)
+                self.down_copy(sd, i).start()
+
+            @pl.when((su >= 0) & (su < n - 1 - p) & at.has_below)
+            def _():
+                self.up_copy(su, i).wait_recv()
+                self.add(self.own.at[n - 1 - su, i], self.uin.at[su, i], i)
+                self.up_copy(su, i).start()
+
+    def final(self, out):
+        at = self.at
+        n, p = at.n, at.p
+
+        @pl.loop(0, self.pieces)
+        def _(i):
+            @pl.when(at.has_above)
+            def _():
+                self.down_copy(p, i).wait_recv()
+
+            @pl.when(at.has_below)
+            def _():
+                self.up_copy(n - 1 - p, i).wait_recv()
+
+            for r in range(0, out.shape[1], 64):
+                rs = pl.ds(r, 64)
+                out[i, rs, :] = self.own[p, i, rs, :].astype(F32)
+
+                @pl.when(at.has_above)
+                def _():
+                    out[i, rs, :] += self.din[p, i, rs, :].astype(F32)
+
+                @pl.when(at.has_below)
+                def _():
+                    out[i, rs, :] += self.uin[n - 1 - p, i, rs, :].astype(F32)
+
+    def drain(self):
+        at = self.at
+        n, p = at.n, at.p
+        for k in range(max(0, n - 2), n):
+            self.core_copy(k).wait_send()
+        for s in range(n - 1):
+
+            @pl.when(s < p)
+            def _():
+                for i in range(self.pieces):
+                    self.down_copy(s, i).wait_send()
+
+            @pl.when(s < n - 1 - p)
+            def _():
+                for i in range(self.pieces):
+                    self.up_copy(s, i).wait_send()
+
+
+def line_sum_scratch(n, pieces, rows, cols):
+    dma = pltpu.SemaphoreType.DMA
+    return [
+        pltpu.VMEM((2, pieces, rows, cols), BF),
+        pltpu.VMEM((n, pieces, rows, cols), BF),
+        pltpu.VMEM((n - 1, pieces, rows, cols), BF),
+        pltpu.VMEM((n - 1, pieces, rows, cols), BF),
+        dma((2,)),
+        dma((n,)),
+        dma((n - 1, pieces)),
+        dma((n - 1, pieces)),
+        dma((n - 1, pieces)),
+        dma((n - 1, pieces)),
+    ]
+
+
+class QuadSum:
+    def __init__(self, at, t, r1, r2, sems):
+        self.at, self.t, self.r1, self.r2 = at, t, r1, r2
+        self.s1, self.v1, self.s2, self.v2 = sems
+
+    def first(self, half, turn):
+        at = self.at
+        dev, quarter = (at.xdev, at.qx) if half == 0 else (at.ydev, at.qy)
+        q = at.qd if turn == 0 else quarter
+        return remote(
+            self.t.at[half, q],
+            self.r1.at[half, turn],
+            self.s1.at[half, turn],
+            self.v1.at[half, turn],
+            dev,
+        )
+
+    def second(self, half):
+        at = self.at
+        dev, q = (at.ydev, at.qy) if half == 0 else (at.xdev, at.qx)
+        return remote(
+            self.r1.at[half, 0], self.r2.at[half], self.s2.at[half], self.v2.at[half], dev
+        )
+
+    def turn(self):
+        at = self.at
+        for half in range(2):
+            q = at.qy if half == 0 else at.qx
+            self.first(half, 0).wait_recv()
+
+            @pl.loop(0, self.t.shape[2] // 64)
+            def _(b):
+                rs = pl.ds(pl.multiple_of(b * 64, 64), 64)
+                total = self.r1[half, 0, rs, :].astype(F32) + self.t[half, q, rs, :].astype(F32)
+                self.r1[half, 0, rs, :] = total.astype(BF)
+
+            self.second(half).start()
+
+    def arrive(self):
+        for half in range(2):
+            self.first(half, 1).wait_recv()
+            self.second(half).wait_recv()
+
+    def total(self, half, rs):
+        own = self.t[half, self.at.m, rs, :].astype(F32)
+        return own + self.r1[half, 1, rs, :].astype(F32) + self.r2[half, rs, :].astype(F32)
+
+    def drain(self):
+        for half in range(2):
+            self.first(half, 0).wait_send()
+            self.first(half, 1).wait_send()
+            self.second(half).wait_send()
+
+
+def quad_sum_scratch(rows, cols):
+    dma = pltpu.SemaphoreType.DMA
+    return [
+        pltpu.VMEM((2, 4, rows, cols), BF),
+        pltpu.VMEM((2, 2, rows, cols), BF),
+        pltpu.VMEM((2, rows, cols), BF),
+        dma((2, 2)),
+        dma((2, 2)),
+        dma((2,)),
+        dma((2,)),
+    ]
+
+
+class QuadGather:
+    def __init__(self, at, own, out, sems):
+        self.at, self.own, self.out = at, own, out
+        self.s, self.v, self.s2, self.v2, self.here = sems
+
+    def spot(self, q, half):
+        rows, cols = self.own.shape[1], self.own.shape[2]
+        rs = pl.ds(pl.multiple_of(q * rows, rows), rows)
+        return self.out.at[rs, pl.ds(half * cols, cols)]
+
+    def direct(self, half, way):
+        at = self.at
+        dev = at.xdev if way == 0 else at.ydev
+        return remote(
+            self.own.at[half],
+            self.spot(at.m, half),
+            self.s.at[half, way],
+            self.v.at[half, way],
+            dev,
+        )
+
+    def onward(self, half):
+        at = self.at
+        q, dev = (at.qy, at.xdev) if half == 0 else (at.qx, at.ydev)
+        return remote(
+            self.spot(q, half), self.spot(q, half), self.s2.at[half], self.v2.at[half], dev
+        )
+
+    def keep(self, half):
+        return pltpu.make_async_copy(self.own.at[half], self.spot(self.at.m, half), self.here.at[half])
+
+    def start(self):
+        for way in ((0, 1), (1, 0), (0, 0), (1, 1)):
+            self.direct(*way).start()
+        for half in range(2):
+            self.keep(half).start()
+
+    def forward(self):
+        self.direct(0, 1).wait_recv()
+        self.onward(0).start()
+        self.direct(1, 0).wait_recv()
+        self.onward(1).start()
+
+    def finish(self):
+        for half in range(2):
+            self.direct(half, half).wait_recv()
+            self.onward(half).wait_recv()
+            self.keep(half).wait()
+            self.onward(half).wait_send()
+            for way in range(2):
+                self.direct(half, way).wait_send()
+
+
+def quad_gather_scratch(rows, cols):
+    dma = pltpu.SemaphoreType.DMA
+    return [
+        pltpu.VMEM((2, rows, cols), BF),
+        dma((2, 2)),
+        dma((2, 2)),
+        dma((2,)),
+        dma((2,)),
+        dma((2,)),
+    ]
+
+
+def halves(fn):
+    return [fn(0), fn(1)]
+
+
+def last_kernel(
+    n_dp,
+    dqkv_hbm,
+    aw_hbm,
+    nt_hbm,
+    gt_hbm,
+    att_hbm,
+    x_ref,
+    gh_ref,
+    gain_ref,
+    gmid_ref,
+    rs_ref,
+    grad_ref,
+    gains_ref,
+    dqkv,
+    aw,
+    nt,
+    gt,
+    att,
+    loads,
+    pout,
+    own,
+    din,
+    uin,
+    po_s,
+    po_r,
+    d_s,
+    d_r,
+    u_s,
+    u_r,
+    t,
+    r1,
+    r2,
+    q1,
+    q2,
+    q3,
+    q4,
+    gown,
+    g1,
+    g2,
+    g3,
+    g4,
+    g5,
+    fold_out,
+    fold_in,
+    fold_s,
+    fold_r,
+):
+    at = Place(n_dp)
+    hh = att_hbm.shape[1]
+    part = t.shape[2]
+    chunk = own.shape[2]
+    half_cols = t.shape[3]
+    copies = [
+        pltpu.make_async_copy(src, dst, loads.at[i])
+        for i, (src, dst) in enumerate(
+            [
+                (dqkv_hbm, dqkv),
+                (aw_hbm.at[:, pl.ds(0, 3 * hh)], aw),
+                (nt_hbm, nt),
+                (att_hbm, att),
+                (gt_hbm, gt),
+            ]
+        )
+    ]
+    for cp in copies:
+        cp.start()
+    bits = [b for b in (2, 4, 8, 16) if b < n_dp]
+    enter(at, [at.fold(b) for b in bits[1:]])
+    quad = QuadSum(at, t, r1, r2, (q1, q2, q3, q4))
+    line = LineSum(at, pout, own, din, uin, (po_s, po_r, d_s, d_r, u_s, u_r))
+    gather = QuadGather(at, gown, grad_ref, (g1, g2, g3, g4, g5))
+    copies[0].wait()
+    copies[1].wait()
+
+    def terms(q):
+        rs = pl.ds(pl.multiple_of(q * part, part), part)
+        width = 512
+
+        @pl.loop(0, half_cols // width)
+        def _(i):
+            for half in range(2):
+                d0 = pl.multiple_of(half * half_cols + i * width, width)
+                v = dot(dqkv[rs, :], aw[pl.ds(d0, width), :], NT)
+                t[half, q, :, pl.ds(pl.multiple_of(i * width, width), width)] = v.astype(BF)
+
+    terms(at.qd)
+    quad.first(0, 0).start()
+    quad.first(1, 0).start()
+    terms(at.qx)
+    quad.first(0, 1).start()
+    terms(at.qy)
+    quad.first(1, 1).start()
+    for cp in copies[2:]:
+        cp.wait()
+
+    def tile(block, put):
+        rs = pl.ds(pl.multiple_of(block * chunk, chunk), chunk)
+
+        @pl.loop(0, 3)
+        def _(i):
+            put(i, dot(nt[rs, :], dqkv[:, pl.ds(pl.multiple_of(i * hh, hh), hh)]))
+
+        put(3, dot(gt[rs, :], att[...]))
+
+    n = at.n
+    for k in range(n + 1):
+        if k < n:
+            line.other(k, tile)
+        if k > 0:
+            line.mine(k - 1, tile)
+    terms(at.m)
+    quad.turn()
+    line.slot(0)
+    quad.arrive()
+
+    fold_out[...] = jnp.zeros_like(fold_out)
+
+    @pl.loop(0, part // 32)
+    def _(b):
+        rs = pl.ds(pl.multiple_of(b * 32, 32), 32)
+        x = x_ref[rs, :].astype(F32)
+        scale = lax.rsqrt(jnp.mean(x * x, axis=1, keepdims=True) + EPS)
+        g = jnp.concatenate([quad.total(0, rs), quad.total(1, rs)], axis=1)
+        unit = x * scale
+        weighted = g * gain_ref[...]
+        field = scale * (weighted - unit * jnp.mean(weighted * unit, axis=1, keepdims=True))
+        res = (gh_ref[rs, :] + field).astype(BF)
+        gown[0, rs, :] = res[:, :half_cols]
+        gown[1, rs, :] = res[:, half_cols:]
+        fold_out[0, 0:1, :] += jnp.sum(g * unit, axis=0, keepdims=True)
+
+    gather.start()
+    fold_out[0, 1:2, :] = gmid_ref[...]
+    devs = [at.core, at.xdev, at.ydev] + [at.fold(b) for b in bits]
+
+    def fold_copy(b):
+        return remote(fold_out.at[b], fold_in.at[b], fold_s.at[b], fold_r.at[b], devs[b])
+
+    def fold_next(b):
+        fold_copy(b).wait_recv()
+        nxt = fold_out[b] + fold_in[b]
+        if b + 1 < len(devs):
+            fold_out[b + 1] = nxt
+            fold_copy(b + 1).start()
+        else:
+            gains_ref[...] = nxt
+
+    fold_copy(0).start()
+    for s in range(1, n - 2):
+        line.slot(s)
+    gather.forward()
+    for b in range(len(devs)):
+        fold_next(b)
+    line.final(rs_ref)
+    gather.finish()
+    line.drain()
+    quad.drain()
+    for b in range(len(devs)):
+        fold_copy(b).wait_send()
+
+
+def last_stage(n_dp, dqkv, aw, nt, gt, att, x, gh, gain, gmid):
+    seq, hh = att.shape
+    d = nt.shape[0]
+    n, part, chunk = n_dp // 2, seq // 4, d // n_dp
+    dma = pltpu.SemaphoreType.DMA
+    anyspace = pl.BlockSpec(memory_space=pl.ANY)
+    vm = pl.BlockSpec(memory_space=pltpu.VMEM)
+    folds = 3 + len([b for b in (2, 4, 8, 16) if b < n_dp])
+    return pl.pallas_call(
+        functools.partial(last_kernel, n_dp),
+        out_shape=[
+            jax.ShapeDtypeStruct((4, chunk, hh), F32),
+            jax.ShapeDtypeStruct((seq, d), BF),
+            jax.ShapeDtypeStruct((8, d), F32),
+        ],
+        in_specs=[anyspace] * 5 + [vm] * 4,
+        out_specs=[vm, anyspace, vm],
+        scratch_shapes=[
+            pltpu.VMEM((seq, 3 * hh), BF),
+            pltpu.VMEM((d, 3 * hh), BF),
+            pltpu.VMEM((d, seq), BF),
+            pltpu.VMEM((d, seq), BF),
+            pltpu.VMEM((seq, hh), BF),
+            dma((5,)),
+        ]
+        + line_sum_scratch(n, 4, chunk, hh)
+        + quad_sum_scratch(part, d // 2)
+        + quad_gather_scratch(part, d // 2)
+        + [
+            pltpu.VMEM((folds, 8, d), F32),
+            pltpu.VMEM((folds, 8, d), F32),
+            dma((folds,)),
+            dma((folds,)),
+        ],
+        compiler_params=pltpu.CompilerParams(
+            collective_id=5, has_side_effects=True, vmem_limit_bytes=VMEM_LIMIT
+        ),
+        name="last_stage",
+    )(dqkv, aw, nt, gt, att, x, gh, gain, gmid)
 
 
 def norm_backward(grad_normed, field, scale, gain):
@@ -198,29 +745,30 @@
     grad_low = mp_gather(grad_hidden.astype(BF))
     grad_attended = dot(grad_low, out_wt).astype(BF)
     dq, dk, dv = attn_bwd(qkv, grad_attended, counts, seq)
-    grads = [dq, dk, dv]
-    grad_attn = jnp.concatenate(
-        [dot(normed_in, g, TN).astype(BF) for g in grads] + [dot(grad_low, attended, TN).astype(BF)],
-        axis=1,
+    rs_attn, grad_low_in, g_gains = last_stage(
+        lax.axis_size("dp"),
+        jnp.concatenate([dq, dk, dv], axis=1),
+        attn_w,
+        normed_in.T,
+        grad_low.T,
+        attended,
+        mine(inputs),
+        grad_hidden,
+        gain_in,
+        g_gain_mid[None],
     )
-    rs_attn = scatter(after(grad_attn, rs_gu))
-    in_terms = sum(dot(g, attn_w[:, i * hh : (i + 1) * hh], NT) for i, g in enumerate(grads))
-    grad_in = mp_scatter(in_terms).astype(F32)
-    g_source, g_gain_in = norm_backward(grad_in, my_source, mine(scale_in), gain_in)
-    input_grad = mp_gather((grad_hidden + g_source).astype(BF)).astype(F32)
-    g_gains = lax.psum(jnp.stack([g_gain_in, g_gain_mid]), ("dp", "mp"))
+    input_grad = grad_low_in.astype(F32)
     width = g_gains.shape[1] // lax.axis_size("dp")
     g_gains = lax.dynamic_slice_in_dim(g_gains, lax.axis_index("dp") * width, width, 1)
-    rs_attn = rs_attn.astype(F32)
     rs_gu = rs_gu.astype(F32)
     return (
         layer_out,
         input_grad,
         g_gains[0],
-        rs_attn[:, :hh],
-        rs_attn[:, hh : 2 * hh],
-        rs_attn[:, 2 * hh : 3 * hh],
-        rs_attn[:, 3 * hh :].T,
+        rs_attn[0],
+        rs_attn[1],
+        rs_attn[2],
+        rs_attn[3].T,
         g_gains[1],
         rs_gu[:, :ff],
         rs_gu[:, ff:],

time: 1230 us -> 1070 us (0.87)
  waiting for transfers between devices: 852 us -> 642 us
  Pallas kernels: 18.2 us -> 149 us
  blocking collectives: 51.9 us -> 13.6 us
  matrix products: 195 us -> 158 us
    pallas_call x0 -> x1, Pallas kernels: none -> 131 us  [last_stage(): pl.pallas_call(functools.partial(last_kernel, n_dp), out_shape=[jax.Shape...]
    reduce_scatter x4 -> x3, waiting for transfers between devices: 201 us -> 119 us  [on_device(): lax.psum_scatter(x.astype(BF), 'mp', scatter_dimension=0, tiled=True)]
    reduce_scatter x3 -> x2, waiting for transfers between devices: 223 us -> 161 us  [on_device(): lax.psum_scatter(x, 'dp', scatter_dimension=0, tiled=True)]
    all_gather x4 -> x3, waiting for transfers between devices: 154 us -> 95.9 us  [on_device(): mp_gather = lambda x: lax.all_gather(x, 'mp', axis=0, tiled=True)]
    psum x1 -> x0, blocking collectives: 38.5 us -> none  [on_device(): g_gains = lax.psum(jnp.stack([g_gain_in, g_gain_mid]), ('dp', 'mp'))]
    dot_general x19 -> x12, matrix products: 195 us -> 158 us  [dot(): return lax.dot_general(a, b, dims, preferred_element_type=F32)]
    unnamed x60 -> x49, local copies, waits for them, and re-layouts: 21.2 us -> 24.8 us
  transfers between devices with their start and end apart: 14 -> 11, of which waited for: 13 -> 10; matrix products, arithmetic and copies ran while one was open for 15% -> 14% of each run, Pallas kernels for 1% -> 13%
where the time goes in v2:
time: 1070 us; the launch traced here: 1060 us
  waiting for transfers between devices  642 us (60%)
  matrix products  158 us (15%)
  Pallas kernels  149 us (14%)
  other arithmetic  47.7 us (4%)
  local copies, waits for them, and re-layouts  38.5 us (4%)
  between operations  15.3 us (1%)
  blocking collectives  13.6 us (1%)
    all_gather x3, waiting for transfers between devices, on_device(): gather = lambda x: lax.all_gather(x, 'dp', axis=0, tiled=True)  265 us
    reduce_scatter x2, waiting for transfers between devices, on_device(): lax.psum_scatter(x, 'dp', scatter_dimension=0, tiled=True)  161 us
    dot_general x12, matrix products, dot(): return lax.dot_general(a, b, dims, preferred_element_type=F32)  158 us
    pallas_call x1, Pallas kernels, last_stage(): pl.pallas_call(functools.partial(last_kernel, n_dp), out_shape=[jax.Shape...  131 us
    reduce_scatter x3, waiting for transfers between devices, on_device(): lax.psum_scatter(x.astype(BF), 'mp', scatter_dimension=0, tiled=True)  119 us
    all_gather x3, waiting for transfers between devices, on_device(): mp_gather = lambda x: lax.all_gather(x, 'mp', axis=0, tiled=True)  95.9 us
    unnamed x49, local copies, waits for them, and re-layouts  24.8 us
  transfers between devices with their start and end apart: 11, of which 10 were waited for; matrix products, arithmetic and copies ran while one was open for 14% of the time, Pallas kernels for 13%

profile of v2, /device:TPU:0, one launch (start us, length us, event | category | flops | bytes accessed | tf_op | source)
XLA Modules:
  0.0 1064.4 jit_solution(12927760289220164783)
XLA Ops:
  13.6 6.4 copy.23
  20.0 13.6 %all_gather.21 = bf16[2,2048]{1,0:T(2,128)(2,1)S(1)} all-gather(bf16[2,256]{1,0:T(2,128)(2,1)S(1)} %pad_maximum_fusion.4), channel_id=1, replica_groups=mesh['dp'=8,'mp'=4] {'dp'}, dimensions={1}, use_global_device_ids=true | all-gather | bytes 9216 | tf_op jit(solution)/shard_map/all_gather | solution.py:703
  36.8 60.9 %all-gather.7.cloned.1.call-done.aw_hbm = bf16[2048,2048]{1,0:T(8,128)(2,1)} async-done(((bf16[256,2048]{1,0:T(8,128)(2,1)}), bf16[2048,2048]{1,0:T(8,128)(2,1)}) %all-gather.7.cloned.1.call-update) | async-done | bytes 8388624 | tf_op jit(solution)/shard_map/all_gather | solution.py:691
  97.7 10.7 %fusion.23.q_ref.k_ref.v_ref = bf16[1024,1536]{1,0:T(8,128)(2,1)S(1)} fusion(bf16[2048,2048]{1,0:T(8,128)(2,1)} %all-gather.7.cloned.1.call-done.aw_hbm, bf16[1024,2048]{0,1:T(8,128)(2,1)} %copy.23, f32[2048]{0:T(1024)S(1)} %bitcast.44, f32[1024]{0:T(1024)S(1)} %add_rsqrt_fusion), kind=kOutput, calls=%fused_computation.35 | convolution fusion | flops 6452412416 | bytes 13643776 | tf_op jit(solution)/shard_map/dot_general | solution.py:21
  108.4 5.9 attn_fwd.1.att_hbm
  115.3 6.0 convolution_convert_fusion.4
  126.2 46.5 %reduce-scatter.6.cloned.1.call-done = bf16[256,2048]{1,0:T(8,128)(2,1)} async-done(((bf16[1024,2048]{1,0:T(8,128)(2,1)}), bf16[256,2048]{1,0:T(8,128)(2,1)}) %reduce-scatter.6.cloned.1.call-update) | async-done | bytes 1048592 | tf_op jit(solution)/shard_map/reduce_scatter | solution.py:694
  179.4 146.7 %all-gather.11.cloned.1.call-done = bf16[2048,4096]{1,0:T(8,128)(2,1)} async-done(((bf16[256,4096]{1,0:T(8,128)(2,1)}), bf16[2048,4096]{1,0:T(8,128)(2,1)}) %all-gather.11.cloned.1.call-update) | async-done | bytes 16777232 | tf_op jit(solution)/shard_map/all_gather | solution.py:691
  331.0 48.5 %all-gather.9.cloned.1.call-done = bf16[1024,2048]{1,0:T(8,128)(2,1)} async-done(((bf16[256,2048]{1,0:T(8,128)(2,1)}), bf16[1024,2048]{1,0:T(8,128)(2,1)}) %all-gather.9.cloned.1.call-update) | async-done | bytes 4194320 | tf_op jit(solution)/shard_map/all_gather | solution.py:693
  379.5 14.7 %fusion.26 = bf16[1024,2048]{1,0:T(8,128)(2,1)} fusion(bf16[1024,2048]{1,0:T(8,128)(2,1)} %all-gather.9.cloned.1.call-done, bf16[2048,4096]{1,0:T(8,128)(2,1)} %all-gather.11.cloned.1.call-done), kind=kOutput, calls=%fused_computation.36 | convolution fusion | flops 8592031744 | bytes 16777216 | tf_op jit(solution)/shard_map/dot_general | solution.py:21
  394.2 12.7 %fusion.29 = bf16[1024,2048]{1,0:T(8,128)(2,1)} fusion(bf16[1024,2048]{1,0:T(8,128)(2,1)S(1)} %copy-done.17, bf16[2048,4096]{1,0:T(8,128)(2,1)} %all-gather.11.cloned.1.call-done), kind=kOutput, calls=%fused_computation.37 | convolution fusion | flops 8592031744 | bytes 16777216 | tf_op jit(solution)/shard_map/dot_general | solution.py:21
  406.9 57.2 %all-gather.13.cloned.1.call-done = bf16[2048,2048]{0,1:T(8,128)(2,1)} async-done(((bf16[256,2048]{0,1:T(8,128)(2,1)}), bf16[2048,2048]{0,1:T(8,128)(2,1)}) %all-gather.13.cloned.1.call-update) | async-done | bytes 8388624 | tf_op jit(solution)/shard_map/all_gather | solution.py:691
  464.2 18.3 %fusion.6 = (bf16[1024,2048]{1,0:T(8,128)(2,1)S(1)}, f32[1024,2048]{1,0:T(8,128)}) fusion(bf16[1024,2048]{1,0:T(8,128)(2,1)} %fusion.29, bf16[1024,2048]{1,0:T(8,128)(2,1)} %fusion.26, bf16[1024,2048]{1,0:T(8,128)(2,1)} %broadcast_select_fusion, bf16[2048,2048]{0,1:T(8,128)(2,1)} %all-gather.13.cloned.1.call-done), kind=kOutput, calls=%fused_computation.14 | convolution fusion | flops 8615100416 | bytes 33554432 | tf_op jit(solution)/shard_map/dot_general | solution.py:21
  482.5 18.2 %fusion.11 = f32[1024,2048]{1,0:T(8,128)} fusion(bf16[2048,4096]{1,0:T(8,128)(2,1)} %all-gather.11.cloned.1.call-done, f32[1024,2048]{1,0:T(8,128)} %get-tuple-element.58, bf16[1024,2048]{1,0:T(8,128)(2,1)} %fusion.26), kind=kOutput, calls=%fused_computation.24 | convolution fusion | flops 8604614656 | bytes 29360128 | tf_op jit(solution)/shard_map/dot_general | solution.py:21
  500.7 14.5 %add_convert_fusion = bf16[1024,2048]{1,0:T(8,128)(2,1)} fusion(f32[1024,2048]{1,0:T(8,128)} %fusion.11, bf16[1024,2048]{1,0:T(8,128)(2,1)S(1)} %get-tuple-element.57, bf16[2048,4096]{1,0:T(8,128)(2,1)} %all-gather.11.cloned.1.call-done), kind=kOutput, calls=%fused_computation.19 | convolution fusion | flops 8594128896 | bytes 25165824 | tf_op jit(solution)/shard_map/dot_general | solution.py:21
  515.3 15.7 %convolution_convert_fusion.3 = bf16[1024,2048]{1,0:T(8,128)(2,1)} fusion(bf16[2048,2048]{0,1:T(8,128)(2,1)} %all-gather.13.cloned.1.call-done, bf16[1024,2048]{1,0:T(8,128)(2,1)} %fusion.29, bf16[1024,2048]{1,0:T(8,128)(2,1)} %fusion.26), kind=kOutput, calls=%fused_computation.38 | convolution fusion | flops 8608808960 | bytes 20971520 | tf_op jit(solution)/shard_map/dot_general | solution.py:21
  531.0 15.4 %convolution_convert_fusion = bf16[2048,2048]{1,0:T(8,128)(2,1)} fusion(bf16[1024,2048]{1,0:T(8,128)(2,1)} %broadcast_select_fusion, bf16[1024,2048]{1,0:T(8,128)(2,1)} %fusion.29, bf16[1024,2048]{1,0:T(8,128)(2,1)} %fusion.26), kind=kOutput, calls=%fused_computation.21 | convolution fusion | flops 8610906112 | bytes 20971520 | tf_op jit(solution)/shard_map/dot_general | solution.py:21
  546.5 19.8 %reduce-scatter.10.cloned.1.call-done = bf16[256,2048]{1,0:T(8,128)(2,1)} async-done(((bf16[1024,2048]{1,0:T(8,128)(2,1)}), bf16[256,2048]{1,0:T(8,128)(2,1)}) %reduce-scatter.10.cloned.1.call-update) | async-done | bytes 1048592 | tf_op jit(solution)/shard_map/reduce_scatter | solution.py:694
  569.0 52.9 %reduce-scatter.8.cloned.1.call-done = bf16[256,2048]{1,0:T(8,128)(2,1)} async-done(((bf16[1024,2048]{1,0:T(8,128)(2,1)}), bf16[256,2048]{1,0:T(8,128)(2,1)}) %reduce-scatter.8.cloned.1.call-update) | async-done | bytes 1048592 | tf_op jit(solution)/shard_map/reduce_scatter | solution.py:694
  622.0 5.0 fusion.49
  627.6 12.5 %convolution_convert_fusion.2 = bf16[2048,2048]{0,1:T(8,128)(2,1)S(1)} fusion(bf16[1024,2048]{1,0:T(8,128)(2,1)} %all-gather.9.cloned.1.call-done, bf16[1024,2048]{1,0:T(8,128)(2,1)} %copy-done.20), kind=kOutput, calls=%fused_computation.23 | convolution fusion | flops 8594128896 | bytes 16777216 | tf_op jit(solution)/shard_map/dot_general | solution.py:21
  640.1 13.9 %convolution_convert_fusion.1 = bf16[2048,2048]{0,1:T(8,128)(2,1)S(1)} fusion(bf16[1024,2048]{1,0:T(8,128)(2,1)} %all-gather.9.cloned.1.call-done, f32[1024,2048]{1,0:T(8,128)} %get-tuple-element.58, bf16[1024,2048]{1,0:T(8,128)(2,1)} %fusion.26), kind=kOutput, calls=%fused_computation.22 | convolution fusion | flops 8608808960 | bytes 25165824 | tf_op jit(solution)/shard_map/dot_general | solution.py:21
  654.0 7.5 pad_maximum_fusion
  661.5 52.5 %reduce-scatter.12.cloned.1.call-done = bf16[256,2048]{1,0:T(8,128)(2,1)} async-done(((bf16[2048,2048]{1,0:T(8,128)(2,1)}), bf16[256,2048]{1,0:T(8,128)(2,1)}) %reduce-scatter.12.cloned.1.call-update) | async-done | bytes 1048592 | tf_op jit(solution)/shard_map/reduce_scatter | solution.py:692
  720.3 47.3 %all-gather.17.cloned.1.call-done = bf16[1024,2048]{1,0:T(8,128)(2,1)} async-done(((bf16[256,2048]{1,0:T(8,128)(2,1)}), bf16[1024,2048]{1,0:T(8,128)(2,1)}) %all-gather.17.cloned.1.call-update) | async-done | bytes 4194320 | tf_op jit(solution)/shard_map/all_gather | solution.py:693
  767.7 5.2 fusion.42.g_ref
  772.8 12.2 %attn_bwd.1 = (bf16[1024,512]{1,0:T(8,128)(2,1)S(1)}, bf16[1024,512]{1,0:T(8,128)(2,1)S(1)}, bf16[1024,512]{1,0:T(8,128)(2,1)S(1)}) custom-call(s32[1]{0:T(128)} %copy.31.count_ref, bf16[1024,1536]{1,0:T(8,128)(2,1)} %copy-done, bf16[1024,1536]{1,0:T(8,128)(2,1)} %copy-done, bf16[1024,1536]{1,0:T(8,128)(2,1)} %copy-done, bf16[1024,512]{1,0:T(8,128)(2,1)S(1)} %fusion.42.g_ref), custom_call_target="tpu_custom_call" | custom-call | tf_op jit(solution)/shard_map/attn_bwd/pallas_call | solution.py:98
  785.0 6.4 copy.25.gt_hbm
  793.2 131.3 %last_stage.1 = (f32[4,256,512]{2,1,0:T(8,128)}, bf16[1024,2048]{1,0:T(8,128)(2,1)}, f32[8,2048]{1,0:T(8,128)}) custom-call(bf16[1024,1536]{1,0:T(8,128)(2,1)} %pad_maximum_fusion.1.dqkv_hbm, bf16[2048,2048]{1,0:T(8,128)(2,1)} %all-gather.7.cloned.1.call-done.aw_hbm, bf16[2048,1024]{1,0:T(8,128)(2,1)} %fusion.45.nt_hbm, bf16[2048,1024]{1,0:T(8,128)(2,1)} %copy.25.gt_hbm, ...), custom_call_target="tpu_custom_call" | custom-call | tf_op jit(solution)/shard_map/last_stage/pallas_call | solution.py:627
  928.2 6.7 convert_element_type.119
  936.3 108.5 %reduce-scatter.14.cloned.1.call-done = bf16[256,4096]{0,1:T(8,128)(2,1)} async-done(((bf16[2048,4096]{0,1:T(8,128)(2,1)}), bf16[256,4096]{0,1:T(8,128)(2,1)}) %reduce-scatter.14.cloned.1.call-update) | async-done | bytes 2097168 | tf_op jit(solution)/shard_map/reduce_scatter | solution.py:692
  1052.7 4.8 copy.32
  (99 shorter events, 50.8 us)
Async XLA Ops:
  7.2 6.3 copy-start.18
  7.2 6.3 copy-start.19
  7.2 90.5 %all-gather.7.cloned.1.call-start = ((), (), s32[]{:S(2)}) async-start(), calls=%async_computation.5 | async-start | bytes 9437184 | tf_op jit(solution)/shard_map/all_gather | solution.py:691
  12.8 159.9 %reduce-scatter.6.cloned.1.call-start = ((), (), s32[]{:S(2)}) async-start(), calls=%async_computation.6 | async-start | bytes 5242880 | tf_op jit(solution)/shard_map/reduce_scatter | solution.py:694
  36.7 71.7 %copy-start.15 = (f32[1024]{0:T(1024)}, f32[1024]{0:T(1024)S(1)}, u32[]{:S(2)}) copy-start(f32[1024]{0:T(1024)S(1)} %add_rsqrt_fusion) | copy-start | bytes 12292
  36.8 71.6 %copy-start.11 = (f32[1,2048]{1,0:T(1,128)}, f32[1,2048]{1,0:T(1,128)S(1)}, u32[]{:S(2)}) copy-start(f32[1,2048]{1,0:T(1,128)S(1)} %get-tuple-element.56.gain_ref) | copy-start | bytes 24580
  36.8 138.0 %copy-start.9 = (f32[1,2048]{1,0:T(1,128)}, f32[1,2048]{1,0:T(1,128)S(1)}, u32[]{:S(2)}) copy-start(f32[1,2048]{1,0:T(1,128)S(1)} %get-tuple-element.55) | copy-start | bytes 24580
  108.4 5.9 copy-start
  114.3 1.0 copy-start.1
  121.3 1.6 copy-start.5
  121.3 204.8 %all-gather.11.cloned.1.call-start = ((), (), s32[]{:S(2)}) async-start(), calls=%async_computation.8 | async-start | bytes 18874368 | tf_op jit(solution)/shard_map/all_gather | solution.py:691
  122.9 1.6 copy-start.6
  126.2 52.2 %copy-start.7 = (f32[2048,256]{1,0:T(8,128)S(1)}, f32[2048,256]{1,0:T(8,128)}, u32[]{:S(2)}) copy-start(f32[2048,256]{1,0:T(8,128)} %param.23) | copy-start | bytes 6291460
  126.2 253.3 %all-gather.9.cloned.1.call-start = ((), (), s32[]{:S(2)}) async-start(), calls=%async_computation.7 | async-start | bytes 5242880 | tf_op jit(solution)/shard_map/all_gather | solution.py:693
  174.7 1.0 copy-start.2
  174.7 1.0 copy-start.13
  178.3 285.8 %all-gather.13.cloned.1.call-start = ((), (), s32[]{:S(2)}) async-start(), calls=%async_computation.9 | async-start | bytes 9437184 | tf_op jit(solution)/shard_map/all_gather | solution.py:691
  326.2 240.1 %reduce-scatter.10.cloned.1.call-start = ((), (), s32[]{:S(2)}) async-start(), calls=%async_computation.12 | async-start | bytes 5242880 | tf_op jit(solution)/shard_map/reduce_scatter | solution.py:694
  379.5 14.7 %copy-start.17 = (bf16[1024,2048]{1,0:T(8,128)(2,1)S(1)}, bf16[1024,2048]{1,0:T(8,128)(2,1)}, u32[]{:S(2)}) copy-start(bf16[1024,2048]{1,0:T(8,128)(2,1)} %all-gather.9.cloned.1.call-done) | copy-start | bytes 12582916
  482.5 18.2 %copy-start.20 = (bf16[1024,2048]{1,0:T(8,128)(2,1)}, bf16[1024,2048]{1,0:T(8,128)(2,1)S(1)}, u32[]{:S(2)}) copy-start(bf16[1024,2048]{1,0:T(8,128)(2,1)S(1)} %get-tuple-element.57) | copy-start | bytes 12582916
  515.3 106.7 %reduce-scatter.8.cloned.1.call-start = ((), (), s32[]{:S(2)}) async-start(), calls=%async_computation.10 | async-start | bytes 5242880 | tf_op jit(solution)/shard_map/reduce_scatter | solution.py:694
  531.0 183.0 %reduce-scatter.12.cloned.1.call-start = ((), (), s32[]{:S(2)}) async-start(), calls=%async_computation.14 | async-start | bytes 9437184 | tf_op jit(solution)/shard_map/reduce_scatter | solution.py:692
  546.4 19.9 %copy-start.3 = (bf16[256,2048]{1,0:T(8,128)(2,1)S(1)}, bf16[256,2048]{1,0:T(8,128)(2,1)}, u32[]{:S(2)}) copy-start(bf16[256,2048]{1,0:T(8,128)(2,1)} %copy-done.2) | copy-start | bytes 3145732
  546.4 19.9 %copy-start.4 = (bf16[256,2048]{1,0:T(8,128)(2,1)S(1)}, bf16[256,2048]{1,0:T(8,128)(2,1)}, u32[]{:S(2)}) copy-start(bf16[256,2048]{1,0:T(8,128)(2,1)} %reduce-scatter.6.cloned.1.call-done) | copy-start | bytes 3145732
  546.4 19.9 %copy-start.10 = (f32[1,2048]{1,0:T(1,128)S(1)}, f32[1,2048]{1,0:T(1,128)}, u32[]{:S(2)}) copy-start(f32[1,2048]{1,0:T(1,128)} %copy-done.9) | copy-start | bytes 24580
  546.4 19.9 %copy-start.14 = (f32[256]{0:T(256)S(1)}, f32[256]{0:T(256)}, u32[]{:S(2)}) copy-start(f32[256]{0:T(256)} %copy-done.13) | copy-start | bytes 3076
  546.5 221.2 %all-gather.17.cloned.1.call-start = ((), (), s32[]{:S(2)}) async-start(), calls=%async_computation.13 | async-start | bytes 5242880 | tf_op jit(solution)/shard_map/all_gather | solution.py:693
  627.0 308.0 %all-gather.15.cloned.1.call-start = ((), (), s32[]{:S(2)}) async-start(), calls=%async_computation.11 | async-start | bytes 5242880 | tf_op jit(solution)/shard_map/all_gather | solution.py:693
  627.5 417.3 %reduce-scatter.14.cloned.1.call-start = ((), (), s32[]{:S(2)}) async-start(), calls=%async_computation.15 | async-start | bytes 18874368 | tf_op jit(solution)/shard_map/reduce_scatter | solution.py:692
  661.5 52.5 %copy-start.12 = (f32[1,2048]{1,0:T(1,128)S(1)}, f32[1,2048]{1,0:T(1,128)}, u32[]{:S(2)}) copy-start(f32[1,2048]{1,0:T(1,128)} %copy-done.11) | copy-start | bytes 24580
  661.5 52.5 %copy-start.16 = (f32[1024]{0:T(1024)S(1)}, f32[1024]{0:T(1024)}, u32[]{:S(2)}) copy-start(f32[1024]{0:T(1024)} %copy-done.15) | copy-start | bytes 12292
  714.1 4.2 copy-start.8
Sparse Core Ops, SparseCore 0:
  12.9 84.7 all-gather.6
  121.4 51.2 reduce-scatter.5
  175.0 151.0 all-gather.10
  328.5 50.9 all-gather.8
  381.6 82.4 all-gather.12
  515.4 50.8 reduce-scatter.9
  569.2 52.6 reduce-scatter.7
  624.4 89.5 reduce-scatter.11
  716.6 51.0 all-gather.16
  769.5 70.8 all-gather.14
  842.8 201.9 reduce-scatter.13

commit v3 on v2

--- a/solution.py
+++ b/solution.py
@@ -178,12 +178,16 @@
     def __init__(self, at, pout, own, din, uin, sems):
         self.at, self.pout, self.own, self.din, self.uin = at, pout, own, din, uin
         self.po_s, self.po_r, self.d_s, self.d_r, self.u_s, self.u_r = sems
-        self.pieces = own.shape[1]
+        self.slots, self.pieces = pout.shape[0], own.shape[1]
 
     def core_copy(self, k):
         j = order_of(k, self.at)
         return remote(
-            self.pout.at[k % 2], self.own.at[j], self.po_s.at[k % 2], self.po_r.at[k], self.at.core
+            self.pout.at[k % self.slots],
+            self.own.at[j],
+            self.po_s.at[k % self.slots],
+            self.po_r.at[k],
+            self.at.core,
         )
 
     def down_copy(self, s, i):
@@ -202,10 +206,10 @@
         )
 
     def other(self, k, tile):
-        if k >= 2:
-            self.core_copy(k - 2).wait_send()
+        if k >= self.slots:
+            self.core_copy(k - self.slots).wait_send()
         j = order_of(k, self.at)
-        tile(2 * j + 1 - self.at.c, lambda i, v: self.store(self.pout, (k % 2,), i, v, False))
+        tile(2 * j + 1 - self.at.c, lambda i, v: self.store(self.pout, (k % self.slots,), i, v, False))
         self.core_copy(k).start()
 
     def store(self, ref, lead, i, value, add):
@@ -231,11 +235,10 @@
                 for i in range(self.pieces):
                     self.up_copy(k, i).start()
 
-    def add(self, dst, src, i):
-        rows = dst.shape[0]
-        step = 64
-        for r in range(0, rows, step):
-            rs = pl.ds(r, step)
+    def add(self, dst, src):
+        @pl.loop(0, dst.shape[0] // 64)
+        def _(b):
+            rs = pl.ds(pl.multiple_of(b * 64, 64), 64)
             dst[rs, :] = (dst[rs, :].astype(F32) + src[rs, :].astype(F32)).astype(BF)
 
     def slot(self, t):
@@ -249,13 +252,13 @@
             @pl.when((sd >= 0) & (sd < p) & at.has_above)
             def _():
                 self.down_copy(sd, i).wait_recv()
-                self.add(self.own.at[sd, i], self.din.at[sd, i], i)
+                self.add(self.own.at[sd, i], self.din.at[sd, i])
                 self.down_copy(sd, i).start()
 
             @pl.when((su >= 0) & (su < n - 1 - p) & at.has_below)
             def _():
                 self.up_copy(su, i).wait_recv()
-                self.add(self.own.at[n - 1 - su, i], self.uin.at[su, i], i)
+                self.add(self.own.at[n - 1 - su, i], self.uin.at[su, i])
                 self.up_copy(su, i).start()
 
     def final(self, out):
@@ -272,22 +275,33 @@
             def _():
                 self.up_copy(n - 1 - p, i).wait_recv()
 
-            for r in range(0, out.shape[1], 64):
-                rs = pl.ds(r, 64)
-                out[i, rs, :] = self.own[p, i, rs, :].astype(F32)
-
-                @pl.when(at.has_above)
-                def _():
-                    out[i, rs, :] += self.din[p, i, rs, :].astype(F32)
-
-                @pl.when(at.has_below)
-                def _():
-                    out[i, rs, :] += self.uin[n - 1 - p, i, rs, :].astype(F32)
+            def close(parts):
+                @pl.loop(0, out.shape[1] // 64)
+                def _(b):
+                    rs = pl.ds(pl.multiple_of(b * 64, 64), 64)
+                    total = self.own[p, i, rs, :].astype(F32)
+                    for ref, s in parts:
+                        total = total + ref[s, i, rs, :].astype(F32)
+                    out[i, rs, :] = total.astype(out.dtype)
+
+            down, up = (self.din, p), (self.uin, n - 1 - p)
+
+            @pl.when(at.has_above & at.has_below)
+            def _():
+                close([down, up])
+
+            @pl.when(jnp.logical_not(at.has_below))
+            def _():
+                close([down])
+
+            @pl.when(jnp.logical_not(at.has_above))
+            def _():
+                close([up])
 
     def drain(self):
         at = self.at
         n, p = at.n, at.p
-        for k in range(max(0, n - 2), n):
+        for k in range(n - self.slots, n):
             self.core_copy(k).wait_send()
         for s in range(n - 1):
 
@@ -302,14 +316,14 @@
                     self.up_copy(s, i).wait_send()
 
 
-def line_sum_scratch(n, pieces, rows, cols):
+def line_sum_scratch(n, pieces, rows, cols, slots=2):
     dma = pltpu.SemaphoreType.DMA
     return [
-        pltpu.VMEM((2, pieces, rows, cols), BF),
+        pltpu.VMEM((slots, pieces, rows, cols), BF),
         pltpu.VMEM((n, pieces, rows, cols), BF),
         pltpu.VMEM((n - 1, pieces, rows, cols), BF),
         pltpu.VMEM((n - 1, pieces, rows, cols), BF),
-        dma((2,)),
+        dma((slots,)),
         dma((n,)),
         dma((n - 1, pieces)),
         dma((n - 1, pieces)),
@@ -323,12 +337,19 @@
         self.at, self.t, self.r1, self.r2 = at, t, r1, r2
         self.s1, self.v1, self.s2, self.v2 = sems
 
+    def source(self, half, q):
+        return self.t.at[half, q]
+
+    def mine(self, half, own, rs):
+        q = self.at.m if own else (self.at.qy if half == 0 else self.at.qx)
+        return self.t[half, q, rs, :].astype(F32)
+
     def first(self, half, turn):
         at = self.at
         dev, quarter = (at.xdev, at.qx) if half == 0 else (at.ydev, at.qy)
         q = at.qd if turn == 0 else quarter
         return remote(
-            self.t.at[half, q],
+            self.source(half, q),
             self.r1.at[half, turn],
             self.s1.at[half, turn],
             self.v1.at[half, turn],
@@ -343,15 +364,13 @@
         )
 
     def turn(self):
-        at = self.at
         for half in range(2):
-            q = at.qy if half == 0 else at.qx
             self.first(half, 0).wait_recv()
 
-            @pl.loop(0, self.t.shape[2] // 64)
+            @pl.loop(0, self.r1.shape[2] // 64)
             def _(b):
                 rs = pl.ds(pl.multiple_of(b * 64, 64), 64)
-                total = self.r1[half, 0, rs, :].astype(F32) + self.t[half, q, rs, :].astype(F32)
+                total = self.r1[half, 0, rs, :].astype(F32) + self.mine(half, False, rs)
                 self.r1[half, 0, rs, :] = total.astype(BF)
 
             self.second(half).start()
@@ -362,7 +381,7 @@
             self.second(half).wait_recv()
 
     def total(self, half, rs):
-        own = self.t[half, self.at.m, rs, :].astype(F32)
+        own = self.mine(half, True, rs)
         return own + self.r1[half, 1, rs, :].astype(F32) + self.r2[half, rs, :].astype(F32)
 
     def drain(self):
@@ -372,10 +391,34 @@
             self.second(half).wait_send()
 
 
-def quad_sum_scratch(rows, cols):
+class QuadSumHbm(QuadSum):
+    def __init__(self, at, hbm, t, r1, r2, sems):
+        super().__init__(at, t, r1, r2, sems[:4])
+        self.hbm = hbm
+        rows, cols = t.shape[2], t.shape[3]
+        self.loads = []
+        for half in range(2):
+            for own in range(2):
+                q = at.m if own else (at.qy if half == 0 else at.qx)
+                self.loads.append(
+                    pltpu.make_async_copy(
+                        self.source(half, q), t.at[half, own], sems[4].at[half, own]
+                    )
+                )
+
+    def source(self, half, q):
+        rows, cols = self.t.shape[2], self.t.shape[3]
+        rs = pl.ds(pl.multiple_of(q * rows, rows), rows)
+        return self.hbm.at[rs, pl.ds(half * cols, cols)]
+
+    def mine(self, half, own, rs):
+        return self.t[half, int(own), rs, :].astype(F32)
+
+
+def quad_sum_scratch(rows, cols, quarters=4):
     dma = pltpu.SemaphoreType.DMA
     return [
-        pltpu.VMEM((2, 4, rows, cols), BF),
+        pltpu.VMEM((2, quarters, rows, cols), BF),
         pltpu.VMEM((2, 2, rows, cols), BF),
         pltpu.VMEM((2, rows, cols), BF),
         dma((2, 2)),
@@ -448,10 +491,6 @@
         dma((2,)),
         dma((2,)),
     ]
-
-
-def halves(fn):
-    return [fn(0), fn(1)]
 
 
 def last_kernel(
@@ -657,11 +696,193 @@
     )(dqkv, aw, nt, gt, att, x, gh, gain, gmid)
 
 
-def norm_backward(grad_normed, field, scale, gain):
-    unit = field * scale
-    weighted = grad_normed * gain
-    grad_field = scale * (weighted - unit * jnp.mean(weighted * unit, axis=1, keepdims=True))
-    return (grad_field, jnp.sum(grad_normed * unit, axis=0))
+def mid_kernel(
+    n_dp,
+    ggu_hbm,
+    gw_hbm,
+    nm_hbm,
+    ft_hbm,
+    hid_ref,
+    cot_ref,
+    gain_ref,
+    rs_ref,
+    low_ref,
+    lay_ref,
+    gh_ref,
+    gg_ref,
+    ggu,
+    wt,
+    wt_s,
+    nm,
+    nm_s,
+    load_s,
+    *rest,
+):
+    at = Place(n_dp)
+    n = at.n
+    line = LineSum(at, *rest[0:4], rest[4:10])
+    mid = QuadSum(at, *rest[10:13], rest[13:17])
+    lay = QuadSumHbm(at, ft_hbm, *rest[17:20], rest[20:25])
+    gather_low = QuadGather(at, rest[25], low_ref, rest[26:31])
+    gather_lay = QuadGather(at, rest[31], lay_ref, rest[32:37])
+    part, half_cols = mid.t.shape[2], mid.t.shape[3]
+    chunk, width = line.own.shape[2], line.own.shape[3]
+    pieces = line.pieces
+    drows = wt.shape[1]
+    tiles = half_cols // drows
+
+    load = pltpu.make_async_copy(ggu_hbm, ggu, load_s.at[0])
+    load.start()
+
+    def nm_copy(e):
+        k, core = e // 2, e % 2
+        block = 2 * order_of(k, at) + (1 - at.c if core == 0 else at.c)
+        cols = pl.ds(pl.multiple_of(block * chunk, chunk), chunk)
+        return pltpu.make_async_copy(nm_hbm.at[:, cols], nm.at[e % 2], nm_s.at[e % 2])
+
+    def wt_copy(half, i, slot):
+        rows = pl.ds(pl.multiple_of(half * half_cols + i * drows, drows), drows)
+        return pltpu.make_async_copy(gw_hbm.at[rows, :], wt.at[slot], wt_s.at[slot])
+
+    nm_copy(0).start()
+    wt_copy(0, 0, 0).start()
+    for cp in lay.loads:
+        cp.start()
+    enter(at)
+    for way in ((0, 0), (1, 0), (0, 1), (1, 1)):
+        lay.first(*way).start()
+    load.wait()
+
+    def run(e):
+        if e + 1 < 2 * n:
+            nm_copy(e + 1).start()
+        nm_copy(e).wait()
+        lhs = nm[e % 2].T
+
+        def tile(block, put):
+            @pl.loop(0, pieces)
+            def _(i):
+                put(i, dot(lhs, ggu[:, pl.ds(pl.multiple_of(i * width, width), width)]))
+
+        if e % 2 == 0:
+            line.other(e // 2, tile)
+        else:
+            line.mine(e // 2, tile)
+
+    def terms(half):
+        @pl.loop(0, tiles)
+        def _(i):
+            slot = lax.rem(i, 2)
+            if half == 0:
+                nxt = wt_copy(jnp.where(i + 1 < tiles, 0, 1), lax.rem(i + 1, tiles), 1 - slot)
+                nxt.start()
+            else:
+
+                @pl.when(i + 1 < tiles)
+                def _():
+                    wt_copy(1, i + 1, 1 - slot).start()
+
+            wt_copy(half, i, slot).wait()
+            v = dot(ggu[...], wt[slot], NT).astype(BF)
+            cols = pl.ds(pl.multiple_of(i * drows, drows), drows)
+            for q in range(4):
+                mid.t[half, q, :, cols] = v[q * part : (q + 1) * part]
+
+        mid.first(half, 0).start()
+        mid.first(half, 1).start()
+
+    run(0)
+    run(1)
+    terms(0)
+    run(2)
+    run(3)
+    terms(1)
+    for cp in lay.loads:
+        cp.wait()
+    lay.turn()
+    for e in range(4, 2 * n):
+        run(e)
+    lay.arrive()
+
+    @pl.loop(0, part // 32)
+    def _(b):
+        rs = pl.ds(pl.multiple_of(b * 32, 32), 32)
+        for half in range(2):
+            h = hid_ref[rs, pl.ds(half * half_cols, half_cols)]
+            gather_lay.own[half, rs, :] = (h + lay.total(half, rs)).astype(BF)
+
+    gather_lay.start()
+    line.slot(0)
+    mid.turn()
+    mid.arrive()
+    gg_ref[...] = jnp.zeros_like(gg_ref)
+
+    @pl.loop(0, part // 32)
+    def _(b):
+        rs = pl.ds(pl.multiple_of(b * 32, 32), 32)
+        h = hid_ref[rs, :]
+        scale = lax.rsqrt(jnp.mean(h * h, axis=1, keepdims=True) + EPS)
+        g = jnp.concatenate([mid.total(0, rs), mid.total(1, rs)], axis=1)
+        unit = h * scale
+        weighted = g * gain_ref[...]
+        field = scale * (weighted - unit * jnp.mean(weighted * unit, axis=1, keepdims=True))
+        res = cot_ref[rs, :].astype(F32) + field
+        gh_ref[rs, :] = res
+        low = res.astype(BF)
+        gather_low.own[0, rs, :] = low[:, :half_cols]
+        gather_low.own[1, rs, :] = low[:, half_cols:]
+        gg_ref[...] += jnp.sum(g * unit, axis=0, keepdims=True)
+
+    gather_low.start()
+    gather_lay.forward()
+    for s in range(1, n - 2):
+        line.slot(s)
+    gather_low.forward()
+    line.final(rs_ref)
+    gather_lay.finish()
+    gather_low.finish()
+    line.drain()
+    mid.drain()
+    lay.drain()
+
+
+def mid_stage(n_dp, ggu, gw, nm, ft, hid, cot, gain):
+    seq, wide = ggu.shape
+    d = gw.shape[0]
+    n, part, chunk = n_dp // 2, seq // 4, d // n_dp
+    dma = pltpu.SemaphoreType.DMA
+    hbm = pl.BlockSpec(memory_space=pl.ANY)
+    vm = pl.BlockSpec(memory_space=pltpu.VMEM)
+    pieces = 4
+    return pl.pallas_call(
+        functools.partial(mid_kernel, n_dp),
+        out_shape=[
+            jax.ShapeDtypeStruct((pieces, chunk, wide // pieces), BF),
+            jax.ShapeDtypeStruct((seq, d), BF),
+            jax.ShapeDtypeStruct((seq, d), BF),
+            jax.ShapeDtypeStruct((part, d), F32),
+            jax.ShapeDtypeStruct((1, d), F32),
+        ],
+        in_specs=[hbm] * 4 + [vm] * 3,
+        out_specs=[vm, hbm, hbm, vm, vm],
+        scratch_shapes=[
+            pltpu.VMEM((seq, wide), BF),
+            pltpu.VMEM((2, 256, wide), BF),
+            dma((2,)),
+            pltpu.VMEM((2, seq, chunk), BF),
+            dma((2,)),
+            dma((1,)),
+        ]
+        + line_sum_scratch(n, pieces, chunk, wide // pieces, 1)
+        + quad_sum_scratch(part, d // 2)
+        + quad_sum_scratch(part, d // 2, 2)
+        + [dma((2, 2))]
+        + quad_gather_scratch(part, d // 2) * 2,
+        compiler_params=pltpu.CompilerParams(
+            collective_id=4, has_side_effects=True, vmem_limit_bytes=VMEM_LIMIT
+        ),
+        name="mid_stage",
+    )(ggu, gw, nm, ft, hid, cot, gain)
 
 
 def after(value, *deps):
@@ -696,7 +917,11 @@
 
     attn_shard = jnp.concatenate([w_query, w_key, w_value, w_output.T], axis=1).astype(BF)
     attn_w = gather(attn_shard)
-    gu_shard = jnp.concatenate([w_gate, w_up], axis=1).astype(BF)
+    pieces = 4
+    pack = lambda g, u: jnp.stack(
+        [g.reshape(g.shape[0], pieces, -1), u.reshape(u.shape[0], pieces, -1)], axis=2
+    ).reshape(g.shape[0], -1)
+    gu_shard = pack(w_gate, w_up).astype(BF)
     gu_w = gather(after(gu_shard, attn_w))
     down_shard = w_down.T.astype(BF)
     down_w = gather(after(down_shard, gu_w))
@@ -717,11 +942,9 @@
     hidden = my_source + attn_sum.astype(F32)
     scale_mid = lax.rsqrt(jnp.mean(hidden * hidden, axis=1, keepdims=True) + EPS)
     normed_mid = mp_gather((hidden * scale_mid * gain_mid).astype(BF))
-    gate_w, up_w = gu_w[:, :ff], gu_w[:, ff:]
-    gate = dot(normed_mid, gate_w).astype(BF)
-    up = dot(normed_mid, up_w).astype(BF)
-    gate_f = gate.astype(F32)
-    up_f = up.astype(F32)
+    gu = dot(normed_mid, gu_w).astype(BF).reshape(seq, pieces, 2, -1)
+    gate_f = gu[:, :, 0].reshape(seq, ff).astype(F32)
+    up_f = gu[:, :, 1].reshape(seq, ff).astype(F32)
     sg = jax.nn.sigmoid(gate_f)
     silu = gate_f * sg
     inner = (silu * up_f).astype(BF)
@@ -730,19 +953,18 @@
     grad_inner = dot(grad_ffn, down_w)
     grad_gate = (grad_inner * up_f * sg * (1.0 + gate_f * (1.0 - sg))).astype(BF)
     grad_up = (grad_inner * silu).astype(BF)
-    mid_terms = dot(grad_gate, gate_w, NT) + dot(grad_up, up_w, NT)
-    grad_mid = mp_scatter(mid_terms).astype(F32)
     rs_down = scatter(grad_down_t)
-    grad_gu = jnp.concatenate(
-        [dot(normed_mid, grad_gate, TN).astype(BF), dot(normed_mid, grad_up, TN).astype(BF)], axis=1
+    ffn_terms = dot(inner, down_w, NT).astype(BF)
+    rs_gu, grad_low, layer_out, grad_hidden, g_gain_mid = mid_stage(
+        lax.axis_size("dp"),
+        pack(grad_gate, grad_up),
+        gu_w,
+        normed_mid,
+        ffn_terms,
+        hidden,
+        mine(grad_ffn),
+        gain_mid,
     )
-    rs_gu = scatter(after(grad_gu, rs_down))
-    ffn_sum = mp_scatter(dot(inner, down_w, NT))
-    layer_out = mp_gather((hidden + ffn_sum.astype(F32)).astype(BF))
-
-    g_norm, g_gain_mid = norm_backward(grad_mid, hidden, scale_mid, gain_mid)
-    grad_hidden = mine(grad_ffn).astype(F32) + g_norm
-    grad_low = mp_gather(grad_hidden.astype(BF))
     grad_attended = dot(grad_low, out_wt).astype(BF)
     dq, dk, dv = attn_bwd(qkv, grad_attended, counts, seq)
     rs_attn, grad_low_in, g_gains = last_stage(
@@ -755,12 +977,15 @@
         mine(inputs),
         grad_hidden,
         gain_in,
-        g_gain_mid[None],
+        g_gain_mid,
     )
     input_grad = grad_low_in.astype(F32)
     width = g_gains.shape[1] // lax.axis_size("dp")
     g_gains = lax.dynamic_slice_in_dim(g_gains, lax.axis_index("dp") * width, width, 1)
-    rs_gu = rs_gu.astype(F32)
+    half = ff // pieces
+    unpack = lambda i: jnp.concatenate(
+        [rs_gu[k, :, i * half : (i + 1) * half] for k in range(pieces)], axis=1
+    ).astype(F32)
     return (
         layer_out,
         input_grad,
@@ -770,8 +995,8 @@
         rs_attn[2],
         rs_attn[3].T,
         g_gains[1],
-        rs_gu[:, :ff],
-        rs_gu[:, ff:],
+        unpack(0),
+        unpack(1),
         rs_down.astype(F32).T,
     )
 

time: 1070 us -> 932 us (0.87)
  waiting for transfers between devices: 642 us -> 288 us
  Pallas kernels: 149 us -> 288 us
  local copies, waits for them, and re-layouts: 38.5 us -> 143 us
  matrix products: 158 us -> 94.7 us
  other arithmetic: 47.7 us -> 77.4 us
    pallas_call x0 -> x1, Pallas kernels: none -> 168 us  [mid_stage(): pl.pallas_call(functools.partial(mid_kernel, n_dp), out_shape=[jax.ShapeD...]
    reduce_scatter x2 -> x1, waiting for transfers between devices: 161 us -> 0.01 us  [on_device(): lax.psum_scatter(x, 'dp', scatter_dimension=0, tiled=True)]
    reduce_scatter x3 -> x1, waiting for transfers between devices: 119 us -> 30.6 us  [on_device(): lax.psum_scatter(x.astype(BF), 'mp', scatter_dimension=0, tiled=True)]
    dot_general x12 -> x7, matrix products: 158 us -> 94.7 us  [dot(): return lax.dot_general(a, b, dims, preferred_element_type=F32)]
    all_gather x3, waiting for transfers between devices: 265 us -> 209 us  [on_device(): gather = lambda x: lax.all_gather(x, 'dp', axis=0, tiled=True)]
    another operation x0 -> x4, local copies, waits for them, and re-layouts: none -> 47.4 us  [on_device(): jnp.stack([g.reshape(g.shape[0], pieces, -1), u.reshape(u.shape[0], piece...]
    all_gather x3 -> x1, waiting for transfers between devices: 95.9 us -> 48.7 us  [on_device(): mp_gather = lambda x: lax.all_gather(x, 'mp', axis=0, tiled=True)]
    pallas_call x1, Pallas kernels: 131 us -> 101 us  [last_stage(): pl.pallas_call(functools.partial(last_kernel, n_dp), out_shape=[jax.Shape...]
  transfers between devices with their start and end apart: 11 -> 6, of which waited for: 10 -> 5; matrix products, arithmetic and copies ran while one was open for 14% -> 27% of each run, Pallas kernels for 13% -> 31%
where the time goes in v3:
time: 932 us; the launch traced here: 921 us
  waiting for transfers between devices  288 us (31%)
  Pallas kernels  288 us (31%)
  local copies, waits for them, and re-layouts  143 us (15%)
  matrix products  94.7 us (10%)
  other arithmetic  77.4 us (8%)
  between operations  15.2 us (2%)
  blocking collectives  13.6 us (1%)
    all_gather x3, waiting for transfers between devices, on_device(): gather = lambda x: lax.all_gather(x, 'dp', axis=0, tiled=True)  209 us
    pallas_call x1, Pallas kernels, mid_stage(): pl.pallas_call(functools.partial(mid_kernel, n_dp), out_shape=[jax.ShapeD...  168 us
    pallas_call x1, Pallas kernels, last_stage(): pl.pallas_call(functools.partial(last_kernel, n_dp), out_shape=[jax.Shape...  101 us
    dot_general x7, matrix products, dot(): return lax.dot_general(a, b, dims, preferred_element_type=F32)  94.7 us
    all_gather x1, waiting for transfers between devices, on_device(): mp_gather = lambda x: lax.all_gather(x, 'mp', axis=0, tiled=True)  48.7 us
    another operation x4, local copies, waits for them, and re-layouts, on_device(): jnp.stack([g.reshape(g.shape[0], pieces, -1), u.reshape(u.shape[0], piece...  47.4 us
    unnamed x31, local copies, waits for them, and re-layouts  33.2 us
    reduce_scatter x1, waiting for transfers between devices, on_device(): lax.psum_scatter(x.astype(BF), 'mp', scatter_dimension=0, tiled=True)  30.6 us
  transfers between devices with their start and end apart: 6, of which 5 were waited for; matrix products, arithmetic and copies ran while one was open for 27% of the time, Pallas kernels for 31%

profile of v3, /device:TPU:0, one launch (start us, length us, event | category | flops | bytes accessed | tf_op | source)
XLA Modules:
  0.0 920.9 jit_solution(10308463389687888263)
XLA Ops:
  12.8 6.4 copy.26
  20.0 13.6 %all_gather.18 = bf16[2,2048]{1,0:T(2,128)(2,1)S(1)} all-gather(bf16[2,256]{1,0:T(2,128)(2,1)S(1)} %pad_maximum_fusion.4), channel_id=1, replica_groups=mesh['dp'=8,'mp'=4] {'dp'}, dimensions={1}, use_global_device_ids=true | all-gather | bytes 9216 | tf_op jit(solution)/shard_map/all_gather | solution.py:928
  36.8 60.9 %all-gather.5.cloned.1.call-done.aw_hbm = bf16[2048,2048]{1,0:T(8,128)(2,1)} async-done(((bf16[256,2048]{1,0:T(8,128)(2,1)}), bf16[2048,2048]{1,0:T(8,128)(2,1)}) %all-gather.5.cloned.1.call-update) | async-done | bytes 8388624 | tf_op jit(solution)/shard_map/all_gather | solution.py:912
  97.7 10.7 %fusion.6.q_ref.k_ref.v_ref = bf16[1024,1536]{1,0:T(8,128)(2,1)S(1)} fusion(bf16[2048,2048]{1,0:T(8,128)(2,1)} %all-gather.5.cloned.1.call-done.aw_hbm, bf16[1024,2048]{0,1:T(8,128)(2,1)} %copy.26, f32[2048]{0:T(1024)S(1)} %bitcast.66, f32[1024]{0:T(1024)S(1)} %add_rsqrt_fusion), kind=kOutput, calls=%fused_computation.18 | convolution fusion | flops 6452412416 | bytes 13643776 | tf_op jit(solution)/shard_map/dot_general | solution.py:21
  108.4 5.9 attn_fwd.1.att_hbm
  115.4 6.0 convolution_convert_fusion.3
  130.4 6.7 pad_maximum_fusion.2
  137.1 4.5 convert_element_type.81
  142.1 30.6 %reduce-scatter.3.cloned.1.call-done = bf16[256,2048]{1,0:T(8,128)(2,1)} async-done(((bf16[1024,2048]{1,0:T(8,128)(2,1)}), bf16[256,2048]{1,0:T(8,128)(2,1)}) %reduce-scatter.3.cloned.1.call-update) | async-done | bytes 1048592 | tf_op jit(solution)/shard_map/reduce_scatter | solution.py:915
  179.8 146.4 %all-gather.7.cloned.1.call-done.gw_hbm = bf16[2048,4096]{1,0:T(8,128)(2,1)} async-done(((bf16[256,4096]{1,0:T(8,128)(2,1)}), bf16[2048,4096]{1,0:T(8,128)(2,1)}) %all-gather.7.cloned.1.call-update) | async-done | bytes 16777232 | tf_op jit(solution)/shard_map/all_gather | solution.py:912
  326.3 4.6 broadcast_select_fusion
  330.9 48.7 %all-gather.11.cloned.1.call-done.nm_hbm = bf16[1024,2048]{1,0:T(8,128)(2,1)} async-done(((bf16[256,2048]{1,0:T(8,128)(2,1)}), bf16[1024,2048]{1,0:T(8,128)(2,1)}) %all-gather.11.cloned.1.call-update) | async-done | bytes 4194320 | tf_op jit(solution)/shard_map/all_gather | solution.py:914
  379.6 22.8 %convolution_convert_fusion.1 = bf16[1024,4096]{1,0:T(8,128)(2,1)} fusion(bf16[1024,2048]{1,0:T(8,128)(2,1)} %all-gather.11.cloned.1.call-done.nm_hbm, bf16[2048,4096]{1,0:T(8,128)(2,1)} %all-gather.7.cloned.1.call-done.gw_hbm), kind=kOutput, calls=%fused_computation.12 | convolution fusion | flops 17184063488 | bytes 29360128 | tf_op jit(solution)/shard_map/dot_general | solution.py:21
  402.4 14.6 %reshape.54 = bf16[1024,4,2,512]{3,2,1,0:T(2,128)(2,1)} reshape(bf16[1024,4096]{1,0:T(8,128)(2,1)} %convolution_convert_fusion.1) | data formatting | bytes 16777216 | tf_op jit(solution)/shard_map/reshape | solution.py:945
  416.9 17.2 %fusion.17 = (bf16[1024,4,1,512]{3,2,1,0:T(2,128)(2,1)}, bf16[1024,4,1,512]{3,2,1,0:T(2,128)(2,1)}) fusion(bf16[1024,4,2,512]{3,2,1,0:T(2,128)(2,1)} %reshape.54), kind=kLoop, calls=%fused_computation.56 | loop fusion | bytes 16777216 | tf_op jit(solution)/shard_map/slice | solution.py:947
  434.2 13.3 %copy_convert_fusion = (f32[1024,4,1,512]{3,1,0,2:T(4,128)S(1)}, f32[1024,4,1,512]{3,1,0,2:T(4,128)S(1)}) fusion(bf16[1024,4,1,512]{3,2,1,0:T(2,128)(2,1)} %get-tuple-element.54, bf16[1024,4,1,512]{3,2,1,0:T(2,128)(2,1)} %get-tuple-element.53), kind=kLoop, calls=%fused_computation.15 | loop fusion | flops 4194304 | bytes 25165824 | tf_op jit(solution)/shard_map/convert_element_type | solution.py:946
  447.5 7.5 copy.36
  455.0 7.4 copy.37
  463.6 22.2 %multiply_convert_fusion = (bf16[1024,2048]{1,0:T(8,128)(2,1)}, bf16[1024,2048]{1,0:T(8,128)(2,1)}, bf16[1024,2048]{1,0:T(8,128)(2,1)}) fusion(f32[1024,2048]{1,0:T(8,128)} %bitcast.63, f32[1024,2048]{1,0:T(8,128)} %bitcast.64, bf16[1024,2048]{1,0:T(8,128)(2,1)} %broadcast_select_fusion, bf16[2048,2048]{0,1:T(8,128)(2,1)} %all-gather.9.cloned.1.call-done), kind=kOutput, calls=%fused_computation.6 | convolution fusion | flops 8621391872 | bytes 41943040 | tf_op jit(solution)/shard_map/dot_general | solution.py:21
  485.8 14.0 %convolution_convert_fusion = bf16[2048,2048]{1,0:T(8,128)(2,1)} fusion(bf16[1024,2048]{1,0:T(8,128)(2,1)} %broadcast_select_fusion, bf16[1024,2048]{1,0:T(8,128)(2,1)} %get-tuple-element.50), kind=kOutput, calls=%fused_computation.11 | convolution fusion | flops 8594128896 | bytes 16777216 | tf_op jit(solution)/shard_map/dot_general | solution.py:21
  506.3 20.9 %stack_reshape.20 = bf16[1024,4,1,512]{3,2,1,0:T(2,128)(2,1)} reshape(bf16[1024,2048]{1,0:T(8,128)(2,1)} %get-tuple-element.51) | data formatting | bytes 8388608 | tf_op jit(solution)/shard_map/stack;reshape | solution.py:921
  527.2 20.9 %stack_reshape.21 = bf16[1024,4,1,512]{3,2,1,0:T(2,128)(2,1)} reshape(bf16[1024,2048]{1,0:T(8,128)(2,1)} %get-tuple-element.52) | data formatting | bytes 8388608 | tf_op jit(solution)/shard_map/stack;reshape | solution.py:921
  548.2 19.8 %pad_maximum_fusion = bf16[1024,4,2,512]{3,2,1,0:T(2,128)(2,1)} fusion(bf16[1024,4,1,512]{3,2,1,0:T(2,128)(2,1)} %stack_reshape.21, bf16[1024,4,1,512]{3,2,1,0:T(2,128)(2,1)} %stack_reshape.20), kind=kLoop, calls=%fused_computation.5 | loop fusion | flops 16777216 | bytes 16777216 | tf_op jit(solution)/shard_map/stack | solution.py:921
  568.0 15.0 %reshape.55.ggu_hbm = bf16[1024,4096]{1,0:T(8,128)(2,1)} reshape(bf16[1024,4,2,512]{3,2,1,0:T(2,128)(2,1)} %pad_maximum_fusion) | data formatting | bytes 16777216 | tf_op jit(solution)/shard_map/reshape | solution.py:923
  582.9 13.9 %convolution_convert_fusion.2.ft_hbm = bf16[1024,2048]{1,0:T(8,128)(2,1)} fusion(bf16[1024,2048]{1,0:T(8,128)(2,1)} %get-tuple-element.50, bf16[2048,2048]{0,1:T(8,128)(2,1)} %all-gather.9.cloned.1.call-done), kind=kOutput, calls=%fused_computation.19 | convolution fusion | flops 8592031744 | bytes 16777216 | tf_op jit(solution)/shard_map/dot_general | solution.py:21
  596.8 168.2 %mid_stage.1 = (bf16[4,256,1024]{2,1,0:T(8,128)(2,1)}, bf16[1024,2048]{1,0:T(8,128)(2,1)}, bf16[1024,2048]{1,0:T(8,128)(2,1)}, f32[256,2048]{1,0:T(8,128)}, f32[1,2048]{1,0:T(1,128)}) custom-call(bf16[1024,4096]{1,0:T(8,128)(2,1)} %reshape.55.ggu_hbm, bf16[2048,4096]{1,0:T(8,128)(2,1)} %all-gather.7.cloned.1.call-done.gw_hbm, ...), custom_call_target="tpu_custom_call" | custom-call | tf_op jit(solution)/shard_map/mid_stage/pallas_call | solution.py:857
  765.0 6.4 copy.31
  771.4 5.2 fusion.12.g_ref
  776.6 12.4 %attn_bwd.1 = (bf16[1024,512]{1,0:T(8,128)(2,1)S(1)}, bf16[1024,512]{1,0:T(8,128)(2,1)S(1)}, bf16[1024,512]{1,0:T(8,128)(2,1)S(1)}) custom-call(s32[1]{0:T(128)} %copy.41.count_ref, bf16[1024,1536]{1,0:T(8,128)(2,1)} %copy-done, bf16[1024,1536]{1,0:T(8,128)(2,1)} %copy-done, bf16[1024,1536]{1,0:T(8,128)(2,1)} %copy-done, bf16[1024,512]{1,0:T(8,128)(2,1)S(1)} %fusion.12.g_ref), custom_call_target="tpu_custom_call" | custom-call | tf_op jit(solution)/shard_map/attn_bwd/pallas_call | solution.py:98
  790.7 101.3 %last_stage.1 = (f32[4,256,512]{2,1,0:T(8,128)}, bf16[1024,2048]{1,0:T(8,128)(2,1)}, f32[8,2048]{1,0:T(8,128)}) custom-call(bf16[1024,1536]{1,0:T(8,128)(2,1)} %pad_maximum_fusion.1.dqkv_hbm, bf16[2048,2048]{1,0:T(8,128)(2,1)} %all-gather.5.cloned.1.call-done.aw_hbm, bf16[2048,1024]{1,0:T(8,128)(2,1)} %fusion.15.nt_hbm, bf16[2048,1024]{1,0:T(8,128)(2,1)} %bitcast.62, ...), custom_call_target="tpu_custom_call" | custom-call | tf_op jit(solution)/shard_map/last_stage/pallas_call | solution.py:666
  892.1 6.8 convert_element_type.100
  909.1 4.8 copy.42
  (72 shorter events, 46.1 us)
Async XLA Ops:
  7.2 90.5 %all-gather.5.cloned.1.call-start = ((), (), s32[]{:S(2)}) async-start(), calls=%async_computation.2 | async-start | bytes 9437184 | tf_op jit(solution)/shard_map/all_gather | solution.py:912
  12.8 6.5 copy-start.10
  12.8 6.5 copy-start.11
  12.8 160.0 %reduce-scatter.3.cloned.1.call-start = ((), (), s32[]{:S(2)}) async-start(), calls=%async_computation.5 | async-start | bytes 5242880 | tf_op jit(solution)/shard_map/reduce_scatter | solution.py:915
  36.7 139.8 %copy-start.9 = (f32[1,2048]{1,0:T(1,128)}, f32[1,2048]{1,0:T(1,128)S(1)}, u32[]{:S(2)}) copy-start(f32[1,2048]{1,0:T(1,128)S(1)} %get-tuple-element.70.gain_ref) | copy-start | bytes 24580
  36.7 465.4 %copy-start.8 = (f32[1,2048]{1,0:T(1,128)}, f32[1,2048]{1,0:T(1,128)S(1)}, u32[]{:S(2)}) copy-start(f32[1,2048]{1,0:T(1,128)S(1)} %get-tuple-element.69.gain_ref) | copy-start | bytes 24580
  108.4 5.9 copy-start
  114.3 1.1 copy-start.1
  121.3 1.6 copy-start.4
  121.4 204.8 %all-gather.7.cloned.1.call-start = ((), (), s32[]{:S(2)}) async-start(), calls=%async_computation.3 | async-start | bytes 18874368 | tf_op jit(solution)/shard_map/all_gather | solution.py:912
  141.6 237.9 %all-gather.11.cloned.1.call-start = ((), (), s32[]{:S(2)}) async-start(), calls=%async_computation.6 | async-start | bytes 5242880 | tf_op jit(solution)/shard_map/all_gather | solution.py:914
  172.8 3.4 copy-start.3
  176.1 1.0 copy-start.2
  176.1 2.6 copy-start.5
  178.6 285.0 %all-gather.9.cloned.1.call-start = ((), (), s32[]{:S(2)}) async-start(), calls=%async_computation.4 | async-start | bytes 9437184 | tf_op jit(solution)/shard_map/all_gather | solution.py:912
  326.2 579.6 %reduce-scatter.5.cloned.1.call-start = ((), (), s32[]{:S(2)}) async-start(), calls=%async_computation.7 | async-start | bytes 9437184 | tf_op jit(solution)/shard_map/reduce_scatter | solution.py:913
  892.1 6.8 copy-start.7
  898.9 3.6 copy-start.6
Sparse Core Ops, SparseCore 0:
  12.9 84.7 all-gather.4
  121.5 51.2 reduce-scatter.2
  175.0 151.0 all-gather.6
  328.6 50.9 all-gather.10
  381.1 82.4 all-gather.8
  500.0 88.2 reduce-scatter.4

commit v4 on v2

--- a/solution.py
+++ b/solution.py
@@ -112,6 +112,7 @@
 
 MESH = pl.DeviceIdType.MESH
 VMEM_LIMIT = 60 * 1024 * 1024
+PIECES = 4
 
 
 class Place:
@@ -178,12 +179,16 @@
     def __init__(self, at, pout, own, din, uin, sems):
         self.at, self.pout, self.own, self.din, self.uin = at, pout, own, din, uin
         self.po_s, self.po_r, self.d_s, self.d_r, self.u_s, self.u_r = sems
-        self.pieces = own.shape[1]
+        self.slots, self.pieces = pout.shape[0], own.shape[1]
 
     def core_copy(self, k):
         j = order_of(k, self.at)
         return remote(
-            self.pout.at[k % 2], self.own.at[j], self.po_s.at[k % 2], self.po_r.at[k], self.at.core
+            self.pout.at[k % self.slots],
+            self.own.at[j],
+            self.po_s.at[k % self.slots],
+            self.po_r.at[k],
+            self.at.core,
         )
 
     def down_copy(self, s, i):
@@ -202,10 +207,10 @@
         )
 
     def other(self, k, tile):
-        if k >= 2:
-            self.core_copy(k - 2).wait_send()
+        if k >= self.slots:
+            self.core_copy(k - self.slots).wait_send()
         j = order_of(k, self.at)
-        tile(2 * j + 1 - self.at.c, lambda i, v: self.store(self.pout, (k % 2,), i, v, False))
+        tile(2 * j + 1 - self.at.c, lambda i, v: self.store(self.pout, (k % self.slots,), i, v, False))
         self.core_copy(k).start()
 
     def store(self, ref, lead, i, value, add):
@@ -231,11 +236,10 @@
                 for i in range(self.pieces):
                     self.up_copy(k, i).start()
 
-    def add(self, dst, src, i):
-        rows = dst.shape[0]
-        step = 64
-        for r in range(0, rows, step):
-            rs = pl.ds(r, step)
+    def add(self, dst, src):
+        @pl.loop(0, dst.shape[0] // 64)
+        def _(b):
+            rs = pl.ds(pl.multiple_of(b * 64, 64), 64)
             dst[rs, :] = (dst[rs, :].astype(F32) + src[rs, :].astype(F32)).astype(BF)
 
     def slot(self, t):
@@ -249,13 +253,13 @@
             @pl.when((sd >= 0) & (sd < p) & at.has_above)
             def _():
                 self.down_copy(sd, i).wait_recv()
-                self.add(self.own.at[sd, i], self.din.at[sd, i], i)
+                self.add(self.own.at[sd, i], self.din.at[sd, i])
                 self.down_copy(sd, i).start()
 
             @pl.when((su >= 0) & (su < n - 1 - p) & at.has_below)
             def _():
                 self.up_copy(su, i).wait_recv()
-                self.add(self.own.at[n - 1 - su, i], self.uin.at[su, i], i)
+                self.add(self.own.at[n - 1 - su, i], self.uin.at[su, i])
                 self.up_copy(su, i).start()
 
     def final(self, out):
@@ -272,22 +276,33 @@
             def _():
                 self.up_copy(n - 1 - p, i).wait_recv()
 
-            for r in range(0, out.shape[1], 64):
-                rs = pl.ds(r, 64)
-                out[i, rs, :] = self.own[p, i, rs, :].astype(F32)
-
-                @pl.when(at.has_above)
-                def _():
-                    out[i, rs, :] += self.din[p, i, rs, :].astype(F32)
-
-                @pl.when(at.has_below)
-                def _():
-                    out[i, rs, :] += self.uin[n - 1 - p, i, rs, :].astype(F32)
+            def close(parts):
+                @pl.loop(0, out.shape[1] // 64)
+                def _(b):
+                    rs = pl.ds(pl.multiple_of(b * 64, 64), 64)
+                    total = self.own[p, i, rs, :].astype(F32)
+                    for ref, s in parts:
+                        total = total + ref[s, i, rs, :].astype(F32)
+                    out[i, rs, :] = total.astype(out.dtype)
+
+            down, up = (self.din, p), (self.uin, n - 1 - p)
+
+            @pl.when(at.has_above & at.has_below)
+            def _():
+                close([down, up])
+
+            @pl.when(jnp.logical_not(at.has_below))
+            def _():
+                close([down])
+
+            @pl.when(jnp.logical_not(at.has_above))
+            def _():
+                close([up])
 
     def drain(self):
         at = self.at
         n, p = at.n, at.p
-        for k in range(max(0, n - 2), n):
+        for k in range(n - self.slots, n):
             self.core_copy(k).wait_send()
         for s in range(n - 1):
 
@@ -302,14 +317,14 @@
                     self.up_copy(s, i).wait_send()
 
 
-def line_sum_scratch(n, pieces, rows, cols):
+def line_sum_scratch(n, pieces, rows, cols, slots=2):
     dma = pltpu.SemaphoreType.DMA
     return [
-        pltpu.VMEM((2, pieces, rows, cols), BF),
+        pltpu.VMEM((slots, pieces, rows, cols), BF),
         pltpu.VMEM((n, pieces, rows, cols), BF),
         pltpu.VMEM((n - 1, pieces, rows, cols), BF),
         pltpu.VMEM((n - 1, pieces, rows, cols), BF),
-        dma((2,)),
+        dma((slots,)),
         dma((n,)),
         dma((n - 1, pieces)),
         dma((n - 1, pieces)),
@@ -323,12 +338,19 @@
         self.at, self.t, self.r1, self.r2 = at, t, r1, r2
         self.s1, self.v1, self.s2, self.v2 = sems
 
+    def source(self, half, q):
+        return self.t.at[half, q]
+
+    def mine(self, half, own, rs):
+        q = self.at.m if own else (self.at.qy if half == 0 else self.at.qx)
+        return self.t[half, q, rs, :].astype(F32)
+
     def first(self, half, turn):
         at = self.at
         dev, quarter = (at.xdev, at.qx) if half == 0 else (at.ydev, at.qy)
         q = at.qd if turn == 0 else quarter
         return remote(
-            self.t.at[half, q],
+            self.source(half, q),
             self.r1.at[half, turn],
             self.s1.at[half, turn],
             self.v1.at[half, turn],
@@ -343,15 +365,13 @@
         )
 
     def turn(self):
-        at = self.at
         for half in range(2):
-            q = at.qy if half == 0 else at.qx
             self.first(half, 0).wait_recv()
 
-            @pl.loop(0, self.t.shape[2] // 64)
+            @pl.loop(0, self.r1.shape[2] // 64)
             def _(b):
                 rs = pl.ds(pl.multiple_of(b * 64, 64), 64)
-                total = self.r1[half, 0, rs, :].astype(F32) + self.t[half, q, rs, :].astype(F32)
+                total = self.r1[half, 0, rs, :].astype(F32) + self.mine(half, False, rs)
                 self.r1[half, 0, rs, :] = total.astype(BF)
 
             self.second(half).start()
@@ -362,7 +382,7 @@
             self.second(half).wait_recv()
 
     def total(self, half, rs):
-        own = self.t[half, self.at.m, rs, :].astype(F32)
+        own = self.mine(half, True, rs)
         return own + self.r1[half, 1, rs, :].astype(F32) + self.r2[half, rs, :].astype(F32)
 
     def drain(self):
@@ -372,10 +392,34 @@
             self.second(half).wait_send()
 
 
-def quad_sum_scratch(rows, cols):
+class QuadSumHbm(QuadSum):
+    def __init__(self, at, hbm, t, r1, r2, sems):
+        super().__init__(at, t, r1, r2, sems[:4])
+        self.hbm = hbm
+        rows, cols = t.shape[2], t.shape[3]
+        self.loads = []
+        for half in range(2):
+            for own in range(2):
+                q = at.m if own else (at.qy if half == 0 else at.qx)
+                self.loads.append(
+                    pltpu.make_async_copy(
+                        self.source(half, q), t.at[half, own], sems[4].at[half, own]
+                    )
+                )
+
+    def source(self, half, q):
+        rows, cols = self.t.shape[2], self.t.shape[3]
+        rs = pl.ds(pl.multiple_of(q * rows, rows), rows)
+        return self.hbm.at[rs, pl.ds(half * cols, cols)]
+
+    def mine(self, half, own, rs):
+        return self.t[half, int(own), rs, :].astype(F32)
+
+
+def quad_sum_scratch(rows, cols, quarters=4):
     dma = pltpu.SemaphoreType.DMA
     return [
-        pltpu.VMEM((2, 4, rows, cols), BF),
+        pltpu.VMEM((2, quarters, rows, cols), BF),
         pltpu.VMEM((2, 2, rows, cols), BF),
         pltpu.VMEM((2, rows, cols), BF),
         dma((2, 2)),
@@ -450,8 +494,647 @@
     ]
 
 
-def halves(fn):
-    return [fn(0), fn(1)]
+class LineGather:
+    def __init__(self, at, pieces, shard, spot, sems):
+        self.at, self.pieces, self.shard, self.spot = at, pieces, shard, spot
+        self.d_s, self.d_r, self.u_s, self.u_r, self.c_s, self.c_r, self.here = sems
+
+    def down_copy(self, h, i, own=False):
+        b = 2 * (self.at.p + h) + self.at.c
+        dst = self.spot(b, i)
+        src = self.shard(i) if own else dst
+        return remote(src, dst, self.d_s.at[h, i], self.d_r.at[h, i], self.at.below)
+
+    def up_copy(self, h, i, own=False):
+        b = 2 * (self.at.p - h) + self.at.c
+        dst = self.spot(b, i)
+        src = self.shard(i) if own else dst
+        return remote(src, dst, self.u_s.at[h, i], self.u_r.at[h, i], self.at.above)
+
+    def core_copy(self, z, i, own=False, incoming=False):
+        b = 2 * z + (1 - self.at.c if incoming else self.at.c)
+        dst = self.spot(b, i)
+        src = self.shard(i) if own else dst
+        return remote(src, dst, self.c_s.at[z, i], self.c_r.at[z, i], self.at.core)
+
+    def keep(self, i):
+        at = self.at
+        return pltpu.make_async_copy(self.shard(i), self.spot(at.dp, i), self.here.at[i])
+
+    def start(self):
+        at = self.at
+        for i in range(self.pieces):
+
+            @pl.when(at.has_below)
+            def _():
+                self.down_copy(0, i, True).start()
+
+            @pl.when(at.has_above)
+            def _():
+                self.up_copy(0, i, True).start()
+
+        for i in range(self.pieces):
+            self.core_copy(at.p, i, True).start()
+            self.keep(i).start()
+
+    def slot(self, h, i):
+        at = self.at
+        n, p = at.n, at.p
+
+        @pl.when(p + h < n)
+        def _():
+            self.down_copy(h - 1, i).wait_recv()
+
+            @pl.when(at.has_below)
+            def _():
+                self.down_copy(h, i).start()
+
+            self.core_copy(p + h, i).start()
+
+        @pl.when(p - h >= 0)
+        def _():
+            self.up_copy(h - 1, i).wait_recv()
+
+            @pl.when(at.has_above)
+            def _():
+                self.up_copy(h, i).start()
+
+            self.core_copy(p - h, i).start()
+
+    def stage(self, h):
+        @pl.loop(0, self.pieces)
+        def _(i):
+            self.slot(h, i)
+
+    def ready(self, z, i):
+        self.core_copy(z, i, incoming=True).wait_recv()
+
+    def drain(self):
+        at = self.at
+        n, p = at.n, at.p
+
+        @pl.loop(0, self.pieces)
+        def _(i):
+            for h in range(n):
+
+                @pl.when((p + h < n) & at.has_below)
+                def _():
+                    self.down_copy(h, i, h == 0).wait_send()
+
+                @pl.when((p - h >= 0) & at.has_above)
+                def _():
+                    self.up_copy(h, i, h == 0).wait_send()
+
+            for z in range(n):
+                self.core_copy(z, i).wait_send()
+
+
+def line_gather_scratch(n, pieces):
+    dma = pltpu.SemaphoreType.DMA
+    return [dma((n, pieces))] * 6 + [dma((pieces,))]
+
+
+def rows_spot(out, rows, width):
+    def spot(b, i):
+        rs = pl.ds(pl.multiple_of(b * rows, rows), rows)
+        return out.at[rs, pl.ds(pl.multiple_of(i * width, width), width)]
+
+    return spot
+
+
+def cols_of(ref, width, base=0):
+    return lambda i: ref.at[:, pl.ds(pl.multiple_of(base + i * width, width), width)]
+
+
+def gate_kernel(
+    n_dp,
+    att_ref,
+    aw_hbm,
+    sh_hbm,
+    x_ref,
+    gain_ref,
+    gw_ref,
+    nm_ref,
+    hid_ref,
+    gu_ref,
+    inner_ref,
+    wo,
+    nm,
+    wbuf,
+    gbuf,
+    ibuf,
+    load_s,
+    wb_s,
+    gb_s,
+    ib_s,
+    *rest,
+):
+    at = Place(n_dp)
+    n = at.n
+    quad = QuadSum(at, *rest[0:3], rest[3:7])
+    gather_nm = QuadGather(at, rest[7], nm_ref, rest[8:13])
+    sems = rest[13:20]
+    hh = wo.shape[1]
+    part, half_cols = quad.t.shape[2], quad.t.shape[3]
+    chunk, wide = sh_hbm.shape
+    pieces = sems[6].shape[0]
+    width = wide // pieces
+    line = LineGather(at, pieces, cols_of(sh_hbm, width), rows_spot(gw_ref, chunk, width), sems)
+
+    load = pltpu.make_async_copy(aw_hbm.at[:, pl.ds(3 * hh, hh)], wo, load_s.at[0])
+    load.start()
+    enter(at)
+    line.start()
+    load.wait()
+
+    def terms(q):
+        rs = pl.ds(pl.multiple_of(q * part, part), part)
+        for half in range(2):
+            w = wo[half * half_cols : (half + 1) * half_cols, :]
+            quad.t[half, q] = dot(att_ref[rs, :], w, NT).astype(BF)
+
+    terms(at.qd)
+    quad.first(0, 0).start()
+    quad.first(1, 0).start()
+    terms(at.qx)
+    quad.first(0, 1).start()
+    terms(at.qy)
+    quad.first(1, 1).start()
+    terms(at.m)
+    quad.turn()
+    quad.arrive()
+
+    @pl.loop(0, part // 32)
+    def _(b):
+        rs = pl.ds(pl.multiple_of(b * 32, 32), 32)
+        h = x_ref[rs, :].astype(F32) + jnp.concatenate(
+            [quad.total(0, rs), quad.total(1, rs)], axis=1
+        )
+        hid_ref[rs, :] = h
+        scale = lax.rsqrt(jnp.mean(h * h, axis=1, keepdims=True) + EPS)
+        res = (h * scale * gain_ref[...]).astype(BF)
+        gather_nm.own[0, rs, :] = res[:, :half_cols]
+        gather_nm.own[1, rs, :] = res[:, half_cols:]
+
+    gather_nm.start()
+    line.stage(1)
+    gather_nm.forward()
+    gather_nm.finish()
+    load = pltpu.make_async_copy(nm_ref, nm, load_s.at[0])
+    load.start()
+    for h in range(2, n - 1):
+        line.stage(h)
+    load.wait()
+
+    def w_copy(i, slot):
+        cols = pl.ds(pl.multiple_of(i * width, width), width)
+        return pltpu.make_async_copy(gw_ref.at[:, cols], wbuf.at[slot], wb_s.at[slot])
+
+    def g_copy(i, slot):
+        cols = pl.ds(pl.multiple_of(i * width, width), width)
+        return pltpu.make_async_copy(gbuf.at[slot], gu_ref.at[:, cols], gb_s.at[slot])
+
+    def i_copy(i, slot):
+        cols = pl.ds(pl.multiple_of(i * (width // 2), width // 2), width // 2)
+        return pltpu.make_async_copy(ibuf.at[slot], inner_ref.at[:, cols], ib_s.at[slot])
+
+    @pl.loop(0, pieces)
+    def _(i):
+        slot = lax.rem(i, 2)
+        line.slot(n - 1, i)
+        line.keep(i).wait()
+        for z in range(n):
+            line.ready(z, i)
+        w_copy(i, slot).start()
+
+        @pl.when(i >= 2)
+        def _():
+            g_copy(i - 2, slot).wait()
+            i_copy(i - 2, slot).wait()
+
+        w_copy(i, slot).wait()
+
+        @pl.loop(0, nm.shape[0] // 256)
+        def _(b):
+            rs = pl.ds(pl.multiple_of(b * 256, 256), 256)
+            v = dot(nm[rs, :], wbuf[slot]).astype(BF)
+            gbuf[slot, rs, :] = v
+            g = v[:, : width // 2].astype(F32)
+            u = v[:, width // 2 :].astype(F32)
+            ibuf[slot, rs, :] = (g / (1.0 + jnp.exp(-g)) * u).astype(BF)
+
+        g_copy(i, slot).start()
+        i_copy(i, slot).start()
+
+    for i in range(max(0, pieces - 2), pieces):
+        g_copy(i, i % 2).wait()
+        i_copy(i, i % 2).wait()
+    line.drain()
+    quad.drain()
+
+
+def gate_stage(n_dp, att, aw, shard, x, gain):
+    seq, hh = att.shape
+    d = aw.shape[0]
+    chunk, wide = shard.shape
+    n, part = n_dp // 2, seq // 4
+    dma = pltpu.SemaphoreType.DMA
+    hbm = pl.BlockSpec(memory_space=pl.ANY)
+    vm = pl.BlockSpec(memory_space=pltpu.VMEM)
+    width = wide // PIECES
+    return pl.pallas_call(
+        functools.partial(gate_kernel, n_dp),
+        out_shape=[
+            jax.ShapeDtypeStruct((d, wide), BF),
+            jax.ShapeDtypeStruct((seq, d), BF),
+            jax.ShapeDtypeStruct((part, d), F32),
+            jax.ShapeDtypeStruct((seq, wide), BF),
+            jax.ShapeDtypeStruct((seq, wide // 2), BF),
+        ],
+        in_specs=[vm, hbm, hbm, vm, vm],
+        out_specs=[hbm, hbm, vm, hbm, hbm],
+        scratch_shapes=[
+            pltpu.VMEM((d, hh), BF),
+            pltpu.VMEM((seq, d), BF),
+            pltpu.VMEM((2, d, width), BF),
+            pltpu.VMEM((2, seq, width), BF),
+            pltpu.VMEM((2, seq, width // 2), BF),
+            dma((1,)),
+            dma((2,)),
+            dma((2,)),
+            dma((2,)),
+        ]
+        + quad_sum_scratch(part, d // 2)
+        + quad_gather_scratch(part, d // 2)
+        + line_gather_scratch(n, PIECES),
+        compiler_params=pltpu.CompilerParams(
+            collective_id=2, has_side_effects=True, vmem_limit_bytes=VMEM_LIMIT
+        ),
+        name="gate_stage",
+    )(att, aw, shard, x, gain)
+
+
+def down_kernel(
+    n_dp,
+    inner_hbm,
+    gu_hbm,
+    cot_hbm,
+    sh_hbm,
+    rs_ref,
+    ft_ref,
+    ggu_ref,
+    dn_ref,
+    inner,
+    gu,
+    cot,
+    dn,
+    acc,
+    ftb,
+    load_s,
+    ft_s,
+    dn_s,
+    gg_s,
+    *rest,
+):
+    at = Place(n_dp)
+    n, p = at.n, at.p
+    line = LineSum(at, *rest[0:4], rest[4:10])
+    sems = rest[10:17]
+    chunk, ff = sh_hbm.shape
+    pieces = sems[6].shape[0]
+    width = ff // pieces
+    gather = LineGather(at, pieces, cols_of(sh_hbm, width), rows_spot(dn_ref, chunk, width), sems)
+    pair = 2 * chunk
+    loads = [
+        pltpu.make_async_copy(src, dst, load_s.at[i])
+        for i, (src, dst) in enumerate([(cot_hbm, cot), (inner_hbm, inner), (gu_hbm, gu)])
+    ]
+    for cp in loads:
+        cp.start()
+    enter(at)
+    gather.start()
+    loads[0].wait()
+    loads[1].wait()
+
+    def run(e):
+        k, core = e // 2, e % 2
+        block = 2 * order_of(k, at) + (1 - at.c if core == 0 else at.c)
+        lhs = cot[:, pl.ds(pl.multiple_of(block * chunk, chunk), chunk)].T
+
+        def tile(_, put):
+            @pl.loop(0, pieces)
+            def _(i):
+                put(i, dot(lhs, inner[:, pl.ds(pl.multiple_of(i * width, width), width)]))
+
+        if core == 0:
+            line.other(k, tile)
+        else:
+            line.mine(k, tile)
+
+    for e in range(2 * n):
+        run(e)
+
+    def ft_copy(z, slot):
+        cols = pl.ds(pl.multiple_of(z * pair, pair), pair)
+        return pltpu.make_async_copy(ftb.at[slot], ft_ref.at[:, cols], ft_s.at[slot])
+
+    def work(z, fresh):
+        rs = pl.ds(pl.multiple_of(z * pair, pair), pair)
+
+        @pl.loop(0, pieces)
+        def _(i):
+            gather.ready(z, i)
+
+        load = pltpu.make_async_copy(dn_ref.at[rs, :], dn, dn_s.at[0])
+        load.start()
+        load.wait()
+
+        @pl.loop(0, ff // 512)
+        def _(i):
+            cols = pl.ds(pl.multiple_of(i * 512, 512), 512)
+            v = dot(cot[:, rs], dn[:, cols])
+            acc[:, cols] = v if fresh else acc[:, cols] + v
+
+        if not fresh:
+            ft_copy(z, 0).wait()
+        ftb[0] = dot(inner[...], dn[...], NT).astype(BF)
+        ft_copy(z, 0).start()
+
+    for i in range(pieces):
+        gather.keep(i).wait()
+    work(p, True)
+    loads[2].wait()
+
+    @pl.loop(1, n)
+    def _(h):
+        gather.stage(h)
+        line.slot(h - 1)
+
+        @pl.when(p + h < n)
+        def _():
+            work(p + h, False)
+
+        @pl.when(p - h >= 0)
+        def _():
+            work(p - h, False)
+
+    half = width
+
+    def gg_copy(i):
+        cols = pl.ds(pl.multiple_of(i * 2 * half, 2 * half), 2 * half)
+        return pltpu.make_async_copy(gu.at[:, cols], ggu_ref.at[:, cols], gg_s.at[i])
+
+    @pl.loop(0, pieces)
+    def _(i):
+        gcols = pl.ds(pl.multiple_of(i * 2 * half, half), half)
+        ucols = pl.ds(pl.multiple_of(i * 2 * half + half, half), half)
+        acols = pl.ds(pl.multiple_of(i * half, half), half)
+
+        @pl.loop(0, gu.shape[0] // 64)
+        def _(b):
+            rs = pl.ds(pl.multiple_of(b * 64, 64), 64)
+            g = gu[rs, gcols].astype(F32)
+            u = gu[rs, ucols].astype(F32)
+            gi = acc[rs, acols]
+            sg = 1.0 / (1.0 + jnp.exp(-g))
+            gu[rs, gcols] = (gi * u * sg * (1.0 + g * (1.0 - sg))).astype(BF)
+            gu[rs, ucols] = (gi * g * sg).astype(BF)
+
+        gg_copy(i).start()
+
+    line.final(rs_ref)
+    for i in range(pieces):
+        gg_copy(i).wait()
+    ft_copy(p, 0).wait()
+    line.drain()
+    gather.drain()
+
+
+def down_stage(n_dp, inner, gu, cot, shard):
+    seq, d = cot.shape
+    chunk, ff = shard.shape
+    n = n_dp // 2
+    dma = pltpu.SemaphoreType.DMA
+    hbm = pl.BlockSpec(memory_space=pl.ANY)
+    vm = pl.BlockSpec(memory_space=pltpu.VMEM)
+    return pl.pallas_call(
+        functools.partial(down_kernel, n_dp),
+        out_shape=[
+            jax.ShapeDtypeStruct((PIECES, chunk, ff // PIECES), BF),
+            jax.ShapeDtypeStruct((seq, d), BF),
+            jax.ShapeDtypeStruct((seq, 2 * ff), BF),
+            jax.ShapeDtypeStruct((d, ff), BF),
+        ],
+        in_specs=[hbm] * 4,
+        out_specs=[vm, hbm, hbm, hbm],
+        scratch_shapes=[
+            pltpu.VMEM((seq, ff), BF),
+            pltpu.VMEM((seq, 2 * ff), BF),
+            pltpu.VMEM((seq, d), BF),
+            pltpu.VMEM((2 * chunk, ff), BF),
+            pltpu.VMEM((seq, ff), F32),
+            pltpu.VMEM((1, seq, 2 * chunk), BF),
+            dma((3,)),
+            dma((1,)),
+            dma((1,)),
+            dma((PIECES,)),
+        ]
+        + line_sum_scratch(n, PIECES, chunk, ff // PIECES)
+        + line_gather_scratch(n, PIECES),
+        compiler_params=pltpu.CompilerParams(
+            collective_id=3, has_side_effects=True, vmem_limit_bytes=VMEM_LIMIT
+        ),
+        name="down_stage",
+    )(inner, gu, cot, shard)[:3]
+
+
+def mid_kernel(
+    n_dp,
+    ggu_hbm,
+    gw_hbm,
+    nm_hbm,
+    ft_hbm,
+    hid_ref,
+    cot_ref,
+    gain_ref,
+    rs_ref,
+    low_ref,
+    lay_ref,
+    gh_ref,
+    gg_ref,
+    ggu,
+    wt,
+    wt_s,
+    nm,
+    nm_s,
+    load_s,
+    *rest,
+):
+    at = Place(n_dp)
+    n = at.n
+    line = LineSum(at, *rest[0:4], rest[4:10])
+    mid = QuadSum(at, *rest[10:13], rest[13:17])
+    lay = QuadSumHbm(at, ft_hbm, *rest[17:20], rest[20:25])
+    gather_low = QuadGather(at, rest[25], low_ref, rest[26:31])
+    gather_lay = QuadGather(at, rest[31], lay_ref, rest[32:37])
+    part, half_cols = mid.t.shape[2], mid.t.shape[3]
+    chunk, width = line.own.shape[2], line.own.shape[3]
+    pieces = line.pieces
+    drows = wt.shape[1]
+    tiles = half_cols // drows
+
+    load = pltpu.make_async_copy(ggu_hbm, ggu, load_s.at[0])
+    load.start()
+
+    def nm_copy(e):
+        k, core = e // 2, e % 2
+        block = 2 * order_of(k, at) + (1 - at.c if core == 0 else at.c)
+        cols = pl.ds(pl.multiple_of(block * chunk, chunk), chunk)
+        return pltpu.make_async_copy(nm_hbm.at[:, cols], nm.at[e % 2], nm_s.at[e % 2])
+
+    def wt_copy(half, i, slot):
+        rows = pl.ds(pl.multiple_of(half * half_cols + i * drows, drows), drows)
+        return pltpu.make_async_copy(gw_hbm.at[rows, :], wt.at[slot], wt_s.at[slot])
+
+    nm_copy(0).start()
+    wt_copy(0, 0, 0).start()
+    for cp in lay.loads:
+        cp.start()
+    enter(at)
+    for way in ((0, 0), (1, 0), (0, 1), (1, 1)):
+        lay.first(*way).start()
+    load.wait()
+
+    def run(e):
+        if e + 1 < 2 * n:
+            nm_copy(e + 1).start()
+        nm_copy(e).wait()
+        lhs = nm[e % 2].T
+
+        def tile(block, put):
+            @pl.loop(0, pieces)
+            def _(i):
+                put(i, dot(lhs, ggu[:, pl.ds(pl.multiple_of(i * width, width), width)]))
+
+        if e % 2 == 0:
+            line.other(e // 2, tile)
+        else:
+            line.mine(e // 2, tile)
+
+    def terms(half):
+        @pl.loop(0, tiles)
+        def _(i):
+            slot = lax.rem(i, 2)
+            if half == 0:
+                nxt = wt_copy(jnp.where(i + 1 < tiles, 0, 1), lax.rem(i + 1, tiles), 1 - slot)
+                nxt.start()
+            else:
+
+                @pl.when(i + 1 < tiles)
+                def _():
+                    wt_copy(1, i + 1, 1 - slot).start()
+
+            wt_copy(half, i, slot).wait()
+            v = dot(ggu[...], wt[slot], NT).astype(BF)
+            cols = pl.ds(pl.multiple_of(i * drows, drows), drows)
+            for q in range(4):
+                mid.t[half, q, :, cols] = v[q * part : (q + 1) * part]
+
+        mid.first(half, 0).start()
+        mid.first(half, 1).start()
+
+    run(0)
+    run(1)
+    terms(0)
+    run(2)
+    run(3)
+    terms(1)
+    for cp in lay.loads:
+        cp.wait()
+    lay.turn()
+    for e in range(4, 2 * n):
+        run(e)
+    lay.arrive()
+
+    @pl.loop(0, part // 32)
+    def _(b):
+        rs = pl.ds(pl.multiple_of(b * 32, 32), 32)
+        for half in range(2):
+            h = hid_ref[rs, pl.ds(half * half_cols, half_cols)]
+            gather_lay.own[half, rs, :] = (h + lay.total(half, rs)).astype(BF)
+
+    gather_lay.start()
+    line.slot(0)
+    mid.turn()
+    mid.arrive()
+    gg_ref[...] = jnp.zeros_like(gg_ref)
+
+    @pl.loop(0, part // 32)
+    def _(b):
+        rs = pl.ds(pl.multiple_of(b * 32, 32), 32)
+        h = hid_ref[rs, :]
+        scale = lax.rsqrt(jnp.mean(h * h, axis=1, keepdims=True) + EPS)
+        g = jnp.concatenate([mid.total(0, rs), mid.total(1, rs)], axis=1)
+        unit = h * scale
+        weighted = g * gain_ref[...]
+        field = scale * (weighted - unit * jnp.mean(weighted * unit, axis=1, keepdims=True))
+        res = cot_ref[rs, :].astype(F32) + field
+        gh_ref[rs, :] = res
+        low = res.astype(BF)
+        gather_low.own[0, rs, :] = low[:, :half_cols]
+        gather_low.own[1, rs, :] = low[:, half_cols:]
+        gg_ref[...] += jnp.sum(g * unit, axis=0, keepdims=True)
+
+    gather_low.start()
+    gather_lay.forward()
+    for s in range(1, n - 2):
+        line.slot(s)
+    gather_low.forward()
+    line.final(rs_ref)
+    gather_lay.finish()
+    gather_low.finish()
+    line.drain()
+    mid.drain()
+    lay.drain()
+
+
+def mid_stage(n_dp, ggu, gw, nm, ft, hid, cot, gain):
+    seq, wide = ggu.shape
+    d = gw.shape[0]
+    n, part, chunk = n_dp // 2, seq // 4, d // n_dp
+    dma = pltpu.SemaphoreType.DMA
+    hbm = pl.BlockSpec(memory_space=pl.ANY)
+    vm = pl.BlockSpec(memory_space=pltpu.VMEM)
+    pieces = 4
+    return pl.pallas_call(
+        functools.partial(mid_kernel, n_dp),
+        out_shape=[
+            jax.ShapeDtypeStruct((pieces, chunk, wide // pieces), BF),
+            jax.ShapeDtypeStruct((seq, d), BF),
+            jax.ShapeDtypeStruct((seq, d), BF),
+            jax.ShapeDtypeStruct((part, d), F32),
+            jax.ShapeDtypeStruct((1, d), F32),
+        ],
+        in_specs=[hbm] * 4 + [vm] * 3,
+        out_specs=[vm, hbm, hbm, vm, vm],
+        scratch_shapes=[
+            pltpu.VMEM((seq, wide), BF),
+            pltpu.VMEM((2, 256, wide), BF),
+            dma((2,)),
+            pltpu.VMEM((2, seq, chunk), BF),
+            dma((2,)),
+            dma((1,)),
+        ]
+        + line_sum_scratch(n, pieces, chunk, wide // pieces, 1)
+        + quad_sum_scratch(part, d // 2)
+        + quad_sum_scratch(part, d // 2, 2)
+        + [dma((2, 2))]
+        + quad_gather_scratch(part, d // 2) * 2,
+        compiler_params=pltpu.CompilerParams(
+            collective_id=4, has_side_effects=True, vmem_limit_bytes=VMEM_LIMIT
+        ),
+        name="mid_stage",
+    )(ggu, gw, nm, ft, hid, cot, gain)
 
 
 def last_kernel(
@@ -657,13 +1340,6 @@
     )(dqkv, aw, nt, gt, att, x, gh, gain, gmid)
 
 
-def norm_backward(grad_normed, field, scale, gain):
-    unit = field * scale
-    weighted = grad_normed * gain
-    grad_field = scale * (weighted - unit * jnp.mean(weighted * unit, axis=1, keepdims=True))
-    return (grad_field, jnp.sum(grad_normed * unit, axis=0))
-
-
 def after(value, *deps):
     return lax.optimization_barrier((value,) + deps)[0]
 
@@ -686,6 +1362,7 @@
     hh = w_query.shape[1]
     ff = w_gate.shape[1]
     mp = lax.axis_size("mp")
+    n_dp = lax.axis_size("dp")
     me = lax.axis_index("mp")
     part = seq // mp
     gather = lambda x: lax.all_gather(x, "dp", axis=0, tiled=True)
@@ -696,10 +1373,11 @@
 
     attn_shard = jnp.concatenate([w_query, w_key, w_value, w_output.T], axis=1).astype(BF)
     attn_w = gather(attn_shard)
-    gu_shard = jnp.concatenate([w_gate, w_up], axis=1).astype(BF)
-    gu_w = gather(after(gu_shard, attn_w))
+    pack = lambda g, u: jnp.stack(
+        [g.reshape(g.shape[0], PIECES, -1), u.reshape(u.shape[0], PIECES, -1)], axis=2
+    ).reshape(g.shape[0], -1)
+    gu_shard = pack(w_gate, w_up).astype(BF)
     down_shard = w_down.T.astype(BF)
-    down_w = gather(after(down_shard, gu_w))
     gains = lax.all_gather(jnp.stack([gain_attn, gain_ffn]).astype(BF), "dp", axis=1, tiled=True)
     gains = gains.astype(F32)
     gain_in, gain_mid = gains[0:1], gains[1:2]
@@ -712,55 +1390,44 @@
     qkv = dot(normed_in, attn_w[:, : 3 * hh]).astype(BF)
     attended = attn_fwd(qkv, counts, seq)
     out_wt = attn_w[:, 3 * hh :]
-    attn_sum = mp_scatter(dot(attended, out_wt, NT))
-    my_source = mine(inputs).astype(F32)
-    hidden = my_source + attn_sum.astype(F32)
-    scale_mid = lax.rsqrt(jnp.mean(hidden * hidden, axis=1, keepdims=True) + EPS)
-    normed_mid = mp_gather((hidden * scale_mid * gain_mid).astype(BF))
-    gate_w, up_w = gu_w[:, :ff], gu_w[:, ff:]
-    gate = dot(normed_mid, gate_w).astype(BF)
-    up = dot(normed_mid, up_w).astype(BF)
-    gate_f = gate.astype(F32)
-    up_f = up.astype(F32)
-    sg = jax.nn.sigmoid(gate_f)
-    silu = gate_f * sg
-    inner = (silu * up_f).astype(BF)
     grad_ffn = jnp.where(valid, cotangent, jnp.zeros_like(cotangent))
-    grad_down_t = dot(grad_ffn, inner, TN).astype(BF)
-    grad_inner = dot(grad_ffn, down_w)
-    grad_gate = (grad_inner * up_f * sg * (1.0 + gate_f * (1.0 - sg))).astype(BF)
-    grad_up = (grad_inner * silu).astype(BF)
-    mid_terms = dot(grad_gate, gate_w, NT) + dot(grad_up, up_w, NT)
-    grad_mid = mp_scatter(mid_terms).astype(F32)
-    rs_down = scatter(grad_down_t)
-    grad_gu = jnp.concatenate(
-        [dot(normed_mid, grad_gate, TN).astype(BF), dot(normed_mid, grad_up, TN).astype(BF)], axis=1
+    my_source = mine(inputs)
+    gu_w, normed_mid, hidden, gu, inner = gate_stage(
+        n_dp, attended, attn_w, gu_shard, my_source, gain_mid
     )
-    rs_gu = scatter(after(grad_gu, rs_down))
-    ffn_sum = mp_scatter(dot(inner, down_w, NT))
-    layer_out = mp_gather((hidden + ffn_sum.astype(F32)).astype(BF))
-
-    g_norm, g_gain_mid = norm_backward(grad_mid, hidden, scale_mid, gain_mid)
-    grad_hidden = mine(grad_ffn).astype(F32) + g_norm
-    grad_low = mp_gather(grad_hidden.astype(BF))
+    rs_down, ffn_terms, ggu = down_stage(n_dp, inner, gu, grad_ffn, down_shard)
+    rs_gu, grad_low, layer_out, grad_hidden, g_gain_mid = mid_stage(
+        n_dp,
+        ggu,
+        gu_w,
+        normed_mid,
+        ffn_terms,
+        hidden,
+        mine(grad_ffn),
+        gain_mid,
+    )
     grad_attended = dot(grad_low, out_wt).astype(BF)
     dq, dk, dv = attn_bwd(qkv, grad_attended, counts, seq)
     rs_attn, grad_low_in, g_gains = last_stage(
-        lax.axis_size("dp"),
+        n_dp,
         jnp.concatenate([dq, dk, dv], axis=1),
         attn_w,
         normed_in.T,
         grad_low.T,
         attended,
-        mine(inputs),
+        my_source,
         grad_hidden,
         gain_in,
-        g_gain_mid[None],
+        g_gain_mid,
     )
     input_grad = grad_low_in.astype(F32)
     width = g_gains.shape[1] // lax.axis_size("dp")
     g_gains = lax.dynamic_slice_in_dim(g_gains, lax.axis_index("dp") * width, width, 1)
-    rs_gu = rs_gu.astype(F32)
+    half = ff // PIECES
+    unpack = lambda i: jnp.concatenate(
+        [rs_gu[k, :, i * half : (i + 1) * half] for k in range(PIECES)], axis=1
+    ).astype(F32)
+    down_t = jnp.concatenate([rs_down[k] for k in range(PIECES)], axis=1)
     return (
         layer_out,
         input_grad,
@@ -770,9 +1437,9 @@
         rs_attn[2],
         rs_attn[3].T,
         g_gains[1],
-        rs_gu[:, :ff],
-        rs_gu[:, ff:],
-        rs_down.astype(F32).T,
+        unpack(0),
+        unpack(1),
+        down_t.astype(F32).T,
     )
 
 

time: 1070 us -> 721 us (0.67)
  waiting for transfers between devices: 642 us -> 32.2 us
  Pallas kernels: 149 us -> 562 us
  matrix products: 158 us -> 15.9 us
  other arithmetic: 47.7 us -> 32.5 us
    pallas_call x0 -> x3, Pallas kernels: none -> 443 us  [the longest x1 170 us: mid_stage(): pl.pallas_call(functools.partial(mid_kernel, n_dp), out_shape=[jax.ShapeD...]
    reduce_scatter x5 -> x0, waiting for transfers between devices: 280 us -> none  [the longest x2 161 us: on_device(): lax.psum_scatter(x, 'dp', scatter_dimension=0, tiled=True)]
    all_gather x3 -> x1, waiting for transfers between devices: 265 us -> 32.2 us  [on_device(): gather = lambda x: lax.all_gather(x, 'dp', axis=0, tiled=True)]
    dot_general x12 -> x2, matrix products: 158 us -> 15.9 us  [dot(): return lax.dot_general(a, b, dims, preferred_element_type=F32)]
    all_gather x3 -> x0, waiting for transfers between devices: 95.9 us -> none  [on_device(): mp_gather = lambda x: lax.all_gather(x, 'mp', axis=0, tiled=True)]
    pallas_call x1, Pallas kernels: 131 us -> 100 us  [last_stage(): pl.pallas_call(functools.partial(last_kernel, n_dp), out_shape=[jax.Shape...]
    unnamed x49 -> x44, local copies, waits for them, and re-layouts: 24.8 us -> 18.1 us
  transfers between devices with their start and end apart: 11 -> 1, of which waited for: 10 -> 1; matrix products, arithmetic and copies ran while one was open for 14% -> 5% of each run, Pallas kernels for 13% -> 0%
where the time goes in v4:
time: 721 us; the launch traced here: 716 us
  Pallas kernels  562 us (78%)
  local copies, waits for them, and re-layouts  45.2 us (6%)
  other arithmetic  32.5 us (5%)
  waiting for transfers between devices  32.2 us (4%)
  matrix products  15.9 us (2%)
  between operations  15.2 us (2%)
  blocking collectives  13.6 us (2%)
    pallas_call x1, Pallas kernels, mid_stage(): pl.pallas_call(functools.partial(mid_kernel, n_dp), out_shape=[jax.ShapeD...  170 us
    pallas_call x1, Pallas kernels, gate_stage(): pl.pallas_call(functools.partial(gate_kernel, n_dp), out_shape=[jax.Shape...  160 us
    pallas_call x1, Pallas kernels, down_stage(): pl.pallas_call(functools.partial(down_kernel, n_dp), out_shape=[jax.Shape...  113 us
    pallas_call x1, Pallas kernels, last_stage(): pl.pallas_call(functools.partial(last_kernel, n_dp), out_shape=[jax.Shape...  100 us
    all_gather x1, waiting for transfers between devices, on_device(): gather = lambda x: lax.all_gather(x, 'dp', axis=0, tiled=True)  32.2 us
    unnamed x44, local copies, waits for them, and re-layouts  18.1 us
    dot_general x2, matrix products, dot(): return lax.dot_general(a, b, dims, preferred_element_type=F32)  15.9 us
  transfers between devices with their start and end apart: 1, of which 1 were waited for; matrix products, arithmetic and copies ran while one was open for 5% of the time, Pallas kernels for 0%

profile of v4, /device:TPU:0, one launch (start us, length us, event | category | flops | bytes accessed | tf_op | source)
XLA Modules:
  0.0 716.4 jit_solution(15002103245916097920)
XLA Ops:
  13.8 1.7 stack_reshape.10
  15.6 1.7 convert.37
  17.3 3.9 stack_reshape.11
  21.2 6.8 pad_maximum_fusion.1
  28.0 4.6 convert_element_type.39.sh_hbm
  32.6 1.4 copy.27
  34.0 6.4 copy.23
  40.4 13.6 %all_gather.6 = bf16[2,2048]{1,0:T(2,128)(2,1)S(1)} all-gather(bf16[2,256]{1,0:T(2,128)(2,1)S(1)} %pad_maximum_fusion.3), channel_id=1, replica_groups=mesh['dp'=8,'mp'=4] {'dp'}, dimensions={1}, use_global_device_ids=true | all-gather | bytes 9216 | tf_op jit(solution)/shard_map/all_gather | solution.py:1381
  54.0 3.1 fusion
  57.6 2.0 copy-done.3
  59.6 2.9 constant_dynamic-slice_fusion.1
  63.1 2.6 fusion.13.nt_hbm
  65.7 32.2 %all-gather.2.cloned.1.call-done.aw_hbm = bf16[2048,2048]{1,0:T(8,128)(2,1)} async-done(((bf16[256,2048]{1,0:T(8,128)(2,1)}), bf16[2048,2048]{1,0:T(8,128)(2,1)}) %all-gather.2.cloned.1.call-update) | async-done | bytes 8388624 | tf_op jit(solution)/shard_map/all_gather | solution.py:1368
  97.9 10.7 %fusion.5.q_ref.k_ref.v_ref = bf16[1024,1536]{1,0:T(8,128)(2,1)S(1)} fusion(bf16[2048,2048]{1,0:T(8,128)(2,1)} %all-gather.2.cloned.1.call-done.aw_hbm, bf16[1024,2048]{0,1:T(8,128)(2,1)} %copy.23, f32[2048]{0:T(1024)S(1)} %bitcast.55, f32[1024]{0:T(1024)S(1)} %add_rsqrt_fusion), kind=kOutput, calls=%fused_computation.8 | convolution fusion | flops 6452412416 | bytes 13643776 | tf_op jit(solution)/shard_map/dot_general | solution.py:21
  108.6 5.9 attn_fwd.1.att_ref.att_hbm
  115.5 160.3 %gate_stage.1 = (bf16[2048,4096]{1,0:T(8,128)(2,1)}, bf16[1024,2048]{1,0:T(8,128)(2,1)}, f32[256,2048]{1,0:T(8,128)}, bf16[1024,4096]{1,0:T(8,128)(2,1)}, bf16[1024,2048]{1,0:T(8,128)(2,1)}) custom-call(bf16[1024,512]{1,0:T(8,128)(2,1)} %copy-done.1, bf16[2048,2048]{1,0:T(8,128)(2,1)} %all-gather.2.cloned.1.call-done.aw_hbm, ...), custom_call_target="tpu_custom_call" | custom-call | tf_op jit(solution)/shard_map/gate_stage/pallas_call | solution.py:745
  275.7 113.4 %down_stage.1 = (bf16[4,256,512]{2,1,0:T(8,128)(2,1)}, bf16[1024,2048]{1,0:T(8,128)(2,1)}, bf16[1024,4096]{1,0:T(8,128)(2,1)}, bf16[2048,2048]{1,0:T(8,128)(2,1)}) custom-call(bf16[1024,2048]{1,0:T(8,128)(2,1)} %get-tuple-element.30.inner_hbm, bf16[1024,4096]{1,0:T(8,128)(2,1)} %get-tuple-element.31.gu_hbm, bf16[1024,2048]{1,0:T(8,128)(2,1)} %copy-done.3, ...), custom_call_target="tpu_custom_call" | custom-call | tf_op jit(solution)/shard_map/down_stage/pallas_call | solution.py:920
  389.1 169.7 %mid_stage.1 = (bf16[4,256,1024]{2,1,0:T(8,128)(2,1)}, bf16[1024,2048]{1,0:T(8,128)(2,1)}, bf16[1024,2048]{1,0:T(8,128)(2,1)}, f32[256,2048]{1,0:T(8,128)}, f32[1,2048]{1,0:T(1,128)}) custom-call(bf16[1024,4096]{1,0:T(8,128)(2,1)} %get-tuple-element.32.ggu_hbm, bf16[2048,4096]{1,0:T(8,128)(2,1)} %get-tuple-element.33.gw_hbm, ...), custom_call_target="tpu_custom_call" | custom-call | tf_op jit(solution)/shard_map/mid_stage/pallas_call | solution.py:1109
  558.9 6.4 copy.28
  565.3 5.2 fusion.10.g_ref
  570.5 12.5 %attn_bwd.1 = (bf16[1024,512]{1,0:T(8,128)(2,1)S(1)}, bf16[1024,512]{1,0:T(8,128)(2,1)S(1)}, bf16[1024,512]{1,0:T(8,128)(2,1)S(1)}) custom-call(s32[1]{0:T(128)} %copy.32.count_ref, bf16[1024,1536]{1,0:T(8,128)(2,1)} %copy-done, bf16[1024,1536]{1,0:T(8,128)(2,1)} %copy-done, bf16[1024,1536]{1,0:T(8,128)(2,1)} %copy-done, bf16[1024,512]{1,0:T(8,128)(2,1)S(1)} %fusion.10.g_ref), custom_call_target="tpu_custom_call" | custom-call | tf_op jit(solution)/shard_map/attn_bwd/pallas_call | solution.py:98
  583.0 1.6 convert_bitcast_fusion
  584.6 2.9 copy.30
  587.5 2.7 slice_bitcast_fusion.11
  590.2 1.8 pad_maximum_fusion.dqkv_hbm
  592.0 100.1 %last_stage.1 = (f32[4,256,512]{2,1,0:T(8,128)}, bf16[1024,2048]{1,0:T(8,128)(2,1)}, f32[8,2048]{1,0:T(8,128)}) custom-call(bf16[1024,1536]{1,0:T(8,128)(2,1)} %pad_maximum_fusion.dqkv_hbm, bf16[2048,2048]{1,0:T(8,128)(2,1)} %all-gather.2.cloned.1.call-done.aw_hbm, bf16[2048,1024]{1,0:T(8,128)(2,1)} %fusion.13.nt_hbm, bf16[2048,1024]{1,0:T(8,128)(2,1)} %bitcast.51, ...), custom_call_target="tpu_custom_call" | custom-call | tf_op jit(solution)/shard_map/last_stage/pallas_call | solution.py:1310
  692.1 2.7 slice_bitcast_fusion
  695.8 6.7 convert_element_type.43
  702.5 1.4 fusion.15
  704.0 1.6 maximum_convert_fusion.1
  705.5 1.6 maximum_convert_fusion
  707.3 2.0 copy.33
  (56 shorter events, 9.2 us)
Async XLA Ops:
  7.2 6.4 copy-start.17
  7.2 6.5 copy-start.18
  7.2 6.5 copy-start.6
  7.2 90.7 %all-gather.2.cloned.1.call-start = ((), (), s32[]{:S(2)}) async-start(), calls=%async_computation | async-start | bytes 9437184 | tf_op jit(solution)/shard_map/all_gather | solution.py:1368
  28.0 4.6 copy-start.7
  40.4 16.7 %copy-start.4 = (bf16[1024,2048]{1,0:T(8,128)(2,1)S(1)}, bf16[1024,2048]{1,0:T(8,128)(2,1)}, u32[]{:S(2)}) copy-start(bf16[1024,2048]{1,0:T(8,128)(2,1)} %param.14) | copy-start | bytes 12582916
  57.5 2.0 copy-start.3
  59.6 3.6 copy-start.2
  63.1 34.8 %copy-start.16 = (f32[1,2048]{1,0:T(1,128)}, f32[1,2048]{1,0:T(1,128)S(1)}, u32[]{:S(2)}) copy-start(f32[1,2048]{1,0:T(1,128)S(1)} %get-tuple-element.79.gain_ref) | copy-start | bytes 24580
  108.6 5.9 copy-start
  114.5 1.0 copy-start.1
  570.5 12.5 %copy-start.15 = (bf16[4,256,512]{2,1,0:T(8,128)(2,1)S(1)}, bf16[4,256,512]{2,1,0:T(8,128)(2,1)}, u32[]{:S(2)}) copy-start(bf16[4,256,512]{2,1,0:T(8,128)(2,1)} %get-tuple-element.48) | copy-start | bytes 3145732
  695.7 8.2 %copy-start.11 = (bf16[256,512]{1,0:T(8,128)(2,1)S(1)}, bf16[256,512]{1,0:T(8,128)(2,1)}, u32[]{:S(2)}) copy-start(bf16[256,512]{1,0:T(8,128)(2,1)} %get-tuple-element.60) | copy-start | bytes 786436
  695.7 8.2 %copy-start.12 = (bf16[256,512]{1,0:T(8,128)(2,1)S(1)}, bf16[256,512]{1,0:T(8,128)(2,1)}, u32[]{:S(2)}) copy-start(bf16[256,512]{1,0:T(8,128)(2,1)} %get-tuple-element.61) | copy-start | bytes 786436
  695.7 8.2 %copy-start.13 = (bf16[256,512]{1,0:T(8,128)(2,1)S(1)}, bf16[256,512]{1,0:T(8,128)(2,1)}, u32[]{:S(2)}) copy-start(bf16[256,512]{1,0:T(8,128)(2,1)} %get-tuple-element.62) | copy-start | bytes 786436
  695.7 8.2 %copy-start.14 = (bf16[256,512]{1,0:T(8,128)(2,1)S(1)}, bf16[256,512]{1,0:T(8,128)(2,1)}, u32[]{:S(2)}) copy-start(bf16[256,512]{1,0:T(8,128)(2,1)} %get-tuple-element.63) | copy-start | bytes 786436
  702.5 3.0 copy-start.8
  702.5 3.0 copy-start.9
  702.5 3.0 copy-start.10
  703.9 3.4 copy-start.5
Sparse Core Ops, SparseCore 0:
  13.1 84.7 all-gather.1

commit v5 on v4

v5 whole, which is shorter than its diff:
```python
import functools
import math

import jax
import jax.numpy as jnp
from jax import lax
from jax.experimental import pallas as pl
from jax.experimental.pallas import tpu as pltpu
from jax.sharding import PartitionSpec as P

HD = 128
EPS = 1e-06
BF = jnp.bfloat16
F32 = jnp.float32
NT = (((1,), (1,)), ((), ()))
TN = (((0,), (0,)), ((), ()))
NN = (((1,), (0,)), ((), ()))


def dot(a, b, dims=NN):
    return lax.dot_general(a, b, dims, preferred_element_type=F32)


def logistic_block(q, k, seq):
    raw = dot(q, k, NT)
    shifted = math.log(seq) - raw * HD ** (-0.5)
    return 1.0 / (1.0 + jnp.exp(shifted))


def allowed_block(row0, rows, col0, cols, count):
    ri = row0 + lax.broadcasted_iota(jnp.int32, (rows, cols), 0)
    ci = col0 + lax.broadcasted_iota(jnp.int32, (rows, cols), 1)
    return (ci <= ri) & (ci < count)


MESH = pl.DeviceIdType.MESH
VMEM_LIMIT = 60 * 1024 * 1024
PIECES = 4


def flipped(index, bit):
    return index + bit - 2 * bit * lax.rem(lax.div(index, bit), 2)


def spread(j, bits):
    return sum(bit for i, bit in enumerate(bits) if j >> i & 1)


class Place:
    def __init__(self, n_dp, n_mp):
        self.n = n_dp // 2
        self.dp = lax.axis_index("dp")
        self.m = lax.axis_index("mp")
        self.p = lax.div(self.dp, 2)
        self.c = lax.rem(self.dp, 2)
        self.above = (self.dp + 2, self.m)
        self.below = (self.dp - 2, self.m)
        self.core = (self.dp + 1 - 2 * self.c, self.m)
        self.bits = [b for b in (1, 2, 4, 8, 16) if b < n_mp]
        self.has_above = self.p < self.n - 1
        self.has_below = self.p > 0

    def fold(self, bit):
        return (flipped(self.dp, bit), self.m)

    def peer(self, bit):
        return (self.dp, flipped(self.m, bit))

    def quarter(self, mask):
        q = self.m
        for bit in self.bits:
            if mask & bit:
                q = flipped(q, bit)
        return q


def signal(dev):
    pl.semaphore_signal(pltpu.get_barrier_semaphore(), inc=1, device_id=dev, device_id_type=MESH)


def enter(at, extra=()):
    always = [at.core] + [at.peer(bit) for bit in at.bits] + list(extra)
    for dev in always:
        signal(dev)

    @pl.when(at.has_above)
    def _():
        signal(at.above)

    @pl.when(at.has_below)
    def _():
        signal(at.below)

    ends = at.has_above.astype(jnp.int32) + at.has_below.astype(jnp.int32)
    pl.semaphore_wait(pltpu.get_barrier_semaphore(), len(always) + ends)


def remote(src, dst, send, recv, dev):
    return pltpu.make_async_remote_copy(
        src_ref=src, dst_ref=dst, send_sem=send, recv_sem=recv, device_id=dev, device_id_type=MESH
    )


def part_rows(at, part):
    return pl.ds(pl.multiple_of(at.m * part, part), part)


def order_of(k, at):
    n, p = at.n, at.p
    if k == n - 1:
        return p
    high = jnp.where(k < p, k, n - 1 - k + p)
    low = jnp.where(k < n - 1 - p, n - 1 - k, k - (n - 1 - p))
    return jnp.where(2 * p >= n, high, low)


class LineSum:
    def __init__(self, at, pout, own, din, uin, sems):
        self.at, self.pout, self.own, self.din, self.uin = at, pout, own, din, uin
        self.po_s, self.po_r, self.d_s, self.d_r, self.u_s, self.u_r = sems
        self.slots, self.pieces = pout.shape[0], own.shape[1]

    def core_copy(self, k, i):
        j = order_of(k, self.at)
        slot = k % self.slots
        return remote(
            self.pout.at[slot, i],
            self.own.at[j, i],
            self.po_s.at[slot, i],
            self.po_r.at[k, i],
            self.at.core,
        )

    def down_copy(self, s, i):
        return remote(
            self.own.at[s, i], self.din.at[s, i], self.d_s.at[s, i], self.d_r.at[s, i], self.at.below
        )

    def up_copy(self, s, i):
        n = self.at.n
        return remote(
            self.own.at[n - 1 - s, i],
            self.uin.at[s, i],
            self.u_s.at[s, i],
            self.u_r.at[s, i],
            self.at.above,
        )

    def other(self, k, tile):
        @pl.loop(0, self.pieces)
        def _(i):
            if k >= self.slots:
                self.core_copy(k - self.slots, i).wait_send()
            self.pout[k % self.slots, i] = tile(i).astype(BF)
            self.core_copy(k, i).start()

    def mine(self, k, tile):
        at = self.at
        j = order_of(k, at)

        @pl.loop(0, self.pieces)
        def _(i):
            value = tile(i)
            self.core_copy(k, i).wait_recv()
            self.own[j, i] = (value + self.own[j, i].astype(F32)).astype(BF)
            if k < at.n - 1:

                @pl.when(at.p == at.n - 1)
                def _():
                    self.down_copy(k, i).start()

                @pl.when(at.p == 0)
                def _():
                    self.up_copy(k, i).start()

    def add(self, dst, src):
        @pl.loop(0, dst.shape[0] // 64)
        def _(b):
            rs = pl.ds(pl.multiple_of(b * 64, 64), 64)
            dst[rs, :] = (dst[rs, :].astype(F32) + src[rs, :].astype(F32)).astype(BF)

    def slot(self, t):
        at = self.at
        n, p = at.n, at.p
        sd = t - (n - 2 - p)
        su = t - (p - 1)

        @pl.loop(0, self.pieces)
        def _(i):
            @pl.when((sd >= 0) & (sd < p) & at.has_above)
            def _():
                self.down_copy(sd, i).wait_recv()
                self.add(self.own.at[sd, i], self.din.at[sd, i])
                self.down_copy(sd, i).start()

            @pl.when((su >= 0) & (su < n - 1 - p) & at.has_below)
            def _():
                self.up_copy(su, i).wait_recv()
                self.add(self.own.at[n - 1 - su, i], self.uin.at[su, i])
                self.up_copy(su, i).start()

    def final(self, out):
        at = self.at
        n, p = at.n, at.p

        @pl.loop(0, self.pieces)
        def _(i):
            @pl.when(at.has_above)
            def _():
                self.down_copy(p, i).wait_recv()

            @pl.when(at.has_below)
            def _():
                self.up_copy(n - 1 - p, i).wait_recv()

            def close(parts):
                @pl.loop(0, out.shape[1] // 64)
                def _(b):
                    rs = pl.ds(pl.multiple_of(b * 64, 64), 64)
                    total = self.own[p, i, rs, :].astype(F32)
                    for ref, s in parts:
                        total = total + ref[s, i, rs, :].astype(F32)
                    out[i, rs, :] = total.astype(out.dtype)

            down, up = (self.din, p), (self.uin, n - 1 - p)

            @pl.when(at.has_above & at.has_below)
            def _():
                close([down, up])

            @pl.when(jnp.logical_not(at.has_below))
            def _():
                close([down])

            @pl.when(jnp.logical_not(at.has_above))
            def _():
                close([up])

    def drain(self):
        at = self.at
        n, p = at.n, at.p
        for k in range(n - self.slots, n):
            for i in range(self.pieces):
                self.core_copy(k, i).wait_send()
        for s in range(n - 1):

            @pl.when(s < p)
            def _():
                for i in range(self.pieces):
                    self.down_copy(s, i).wait_send()

            @pl.when(s < n - 1 - p)
            def _():
                for i in range(self.pieces):
                    self.up_copy(s, i).wait_send()


def line_sum_scratch(n, pieces, rows, cols, slots=2):
    dma = pltpu.SemaphoreType.DMA
    return [
        pltpu.VMEM((slots, pieces, rows, cols), BF),
        pltpu.VMEM((n, pieces, rows, cols), BF),
        pltpu.VMEM((n - 1, pieces, rows, cols), BF),
        pltpu.VMEM((n - 1, pieces, rows, cols), BF),
        dma((slots, pieces)),
        dma((n, pieces)),
        dma((n - 1, pieces)),
        dma((n - 1, pieces)),
        dma((n - 1, pieces)),
        dma((n - 1, pieces)),
    ]


class QuadSum:
    def __init__(self, at, t, r, sems):
        self.at, self.t, self.r = at, t, r
        self.s, self.v = sems
        self.order = [at.bits, at.bits[::-1]]
        self.levels = len(at.bits)
        self.seen = set()

    def count(self, k):
        return 1 << (self.levels - 1 - k)

    def slot(self, k, j):
        return sum(self.count(i) for i in range(k)) + j

    def rest(self, half, k):
        return self.order[half][k + 1 :]

    def index(self, half, k, mask):
        rest = self.rest(half, k)
        return self.slot(k, sum(1 << i for i, bit in enumerate(rest) if mask & bit))

    def source(self, half, mask):
        return self.t.at[half, self.at.quarter(mask)]

    def terms(self, half, mask, rs):
        return self.t[half, self.at.quarter(mask), rs, :].astype(F32)

    def copy(self, half, k, j):
        bit = self.order[half][k]
        mask = bit + spread(j, self.rest(half, k))
        src = self.source(half, mask) if k == 0 else self.r.at[half, self.index(half, k - 1, mask)]
        at = self.slot(k, j)
        return remote(
            src, self.r.at[half, at], self.s.at[half, at], self.v.at[half, at], self.at.peer(bit)
        )

    def offer(self, mask, only=(0, 1)):
        for half in only:
            if mask & self.order[half][0]:
                rest = self.rest(half, 0)
                self.copy(half, 0, sum(1 << i for i, b in enumerate(rest) if mask & b)).start()

    def masks(self):
        return sorted(range(1, 2 * self.count(0)), key=lambda m: -bin(m).count("1")) + [0]

    def come(self, half, k, mask):
        at = self.index(half, k, mask)
        if (half, at) not in self.seen:
            self.seen.add((half, at))
            self.copy(half, k, at - self.slot(k, 0)).wait_recv()
        return at

    def turn(self):
        for k in range(1, self.levels):
            for half in range(2):
                for j in range(self.count(k)):
                    mask = self.order[half][k] + spread(j, self.rest(half, k))
                    got = [self.come(half, i, mask) for i in range(k)]

                    @pl.loop(0, self.r.shape[2] // 64)
                    def _(b):
                        rs = pl.ds(pl.multiple_of(b * 64, 64), 64)
                        total = self.terms(half, mask, rs)
                        for i in got:
                            total = total + self.r[half, i, rs, :].astype(F32)
                        self.r[half, got[-1], rs, :] = total.astype(BF)

                    self.copy(half, k, j).start()

    def arrive(self):
        self.got = [[self.come(half, k, 0) for k in range(self.levels)] for half in range(2)]

    def total(self, half, rs):
        total = self.terms(half, 0, rs)
        for i in self.got[half]:
            total = total + self.r[half, i, rs, :].astype(F32)
        return total

    def drain(self):
        for half in range(2):
            for k in range(self.levels):
                for j in range(self.count(k)):
                    self.copy(half, k, j).wait_send()


class QuadSumHbm(QuadSum):
    def __init__(self, at, hbm, t, r, sems):
        super().__init__(at, t, r, sems[:2])
        self.hbm = hbm
        self.loads = [
            pltpu.make_async_copy(
                self.source(half, spread(j, self.rest(half, 0))), t.at[half, j], sems[2].at[half, j]
            )
            for half in range(2)
            for j in range(self.count(0))
        ]

    def source(self, half, mask):
        rows, cols = self.t.shape[2], self.t.shape[3]
        rs = pl.ds(pl.multiple_of(self.at.quarter(mask) * rows, rows), rows)
        return self.hbm.at[rs, pl.ds(half * cols, cols)]

    def terms(self, half, mask, rs):
        return self.t[half, self.index(half, 0, mask), rs, :].astype(F32)


def quad_sum_scratch(mp, rows, cols, parts=None):
    dma = pltpu.SemaphoreType.DMA
    return [
        pltpu.VMEM((2, parts or mp, rows, cols), BF),
        pltpu.VMEM((2, mp - 1, rows, cols), BF),
        dma((2, mp - 1)),
        dma((2, mp - 1)),
    ]


class QuadGather:
    def __init__(self, at, own, out, sems):
        self.at, self.own, self.out = at, own, out
        self.s, self.v, self.here = sems
        self.order = [at.bits[::-1], at.bits]
        self.levels = len(at.bits)
        self.seen = set()

    def spot(self, mask, half):
        rows, cols = self.own.shape[1], self.own.shape[2]
        rs = pl.ds(pl.multiple_of(self.at.quarter(mask) * rows, rows), rows)
        return self.out.at[rs, pl.ds(half * cols, cols)]

    def copy(self, half, k, j):
        mask = spread(j, self.order[half][:k])
        dst = self.spot(mask, half)
        src = self.own.at[half] if j == 0 else dst
        at = (1 << k) - 1 + j
        dev = self.at.peer(self.order[half][k])
        return remote(src, dst, self.s.at[half, at], self.v.at[half, at], dev)

    def come(self, half, k, j):
        if (half, k, j) not in self.seen:
            self.seen.add((half, k, j))
            self.copy(half, k, j).wait_recv()

    def keep(self, half):
        return pltpu.make_async_copy(self.own.at[half], self.spot(0, half), self.here.at[half])

    def start(self):
        for k in range(self.levels):
            for half in range(2):
                self.copy(half, k, 0).start()
        for half in range(2):
            self.keep(half).start()

    def forward(self):
        for k in range(1, self.levels):
            for half in range(2):
                for j in range(1, 1 << k):
                    top = j.bit_length() - 1
                    self.come(half, top, j - (1 << top))
                    self.copy(half, k, j).start()

    def finish(self):
        for half in range(2):
            for k in range(self.levels):
                for j in range(1 << k):
                    self.come(half, k, j)
                    self.copy(half, k, j).wait_send()
            self.keep(half).wait()


def quad_gather_scratch(mp, rows, cols):
    dma = pltpu.SemaphoreType.DMA
    return [pltpu.VMEM((2, rows, cols), BF), dma((2, mp - 1)), dma((2, mp - 1)), dma((2,))]


class LineGather:
    def __init__(self, at, pieces, shard, spot, sems):
        self.at, self.pieces, self.shard, self.spot = at, pieces, shard, spot
        self.d_s, self.d_r, self.u_s, self.u_r, self.c_s, self.c_r, self.here = sems

    def down_copy(self, h, i, own=False):
        b = 2 * (self.at.p + h) + self.at.c
        dst = self.spot(b, i)
        src = self.shard(i) if own else dst
        return remote(src, dst, self.d_s.at[h, i], self.d_r.at[h, i], self.at.below)

    def up_copy(self, h, i, own=False):
        b = 2 * (self.at.p - h) + self.at.c
        dst = self.spot(b, i)
        src = self.shard(i) if own else dst
        return remote(src, dst, self.u_s.at[h, i], self.u_r.at[h, i], self.at.above)

    def core_copy(self, z, i, own=False, incoming=False):
        b = 2 * z + (1 - self.at.c if incoming else self.at.c)
        dst = self.spot(b, i)
        src = self.shard(i) if own else dst
        return remote(src, dst, self.c_s.at[z, i], self.c_r.at[z, i], self.at.core)

    def keep(self, i):
        at = self.at
        return pltpu.make_async_copy(self.shard(i), self.spot(at.dp, i), self.here.at[i])

    def start(self):
        at = self.at
        for i in range(self.pieces):

            @pl.when(at.has_below)
            def _():
                self.down_copy(0, i, True).start()

            @pl.when(at.has_above)
            def _():
                self.up_copy(0, i, True).start()

        for i in range(self.pieces):
            self.core_copy(at.p, i, True).start()
            self.keep(i).start()

    def slot(self, h, i):
        at = self.at
        n, p = at.n, at.p

        @pl.when(p + h < n)
        def _():
            self.down_copy(h - 1, i).wait_recv()

            @pl.when(at.has_below)
            def _():
                self.down_copy(h, i).start()

            self.core_copy(p + h, i).start()

        @pl.when(p - h >= 0)
        def _():
            self.up_copy(h - 1, i).wait_recv()

            @pl.when(at.has_above)
            def _():
                self.up_copy(h, i).start()

            self.core_copy(p - h, i).start()

    def stage(self, h):
        @pl.loop(0, self.pieces)
        def _(i):
            self.slot(h, i)

    def ready(self, z, i):
        self.core_copy(z, i, incoming=True).wait_recv()

    def drain(self):
        at = self.at
        n, p = at.n, at.p

        @pl.loop(0, self.pieces)
        def _(i):
            for h in range(n):

                @pl.when((p + h < n) & at.has_below)
                def _():
                    self.down_copy(h, i, h == 0).wait_send()

                @pl.when((p - h >= 0) & at.has_above)
                def _():
                    self.up_copy(h, i, h == 0).wait_send()

            for z in range(n):
                self.core_copy(z, i).wait_send()


def line_gather_scratch(n, pieces):
    dma = pltpu.SemaphoreType.DMA
    return [dma((n, pieces))] * 6 + [dma((pieces,))]


def rows_spot(out, rows, width):
    def spot(b, i):
        rs = pl.ds(pl.multiple_of(b * rows, rows), rows)
        return out.at[rs, pl.ds(pl.multiple_of(i * width, width), width)]

    return spot


def cols_of(ref, width, base=0):
    return lambda i: ref.at[:, pl.ds(pl.multiple_of(base + i * width, width), width)]


def attend_rows(qkv, out, seq, hh, count, head):
    cols = lambda first: pl.ds(pl.multiple_of(first + head * HD, HD), HD)
    blk = 256
    for i in range(seq // blk):
        rows = pl.ds(i * blk, blk)
        span = (i + 1) * blk
        lg = logistic_block(qkv[rows, cols(0)], qkv[pl.ds(0, span), cols(hh)], seq)
        w = jnp.where(allowed_block(i * blk, blk, 0, span, count), lg, 0.0).astype(BF)
        out[rows, cols(0)] = dot(w, qkv[pl.ds(0, span), cols(2 * hh)]).astype(BF)


def attn_kernel(
    n_dp,
    n_mp,
    count_ref,
    gains_in,
    wq_hbm,
    wk_hbm,
    wv_hbm,
    wo_hbm,
    wg_hbm,
    wu_hbm,
    wd_hbm,
    x_hbm,
    cot_hbm,
    aw_ref,
    qkv_ref,
    att_ref,
    nin_ref,
    gains_ref,
    gush_ref,
    dnsh_ref,
    cotm_ref,
    w4,
    wo,
    shard,
    x,
    qkv,
    wbuf,
    wgu,
    wd,
    gush,
    dnsh,
    cot,
    load_s,
    wb_s,
    out_s,
    *rest,
):
    at = Place(n_dp, n_mp)
    n = at.n
    chunk, hh = wq_hbm.shape
    seq, d = x.shape
    ff = wgu.shape[2]
    loads = [
        pltpu.make_async_copy(src, dst, load_s.at[i])
        for i, (src, dst) in enumerate(
            [
                (wq_hbm, w4.at[0]),
                (wk_hbm, w4.at[1]),
                (wv_hbm, w4.at[2]),
                (wo_hbm, wo),
                (x_hbm, x),
                (wg_hbm, wgu.at[0]),
                (wu_hbm, wgu.at[1]),
                (wd_hbm, wd),
                (cot_hbm, cot),
            ]
        )
    ]
    for cp in loads:
        cp.start()
    spot = rows_spot(aw_ref, chunk, hh)
    three = LineGather(at, 3, cols_of(shard, hh), spot, rest[0:7])
    last = LineGather(
        at, 1, lambda i: shard.at[:, pl.ds(3 * hh, hh)], lambda b, i: spot(b, 3), rest[7:14]
    )
    small = LineGather(
        at,
        1,
        lambda i: gains_in,
        lambda b, i: gains_ref.at[:, pl.ds(pl.multiple_of(b * chunk, chunk), chunk)],
        rest[14:21],
    )
    enter(at)
    small.start()
    for i in range(3):
        loads[i].wait()
        shard[:, i * hh : (i + 1) * hh] = w4[i].astype(BF)
    three.start()
    loads[3].wait()
    shard[:, 3 * hh :] = wo[...].T.astype(BF)
    small.slot(1, 0)
    loads[5].wait()
    loads[6].wait()
    half = ff // PIECES

    @pl.loop(0, PIECES)
    def _(i):
        cols = pl.ds(pl.multiple_of(i * half, half), half)
        for k in range(2):
            to = pl.ds(pl.multiple_of((2 * i + k) * half, half), half)
            gush[:, to] = wgu[k, :, cols].astype(BF)

    outs = [pltpu.make_async_copy(gush, gush_ref, out_s.at[0])]
    outs[0].start()
    for h in range(2, n):
        small.slot(h, 0)
    small.keep(0).wait()
    for z in range(n):
        small.ready(z, 0)
    loads[4].wait()

    @pl.loop(0, seq // 32)
    def _(b):
        rs = pl.ds(pl.multiple_of(b * 32, 32), 32)
        v = x[rs, :].astype(F32)
        scale = lax.rsqrt(jnp.mean(v * v, axis=1, keepdims=True) + EPS)
        x[rs, :] = (v * scale * gains_ref[0:1, :]).astype(BF)

    outs.append(pltpu.make_async_copy(x, nin_ref, out_s.at[1]))
    outs[1].start()
    three.stage(1)
    loads[7].wait()

    @pl.loop(0, ff // 256)
    def _(i):
        rs = pl.ds(pl.multiple_of(i * 256, 256), 256)
        dnsh[:, rs] = wd[rs, :].T.astype(BF)

    outs.append(pltpu.make_async_copy(dnsh, dnsh_ref, out_s.at[2]))
    outs[2].start()
    loads[8].wait()
    count = count_ref[0]

    @pl.loop(0, seq // 32)
    def _(b):
        rs = pl.ds(pl.multiple_of(b * 32, 32), 32)
        row = b * 32 + lax.broadcasted_iota(jnp.int32, (32, d), 0)
        cot[rs, :] = jnp.where(row < count, cot[rs, :].astype(F32), 0.0).astype(BF)

    outs.append(pltpu.make_async_copy(cot, cotm_ref, out_s.at[3]))
    outs[3].start()
    for h in range(2, n - 1):
        three.stage(h)
    last.start()

    def w_copy(i):
        cols = pl.ds(pl.multiple_of(i * hh, hh), hh)
        return pltpu.make_async_copy(aw_ref.at[:, cols], wbuf.at[i], wb_s.at[i])

    for i in range(3):
        three.slot(n - 1, i)
        three.keep(i).wait()
        for z in range(n):
            three.ready(z, i)
        w_copy(i).start()
        if i == 1:
            last.slot(1, 0)
        w_copy(i).wait()

        @pl.loop(0, seq // 256)
        def _(b):
            rs = pl.ds(pl.multiple_of(b * 256, 256), 256)
            qkv[rs, i * hh : (i + 1) * hh] = dot(x[rs, :], wbuf[i]).astype(BF)

    outs.append(pltpu.make_async_copy(qkv, qkv_ref, out_s.at[4]))
    outs[4].start()
    for h in range(2, n - 1):
        last.slot(h, 0)
    heads = hh // HD

    @pl.loop(0, heads // 2)
    def _(head):
        attend_rows(qkv, att_ref, seq, hh, count, head)

    last.slot(n - 1, 0)

    @pl.loop(heads // 2, heads)
    def _(head):
        attend_rows(qkv, att_ref, seq, hh, count, head)

    last.keep(0).wait()
    for z in range(n):
        last.ready(z, 0)
    for cp in outs:
        cp.wait()
    small.drain()
    three.drain()
    last.drain()


def attn_stage(n_dp, n_mp, counts, gains, wq, wk, wv, wo, wg, wu, wd, x, cot):
    seq, d = x.shape
    chunk, hh = wq.shape
    ff = wg.shape[1]
    n = n_dp // 2
    dma = pltpu.SemaphoreType.DMA
    hbm = pl.BlockSpec(memory_space=pl.ANY)
    vm = pl.BlockSpec(memory_space=pltpu.VMEM)
    shapes = [
        ((d, 4 * hh), BF),
        ((seq, 3 * hh), BF),
        ((seq, hh), BF),
        ((seq, d), BF),
        ((8, d), F32),
        ((chunk, 2 * ff), BF),
        ((chunk, ff), BF),
        ((seq, d), BF),
    ]
    return pl.pallas_call(
        functools.partial(attn_kernel, n_dp, n_mp),
        out_shape=[jax.ShapeDtypeStruct(*s) for s in shapes],
        in_specs=[pl.BlockSpec(memory_space=pltpu.SMEM), vm] + [hbm] * 9,
        out_specs=[hbm, hbm, vm, hbm, vm, hbm, hbm, hbm],
        scratch_shapes=[
            pltpu.VMEM((3, chunk, hh), F32),
            pltpu.VMEM((hh, chunk), F32),
            pltpu.VMEM((chunk, 4 * hh), BF),
            pltpu.VMEM((seq, d), BF),
            pltpu.VMEM((seq, 3 * hh), BF),
            pltpu.VMEM((3, d, hh), BF),
            pltpu.VMEM((2, chunk, ff), F32),
            pltpu.VMEM((ff, chunk), F32),
            pltpu.VMEM((chunk, 2 * ff), BF),
            pltpu.VMEM((chunk, ff), BF),
            pltpu.VMEM((seq, d), BF),
            dma((9,)),
            dma((3,)),
            dma((5,)),
        ]
        + line_gather_scratch(n, 3)
        + line_gather_scratch(n, 1) * 2,
        compiler_params=pltpu.CompilerParams(
            collective_id=1, has_side_effects=True, vmem_limit_bytes=VMEM_LIMIT
        ),
        name="attn_stage",
    )(counts, gains, wq, wk, wv, wo, wg, wu, wd, x, cot)


def gate_kernel(
    n_dp,
    n_mp,
    att_ref,
    aw_hbm,
    sh_hbm,
    x_hbm,
    gain_ref,
    gw_ref,
    nm_ref,
    hid_ref,
    gu_ref,
    inner_ref,
    wo,
    xs,
    nm,
    wbuf,
    gbuf,
    ibuf,
    load_s,
    wb_s,
    gb_s,
    ib_s,
    *rest,
):
    at = Place(n_dp, n_mp)
    n = at.n
    quad = QuadSum(at, *rest[0:2], rest[2:4])
    gather_nm = QuadGather(at, rest[4], nm_ref, rest[5:8])
    sems = rest[8:15]
    hh = wo.shape[1]
    part, half_cols = quad.t.shape[2], quad.t.shape[3]
    chunk, wide = sh_hbm.shape
    pieces = sems[6].shape[0]
    width = wide // pieces
    line = LineGather(at, pieces, cols_of(sh_hbm, width), rows_spot(gw_ref, chunk, width), sems)

    load = pltpu.make_async_copy(aw_hbm.at[:, pl.ds(3 * hh, hh)], wo, load_s.at[0])
    load.start()
    load_x = pltpu.make_async_copy(x_hbm.at[part_rows(at, part), :], xs, load_s.at[1])
    load_x.start()
    enter(at)
    line.start()
    load.wait()

    def terms(q):
        rs = pl.ds(pl.multiple_of(q * part, part), part)
        for half in range(2):
            w = wo[half * half_cols : (half + 1) * half_cols, :]
            quad.t[half, q] = dot(att_ref[rs, :], w, NT).astype(BF)

    for mask in quad.masks():
        terms(at.quarter(mask))
        quad.offer(mask)
    quad.turn()
    quad.arrive()
    load_x.wait()

    @pl.loop(0, part // 32)
    def _(b):
        rs = pl.ds(pl.multiple_of(b * 32, 32), 32)
        h = xs[rs, :].astype(F32) + jnp.concatenate(
            [quad.total(0, rs), quad.total(1, rs)], axis=1
        )
        hid_ref[rs, :] = h
        scale = lax.rsqrt(jnp.mean(h * h, axis=1, keepdims=True) + EPS)
        res = (h * scale * gain_ref[1:2, :]).astype(BF)
        gather_nm.own[0, rs, :] = res[:, :half_cols]
        gather_nm.own[1, rs, :] = res[:, half_cols:]

    gather_nm.start()
    line.stage(1)
    gather_nm.forward()
    gather_nm.finish()
    load = pltpu.make_async_copy(nm_ref, nm, load_s.at[0])
    load.start()
    for h in range(2, n - 1):
        line.stage(h)
    load.wait()

    def w_copy(i, slot):
        cols = pl.ds(pl.multiple_of(i * width, width), width)
        return pltpu.make_async_copy(gw_ref.at[:, cols], wbuf.at[slot], wb_s.at[slot])

    def g_copy(i, slot):
        cols = pl.ds(pl.multiple_of(i * width, width), width)
        return pltpu.make_async_copy(gbuf.at[slot], gu_ref.at[:, cols], gb_s.at[slot])

    def i_copy(i, slot):
        cols = pl.ds(pl.multiple_of(i * (width // 2), width // 2), width // 2)
        return pltpu.make_async_copy(ibuf.at[slot], inner_ref.at[:, cols], ib_s.at[slot])

    @pl.loop(0, pieces)
    def _(i):
        slot = lax.rem(i, 2)
        line.slot(n - 1, i)
        line.keep(i).wait()
        for z in range(n):
            line.ready(z, i)
        w_copy(i, slot).start()

        @pl.when(i >= 2)
        def _():
            g_copy(i - 2, slot).wait()
            i_copy(i - 2, slot).wait()

        w_copy(i, slot).wait()

        @pl.loop(0, nm.shape[0] // 256)
        def _(b):
            rs = pl.ds(pl.multiple_of(b * 256, 256), 256)
            v = dot(nm[rs, :], wbuf[slot]).astype(BF)
            gbuf[slot, rs, :] = v
            g = v[:, : width // 2].astype(F32)
            u = v[:, width // 2 :].astype(F32)
            ibuf[slot, rs, :] = (g / (1.0 + jnp.exp(-g)) * u).astype(BF)

        g_copy(i, slot).start()
        i_copy(i, slot).start()

    for i in range(max(0, pieces - 2), pieces):
        g_copy(i, i % 2).wait()
        i_copy(i, i % 2).wait()
    line.drain()
    quad.drain()


def gate_stage(n_dp, n_mp, att, aw, shard, x, gain):
    seq, hh = att.shape
    d = aw.shape[0]
    chunk, wide = shard.shape
    n, part = n_dp // 2, seq // n_mp
    dma = pltpu.SemaphoreType.DMA
    hbm = pl.BlockSpec(memory_space=pl.ANY)
    vm = pl.BlockSpec(memory_space=pltpu.VMEM)
    width = wide // PIECES
    return pl.pallas_call(
        functools.partial(gate_kernel, n_dp, n_mp),
        out_shape=[
            jax.ShapeDtypeStruct((d, wide), BF),
            jax.ShapeDtypeStruct((seq, d), BF),
            jax.ShapeDtypeStruct((part, d), F32),
            jax.ShapeDtypeStruct((seq, wide), BF),
            jax.ShapeDtypeStruct((seq, wide // 2), BF),
        ],
        in_specs=[vm, hbm, hbm, hbm, vm],
        out_specs=[hbm, hbm, vm, hbm, hbm],
        scratch_shapes=[
            pltpu.VMEM((d, hh), BF),
            pltpu.VMEM((part, d), BF),
            pltpu.VMEM((seq, d), BF),
            pltpu.VMEM((2, d, width), BF),
            pltpu.VMEM((2, seq, width), BF),
            pltpu.VMEM((2, seq, width // 2), BF),
            dma((2,)),
            dma((2,)),
            dma((2,)),
            dma((2,)),
        ]
        + quad_sum_scratch(n_mp, part, d // 2)
        + quad_gather_scratch(n_mp, part, d // 2)
        + line_gather_scratch(n, PIECES),
        compiler_params=pltpu.CompilerParams(
            collective_id=2, has_side_effects=True, vmem_limit_bytes=VMEM_LIMIT
        ),
        name="gate_stage",
    )(att, aw, shard, x, gain)


def down_kernel(
    n_dp,
    n_mp,
    inner_hbm,
    gu_hbm,
    cot_hbm,
    sh_hbm,
    rs_ref,
    ft_ref,
    ggu_ref,
    dn_ref,
    inner,
    gu,
    cot,
    dn,
    acc,
    ftb,
    load_s,
    ft_s,
    dn_s,
    gg_s,
    *rest,
):
    at = Place(n_dp, n_mp)
    n, p = at.n, at.p
    line = LineSum(at, *rest[0:4], rest[4:10])
    sems = rest[10:17]
    chunk, ff = sh_hbm.shape
    pieces = sems[6].shape[0]
    width = ff // pieces
    gather = LineGather(at, pieces, cols_of(sh_hbm, width), rows_spot(dn_ref, chunk, width), sems)
    pair = 2 * chunk
    loads = [
        pltpu.make_async_copy(src, dst, load_s.at[i])
        for i, (src, dst) in enumerate([(cot_hbm, cot), (inner_hbm, inner), (gu_hbm, gu)])
    ]
    for cp in loads:
        cp.start()
    enter(at)
    gather.start()
    loads[0].wait()
    loads[1].wait()

    def run(e):
        k, core = e // 2, e % 2
        block = 2 * order_of(k, at) + (1 - at.c if core == 0 else at.c)
        lhs = cot[:, pl.ds(pl.multiple_of(block * chunk, chunk), chunk)].T

        def tile(i):
            return dot(lhs, inner[:, pl.ds(pl.multiple_of(i * width, width), width)])

        if core == 0:
            line.other(k, tile)
        else:
            line.mine(k, tile)

    for e in range(2 * n):
        run(e)

    def ft_copy(z, slot):
        cols = pl.ds(pl.multiple_of(z * pair, pair), pair)
        return pltpu.make_async_copy(ftb.at[slot], ft_ref.at[:, cols], ft_s.at[slot])

    def work(z, fresh):
        rs = pl.ds(pl.multiple_of(z * pair, pair), pair)

        @pl.loop(0, pieces)
        def _(i):
            gather.ready(z, i)

        load = pltpu.make_async_copy(dn_ref.at[rs, :], dn, dn_s.at[0])
        load.start()
        load.wait()

        @pl.loop(0, ff // 512)
        def _(i):
            cols = pl.ds(pl.multiple_of(i * 512, 512), 512)
            v = dot(cot[:, rs], dn[:, cols])
            acc[:, cols] = v if fresh else acc[:, cols] + v

        if not fresh:
            ft_copy(z, 0).wait()
        ftb[0] = dot(inner[...], dn[...], NT).astype(BF)
        ft_copy(z, 0).start()

    for i in range(pieces):
        gather.keep(i).wait()
    work(p, True)
    loads[2].wait()

    @pl.loop(1, n)
    def _(h):
        gather.stage(h)
        line.slot(h - 1)

        @pl.when(p + h < n)
        def _():
            work(p + h, False)

        @pl.when(p - h >= 0)
        def _():
            work(p - h, False)

    half = width

    def gg_copy(i):
        cols = pl.ds(pl.multiple_of(i * 2 * half, 2 * half), 2 * half)
        return pltpu.make_async_copy(gu.at[:, cols], ggu_ref.at[:, cols], gg_s.at[i])

    @pl.loop(0, pieces)
    def _(i):
        gcols = pl.ds(pl.multiple_of(i * 2 * half, half), half)
        ucols = pl.ds(pl.multiple_of(i * 2 * half + half, half), half)
        acols = pl.ds(pl.multiple_of(i * half, half), half)

        @pl.loop(0, gu.shape[0] // 64)
        def _(b):
            rs = pl.ds(pl.multiple_of(b * 64, 64), 64)
            g = gu[rs, gcols].astype(F32)
            u = gu[rs, ucols].astype(F32)
            gi = acc[rs, acols]
            sg = 1.0 / (1.0 + jnp.exp(-g))
            gu[rs, gcols] = (gi * u * sg * (1.0 + g * (1.0 - sg))).astype(BF)
            gu[rs, ucols] = (gi * g * sg).astype(BF)

        gg_copy(i).start()

    line.final(rs_ref)
    for i in range(pieces):
        gg_copy(i).wait()
    ft_copy(p, 0).wait()
    line.drain()
    gather.drain()


def down_stage(n_dp, n_mp, inner, gu, cot, shard):
    seq, d = cot.shape
    chunk, ff = shard.shape
    n = n_dp // 2
    dma = pltpu.SemaphoreType.DMA
    hbm = pl.BlockSpec(memory_space=pl.ANY)
    vm = pl.BlockSpec(memory_space=pltpu.VMEM)
    return pl.pallas_call(
        functools.partial(down_kernel, n_dp, n_mp),
        out_shape=[
            jax.ShapeDtypeStruct((PIECES, chunk, ff // PIECES), BF),
            jax.ShapeDtypeStruct((seq, d), BF),
            jax.ShapeDtypeStruct((seq, 2 * ff), BF),
            jax.ShapeDtypeStruct((d, ff), BF),
        ],
        in_specs=[hbm] * 4,
        out_specs=[vm, hbm, hbm, hbm],
        scratch_shapes=[
            pltpu.VMEM((seq, ff), BF),
            pltpu.VMEM((seq, 2 * ff), BF),
            pltpu.VMEM((seq, d), BF),
            pltpu.VMEM((2 * chunk, ff), BF),
            pltpu.VMEM((seq, ff), F32),
            pltpu.VMEM((1, seq, 2 * chunk), BF),
            dma((3,)),
            dma((1,)),
            dma((1,)),
            dma((PIECES,)),
        ]
        + line_sum_scratch(n, PIECES, chunk, ff // PIECES)
        + line_gather_scratch(n, PIECES),
        compiler_params=pltpu.CompilerParams(
            collective_id=3, has_side_effects=True, vmem_limit_bytes=VMEM_LIMIT
        ),
        name="down_stage",
    )(inner, gu, cot, shard)[:3]


def mid_kernel(
    n_dp,
    n_mp,
    ggu_hbm,
    gw_hbm,
    nm_hbm,
    ft_hbm,
    cot_hbm,
    qkv_hbm,
    aw_hbm,
    count_ref,
    hid_ref,
    gain_ref,
    rs_ref,
    low_ref,
    lay_ref,
    gh_ref,
    gg_ref,
    dq_ref,
    space,
    wt,
    wt_s,
    nm,
    nm_s,
    cot,
    dka,
    dva,
    load_s,
    *rest,
):
    at = Place(n_dp, n_mp)
    n = at.n
    line = LineSum(at, *rest[0:4], rest[4:10])
    mid = QuadSum(at, *rest[10:12], rest[12:14])
    lay = QuadSumHbm(at, ft_hbm, *rest[14:16], rest[16:19])
    gather_low = QuadGather(at, rest[19], low_ref, rest[20:23])
    gather_lay = QuadGather(at, rest[23], lay_ref, rest[24:27])
    part, half_cols = mid.t.shape[2], mid.t.shape[3]
    chunk, width = line.own.shape[2], line.own.shape[3]
    pieces = line.pieces
    hh = qkv_hbm.shape[1] // 3
    drows = wt.shape[1]
    tiles = half_cols // drows

    wide = ggu_hbm.shape[1]
    ggu = space.at[:, pl.ds(0, wide)]
    load = pltpu.make_async_copy(ggu_hbm, ggu, load_s.at[0])
    load.start()
    load_cot = pltpu.make_async_copy(cot_hbm.at[part_rows(at, part), :], cot, load_s.at[1])
    load_cot.start()

    def nm_copy(e):
        k, core = e // 2, e % 2
        block = 2 * order_of(k, at) + (1 - at.c if core == 0 else at.c)
        cols = pl.ds(pl.multiple_of(block * chunk, chunk), chunk)
        return pltpu.make_async_copy(nm_hbm.at[:, cols], nm.at[e % 2], nm_s.at[e % 2])

    def wt_copy(half, i, slot):
        rows = pl.ds(pl.multiple_of(half * half_cols + i * drows, drows), drows)
        return pltpu.make_async_copy(gw_hbm.at[rows, :], wt.at[slot], wt_s.at[slot])

    nm_copy(0).start()
    wt_copy(0, 0, 0).start()
    for cp in lay.loads:
        cp.start()
    enter(at)
    for mask in lay.masks():
        lay.offer(mask)
    load.wait()

    def run(e):
        if e + 1 < 2 * n:
            nm_copy(e + 1).start()
        nm_copy(e).wait()
        lhs = nm[e % 2].T

        def tile(i):
            return dot(lhs, ggu[:, pl.ds(pl.multiple_of(i * width, width), width)])

        if e % 2 == 0:
            line.other(e // 2, tile)
        else:
            line.mine(e // 2, tile)

    def terms(half):
        @pl.loop(0, tiles)
        def _(i):
            slot = lax.rem(i, 2)
            if half == 0:
                nxt = wt_copy(jnp.where(i + 1 < tiles, 0, 1), lax.rem(i + 1, tiles), 1 - slot)
                nxt.start()
            else:

                @pl.when(i + 1 < tiles)
                def _():
                    wt_copy(1, i + 1, 1 - slot).start()

            wt_copy(half, i, slot).wait()
            v = dot(ggu[...], wt[slot], NT).astype(BF)
            cols = pl.ds(pl.multiple_of(i * drows, drows), drows)
            for q in range(n_mp):
                mid.t[half, q, :, cols] = v[q * part : (q + 1) * part]

        for mask in mid.masks():
            mid.offer(mask, (half,))

    run(0)
    run(1)
    terms(0)
    run(2)
    run(3)
    terms(1)
    for cp in lay.loads:
        cp.wait()
    lay.turn()
    for e in range(4, 2 * n):
        run(e)
    lay.arrive()

    @pl.loop(0, part // 32)
    def _(b):
        rs = pl.ds(pl.multiple_of(b * 32, 32), 32)
        for half in range(2):
            h = hid_ref[rs, pl.ds(half * half_cols, half_cols)]
            gather_lay.own[half, rs, :] = (h + lay.total(half, rs)).astype(BF)

    line.slot(0)
    per = half_cols // hh
    blocks_d = 2 * half_cols // part
    wo_spot = [(e // per // (n_mp // 2), e // per % (n_mp // 2), e % per) for e in range(blocks_d)]
    wo_parts = [
        pltpu.make_async_copy(
            aw_hbm.at[pl.ds(e * part, part), pl.ds(3 * hh, hh)],
            lay.t.at[i, j, :, pl.ds(k * hh, hh)],
            load_s.at[4 + e],
        )
        for e, (i, j, k) in enumerate(wo_spot)
    ]
    for cp in wo_parts:
        cp.start()
    load_qkv = pltpu.make_async_copy(
        qkv_hbm, space.at[:, pl.ds(2 * half_cols, 3 * hh)], load_s.at[2]
    )
    load_qkv.start()
    mid.turn()
    mid.arrive()
    load_cot.wait()
    gg_ref[...] = jnp.zeros_like(gg_ref)

    @pl.loop(0, part // 32)
    def _(b):
        rs = pl.ds(pl.multiple_of(b * 32, 32), 32)
        h = hid_ref[rs, :]
        scale = lax.rsqrt(jnp.mean(h * h, axis=1, keepdims=True) + EPS)
        g = jnp.concatenate([mid.total(0, rs), mid.total(1, rs)], axis=1)
        unit = h * scale
        weighted = g * gain_ref[1:2, :]
        field = scale * (weighted - unit * jnp.mean(weighted * unit, axis=1, keepdims=True))
        res = cot[rs, :].astype(F32) + field
        gh_ref[rs, :] = res
        low = res.astype(BF)
        gather_low.own[0, rs, :] = low[:, :half_cols]
        gather_low.own[1, rs, :] = low[:, half_cols:]
        gg_ref[...] += jnp.sum(g * unit, axis=0, keepdims=True)

    gather_low.start()
    gather_low.forward()
    gather_lay.start()
    gather_low.finish()
    load_low = pltpu.make_async_copy(low_ref, space.at[:, pl.ds(0, 2 * half_cols)], load_s.at[3])
    load_low.start()
    for s in range(1, n - 2):
        line.slot(s)
    gather_lay.forward()
    load_low.wait()
    load_qkv.wait()
    for cp in wo_parts:
        cp.wait()
    seq = space.shape[0]
    base = 2 * half_cols
    gbase = base + 3 * hh

    @pl.loop(0, seq // 256)
    def _(b):
        rs = pl.ds(pl.multiple_of(b * 256, 256), 256)
        total = jnp.zeros((256, hh), F32)
        for e, (i, j, k) in enumerate(wo_spot):
            wo = lay.t[i, j, :, k * hh : (k + 1) * hh]
            total += dot(space[rs, e * part : (e + 1) * part], wo)
        space[rs, gbase : gbase + hh] = total.astype(BF)

    count = count_ref[0]
    blk = 256
    blocks = seq // blk

    @pl.loop(0, hh // HD)
    def _(head):
        at_cols = lambda first: pl.ds(pl.multiple_of(first + head * HD, HD), HD)
        for i in range(blocks - 1, -1, -1):
            rows = pl.ds(i * blk, blk)
            span = (i + 1) * blk
            keys = pl.ds(0, span)
            q = space[rows, at_cols(base)]
            g = space[rows, at_cols(gbase)]
            k = space[keys, at_cols(base + hh)]
            lg = jnp.where(
                allowed_block(i * blk, blk, 0, span, count), logistic_block(q, k, seq), 0.0
            )
            w = lg.astype(BF)
            gw = dot(g, space[keys, at_cols(base + 2 * hh)], NT)
            gs = (gw * lg * (1.0 - lg) * HD ** (-0.5)).astype(BF)
            wt[i // 2, :, at_cols((i % 2) * (wide // 2))] = dot(gs, k).astype(BF)
            dk = dot(gs, q, TN)
            dv = dot(w, g, TN)
            if i == blocks - 1:
                dka[...] = dk
                dva[...] = dv
            else:
                dka[keys, :] += dk
                dva[keys, :] += dv
        for i in range(blocks):
            rows = pl.ds(i * blk, blk)
            wt[i // 2, :, at_cols((i % 2) * (wide // 2) + hh)] = dka[rows, :].astype(BF)
            wt[i // 2, :, at_cols((i % 2) * (wide // 2) + 2 * hh)] = dva[rows, :].astype(BF)

    stores = [
        pltpu.make_async_copy(
            wt.at[i // 2, :, pl.ds((i % 2) * (wide // 2), 3 * hh)],
            dq_ref.at[pl.ds(i * blk, blk), :],
            load_s.at[4 + i],
        )
        for i in range(blocks)
    ]
    for cp in stores:
        cp.start()
    line.final(rs_ref)
    gather_lay.finish()
    for cp in stores:
        cp.wait()
    line.drain()
    mid.drain()
    lay.drain()


def mid_stage(n_dp, n_mp, ggu, gw, nm, ft, cot, qkv, aw, counts, hid, gain):
    seq, wide = ggu.shape
    hh = qkv.shape[1] // 3
    d = gw.shape[0]
    n, part, chunk = n_dp // 2, seq // n_mp, d // n_dp
    dma = pltpu.SemaphoreType.DMA
    hbm = pl.BlockSpec(memory_space=pl.ANY)
    vm = pl.BlockSpec(memory_space=pltpu.VMEM)
    pieces = PIECES
    return pl.pallas_call(
        functools.partial(mid_kernel, n_dp, n_mp),
        out_shape=[
            jax.ShapeDtypeStruct((pieces, chunk, wide // pieces), BF),
            jax.ShapeDtypeStruct((seq, d), BF),
            jax.ShapeDtypeStruct((seq, d), BF),
            jax.ShapeDtypeStruct((part, d), F32),
            jax.ShapeDtypeStruct((1, d), F32),
            jax.ShapeDtypeStruct((seq, 3 * hh), BF),
        ],
        in_specs=[hbm] * 7 + [pl.BlockSpec(memory_space=pltpu.SMEM)] + [vm] * 2,
        out_specs=[vm, hbm, hbm, vm, vm, hbm],
        scratch_shapes=[
            pltpu.VMEM((seq, max(wide, d + 4 * hh)), BF),
            pltpu.VMEM((2, 256, wide), BF),
            dma((2,)),
            pltpu.VMEM((2, seq, chunk), BF),
            dma((2,)),
            pltpu.VMEM((part, d), BF),
            pltpu.VMEM((seq, HD), F32),
            pltpu.VMEM((seq, HD), F32),
            dma((4 + max(d // part, seq // 256),)),
        ]
        + line_sum_scratch(n, pieces, chunk, wide // pieces, 1)
        + quad_sum_scratch(n_mp, part, d // 2)
        + quad_sum_scratch(n_mp, part, d // 2, n_mp // 2)
        + [dma((2, n_mp // 2))]
        + quad_gather_scratch(n_mp, part, d // 2) * 2,
        compiler_params=pltpu.CompilerParams(
            collective_id=4, has_side_effects=True, vmem_limit_bytes=VMEM_LIMIT
        ),
        name="mid_stage",
    )(ggu, gw, nm, ft, cot, qkv, aw, counts, hid, gain)


def last_kernel(
    n_dp,
    n_mp,
    dqkv_hbm,
    aw_hbm,
    nin_hbm,
    low_hbm,
    att_hbm,
    x_hbm,
    gh_ref,
    gain_ref,
    gmid_ref,
    rs_ref,
    grad_ref,
    gains_ref,
    rhs,
    aw,
    nin,
    low,
    lhs,
    x,
    loads,
    pout,
    own,
    din,
    uin,
    po_s,
    po_r,
    d_s,
    d_r,
    u_s,
    u_r,
    t,
    r,
    q1,
    q2,
    gown,
    g1,
    g2,
    g3,
    fold_out,
    fold_in,
    fold_s,
    fold_r,
):
    at = Place(n_dp, n_mp)
    hh = att_hbm.shape[1]
    part = t.shape[2]
    chunk = own.shape[2]
    half_cols = t.shape[3]
    copies = [
        pltpu.make_async_copy(src, dst, loads.at[i])
        for i, (src, dst) in enumerate(
            [
                (dqkv_hbm, rhs.at[:, pl.ds(0, 3 * hh)]),
                (aw_hbm.at[:, pl.ds(0, 3 * hh)], aw),
                (nin_hbm, nin),
                (att_hbm, rhs.at[:, pl.ds(3 * hh, hh)]),
                (low_hbm, low),
                (x_hbm.at[part_rows(at, part), :], x),
            ]
        )
    ]
    for cp in copies:
        cp.start()
    bits = [b for b in (2, 4, 8, 16) if b < n_dp]
    enter(at, [at.fold(b) for b in bits[1:]])
    quad = QuadSum(at, t, r, (q1, q2))
    line = LineSum(at, pout, own, din, uin, (po_s, po_r, d_s, d_r, u_s, u_r))
    gather = QuadGather(at, gown, grad_ref, (g1, g2, g3))
    copies[0].wait()
    copies[1].wait()

    def terms(q):
        rs = pl.ds(pl.multiple_of(q * part, part), part)
        width = 512

        @pl.loop(0, half_cols // width)
        def _(i):
            for half in range(2):
                d0 = pl.multiple_of(half * half_cols + i * width, width)
                v = dot(rhs[rs, 0 : 3 * hh], aw[pl.ds(d0, width), :], NT)
                t[half, q, :, pl.ds(pl.multiple_of(i * width, width), width)] = v.astype(BF)

    for mask in quad.masks()[:-1]:
        terms(at.quarter(mask))
        quad.offer(mask)
    for cp in copies[2:]:
        cp.wait()

    def run(k, core):
        block = 2 * order_of(k, at) + (at.c if core else 1 - at.c)
        cols = pl.ds(pl.multiple_of(block * chunk, chunk), chunk)
        lhs[0] = nin[:, cols].T
        lhs[1] = low[:, cols].T

        def tile(i):
            return dot(lhs[lax.div(i, 3)], rhs[:, pl.ds(pl.multiple_of(i * hh, hh), hh)])

        if core:
            line.mine(k, tile)
        else:
            line.other(k, tile)

    n = at.n
    for k in range(n + 1):
        if k < n:
            run(k, 0)
        if k > 0:
            run(k - 1, 1)
    terms(at.m)
    quad.turn()
    line.slot(0)
    quad.arrive()

    fold_out[...] = jnp.zeros_like(fold_out)

    @pl.loop(0, part // 32)
    def _(b):
        rs = pl.ds(pl.multiple_of(b * 32, 32), 32)
        v = x[rs, :].astype(F32)
        scale = lax.rsqrt(jnp.mean(v * v, axis=1, keepdims=True) + EPS)
        g = jnp.concatenate([quad.total(0, rs), quad.total(1, rs)], axis=1)
        unit = v * scale
        weighted = g * gain_ref[0:1, :]
        field = scale * (weighted - unit * jnp.mean(weighted * unit, axis=1, keepdims=True))
        res = (gh_ref[rs, :] + field).astype(BF)
        gown[0, rs, :] = res[:, :half_cols]
        gown[1, rs, :] = res[:, half_cols:]
        fold_out[0, 0:1, :] += jnp.sum(g * unit, axis=0, keepdims=True)

    gather.start()
    fold_out[0, 1:2, :] = gmid_ref[...]
    devs = [at.core] + [at.peer(b) for b in at.bits] + [at.fold(b) for b in bits]

    def fold_copy(b):
        return remote(fold_out.at[b], fold_in.at[b], fold_s.at[b], fold_r.at[b], devs[b])

    def fold_next(b):
        fold_copy(b).wait_recv()
        nxt = fold_out[b] + fold_in[b]
        if b + 1 < len(devs):
            fold_out[b + 1] = nxt
            fold_copy(b + 1).start()
        else:
            gains_ref[...] = nxt

    fold_copy(0).start()
    for s in range(1, n - 2):
        line.slot(s)
    gather.forward()
    for b in range(len(devs)):
        fold_next(b)
    line.final(rs_ref)
    gather.finish()
    line.drain()
    quad.drain()
    for b in range(len(devs)):
        fold_copy(b).wait_send()


def last_stage(n_dp, n_mp, dqkv, aw, nin, low, att, x, gh, gain, gmid):
    seq, hh = att.shape
    d = aw.shape[0]
    n, part, chunk = n_dp // 2, seq // n_mp, d // n_dp
    dma = pltpu.SemaphoreType.DMA
    anyspace = pl.BlockSpec(memory_space=pl.ANY)
    vm = pl.BlockSpec(memory_space=pltpu.VMEM)
    folds = 1 + len([b for b in (1, 2, 4, 8) if b < n_mp]) + len([b for b in (2, 4, 8, 16) if b < n_dp])
    return pl.pallas_call(
        functools.partial(last_kernel, n_dp, n_mp),
        out_shape=[
            jax.ShapeDtypeStruct((4, chunk, hh), BF),
            jax.ShapeDtypeStruct((seq, d), BF),
            jax.ShapeDtypeStruct((8, d), F32),
        ],
        in_specs=[anyspace] * 6 + [vm] * 3,
        out_specs=[vm, anyspace, vm],
        scratch_shapes=[
            pltpu.VMEM((seq, 4 * hh), BF),
            pltpu.VMEM((d, 3 * hh), BF),
            pltpu.VMEM((seq, d), BF),
            pltpu.VMEM((seq, d), BF),
            pltpu.VMEM((2, chunk, seq), BF),
            pltpu.VMEM((part, d), BF),
            dma((6,)),
        ]
        + line_sum_scratch(n, 4, chunk, hh)
        + quad_sum_scratch(n_mp, part, d // 2)
        + quad_gather_scratch(n_mp, part, d // 2)
        + [
            pltpu.VMEM((folds, 8, d), F32),
            pltpu.VMEM((folds, 8, d), F32),
            dma((folds,)),
            dma((folds,)),
        ],
        compiler_params=pltpu.CompilerParams(
            collective_id=5, has_side_effects=True, vmem_limit_bytes=VMEM_LIMIT
        ),
        name="last_stage",
    )(dqkv, aw, nin, low, att, x, gh, gain, gmid)


def on_device(
    inputs,
    counts,
    cotangent,
    gain_attn,
    w_query,
    w_key,
    w_value,
    w_output,
    gain_ffn,
    w_gate,
    w_up,
    w_down,
):
    ff = w_gate.shape[1]
    n_dp, n_mp = lax.axis_size("dp"), lax.axis_size("mp")
    gains = jnp.pad(jnp.stack([gain_attn, gain_ffn]), ((0, 6), (0, 0)))
    gains = gains.astype(BF).astype(F32)
    attn_w, qkv, attended, normed_in, gains, gu_shard, down_shard, grad_ffn = attn_stage(
        n_dp, n_mp, counts, gains, w_query, w_key, w_value, w_output, w_gate, w_up, w_down, inputs, cotangent
    )
    gu_w, normed_mid, hidden, gu, inner = gate_stage(
        n_dp, n_mp, attended, attn_w, gu_shard, inputs, gains
    )
    rs_down, ffn_terms, ggu = down_stage(n_dp, n_mp, inner, gu, grad_ffn, down_shard)
    rs_gu, grad_low, layer_out, grad_hidden, g_gain_mid, dqkv = mid_stage(
        n_dp, n_mp, ggu, gu_w, normed_mid, ffn_terms, grad_ffn, qkv, attn_w, counts, hidden, gains
    )
    rs_attn, grad_low_in, g_gains = last_stage(
        n_dp, n_mp, dqkv, attn_w, normed_in, grad_low, attended, inputs, grad_hidden, gains, g_gain_mid
    )
    input_grad = grad_low_in.astype(F32)
    width = g_gains.shape[1] // lax.axis_size("dp")
    g_gains = lax.dynamic_slice_in_dim(g_gains, lax.axis_index("dp") * width, width, 1)
    half = ff // PIECES
    unpack = lambda i: jnp.concatenate(
        [rs_gu[k, :, i * half : (i + 1) * half] for k in range(PIECES)], axis=1
    ).astype(F32)
    down_t = jnp.concatenate([rs_down[k] for k in range(PIECES)], axis=1)
    return (
        layer_out,
        input_grad,
        g_gains[0],
        rs_attn[0].astype(F32),
        rs_attn[1].astype(F32),
        rs_attn[2].astype(F32),
        rs_attn[3].astype(F32).T,
        g_gains[1],
        unpack(0),
        unpack(1),
        down_t.astype(F32).T,
    )


def solution(mesh):
    row, both, swapped = P("dp", None), P("dp", "mp"), P("mp", "dp")
    weights = (both, both, both, swapped)
    ffn = (both, both, swapped)
    return jax.shard_map(
        on_device,
        mesh=mesh,
        in_specs=(row, P("dp"), row, P("dp")) + weights + (P("dp"),) + ffn,
        out_specs=(row, row, P("dp")) + weights + (P("dp"),) + ffn,
        check_vma=False,
    )
```

time: 721 us -> 652 us (0.904)
  Pallas kernels: 562 us -> 618 us
  local copies, waits for them, and re-layouts: 45.2 us -> 11.9 us
  waiting for transfers between devices: 32.2 us -> 0 us
  other arithmetic: 32.5 us -> 12.7 us
  matrix products: 15.9 us -> 0 us
  blocking collectives: 13.6 us -> 0 us
  between operations: 15.2 us -> 1.8 us
    pallas_call x6 -> x5, Pallas kernels: 562 us -> 618 us  [the longest x1 172 us: mid_stage(): pl.pallas_call(functools.partial(mid_kernel, n_dp, n_mp), out_shape=[jax....]
    all_gather x1 -> x0, waiting for transfers between devices: 32.2 us -> none  [on_device(): gather = lambda x: lax.all_gather(x, 'dp', axis=0, tiled=True)]
    dot_general x2 -> x0, matrix products: 15.9 us -> none  [dot(): return lax.dot_general(a, b, dims, preferred_element_type=F32)]
    all_gather x1 -> x0, blocking collectives: 13.6 us -> none  [on_device(): lax.all_gather(jnp.stack([gain_attn, gain_ffn]).astype(BF), 'dp', axis=1,...]
    another operation x9 -> x2, other arithmetic: 12.1 us -> 1.36 us  [the longest x1 6.83 us: on_device(): jnp.stack([g.reshape(g.shape[0], PIECES, -1), u.reshape(u.shape[0], PIECE...]
    unnamed x44 -> x5, local copies, waits for them, and re-layouts: 18.1 us -> 7.6 us
  transfers between devices with their start and end apart: 1 -> 0, of which waited for: 1 -> 0; matrix products, arithmetic and copies ran while one was open for 5% -> 0% of each run, Pallas kernels for 0% -> 0%
where the time goes in v5:
time: 652 us; the launch traced here: 645 us
  Pallas kernels  618 us (95%)
  other arithmetic  12.7 us (2%)
  local copies, waits for them, and re-layouts  11.9 us (2%)
    pallas_call x1, Pallas kernels, mid_stage(): pl.pallas_call(functools.partial(mid_kernel, n_dp, n_mp), out_shape=[jax....  172 us
    pallas_call x1, Pallas kernels, gate_stage(): pl.pallas_call(functools.partial(gate_kernel, n_dp, n_mp), out_shape=[jax...  152 us
    pallas_call x1, Pallas kernels, down_stage(): pl.pallas_call(functools.partial(down_kernel, n_dp, n_mp), out_shape=[jax...  113 us
    pallas_call x1, Pallas kernels, last_stage(): pl.pallas_call(functools.partial(last_kernel, n_dp, n_mp), out_shape=[jax...  93.9 us
    pallas_call x1, Pallas kernels, attn_stage(): pl.pallas_call(functools.partial(attn_kernel, n_dp, n_mp), out_shape=[jax...  86.6 us

profile of v5, /device:TPU:0, one launch (start us, length us, event | category | flops | bytes accessed | tf_op | source)
XLA Modules:
  0.0 644.8 jit_solution(2530821513307439687)
XLA Ops:
  1.3 0.7 convert.16
  2.0 0.7 convert.17
  2.7 0.6 fusion.3.gains_in
  3.3 86.6 %attn_stage.1 = (bf16[2048,2048]{1,0:T(8,128)(2,1)}, bf16[1024,1536]{1,0:T(8,128)(2,1)}, bf16[1024,512]{1,0:T(8,128)(2,1)}, bf16[1024,2048]{1,0:T(8,128)(2,1)}, ...) custom-call(s32[1]{0:T(128)S(6)} %copy.26.count_ref, ...), custom_call_target="tpu_custom_call" | custom-call | tf_op jit(solution)/shard_map/attn_stage/pallas_call | solution.py:770
  89.9 152.0 %gate_stage.1 = (bf16[2048,4096]{1,0:T(8,128)(2,1)}, bf16[1024,2048]{1,0:T(8,128)(2,1)}, f32[256,2048]{1,0:T(8,128)}, bf16[1024,4096]{1,0:T(8,128)(2,1)}, bf16[1024,2048]{1,0:T(8,128)(2,1)}) custom-call(bf16[1024,512]{1,0:T(8,128)(2,1)} %get-tuple-element.36.att_ref.att_hbm, bf16[2048,2048]{1,0:T(8,128)(2,1)} %get-tuple-element.37.aw_hbm, ...), custom_call_target="tpu_custom_call" | custom-call | tf_op jit(solution)/shard_map/gate_stage/pallas_call | solution.py:936
  241.8 113.5 %down_stage.1 = (bf16[4,256,512]{2,1,0:T(8,128)(2,1)}, bf16[1024,2048]{1,0:T(8,128)(2,1)}, bf16[1024,4096]{1,0:T(8,128)(2,1)}, bf16[2048,2048]{1,0:T(8,128)(2,1)}) custom-call(bf16[1024,2048]{1,0:T(8,128)(2,1)} %get-tuple-element.40.inner_hbm, bf16[1024,4096]{1,0:T(8,128)(2,1)} %get-tuple-element.41.gu_hbm, bf16[1024,2048]{1,0:T(8,128)(2,1)} %get-tuple-element.42.cot_hbm, ...), custom_call_target="tpu_custom_call" | custom-call | tf_op jit(solution)/shard_map/down_stage/pallas_call | solution.py:1111
  355.3 1.3 slice_bitcast_fusion.3
  356.6 0.2 convert_bitcast_fusion
  356.9 1.8 copy.24
  358.7 172.3 %mid_stage.1 = (bf16[4,256,1024]{2,1,0:T(8,128)(2,1)}, bf16[1024,2048]{1,0:T(8,128)(2,1)}, bf16[1024,2048]{1,0:T(8,128)(2,1)}, f32[256,2048]{1,0:T(8,128)}, f32[...) custom-call(bf16[1024,4096]{1,0:T(8,128)(2,1)} %get-tuple-element.44.ggu_hbm, bf16[2048,4096]{1,0:T(8,128)(2,1)} %get-tuple-element.45.gw_hbm, ...), custom_call_target="tpu_custom_call" | custom-call | tf_op jit(solution)/shard_map/mid_stage/pallas_call | solution.py:1395
  531.0 1.6 slice_bitcast_fusion.7
  532.6 2.6 maximum_convert_fusion
  535.2 93.9 %last_stage.1 = (bf16[4,256,512]{2,1,0:T(8,128)(2,1)}, bf16[1024,2048]{1,0:T(8,128)(2,1)}, f32[8,2048]{1,0:T(8,128)}) custom-call(bf16[1024,1536]{1,0:T(8,128)(2,1)} %get-tuple-element.51.dqkv_hbm, bf16[2048,2048]{1,0:T(8,128)(2,1)} %get-tuple-element.37.aw_hbm, bf16[1024,2048]{1,0:T(8,128)(2,1)} %get-tuple-element.52.nin_hbm, ...), custom_call_target="tpu_custom_call" | custom-call | tf_op jit(solution)/shard_map/last_stage/pallas_call | solution.py:1599
  629.1 0.0 copy-start
  629.1 6.7 %convert_element_type.39 = f32[1024,2048]{1,0:T(8,128)} convert(bf16[1024,2048]{1,0:T(8,128)(2,1)} %get-tuple-element.56) | non-fusion elementwise | flops 2097152 | bytes 12582912 | tf_op jit(solution)/shard_map/convert_element_type | solution.py:1664
  635.9 0.0 copy-done
  635.9 1.2 convert_bitcast_fusion.1
  637.1 1.0 copy.23
  638.1 1.4 fusion.4
  639.5 4.8 copy.27
  (2 shorter events, 0.0 us)
Async XLA Ops:
  629.1 6.8 %copy-start = (bf16[4,256,512]{2,1,0:T(8,128)(2,1)S(1)}, bf16[4,256,512]{2,1,0:T(8,128)(2,1)}, u32[]{:S(2)}) copy-start(bf16[4,256,512]{2,1,0:T(8,128)(2,1)} %get-tuple-element.58) | copy-start | bytes 3145732

commit v6 on v5

--- a/solution.py
+++ b/solution.py
@@ -115,7 +115,8 @@
 
 
 class LineSum:
-    def __init__(self, at, pout, own, din, uin, sems):
+    def __init__(self, at, pout, own, din, uin, sems, paced=False):
+        self.paced = paced
         self.at, self.pout, self.own, self.din, self.uin = at, pout, own, din, uin
         self.po_s, self.po_r, self.d_s, self.d_r, self.u_s, self.u_r = sems
         self.slots, self.pieces = pout.shape[0], own.shape[1]
@@ -163,7 +164,7 @@
             value = tile(i)
             self.core_copy(k, i).wait_recv()
             self.own[j, i] = (value + self.own[j, i].astype(F32)).astype(BF)
-            if k < at.n - 1:
+            if k < (1 if self.paced else at.n - 1):
 
                 @pl.when(at.p == at.n - 1)
                 def _():
@@ -198,6 +199,18 @@
                 self.up_copy(su, i).wait_recv()
                 self.add(self.own.at[n - 1 - su, i], self.uin.at[su, i])
                 self.up_copy(su, i).start()
+
+            if self.paced:
+
+                @pl.when(p == n - 1)
+                def _():
+                    self.down_copy(t, i).wait_send()
+                    self.down_copy(t + 1, i).start()
+
+                @pl.when(p == 0)
+                def _():
+                    self.up_copy(t, i).wait_send()
+                    self.up_copy(t + 1, i).start()
 
     def final(self, out):
         at = self.at
@@ -243,13 +256,14 @@
             for i in range(self.pieces):
                 self.core_copy(k, i).wait_send()
         for s in range(n - 1):
-
-            @pl.when(s < p)
+            done = self.paced and s < n - 2
+
+            @pl.when((s < p) & (at.has_above if done else at.has_below))
             def _():
                 for i in range(self.pieces):
                     self.down_copy(s, i).wait_send()
 
-            @pl.when(s < n - 1 - p)
+            @pl.when((s < n - 1 - p) & (at.has_below if done else at.has_above))
             def _():
                 for i in range(self.pieces):
                     self.up_copy(s, i).wait_send()
@@ -453,19 +467,19 @@
     def down_copy(self, h, i, own=False):
         b = 2 * (self.at.p + h) + self.at.c
         dst = self.spot(b, i)
-        src = self.shard(i) if own else dst
+        src = self.shard(i) if own and self.shard else dst
         return remote(src, dst, self.d_s.at[h, i], self.d_r.at[h, i], self.at.below)
 
     def up_copy(self, h, i, own=False):
         b = 2 * (self.at.p - h) + self.at.c
         dst = self.spot(b, i)
-        src = self.shard(i) if own else dst
+        src = self.shard(i) if own and self.shard else dst
         return remote(src, dst, self.u_s.at[h, i], self.u_r.at[h, i], self.at.above)
 
     def core_copy(self, z, i, own=False, incoming=False):
         b = 2 * z + (1 - self.at.c if incoming else self.at.c)
         dst = self.spot(b, i)
-        src = self.shard(i) if own else dst
+        src = self.shard(i) if own and self.shard else dst
         return remote(src, dst, self.c_s.at[z, i], self.c_r.at[z, i], self.at.core)
 
     def keep(self, i):
@@ -486,7 +500,8 @@
 
         for i in range(self.pieces):
             self.core_copy(at.p, i, True).start()
-            self.keep(i).start()
+            if self.shard:
+                self.keep(i).start()
 
     def slot(self, h, i):
         at = self.at
@@ -811,6 +826,7 @@
     gu_ref,
     inner_ref,
     wo,
+    sh,
     xs,
     nm,
     wbuf,
@@ -832,13 +848,16 @@
     chunk, wide = sh_hbm.shape
     pieces = sems[6].shape[0]
     width = wide // pieces
-    line = LineGather(at, pieces, cols_of(sh_hbm, width), rows_spot(gw_ref, chunk, width), sems)
-
+    line = LineGather(at, pieces, cols_of(sh, width), rows_spot(gw_ref, chunk, width), sems)
+
+    load_sh = pltpu.make_async_copy(sh_hbm, sh, load_s.at[2])
+    load_sh.start()
     load = pltpu.make_async_copy(aw_hbm.at[:, pl.ds(3 * hh, hh)], wo, load_s.at[0])
     load.start()
     load_x = pltpu.make_async_copy(x_hbm.at[part_rows(at, part), :], xs, load_s.at[1])
     load_x.start()
     enter(at)
+    load_sh.wait()
     line.start()
     load.wait()
 
@@ -946,12 +965,13 @@
         out_specs=[hbm, hbm, vm, hbm, hbm],
         scratch_shapes=[
             pltpu.VMEM((d, hh), BF),
+            pltpu.VMEM((chunk, wide), BF),
             pltpu.VMEM((part, d), BF),
             pltpu.VMEM((seq, d), BF),
             pltpu.VMEM((2, d, width), BF),
             pltpu.VMEM((2, seq, width), BF),
             pltpu.VMEM((2, seq, width // 2), BF),
-            dma((2,)),
+            dma((3,)),
             dma((2,)),
             dma((2,)),
             dma((2,)),
@@ -976,7 +996,6 @@
     rs_ref,
     ft_ref,
     ggu_ref,
-    dn_ref,
     inner,
     gu,
     cot,
@@ -996,15 +1015,20 @@
     chunk, ff = sh_hbm.shape
     pieces = sems[6].shape[0]
     width = ff // pieces
-    gather = LineGather(at, pieces, cols_of(sh_hbm, width), rows_spot(dn_ref, chunk, width), sems)
+    gather = LineGather(at, pieces, None, rows_spot(dn, chunk, width), sems)
     pair = 2 * chunk
     loads = [
         pltpu.make_async_copy(src, dst, load_s.at[i])
         for i, (src, dst) in enumerate([(cot_hbm, cot), (inner_hbm, inner), (gu_hbm, gu)])
     ]
+    own = pltpu.make_async_copy(
+        sh_hbm, dn.at[pl.ds(pl.multiple_of(at.dp * chunk, chunk), chunk), :], dn_s.at[0]
+    )
+    own.start()
     for cp in loads:
         cp.start()
     enter(at)
+    own.wait()
     gather.start()
     loads[0].wait()
     loads[1].wait()
@@ -1029,69 +1053,99 @@
         cols = pl.ds(pl.multiple_of(z * pair, pair), pair)
         return pltpu.make_async_copy(ftb.at[slot], ft_ref.at[:, cols], ft_s.at[slot])
 
-    def work(z, fresh):
-        rs = pl.ds(pl.multiple_of(z * pair, pair), pair)
-
+    def rows_of(z):
+        return pl.ds(pl.multiple_of(z * pair, pair), pair)
+
+    def grads(z, fresh):
         @pl.loop(0, pieces)
         def _(i):
             gather.ready(z, i)
 
-        load = pltpu.make_async_copy(dn_ref.at[rs, :], dn, dn_s.at[0])
-        load.start()
-        load.wait()
-
         @pl.loop(0, ff // 512)
         def _(i):
             cols = pl.ds(pl.multiple_of(i * 512, 512), 512)
-            v = dot(cot[:, rs], dn[:, cols])
+            v = dot(cot[:, rows_of(z)], dn[rows_of(z), cols])
             acc[:, cols] = v if fresh else acc[:, cols] + v
 
+    def branch(z, fresh):
         if not fresh:
             ft_copy(z, 0).wait()
-        ftb[0] = dot(inner[...], dn[...], NT).astype(BF)
+        ftb[0] = dot(inner[...], dn[rows_of(z), :], NT).astype(BF)
         ft_copy(z, 0).start()
 
-    for i in range(pieces):
-        gather.keep(i).wait()
-    work(p, True)
+    grads(p, True)
+    branch(p, True)
     loads[2].wait()
-
-    @pl.loop(1, n)
-    def _(h):
-        gather.stage(h)
-        line.slot(h - 1)
-
-        @pl.when(p + h < n)
-        def _():
-            work(p + h, False)
-
-        @pl.when(p - h >= 0)
-        def _():
-            work(p - h, False)
-
     half = width
 
-    def gg_copy(i):
-        cols = pl.ds(pl.multiple_of(i * 2 * half, 2 * half), 2 * half)
-        return pltpu.make_async_copy(gu.at[:, cols], ggu_ref.at[:, cols], gg_s.at[i])
+    def cols_at(i):
+        g = pl.ds(pl.multiple_of(i * 2 * half, half), half)
+        u = pl.ds(pl.multiple_of(i * 2 * half + half, half), half)
+        return g, u, pl.ds(pl.multiple_of(i * half, half), half)
 
     @pl.loop(0, pieces)
     def _(i):
-        gcols = pl.ds(pl.multiple_of(i * 2 * half, half), half)
-        ucols = pl.ds(pl.multiple_of(i * 2 * half + half, half), half)
-        acols = pl.ds(pl.multiple_of(i * half, half), half)
+        gcols, ucols, _ = cols_at(i)
 
         @pl.loop(0, gu.shape[0] // 64)
         def _(b):
             rs = pl.ds(pl.multiple_of(b * 64, 64), 64)
             g = gu[rs, gcols].astype(F32)
             u = gu[rs, ucols].astype(F32)
+            sg = 1.0 / (1.0 + jnp.exp(-g))
+            gu[rs, gcols] = (u * sg * (1.0 + g * (1.0 - sg))).astype(BF)
+            gu[rs, ucols] = (g * sg).astype(BF)
+
+    @pl.loop(1, n - 1)
+    def _(h):
+        gather.stage(h)
+
+        @pl.when(p + h < n)
+        def _():
+            grads(p + h, False)
+            branch(p + h, False)
+
+        @pl.when(p - h >= 0)
+        def _():
+            grads(p - h, False)
+            branch(p - h, False)
+
+        line.slot(h - 1)
+
+    gather.stage(n - 1)
+
+    @pl.when(jnp.logical_not(at.has_below))
+    def _():
+        grads(n - 1, False)
+
+    @pl.when(jnp.logical_not(at.has_above))
+    def _():
+        grads(0, False)
+
+    def gg_copy(i):
+        cols = pl.ds(pl.multiple_of(i * 2 * half, 2 * half), 2 * half)
+        return pltpu.make_async_copy(gu.at[:, cols], ggu_ref.at[:, cols], gg_s.at[i])
+
+    @pl.loop(0, pieces)
+    def _(i):
+        gcols, ucols, acols = cols_at(i)
+
+        @pl.loop(0, gu.shape[0] // 64)
+        def _(b):
+            rs = pl.ds(pl.multiple_of(b * 64, 64), 64)
             gi = acc[rs, acols]
-            sg = 1.0 / (1.0 + jnp.exp(-g))
-            gu[rs, gcols] = (gi * u * sg * (1.0 + g * (1.0 - sg))).astype(BF)
-            gu[rs, ucols] = (gi * g * sg).astype(BF)
+            gu[rs, gcols] = (gi * gu[rs, gcols].astype(F32)).astype(BF)
+            gu[rs, ucols] = (gi * gu[rs, ucols].astype(F32)).astype(BF)
 
         gg_copy(i).start()
+
+    @pl.when(jnp.logical_not(at.has_below))
+    def _():
+        branch(n - 1, False)
+
+    @pl.when(jnp.logical_not(at.has_above))
+    def _():
+        branch(0, False)
 
     line.final(rs_ref)
     for i in range(pieces):
@@ -1114,15 +1168,14 @@
             jax.ShapeDtypeStruct((PIECES, chunk, ff // PIECES), BF),
             jax.ShapeDtypeStruct((seq, d), BF),
             jax.ShapeDtypeStruct((seq, 2 * ff), BF),
-            jax.ShapeDtypeStruct((d, ff), BF),
         ],
         in_specs=[hbm] * 4,
-        out_specs=[vm, hbm, hbm, hbm],
+        out_specs=[vm, hbm, hbm],
         scratch_shapes=[
             pltpu.VMEM((seq, ff), BF),
             pltpu.VMEM((seq, 2 * ff), BF),
             pltpu.VMEM((seq, d), BF),
-            pltpu.VMEM((2 * chunk, ff), BF),
+            pltpu.VMEM((d, ff), BF),
             pltpu.VMEM((seq, ff), F32),
             pltpu.VMEM((1, seq, 2 * chunk), BF),
             dma((3,)),
@@ -1136,7 +1189,7 @@
             collective_id=3, has_side_effects=True, vmem_limit_bytes=VMEM_LIMIT
         ),
         name="down_stage",
-    )(inner, gu, cot, shard)[:3]
+    )(inner, gu, cot, shard)
 
 
 def mid_kernel(
@@ -1250,10 +1303,10 @@
     terms(0)
     run(2)
     run(3)
-    terms(1)
     for cp in lay.loads:
         cp.wait()
     lay.turn()
+    terms(1)
     for e in range(4, 2 * n):
         run(e)
     lay.arrive()
@@ -1305,14 +1358,13 @@
         gg_ref[...] += jnp.sum(g * unit, axis=0, keepdims=True)
 
     gather_low.start()
+    for s in range(1, n - 2):
+        line.slot(s)
     gather_low.forward()
     gather_lay.start()
     gather_low.finish()
     load_low = pltpu.make_async_copy(low_ref, space.at[:, pl.ds(0, 2 * half_cols)], load_s.at[3])
     load_low.start()
-    for s in range(1, n - 2):
-        line.slot(s)
-    gather_lay.forward()
     load_low.wait()
     load_qkv.wait()
     for cp in wo_parts:
@@ -1364,6 +1416,7 @@
             wt[i // 2, :, at_cols((i % 2) * (wide // 2) + hh)] = dka[rows, :].astype(BF)
             wt[i // 2, :, at_cols((i % 2) * (wide // 2) + 2 * hh)] = dva[rows, :].astype(BF)
 
+    gather_lay.forward()
     stores = [
         pltpu.make_async_copy(
             wt.at[i // 2, :, pl.ds((i % 2) * (wide // 2), 3 * hh)],
@@ -1467,6 +1520,7 @@
     g1,
     g2,
     g3,
+    gsum,
     fold_out,
     fold_in,
     fold_s,
@@ -1495,10 +1549,14 @@
     bits = [b for b in (2, 4, 8, 16) if b < n_dp]
     enter(at, [at.fold(b) for b in bits[1:]])
     quad = QuadSum(at, t, r, (q1, q2))
-    line = LineSum(at, pout, own, din, uin, (po_s, po_r, d_s, d_r, u_s, u_r))
+    line = LineSum(at, pout, own, din, uin, (po_s, po_r, d_s, d_r, u_s, u_r), True)
     gather = QuadGather(at, gown, grad_ref, (g1, g2, g3))
     copies[0].wait()
     copies[1].wait()
+
+    d = aw.shape[0]
+    fold = fold_out.shape[2]
+    per_row = d // fold
 
     def terms(q):
         rs = pl.ds(pl.multiple_of(q * part, part), part)
@@ -1510,12 +1568,17 @@
                 d0 = pl.multiple_of(half * half_cols + i * width, width)
                 v = dot(rhs[rs, 0 : 3 * hh], aw[pl.ds(d0, width), :], NT)
                 t[half, q, :, pl.ds(pl.multiple_of(i * width, width), width)] = v.astype(BF)
-
-    for mask in quad.masks()[:-1]:
-        terms(at.quarter(mask))
-        quad.offer(mask)
-    for cp in copies[2:]:
+                u = v * nin[rs, pl.ds(d0, width)].astype(F32)
+                gsum[0:1, pl.ds(d0, width)] += jnp.sum(u, axis=0, keepdims=True)
+
+    gsum[...] = jnp.zeros_like(gsum)
+    copies[2].wait()
+    masks = quad.masks()
+    terms(at.quarter(masks[0]))
+    quad.offer(masks[0])
+    for cp in copies[3:5]:
         cp.wait()
+    load_x = copies[5]
 
     def run(k, core):
         block = 2 * order_of(k, at) + (at.c if core else 1 - at.c)
@@ -1532,18 +1595,41 @@
             line.other(k, tile)
 
     n = at.n
-    for k in range(n + 1):
-        if k < n:
-            run(k, 0)
-        if k > 0:
-            run(k - 1, 1)
-    terms(at.m)
+    devs = [at.core] + [at.fold(b) for b in bits] + [at.peer(b) for b in at.bits]
+
+    def fold_copy(b):
+        return remote(fold_out.at[b], fold_in.at[b], fold_s.at[b], fold_r.at[b], devs[b])
+
+    def fold_next(b):
+        fold_copy(b).wait_recv()
+        fold_out[b + 1] = fold_out[b] + fold_in[b]
+        if b + 1 < len(devs):
+            fold_copy(b + 1).start()
+
+    run(0, 0)
+    run(0, 1)
+    for mask in masks[1:]:
+        terms(at.quarter(mask))
+        quad.offer(mask)
+    gsum[0:1, :] = gsum[0:1, :] / gain_ref[0:1, :]
+    gsum[1:2, :] = gmid_ref[...]
+    for i in range(2):
+        for j in range(per_row):
+            fold_out[0, i * per_row + j] = gsum[i, j * fold : (j + 1) * fold]
+    fold_copy(0).start()
+    run(1, 0)
+    run(1, 1)
+    fold_next(0)
+    for k in range(2, n):
+        run(k, 0)
+        run(k, 1)
     quad.turn()
+    for b in range(1, len(bits)):
+        fold_next(b)
     line.slot(0)
     quad.arrive()
-
-    fold_out[...] = jnp.zeros_like(fold_out)
-
+    load_x.wait()
+    fold_next(len(bits))
     @pl.loop(0, part // 32)
     def _(b):
         rs = pl.ds(pl.multiple_of(b * 32, 32), 32)
@@ -1556,30 +1642,18 @@
         res = (gh_ref[rs, :] + field).astype(BF)
         gown[0, rs, :] = res[:, :half_cols]
         gown[1, rs, :] = res[:, half_cols:]
-        fold_out[0, 0:1, :] += jnp.sum(g * unit, axis=0, keepdims=True)
-
+
+    for b in range(len(bits) + 1, len(devs) - 1):
+        fold_next(b)
     gather.start()
-    fold_out[0, 1:2, :] = gmid_ref[...]
-    devs = [at.core] + [at.peer(b) for b in at.bits] + [at.fold(b) for b in bits]
-
-    def fold_copy(b):
-        return remote(fold_out.at[b], fold_in.at[b], fold_s.at[b], fold_r.at[b], devs[b])
-
-    def fold_next(b):
-        fold_copy(b).wait_recv()
-        nxt = fold_out[b] + fold_in[b]
-        if b + 1 < len(devs):
-            fold_out[b + 1] = nxt
-            fold_copy(b + 1).start()
-        else:
-            gains_ref[...] = nxt
-
-    fold_copy(0).start()
     for s in range(1, n - 2):
         line.slot(s)
+    fold_next(len(devs) - 1)
     gather.forward()
-    for b in range(len(devs)):
-        fold_next(b)
+    for i in range(2):
+        for j in range(per_row):
+            gsum[i, j * fold : (j + 1) * fold] = fold_out[len(devs), i * per_row + j]
+    gains_ref[...] = gsum[:, pl.ds(pl.multiple_of(at.dp * chunk, chunk), chunk)]
     line.final(rs_ref)
     gather.finish()
     line.drain()
@@ -1601,7 +1675,7 @@
         out_shape=[
             jax.ShapeDtypeStruct((4, chunk, hh), BF),
             jax.ShapeDtypeStruct((seq, d), BF),
-            jax.ShapeDtypeStruct((8, d), F32),
+            jax.ShapeDtypeStruct((8, chunk), F32),
         ],
         in_specs=[anyspace] * 6 + [vm] * 3,
         out_specs=[vm, anyspace, vm],
@@ -1618,8 +1692,9 @@
         + quad_sum_scratch(n_mp, part, d // 2)
         + quad_gather_scratch(n_mp, part, d // 2)
         + [
-            pltpu.VMEM((folds, 8, d), F32),
-            pltpu.VMEM((folds, 8, d), F32),
+            pltpu.VMEM((8, d), F32),
+            pltpu.VMEM((folds + 1, 8, d // 4), F32),
+            pltpu.VMEM((folds, 8, d // 4), F32),
             dma((folds,)),
             dma((folds,)),
         ],
@@ -1628,6 +1703,73 @@
         ),
         name="last_stage",
     )(dqkv, aw, nin, low, att, x, gh, gain, gmid)
+
+
+def finish_kernel(
+    low_ref,
+    lay_ref,
+    gu_ref,
+    down_ref,
+    attn_ref,
+    gains_ref,
+    lay_out,
+    in_out,
+    gate_out,
+    up_out,
+    down_out,
+    q_out,
+    k_out,
+    v_out,
+    o_out,
+    g1_out,
+    g2_out,
+):
+    lay_out[...] = lay_ref[...]
+    in_out[...] = low_ref[...].astype(F32)
+    half = gate_out.shape[1]
+    gate_out[...] = gu_ref[0, :, :half].astype(F32)
+    up_out[...] = gu_ref[0, :, half:].astype(F32)
+    down_out[...] = down_ref[0].T.astype(F32)
+
+    @pl.when(pl.program_id(0) == 0)
+    def _():
+        for i, ref in enumerate((q_out, k_out, v_out)):
+            ref[...] = attn_ref[i].astype(F32)
+        o_out[...] = attn_ref[3].T.astype(F32)
+        g1_out[...] = gains_ref[0]
+        g2_out[...] = gains_ref[1]
+
+
+def finish_stage(low, lay, gu, down, attn, gains):
+    seq, d = low.shape
+    steps, chunk, wide = gu.shape
+    width, hh = down.shape[2], attn.shape[2]
+    row = pl.BlockSpec((seq // steps, d), lambda i: (i, 0))
+    fixed = lambda *shape: pl.BlockSpec(shape, lambda i: (0,) * len(shape))
+    piece = lambda w: pl.BlockSpec((1, chunk, w), lambda i: (i, 0, 0))
+    cols = pl.BlockSpec((chunk, wide // 2), lambda i: (0, i))
+    f32 = lambda *shape: jax.ShapeDtypeStruct(shape, F32)
+    return pl.pallas_call(
+        finish_kernel,
+        grid=(steps,),
+        in_specs=[row, row, piece(wide), piece(width), fixed(4, chunk, hh), fixed(*gains.shape)],
+        out_specs=[row, row, cols, cols, pl.BlockSpec((width, chunk), lambda i: (i, 0))]
+        + [fixed(chunk, hh)] * 3
+        + [fixed(hh, chunk)]
+        + [fixed(chunk)] * 2,
+        out_shape=[
+            jax.ShapeDtypeStruct((seq, d), BF),
+            f32(seq, d),
+            f32(chunk, steps * wide // 2),
+            f32(chunk, steps * wide // 2),
+            f32(steps * width, chunk),
+        ]
+        + [f32(chunk, hh)] * 3
+        + [f32(hh, chunk)]
+        + [f32(chunk)] * 2,
+        compiler_params=pltpu.CompilerParams(vmem_limit_bytes=VMEM_LIMIT),
+        name="finish_stage",
+    )(low, lay, gu, down, attn, gains)
 
 
 def on_device(
@@ -1644,7 +1786,6 @@
     w_up,
     w_down,
 ):
-    ff = w_gate.shape[1]
     n_dp, n_mp = lax.axis_size("dp"), lax.axis_size("mp")
     gains = jnp.pad(jnp.stack([gain_attn, gain_ffn]), ((0, 6), (0, 0)))
     gains = gains.astype(BF).astype(F32)
@@ -1661,27 +1802,10 @@
     rs_attn, grad_low_in, g_gains = last_stage(
         n_dp, n_mp, dqkv, attn_w, normed_in, grad_low, attended, inputs, grad_hidden, gains, g_gain_mid
     )
-    input_grad = grad_low_in.astype(F32)
-    width = g_gains.shape[1] // lax.axis_size("dp")
-    g_gains = lax.dynamic_slice_in_dim(g_gains, lax.axis_index("dp") * width, width, 1)
-    half = ff // PIECES
-    unpack = lambda i: jnp.concatenate(
-        [rs_gu[k, :, i * half : (i + 1) * half] for k in range(PIECES)], axis=1
-    ).astype(F32)
-    down_t = jnp.concatenate([rs_down[k] for k in range(PIECES)], axis=1)
-    return (
-        layer_out,
-        input_grad,
-        g_gains[0],
-        rs_attn[0].astype(F32),
-        rs_attn[1].astype(F32),
-        rs_attn[2].astype(F32),
-        rs_attn[3].astype(F32).T,
-        g_gains[1],
-        unpack(0),
-        unpack(1),
-        down_t.astype(F32).T,
+    lay, grad_x, g_gate, g_up, g_down, g_q, g_k, g_v, g_o, g_attn, g_ffn = finish_stage(
+        grad_low_in, layer_out, rs_gu, rs_down, rs_attn, g_gains
     )
+    return (lay, grad_x, g_attn, g_q, g_k, g_v, g_o, g_ffn, g_gate, g_up, g_down)
 
 
 def solution(mesh):

time: 652 us -> 605 us (0.928)
  Pallas kernels: 618 us -> 593 us
  local copies, waits for them, and re-layouts: 11.9 us -> 0.01 us
  other arithmetic: 12.7 us -> 1.97 us
    pallas_call x1, Pallas kernels: 172 us -> 150 us  [mid_stage(): pl.pallas_call(functools.partial(mid_kernel, n_dp, n_mp), out_shape=[jax....]
    pallas_call x0 -> x1, Pallas kernels: none -> 13.1 us  [finish_stage(): pl.pallas_call(finish_kernel, grid=(steps,), in_specs=[row, row, piece(wi...]
    pallas_call x1, Pallas kernels: 113 us -> 103 us  [down_stage(): pl.pallas_call(functools.partial(down_kernel, n_dp, n_mp), out_shape=[jax...]
    convert_element_type x2 -> x0, other arithmetic: 9.3 us -> none  [the longest x1 6.74 us: on_device(): input_grad = grad_low_in.astype(F32)]
    unnamed x5 -> x0, local copies, waits for them, and re-layouts: 7.6 us -> none
where the time goes in v6:
time: 605 us; the launch traced here: 596 us
  Pallas kernels  593 us (98%)
    pallas_call x1, Pallas kernels, gate_stage(): pl.pallas_call(functools.partial(gate_kernel, n_dp, n_mp), out_shape=[jax...  152 us
    pallas_call x1, Pallas kernels, mid_stage(): pl.pallas_call(functools.partial(mid_kernel, n_dp, n_mp), out_shape=[jax....  150 us
    pallas_call x1, Pallas kernels, down_stage(): pl.pallas_call(functools.partial(down_kernel, n_dp, n_mp), out_shape=[jax...  103 us
    pallas_call x1, Pallas kernels, last_stage(): pl.pallas_call(functools.partial(last_kernel, n_dp, n_mp), out_shape=[jax...  87.7 us
    pallas_call x1, Pallas kernels, attn_stage(): pl.pallas_call(functools.partial(attn_kernel, n_dp, n_mp), out_shape=[jax...  86.7 us
    pallas_call x1, Pallas kernels, finish_stage(): pl.pallas_call(finish_kernel, grid=(steps,), in_specs=[row, row, piece(wi...  13.1 us

profile of v6, /device:TPU:0, one launch (start us, length us, event | category | flops | bytes accessed | tf_op | source)
XLA Modules:
  0.0 596.4 jit_solution(16741486398111541533)
XLA Ops:
  1.3 0.7 convert.10
  2.0 0.7 convert.11
  2.7 0.6 fusion.3.gains_in
  3.3 86.7 %attn_stage.1 = (bf16[2048,2048]{1,0:T(8,128)(2,1)}, bf16[1024,1536]{1,0:T(8,128)(2,1)}, bf16[1024,512]{1,0:T(8,128)(2,1)}, bf16[1024,2048]{1,0:T(8,128)(2,1)}, ...) custom-call(s32[1]{0:T(128)S(6)} %copy.23.count_ref, ...), custom_call_target="tpu_custom_call" | custom-call | tf_op jit(solution)/shard_map/attn_stage/pallas_call | solution.py:785
  89.9 151.8 %gate_stage.1 = (bf16[2048,4096]{1,0:T(8,128)(2,1)}, bf16[1024,2048]{1,0:T(8,128)(2,1)}, f32[256,2048]{1,0:T(8,128)}, bf16[1024,4096]{1,0:T(8,128)(2,1)}, bf16[1024,2048]{1,0:T(8,128)(2,1)}) custom-call(bf16[1024,512]{1,0:T(8,128)(2,1)} %get-tuple-element.47.att_ref.att_hbm, bf16[2048,2048]{1,0:T(8,128)(2,1)} %get-tuple-element.48.aw_hbm, ...), custom_call_target="tpu_custom_call" | custom-call | tf_op jit(solution)/shard_map/gate_stage/pallas_call | solution.py:955
  241.8 103.4 %down_stage.1 = (bf16[4,256,512]{2,1,0:T(8,128)(2,1)}, bf16[1024,2048]{1,0:T(8,128)(2,1)}, bf16[1024,4096]{1,0:T(8,128)(2,1)}) custom-call(bf16[1024,2048]{1,0:T(8,128)(2,1)} %get-tuple-element.51.inner_hbm, bf16[1024,4096]{1,0:T(8,128)(2,1)} %get-tuple-element.52.gu_hbm, bf16[1024,2048]{1,0:T(8,128)(2,1)} %get-tuple-element.53.cot_hbm, ...), custom_call_target="tpu_custom_call" | custom-call | tf_op jit(solution)/shard_map/down_stage/pallas_call | solution.py:1165
  345.1 150.3 %mid_stage.1 = (bf16[4,256,1024]{2,1,0:T(8,128)(2,1)}, bf16[1024,2048]{1,0:T(8,128)(2,1)}, bf16[1024,2048]{1,0:T(8,128)(2,1)}, f32[256,2048]{1,0:T(8,128)}, f32[...) custom-call(bf16[1024,4096]{1,0:T(8,128)(2,1)} %get-tuple-element.55.ggu_hbm, bf16[2048,4096]{1,0:T(8,128)(2,1)} %get-tuple-element.56.gw_hbm, ...), custom_call_target="tpu_custom_call" | custom-call | tf_op jit(solution)/shard_map/mid_stage/pallas_call | solution.py:1448
  495.4 87.7 %last_stage.1 = (bf16[4,256,512]{2,1,0:T(8,128)(2,1)}, bf16[1024,2048]{1,0:T(8,128)(2,1)}, f32[8,256]{1,0:T(8,128)}) custom-call(bf16[1024,1536]{1,0:T(8,128)(2,1)} %get-tuple-element.61.dqkv_hbm, bf16[2048,2048]{1,0:T(8,128)(2,1)} %get-tuple-element.48.aw_hbm, bf16[1024,2048]{1,0:T(8,128)(2,1)} %get-tuple-element.62.nin_hbm, ...), custom_call_target="tpu_custom_call" | custom-call | tf_op jit(solution)/shard_map/last_stage/pallas_call | solution.py:1673
  583.1 13.1 %finish_stage.1 = (bf16[1024,2048]{1,0:T(8,128)(2,1)}, f32[1024,2048]{1,0:T(8,128)}, f32[256,2048]{1,0:T(8,128)}, f32[256,2048]{1,0:T(8,128)}, f32[2048,256]{1,0...) custom-call(bf16[1024,2048]{1,0:T(8,128)(2,1)} %get-tuple-element.66, ...), custom_call_target="tpu_custom_call" | custom-call | tf_op jit(solution)/shard_map/finish_stage/pallas_call | solution.py:1752
  (2 shorter events, 0.0 us)

commit v7 on v6

--- a/solution.py
+++ b/solution.py
@@ -212,7 +212,7 @@
                     self.up_copy(t, i).wait_send()
                     self.up_copy(t + 1, i).start()
 
-    def final(self, out):
+    def final(self, out, sink, sems):
         at = self.at
         n, p = at.n, at.p
 
@@ -248,6 +248,12 @@
             @pl.when(jnp.logical_not(at.has_above))
             def _():
                 close([up])
+
+            pltpu.make_async_copy(out.at[i], sink.at[i], sems.at[i]).start()
+
+        return [
+            pltpu.make_async_copy(out.at[i], sink.at[i], sems.at[i]) for i in range(self.pieces)
+        ]
 
     def drain(self):
         at = self.at
@@ -430,12 +436,12 @@
     def keep(self, half):
         return pltpu.make_async_copy(self.own.at[half], self.spot(0, half), self.here.at[half])
 
-    def start(self):
-        for k in range(self.levels):
+    def start(self, levels=None):
+        for k in range(self.levels) if levels is None else levels:
             for half in range(2):
                 self.copy(half, k, 0).start()
-        for half in range(2):
-            self.keep(half).start()
+                if k == 0:
+                    self.keep(half).start()
 
     def forward(self):
         for k in range(1, self.levels):
@@ -678,8 +684,31 @@
 
     outs = [pltpu.make_async_copy(gush, gush_ref, out_s.at[0])]
     outs[0].start()
-    for h in range(2, n):
-        small.slot(h, 0)
+    loads[7].wait()
+
+    @pl.loop(0, ff // 256)
+    def _(i):
+        rs = pl.ds(pl.multiple_of(i * 256, 256), 256)
+        dnsh[:, rs] = wd[rs, :].T.astype(BF)
+
+    outs.append(pltpu.make_async_copy(dnsh, dnsh_ref, out_s.at[2]))
+    outs[-1].start()
+    loads[8].wait()
+    count = count_ref[0]
+
+    @pl.loop(0, seq // 32)
+    def _(b):
+        rs = pl.ds(pl.multiple_of(b * 32, 32), 32)
+        row = b * 32 + lax.broadcasted_iota(jnp.int32, (32, d), 0)
+        cot[rs, :] = jnp.where(row < count, cot[rs, :].astype(F32), 0.0).astype(BF)
+
+    outs.append(pltpu.make_async_copy(cot, cotm_ref, out_s.at[3]))
+    outs[-1].start()
+    for h in range(1, n - 1):
+        small.slot(h + 1, 0)
+        three.stage(h)
+        if h == n - 2:
+            last.start()
     small.keep(0).wait()
     for z in range(n):
         small.ready(z, 0)
@@ -693,31 +722,7 @@
         x[rs, :] = (v * scale * gains_ref[0:1, :]).astype(BF)
 
     outs.append(pltpu.make_async_copy(x, nin_ref, out_s.at[1]))
-    outs[1].start()
-    three.stage(1)
-    loads[7].wait()
-
-    @pl.loop(0, ff // 256)
-    def _(i):
-        rs = pl.ds(pl.multiple_of(i * 256, 256), 256)
-        dnsh[:, rs] = wd[rs, :].T.astype(BF)
-
-    outs.append(pltpu.make_async_copy(dnsh, dnsh_ref, out_s.at[2]))
-    outs[2].start()
-    loads[8].wait()
-    count = count_ref[0]
-
-    @pl.loop(0, seq // 32)
-    def _(b):
-        rs = pl.ds(pl.multiple_of(b * 32, 32), 32)
-        row = b * 32 + lax.broadcasted_iota(jnp.int32, (32, d), 0)
-        cot[rs, :] = jnp.where(row < count, cot[rs, :].astype(F32), 0.0).astype(BF)
-
-    outs.append(pltpu.make_async_copy(cot, cotm_ref, out_s.at[3]))
-    outs[3].start()
-    for h in range(2, n - 1):
-        three.stage(h)
-    last.start()
+    outs[-1].start()
 
     def w_copy(i):
         cols = pl.ds(pl.multiple_of(i * hh, hh), hh)
@@ -739,7 +744,7 @@
             qkv[rs, i * hh : (i + 1) * hh] = dot(x[rs, :], wbuf[i]).astype(BF)
 
     outs.append(pltpu.make_async_copy(qkv, qkv_ref, out_s.at[4]))
-    outs[4].start()
+    outs[-1].start()
     for h in range(2, n - 1):
         last.slot(h, 0)
     heads = hh // HD
@@ -822,12 +827,14 @@
     gain_ref,
     gw_ref,
     nm_ref,
-    hid_ref,
+    hid_hbm,
     gu_ref,
     inner_ref,
     wo,
     sh,
     xs,
+    hid,
+    acc,
     nm,
     wbuf,
     gbuf,
@@ -880,13 +887,15 @@
         h = xs[rs, :].astype(F32) + jnp.concatenate(
             [quad.total(0, rs), quad.total(1, rs)], axis=1
         )
-        hid_ref[rs, :] = h
+        hid[rs, :] = h
         scale = lax.rsqrt(jnp.mean(h * h, axis=1, keepdims=True) + EPS)
         res = (h * scale * gain_ref[1:2, :]).astype(BF)
         gather_nm.own[0, rs, :] = res[:, :half_cols]
         gather_nm.own[1, rs, :] = res[:, half_cols:]
 
     gather_nm.start()
+    store_hid = pltpu.make_async_copy(hid, hid_hbm, load_s.at[1])
+    store_hid.start()
     line.stage(1)
     gather_nm.forward()
     gather_nm.finish()
@@ -896,9 +905,33 @@
         line.stage(h)
     load.wait()
 
-    def w_copy(i, slot):
+    pair = 2 * chunk
+    near = jnp.where(2 * at.p < n, 0, 1)
+    far = jnp.where(2 * at.p < n, n - 1, 0)
+    most = (n - 1) * pair
+    most_rows = pl.ds(pl.multiple_of(near * pair, pair), most)
+    far_rows = pl.ds(pl.multiple_of(far * pair, pair), pair)
+
+    def w_copy(i, slot, rows):
         cols = pl.ds(pl.multiple_of(i * width, width), width)
-        return pltpu.make_async_copy(gw_ref.at[:, cols], wbuf.at[slot], wb_s.at[slot])
+        return pltpu.make_async_copy(
+            gw_ref.at[rows, cols], wbuf.at[slot, rows, :], wb_s.at[slot]
+        )
+
+    def first_part(i, slot):
+        line.keep(i).wait()
+
+        @pl.loop(0, n - 1)
+        def _(z):
+            line.ready(near + z, i)
+
+        w_copy(i, slot, most_rows).start()
+        w_copy(i, slot, most_rows).wait()
+
+        @pl.loop(0, nm.shape[0] // 256)
+        def _(b):
+            rs = pl.ds(pl.multiple_of(b * 256, 256), 256)
+            acc[rs, :] = dot(nm[rs, most_rows], wbuf[slot, most_rows, :])
 
     def g_copy(i, slot):
         cols = pl.ds(pl.multiple_of(i * width, width), width)
@@ -911,23 +944,22 @@
     @pl.loop(0, pieces)
     def _(i):
         slot = lax.rem(i, 2)
+        first_part(i, slot)
         line.slot(n - 1, i)
-        line.keep(i).wait()
-        for z in range(n):
-            line.ready(z, i)
-        w_copy(i, slot).start()
+        line.ready(far, i)
+        w_copy(i, slot, far_rows).start()
 
         @pl.when(i >= 2)
         def _():
             g_copy(i - 2, slot).wait()
             i_copy(i - 2, slot).wait()
 
-        w_copy(i, slot).wait()
+        w_copy(i, slot, far_rows).wait()
 
         @pl.loop(0, nm.shape[0] // 256)
         def _(b):
             rs = pl.ds(pl.multiple_of(b * 256, 256), 256)
-            v = dot(nm[rs, :], wbuf[slot]).astype(BF)
+            v = (acc[rs, :] + dot(nm[rs, far_rows], wbuf[slot, far_rows, :])).astype(BF)
             gbuf[slot, rs, :] = v
             g = v[:, : width // 2].astype(F32)
             u = v[:, width // 2 :].astype(F32)
@@ -939,6 +971,7 @@
     for i in range(max(0, pieces - 2), pieces):
         g_copy(i, i % 2).wait()
         i_copy(i, i % 2).wait()
+    store_hid.wait()
     line.drain()
     quad.drain()
 
@@ -962,11 +995,13 @@
             jax.ShapeDtypeStruct((seq, wide // 2), BF),
         ],
         in_specs=[vm, hbm, hbm, hbm, vm],
-        out_specs=[hbm, hbm, vm, hbm, hbm],
+        out_specs=[hbm] * 5,
         scratch_shapes=[
             pltpu.VMEM((d, hh), BF),
             pltpu.VMEM((chunk, wide), BF),
             pltpu.VMEM((part, d), BF),
+            pltpu.VMEM((part, d), F32),
+            pltpu.VMEM((seq, width), F32),
             pltpu.VMEM((seq, d), BF),
             pltpu.VMEM((2, d, width), BF),
             pltpu.VMEM((2, seq, width), BF),
@@ -1002,7 +1037,11 @@
     dn,
     acc,
     ftb,
+    res,
     load_s,
+    cot_s,
+    in_s,
+    rs_s,
     ft_s,
     dn_s,
     gg_s,
@@ -1017,28 +1056,39 @@
     width = ff // pieces
     gather = LineGather(at, pieces, None, rows_spot(dn, chunk, width), sems)
     pair = 2 * chunk
-    loads = [
-        pltpu.make_async_copy(src, dst, load_s.at[i])
-        for i, (src, dst) in enumerate([(cot_hbm, cot), (inner_hbm, inner), (gu_hbm, gu)])
-    ]
+    def cot_copy(k):
+        cols = pl.ds(pl.multiple_of(order_of(k, at) * pair, pair), pair)
+        return pltpu.make_async_copy(cot_hbm.at[:, cols], cot.at[:, cols], cot_s.at[k])
+
+    def in_copy(i):
+        cols = pl.ds(pl.multiple_of(i * width, width), width)
+        return pltpu.make_async_copy(inner_hbm.at[:, cols], inner.at[:, cols], in_s.at[i])
+
+    load_gu = pltpu.make_async_copy(gu_hbm, gu, load_s.at[0])
     own = pltpu.make_async_copy(
         sh_hbm, dn.at[pl.ds(pl.multiple_of(at.dp * chunk, chunk), chunk), :], dn_s.at[0]
     )
     own.start()
-    for cp in loads:
-        cp.start()
+    cot_copy(0).start()
+    for i in range(pieces):
+        in_copy(i).start()
+    for k in range(1, n):
+        cot_copy(k).start()
+    load_gu.start()
     enter(at)
     own.wait()
     gather.start()
-    loads[0].wait()
-    loads[1].wait()
 
     def run(e):
         k, core = e // 2, e % 2
         block = 2 * order_of(k, at) + (1 - at.c if core == 0 else at.c)
+        if core == 0:
+            cot_copy(k).wait()
         lhs = cot[:, pl.ds(pl.multiple_of(block * chunk, chunk), chunk)].T
 
         def tile(i):
+            if e == 0:
+                in_copy(i).wait()
             return dot(lhs, inner[:, pl.ds(pl.multiple_of(i * width, width), width)])
 
         if core == 0:
@@ -1075,7 +1125,7 @@
 
     grads(p, True)
     branch(p, True)
-    loads[2].wait()
+    load_gu.wait()
     half = width
 
     def cols_at(i):
@@ -1147,10 +1197,12 @@
     def _():
         branch(0, False)
 
-    line.final(rs_ref)
+    stores = line.final(res, rs_ref, rs_s)
     for i in range(pieces):
         gg_copy(i).wait()
     ft_copy(p, 0).wait()
+    for cp in stores:
+        cp.wait()
     line.drain()
     gather.drain()
 
@@ -1161,7 +1213,6 @@
     n = n_dp // 2
     dma = pltpu.SemaphoreType.DMA
     hbm = pl.BlockSpec(memory_space=pl.ANY)
-    vm = pl.BlockSpec(memory_space=pltpu.VMEM)
     return pl.pallas_call(
         functools.partial(down_kernel, n_dp, n_mp),
         out_shape=[
@@ -1170,7 +1221,7 @@
             jax.ShapeDtypeStruct((seq, 2 * ff), BF),
         ],
         in_specs=[hbm] * 4,
-        out_specs=[vm, hbm, hbm],
+        out_specs=[hbm] * 3,
         scratch_shapes=[
             pltpu.VMEM((seq, ff), BF),
             pltpu.VMEM((seq, 2 * ff), BF),
@@ -1178,7 +1229,11 @@
             pltpu.VMEM((d, ff), BF),
             pltpu.VMEM((seq, ff), F32),
             pltpu.VMEM((1, seq, 2 * chunk), BF),
-            dma((3,)),
+            pltpu.VMEM((PIECES, chunk, ff // PIECES), BF),
+            dma((1,)),
+            dma((n,)),
+            dma((PIECES,)),
+            dma((PIECES,)),
             dma((1,)),
             dma((1,)),
             dma((PIECES,)),
@@ -1203,12 +1258,12 @@
     qkv_hbm,
     aw_hbm,
     count_ref,
-    hid_ref,
+    hid_hbm,
     gain_ref,
     rs_ref,
     low_ref,
     lay_ref,
-    gh_ref,
+    gh_hbm,
     gg_ref,
     dq_ref,
     space,
@@ -1217,6 +1272,11 @@
     nm,
     nm_s,
     cot,
+    hid,
+    gh,
+    res,
+    gg_s,
+    rs_s,
     dka,
     dva,
     load_s,
@@ -1238,10 +1298,12 @@
 
     wide = ggu_hbm.shape[1]
     ggu = space.at[:, pl.ds(0, wide)]
-    load = pltpu.make_async_copy(ggu_hbm, ggu, load_s.at[0])
-    load.start()
+
+    def gg_copy(i):
+        cols = pl.ds(pl.multiple_of(i * width, width), width)
+        return pltpu.make_async_copy(ggu_hbm.at[:, cols], ggu.at[:, cols], gg_s.at[i])
+
     load_cot = pltpu.make_async_copy(cot_hbm.at[part_rows(at, part), :], cot, load_s.at[1])
-    load_cot.start()
 
     def nm_copy(e):
         k, core = e // 2, e % 2
@@ -1254,13 +1316,17 @@
         return pltpu.make_async_copy(gw_hbm.at[rows, :], wt.at[slot], wt_s.at[slot])
 
     nm_copy(0).start()
+    for i in range(pieces):
+        gg_copy(i).start()
     wt_copy(0, 0, 0).start()
+    load_cot.start()
+    load_hid = pltpu.make_async_copy(hid_hbm, hid, load_s.at[0])
+    load_hid.start()
     for cp in lay.loads:
         cp.start()
     enter(at)
     for mask in lay.masks():
         lay.offer(mask)
-    load.wait()
 
     def run(e):
         if e + 1 < 2 * n:
@@ -1269,6 +1335,8 @@
         lhs = nm[e % 2].T
 
         def tile(i):
+            if e == 0:
+                gg_copy(i).wait()
             return dot(lhs, ggu[:, pl.ds(pl.multiple_of(i * width, width), width)])
 
         if e % 2 == 0:
@@ -1310,14 +1378,16 @@
     for e in range(4, 2 * n):
         run(e)
     lay.arrive()
+    load_hid.wait()
 
     @pl.loop(0, part // 32)
     def _(b):
         rs = pl.ds(pl.multiple_of(b * 32, 32), 32)
         for half in range(2):
-            h = hid_ref[rs, pl.ds(half * half_cols, half_cols)]
+            h = hid[rs, pl.ds(half * half_cols, half_cols)]
             gather_lay.own[half, rs, :] = (h + lay.total(half, rs)).astype(BF)
 
+    gather_lay.start([0])
     line.slot(0)
     per = half_cols // hh
     blocks_d = 2 * half_cols // part
@@ -1344,24 +1414,26 @@
     @pl.loop(0, part // 32)
     def _(b):
         rs = pl.ds(pl.multiple_of(b * 32, 32), 32)
-        h = hid_ref[rs, :]
+        h = hid[rs, :]
         scale = lax.rsqrt(jnp.mean(h * h, axis=1, keepdims=True) + EPS)
         g = jnp.concatenate([mid.total(0, rs), mid.total(1, rs)], axis=1)
         unit = h * scale
         weighted = g * gain_ref[1:2, :]
         field = scale * (weighted - unit * jnp.mean(weighted * unit, axis=1, keepdims=True))
-        res = cot[rs, :].astype(F32) + field
-        gh_ref[rs, :] = res
-        low = res.astype(BF)
+        out = cot[rs, :].astype(F32) + field
+        gh[rs, :] = out
+        low = out.astype(BF)
         gather_low.own[0, rs, :] = low[:, :half_cols]
         gather_low.own[1, rs, :] = low[:, half_cols:]
         gg_ref[...] += jnp.sum(g * unit, axis=0, keepdims=True)
 
     gather_low.start()
+    store_gh = pltpu.make_async_copy(gh, gh_hbm, load_s.at[1])
+    store_gh.start()
     for s in range(1, n - 2):
         line.slot(s)
     gather_low.forward()
-    gather_lay.start()
+    gather_lay.start(range(1, gather_lay.levels))
     gather_low.finish()
     load_low = pltpu.make_async_copy(low_ref, space.at[:, pl.ds(0, 2 * half_cols)], load_s.at[3])
     load_low.start()
@@ -1386,8 +1458,7 @@
     blk = 256
     blocks = seq // blk
 
-    @pl.loop(0, hh // HD)
-    def _(head):
+    def back(head):
         at_cols = lambda first: pl.ds(pl.multiple_of(first + head * HD, HD), HD)
         for i in range(blocks - 1, -1, -1):
             rows = pl.ds(i * blk, blk)
@@ -1416,7 +1487,10 @@
             wt[i // 2, :, at_cols((i % 2) * (wide // 2) + hh)] = dka[rows, :].astype(BF)
             wt[i // 2, :, at_cols((i % 2) * (wide // 2) + 2 * hh)] = dva[rows, :].astype(BF)
 
+    heads = hh // HD
+    pl.loop(0, heads // 2)(back)
     gather_lay.forward()
+    pl.loop(heads // 2, heads)(back)
     stores = [
         pltpu.make_async_copy(
             wt.at[i // 2, :, pl.ds((i % 2) * (wide // 2), 3 * hh)],
@@ -1427,7 +1501,7 @@
     ]
     for cp in stores:
         cp.start()
-    line.final(rs_ref)
+    stores += line.final(res, rs_ref, rs_s) + [store_gh]
     gather_lay.finish()
     for cp in stores:
         cp.wait()
@@ -1455,8 +1529,8 @@
             jax.ShapeDtypeStruct((1, d), F32),
             jax.ShapeDtypeStruct((seq, 3 * hh), BF),
         ],
-        in_specs=[hbm] * 7 + [pl.BlockSpec(memory_space=pltpu.SMEM)] + [vm] * 2,
-        out_specs=[vm, hbm, hbm, vm, vm, hbm],
+        in_specs=[hbm] * 7 + [pl.BlockSpec(memory_space=pltpu.SMEM), hbm, vm],
+        out_specs=[hbm, hbm, hbm, hbm, vm, hbm],
         scratch_shapes=[
             pltpu.VMEM((seq, max(wide, d + 4 * hh)), BF),
             pltpu.VMEM((2, 256, wide), BF),
@@ -1464,6 +1538,11 @@
             pltpu.VMEM((2, seq, chunk), BF),
             dma((2,)),
             pltpu.VMEM((part, d), BF),
+            pltpu.VMEM((part, d), F32),
+            pltpu.VMEM((part, d), F32),
+            pltpu.VMEM((pieces, chunk, wide // pieces), BF),
+            dma((pieces,)),
+            dma((pieces,)),
             pltpu.VMEM((seq, HD), F32),
             pltpu.VMEM((seq, HD), F32),
             dma((4 + max(d // part, seq // 256),)),
@@ -1489,7 +1568,7 @@
     low_hbm,
     att_hbm,
     x_hbm,
-    gh_ref,
+    gh_hbm,
     gain_ref,
     gmid_ref,
     rs_ref,
@@ -1501,6 +1580,9 @@
     low,
     lhs,
     x,
+    gh,
+    res,
+    rs_s,
     loads,
     pout,
     own,
@@ -1541,6 +1623,7 @@
                 (att_hbm, rhs.at[:, pl.ds(3 * hh, hh)]),
                 (low_hbm, low),
                 (x_hbm.at[part_rows(at, part), :], x),
+                (gh_hbm, gh),
             ]
         )
     ]
@@ -1629,6 +1712,7 @@
     line.slot(0)
     quad.arrive()
     load_x.wait()
+    copies[6].wait()
     fold_next(len(bits))
     @pl.loop(0, part // 32)
     def _(b):
@@ -1639,9 +1723,9 @@
         unit = v * scale
         weighted = g * gain_ref[0:1, :]
         field = scale * (weighted - unit * jnp.mean(weighted * unit, axis=1, keepdims=True))
-        res = (gh_ref[rs, :] + field).astype(BF)
-        gown[0, rs, :] = res[:, :half_cols]
-        gown[1, rs, :] = res[:, half_cols:]
+        total = (gh[rs, :] + field).astype(BF)
+        gown[0, rs, :] = total[:, :half_cols]
+        gown[1, rs, :] = total[:, half_cols:]
 
     for b in range(len(bits) + 1, len(devs) - 1):
         fold_next(b)
@@ -1654,8 +1738,10 @@
         for j in range(per_row):
             gsum[i, j * fold : (j + 1) * fold] = fold_out[len(devs), i * per_row + j]
     gains_ref[...] = gsum[:, pl.ds(pl.multiple_of(at.dp * chunk, chunk), chunk)]
-    line.final(rs_ref)
+    stores = line.final(res, rs_ref, rs_s)
     gather.finish()
+    for cp in stores:
+        cp.wait()
     line.drain()
     quad.drain()
     for b in range(len(devs)):
@@ -1677,8 +1763,8 @@
             jax.ShapeDtypeStruct((seq, d), BF),
             jax.ShapeDtypeStruct((8, chunk), F32),
         ],
-        in_specs=[anyspace] * 6 + [vm] * 3,
-        out_specs=[vm, anyspace, vm],
+        in_specs=[anyspace] * 7 + [vm] * 2,
+        out_specs=[anyspace, anyspace, vm],
         scratch_shapes=[
             pltpu.VMEM((seq, 4 * hh), BF),
             pltpu.VMEM((d, 3 * hh), BF),
@@ -1686,7 +1772,10 @@
             pltpu.VMEM((seq, d), BF),
             pltpu.VMEM((2, chunk, seq), BF),
             pltpu.VMEM((part, d), BF),
-            dma((6,)),
+            pltpu.VMEM((part, d), F32),
+            pltpu.VMEM((4, chunk, hh), BF),
+            dma((4,)),
+            dma((7,)),
         ]
         + line_sum_scratch(n, 4, chunk, hh)
         + quad_sum_scratch(n_mp, part, d // 2)
@@ -1729,9 +1818,13 @@
     half = gate_out.shape[1]
     gate_out[...] = gu_ref[0, :, :half].astype(F32)
     up_out[...] = gu_ref[0, :, half:].astype(F32)
-    down_out[...] = down_ref[0].T.astype(F32)
-
-    @pl.when(pl.program_id(0) == 0)
+    step = pl.program_id(0)
+
+    @pl.when(lax.rem(step, 2) == 0)
+    def _():
+        down_out[...] = down_ref[0].T.astype(F32)
+
+    @pl.when(step == 0)
     def _():
         for i, ref in enumerate((q_out, k_out, v_out)):
             ref[...] = attn_ref[i].astype(F32)
@@ -1744,16 +1837,17 @@
     seq, d = low.shape
     steps, chunk, wide = gu.shape
     width, hh = down.shape[2], attn.shape[2]
-    row = pl.BlockSpec((seq // steps, d), lambda i: (i, 0))
+    row = pl.BlockSpec((seq // (2 * steps), d), lambda i: (i, 0))
     fixed = lambda *shape: pl.BlockSpec(shape, lambda i: (0,) * len(shape))
-    piece = lambda w: pl.BlockSpec((1, chunk, w), lambda i: (i, 0, 0))
-    cols = pl.BlockSpec((chunk, wide // 2), lambda i: (0, i))
+    two = pl.BlockSpec((1, chunk // 2, wide), lambda i: (i // 2, i % 2, 0))
+    piece = pl.BlockSpec((1, chunk, width), lambda i: (i // 2, 0, 0))
+    cols = pl.BlockSpec((chunk // 2, wide // 2), lambda i: (i % 2, i // 2))
     f32 = lambda *shape: jax.ShapeDtypeStruct(shape, F32)
     return pl.pallas_call(
         finish_kernel,
-        grid=(steps,),
-        in_specs=[row, row, piece(wide), piece(width), fixed(4, chunk, hh), fixed(*gains.shape)],
-        out_specs=[row, row, cols, cols, pl.BlockSpec((width, chunk), lambda i: (i, 0))]
+        grid=(2 * steps,),
+        in_specs=[row, row, two, piece, fixed(4, chunk, hh), fixed(*gains.shape)],
+        out_specs=[row, row, cols, cols, pl.BlockSpec((width, chunk), lambda i: (i // 2, 0))]
         + [fixed(chunk, hh)] * 3
         + [fixed(hh, chunk)]
         + [fixed(chunk)] * 2,

time: 605 us -> 597 us (0.987)
  Pallas kernels: 593 us -> 583 us
where the time goes in v7:
time: 597 us; the launch traced here: 587 us
  Pallas kernels  583 us (98%)
    pallas_call x1, Pallas kernels, gate_stage(): pl.pallas_call(functools.partial(gate_kernel, n_dp, n_mp), out_shape=[jax...  151 us
    pallas_call x1, Pallas kernels, mid_stage(): pl.pallas_call(functools.partial(mid_kernel, n_dp, n_mp), out_shape=[jax....  148 us
    pallas_call x1, Pallas kernels, down_stage(): pl.pallas_call(functools.partial(down_kernel, n_dp, n_mp), out_shape=[jax...  101 us
    pallas_call x1, Pallas kernels, last_stage(): pl.pallas_call(functools.partial(last_kernel, n_dp, n_mp), out_shape=[jax...  88.8 us
    pallas_call x1, Pallas kernels, attn_stage(): pl.pallas_call(functools.partial(attn_kernel, n_dp, n_mp), out_shape=[jax...  81.3 us
    pallas_call x1, Pallas kernels, finish_stage(): pl.pallas_call(finish_kernel, grid=(2 * steps,), in_specs=[row, row, two,...  13.9 us

profile of v7, /device:TPU:0, one launch (start us, length us, event | category | flops | bytes accessed | tf_op | source)
XLA Modules:
  0.0 586.8 jit_solution(6287423568930081108)
XLA Ops:
  1.3 0.7 convert.10
  2.0 0.7 convert.11
  2.7 0.6 fusion.3.gains_in
  3.3 81.3 %attn_stage.1 = (bf16[2048,2048]{1,0:T(8,128)(2,1)}, bf16[1024,1536]{1,0:T(8,128)(2,1)}, bf16[1024,512]{1,0:T(8,128)(2,1)}, bf16[1024,2048]{1,0:T(8,128)(2,1)}, ...) custom-call(s32[1]{0:T(128)S(6)} %copy.23.count_ref, ...), custom_call_target="tpu_custom_call" | custom-call | tf_op jit(solution)/shard_map/attn_stage/pallas_call | solution.py:790
  84.5 150.7 %gate_stage.1 = (bf16[2048,4096]{1,0:T(8,128)(2,1)}, bf16[1024,2048]{1,0:T(8,128)(2,1)}, f32[256,2048]{1,0:T(8,128)}, bf16[1024,4096]{1,0:T(8,128)(2,1)}, bf16[1024,2048]{1,0:T(8,128)(2,1)}) custom-call(bf16[1024,512]{1,0:T(8,128)(2,1)} %get-tuple-element.47.att_ref.att_hbm, bf16[2048,2048]{1,0:T(8,128)(2,1)} %get-tuple-element.48.aw_hbm, ...), custom_call_target="tpu_custom_call" | custom-call | tf_op jit(solution)/shard_map/gate_stage/pallas_call | solution.py:988
  235.2 101.1 %down_stage.1 = (bf16[4,256,512]{2,1,0:T(8,128)(2,1)}, bf16[1024,2048]{1,0:T(8,128)(2,1)}, bf16[1024,4096]{1,0:T(8,128)(2,1)}) custom-call(bf16[1024,2048]{1,0:T(8,128)(2,1)} %get-tuple-element.51.inner_hbm, bf16[1024,4096]{1,0:T(8,128)(2,1)} %get-tuple-element.52.gu_hbm, bf16[1024,2048]{1,0:T(8,128)(2,1)} %get-tuple-element.53.cot_hbm, ...), custom_call_target="tpu_custom_call" | custom-call | tf_op jit(solution)/shard_map/down_stage/pallas_call | solution.py:1216
  336.3 147.5 %mid_stage.1 = (bf16[4,256,1024]{2,1,0:T(8,128)(2,1)}, bf16[1024,2048]{1,0:T(8,128)(2,1)}, bf16[1024,2048]{1,0:T(8,128)(2,1)}, f32[256,2048]{1,0:T(8,128)}, f32[...) custom-call(bf16[1024,4096]{1,0:T(8,128)(2,1)} %get-tuple-element.55.ggu_hbm, bf16[2048,4096]{1,0:T(8,128)(2,1)} %get-tuple-element.56.gw_hbm, ...), custom_call_target="tpu_custom_call" | custom-call | tf_op jit(solution)/shard_map/mid_stage/pallas_call | solution.py:1522
  483.8 88.8 %last_stage.1 = (bf16[4,256,512]{2,1,0:T(8,128)(2,1)}, bf16[1024,2048]{1,0:T(8,128)(2,1)}, f32[8,256]{1,0:T(8,128)}) custom-call(bf16[1024,1536]{1,0:T(8,128)(2,1)} %get-tuple-element.61.dqkv_hbm, bf16[2048,2048]{1,0:T(8,128)(2,1)} %get-tuple-element.48.aw_hbm, bf16[1024,2048]{1,0:T(8,128)(2,1)} %get-tuple-element.62.nin_hbm, ...), custom_call_target="tpu_custom_call" | custom-call | tf_op jit(solution)/shard_map/last_stage/pallas_call | solution.py:1759
  572.6 13.9 %finish_stage.1 = (bf16[1024,2048]{1,0:T(8,128)(2,1)}, f32[1024,2048]{1,0:T(8,128)}, f32[256,2048]{1,0:T(8,128)}, f32[256,2048]{1,0:T(8,128)}, f32[2048,256]{1,0...) custom-call(bf16[1024,2048]{1,0:T(8,128)(2,1)} %get-tuple-element.66, ...), custom_call_target="tpu_custom_call" | custom-call | tf_op jit(solution)/shard_map/finish_stage/pallas_call | solution.py:1846
  (2 shorter events, 0.0 us)

commit v8 on v7

--- a/solution.py
+++ b/solution.py
@@ -36,6 +36,8 @@
 MESH = pl.DeviceIdType.MESH
 VMEM_LIMIT = 60 * 1024 * 1024
 PIECES = 4
+AHEAD = 1
+DOWN_AHEAD = 2
 
 
 def flipped(index, bit):
@@ -295,6 +297,8 @@
     def __init__(self, at, t, r, sems):
         self.at, self.t, self.r = at, t, r
         self.s, self.v = sems
+        self.blocks = self.s.shape[2]
+        self.step = r.shape[2] // self.blocks
         self.order = [at.bits, at.bits[::-1]]
         self.levels = len(at.bits)
         self.seen = set()
@@ -318,14 +322,20 @@
     def terms(self, half, mask, rs):
         return self.t[half, self.at.quarter(mask), rs, :].astype(F32)
 
-    def copy(self, half, k, j):
+    def split(self, k):
+        return self.blocks if k == self.levels - 1 else 1
+
+    def copy(self, half, k, j, block=0):
         bit = self.order[half][k]
         mask = bit + spread(j, self.rest(half, k))
         src = self.source(half, mask) if k == 0 else self.r.at[half, self.index(half, k - 1, mask)]
         at = self.slot(k, j)
-        return remote(
-            src, self.r.at[half, at], self.s.at[half, at], self.v.at[half, at], self.at.peer(bit)
-        )
+        dst = self.r.at[half, at]
+        if self.split(k) > 1:
+            rows = pl.ds(block * self.step, self.step)
+            src, dst = src.at[rows, :], dst.at[rows, :]
+        send, recv = self.s.at[half, at, block], self.v.at[half, at, block]
+        return remote(src, dst, send, recv, self.at.peer(bit))
 
     def offer(self, mask, only=(0, 1)):
         for half in only:
@@ -336,32 +346,40 @@
     def masks(self):
         return sorted(range(1, 2 * self.count(0)), key=lambda m: -bin(m).count("1")) + [0]
 
-    def come(self, half, k, mask):
+    def come(self, half, k, mask, block=0):
         at = self.index(half, k, mask)
-        if (half, at) not in self.seen:
-            self.seen.add((half, at))
-            self.copy(half, k, at - self.slot(k, 0)).wait_recv()
+        block = min(block, self.split(k) - 1)
+        if (half, at, block) not in self.seen:
+            self.seen.add((half, at, block))
+            self.copy(half, k, at - self.slot(k, 0), block).wait_recv()
         return at
 
     def turn(self):
         for k in range(1, self.levels):
-            for half in range(2):
-                for j in range(self.count(k)):
-                    mask = self.order[half][k] + spread(j, self.rest(half, k))
-                    got = [self.come(half, i, mask) for i in range(k)]
-
-                    @pl.loop(0, self.r.shape[2] // 64)
-                    def _(b):
-                        rs = pl.ds(pl.multiple_of(b * 64, 64), 64)
-                        total = self.terms(half, mask, rs)
-                        for i in got:
-                            total = total + self.r[half, i, rs, :].astype(F32)
-                        self.r[half, got[-1], rs, :] = total.astype(BF)
-
-                    self.copy(half, k, j).start()
-
-    def arrive(self):
-        self.got = [[self.come(half, k, 0) for k in range(self.levels)] for half in range(2)]
+            for block in range(self.split(k)):
+                for half in range(2):
+                    for j in range(self.count(k)):
+                        self.pass_on(half, k, j, block)
+
+    def pass_on(self, half, k, j, block):
+        mask = self.order[half][k] + spread(j, self.rest(half, k))
+        got = [self.come(half, i, mask) for i in range(k)]
+        rows = self.r.shape[2] // self.split(k)
+
+        @pl.loop(0, rows // 64)
+        def _(b):
+            rs = pl.ds(pl.multiple_of(block * rows + b * 64, 64), 64)
+            total = self.terms(half, mask, rs)
+            for i in got:
+                total = total + self.r[half, i, rs, :].astype(F32)
+            self.r[half, got[-1], rs, :] = total.astype(BF)
+
+        self.copy(half, k, j, block).start()
+
+    def arrive(self, block=0):
+        self.got = [
+            [self.come(half, k, 0, block) for k in range(self.levels)] for half in range(2)
+        ]
 
     def total(self, half, rs):
         total = self.terms(half, 0, rs)
@@ -373,7 +391,8 @@
         for half in range(2):
             for k in range(self.levels):
                 for j in range(self.count(k)):
-                    self.copy(half, k, j).wait_send()
+                    for block in range(self.split(k)):
+                        self.copy(half, k, j, block).wait_send()
 
 
 class QuadSumHbm(QuadSum):
@@ -397,13 +416,13 @@
         return self.t[half, self.index(half, 0, mask), rs, :].astype(F32)
 
 
-def quad_sum_scratch(mp, rows, cols, parts=None):
+def quad_sum_scratch(mp, rows, cols, parts=None, blocks=1):
     dma = pltpu.SemaphoreType.DMA
     return [
         pltpu.VMEM((2, parts or mp, rows, cols), BF),
         pltpu.VMEM((2, mp - 1, rows, cols), BF),
-        dma((2, mp - 1)),
-        dma((2, mp - 1)),
+        dma((2, mp - 1, blocks)),
+        dma((2, mp - 1, blocks)),
     ]
 
 
@@ -411,62 +430,77 @@
     def __init__(self, at, own, out, sems):
         self.at, self.own, self.out = at, own, out
         self.s, self.v, self.here = sems
+        self.blocks = self.s.shape[2]
         self.order = [at.bits[::-1], at.bits]
         self.levels = len(at.bits)
         self.seen = set()
 
-    def spot(self, mask, half):
+    def mine(self, half, block):
+        step = self.own.shape[1] // self.blocks
+        return self.own.at[half, pl.ds(block * step, step), :]
+
+    def spot(self, mask, half, block):
         rows, cols = self.own.shape[1], self.own.shape[2]
-        rs = pl.ds(pl.multiple_of(self.at.quarter(mask) * rows, rows), rows)
+        step = rows // self.blocks
+        rs = pl.ds(pl.multiple_of(self.at.quarter(mask) * rows + block * step, step), step)
         return self.out.at[rs, pl.ds(half * cols, cols)]
 
-    def copy(self, half, k, j):
+    def copy(self, half, k, j, block):
         mask = spread(j, self.order[half][:k])
-        dst = self.spot(mask, half)
-        src = self.own.at[half] if j == 0 else dst
+        dst = self.spot(mask, half, block)
+        src = self.mine(half, block) if j == 0 else dst
         at = (1 << k) - 1 + j
         dev = self.at.peer(self.order[half][k])
-        return remote(src, dst, self.s.at[half, at], self.v.at[half, at], dev)
-
-    def come(self, half, k, j):
-        if (half, k, j) not in self.seen:
-            self.seen.add((half, k, j))
-            self.copy(half, k, j).wait_recv()
-
-    def keep(self, half):
-        return pltpu.make_async_copy(self.own.at[half], self.spot(0, half), self.here.at[half])
-
-    def start(self, levels=None):
+        return remote(src, dst, self.s.at[half, at, block], self.v.at[half, at, block], dev)
+
+    def come(self, half, k, j, block):
+        if (half, k, j, block) not in self.seen:
+            self.seen.add((half, k, j, block))
+            self.copy(half, k, j, block).wait_recv()
+
+    def keep(self, half, block):
+        return pltpu.make_async_copy(
+            self.mine(half, block), self.spot(0, half, block), self.here.at[half, block]
+        )
+
+    def start(self, levels=None, block=0):
         for k in range(self.levels) if levels is None else levels:
             for half in range(2):
-                self.copy(half, k, 0).start()
+                self.copy(half, k, 0, block).start()
                 if k == 0:
-                    self.keep(half).start()
-
-    def forward(self):
+                    self.keep(half, block).start()
+
+    def forward(self, block=0):
         for k in range(1, self.levels):
             for half in range(2):
                 for j in range(1, 1 << k):
                     top = j.bit_length() - 1
-                    self.come(half, top, j - (1 << top))
-                    self.copy(half, k, j).start()
+                    self.come(half, top, j - (1 << top), block)
+                    self.copy(half, k, j, block).start()
 
     def finish(self):
         for half in range(2):
-            for k in range(self.levels):
-                for j in range(1 << k):
-                    self.come(half, k, j)
-                    self.copy(half, k, j).wait_send()
-            self.keep(half).wait()
-
-
-def quad_gather_scratch(mp, rows, cols):
+            for block in range(self.blocks):
+                for k in range(self.levels):
+                    for j in range(1 << k):
+                        self.come(half, k, j, block)
+                        self.copy(half, k, j, block).wait_send()
+                self.keep(half, block).wait()
+
+
+def quad_gather_scratch(mp, rows, cols, blocks=1):
     dma = pltpu.SemaphoreType.DMA
-    return [pltpu.VMEM((2, rows, cols), BF), dma((2, mp - 1)), dma((2, mp - 1)), dma((2,))]
+    return [
+        pltpu.VMEM((2, rows, cols), BF),
+        dma((2, mp - 1, blocks)),
+        dma((2, mp - 1, blocks)),
+        dma((2, blocks)),
+    ]
 
 
 class LineGather:
-    def __init__(self, at, pieces, shard, spot, sems):
+    def __init__(self, at, pieces, shard, spot, sems, pre=0):
+        self.pre = pre
         self.at, self.pieces, self.shard, self.spot = at, pieces, shard, spot
         self.d_s, self.d_r, self.u_s, self.u_r, self.c_s, self.c_r, self.here = sems
 
@@ -494,7 +528,7 @@
 
     def start(self):
         at = self.at
-        for i in range(self.pieces):
+        for i in range(self.pre, self.pieces):
 
             @pl.when(at.has_below)
             def _():
@@ -534,9 +568,36 @@
             self.core_copy(p - h, i).start()
 
     def stage(self, h):
-        @pl.loop(0, self.pieces)
+        @pl.loop(self.pre if h == 1 else 0, self.pieces)
         def _(i):
             self.slot(h, i)
+
+    def early(self, i, above, below):
+        at = self.at
+
+        @pl.when(at.has_above)
+        def _():
+            b = 2 * at.p + 2 + at.c
+            dst = self.spot(b, i)
+
+            @pl.when(at.has_below)
+            def _():
+                remote(above, dst, self.d_s.at[1, i], self.d_r.at[1, i], at.below).start()
+
+            z = at.p + 1
+            remote(above, dst, self.c_s.at[z, i], self.c_r.at[z, i], at.core).start()
+
+        @pl.when(at.has_below)
+        def _():
+            b = 2 * at.p - 2 + at.c
+            dst = self.spot(b, i)
+
+            @pl.when(at.has_above)
+            def _():
+                remote(below, dst, self.u_s.at[1, i], self.u_r.at[1, i], at.above).start()
+
+            z = at.p - 1
+            remote(below, dst, self.c_s.at[z, i], self.c_r.at[z, i], at.core).start()
 
     def ready(self, z, i):
         self.core_copy(z, i, incoming=True).wait_recv()
@@ -549,11 +610,13 @@
         def _(i):
             for h in range(n):
 
-                @pl.when((p + h < n) & at.has_below)
+                sent = (i >= self.pre) if h == 0 else True
+
+                @pl.when((p + h < n) & at.has_below & sent)
                 def _():
                     self.down_copy(h, i, h == 0).wait_send()
 
-                @pl.when((p - h >= 0) & at.has_above)
+                @pl.when((p - h >= 0) & at.has_above & sent)
                 def _():
                     self.up_copy(h, i, h == 0).wait_send()
 
@@ -576,6 +639,24 @@
 
 def cols_of(ref, width, base=0):
     return lambda i: ref.at[:, pl.ds(pl.multiple_of(base + i * width, width), width)]
+
+
+class Presend:
+    def __init__(self, at, src, got, sems):
+        s, r = sems
+        self.at = at
+        self.down = remote(src, got.at[0], s.at[0], r.at[0], at.below)
+        self.up = remote(src, got.at[1], s.at[1], r.at[1], at.above)
+
+    def start(self):
+        pl.when(self.at.has_below)(self.down.start)
+        pl.when(self.at.has_above)(self.up.start)
+
+    def finish(self):
+        pl.when(self.at.has_above)(self.down.wait_recv)
+        pl.when(self.at.has_below)(self.up.wait_recv)
+        pl.when(self.at.has_below)(self.down.wait_send)
+        pl.when(self.at.has_above)(self.up.wait_send)
 
 
 def attend_rows(qkv, out, seq, hh, count, head):
@@ -593,7 +674,8 @@
     n_dp,
     n_mp,
     count_ref,
-    gains_in,
+    ga_ref,
+    gf_ref,
     wq_hbm,
     wk_hbm,
     wv_hbm,
@@ -611,6 +693,8 @@
     gush_ref,
     dnsh_ref,
     cotm_ref,
+    gpre_ref,
+    gains_in,
     w4,
     wo,
     shard,
@@ -662,6 +746,8 @@
         lambda b, i: gains_ref.at[:, pl.ds(pl.multiple_of(b * chunk, chunk), chunk)],
         rest[14:21],
     )
+    for i, ref in enumerate((ga_ref, gf_ref)):
+        gains_in[i, :] = ref[...].astype(BF).astype(F32)
     enter(at)
     small.start()
     for i in range(3):
@@ -747,6 +833,8 @@
     outs[-1].start()
     for h in range(2, n - 1):
         last.slot(h, 0)
+    ahead = Presend(at, gush.at[:, pl.ds(0, 2 * half * AHEAD)], gpre_ref, rest[21:23])
+    ahead.start()
     heads = hh // HD
 
     @pl.loop(0, heads // 2)
@@ -764,12 +852,13 @@
         last.ready(z, 0)
     for cp in outs:
         cp.wait()
+    ahead.finish()
     small.drain()
     three.drain()
     last.drain()
 
 
-def attn_stage(n_dp, n_mp, counts, gains, wq, wk, wv, wo, wg, wu, wd, x, cot):
+def attn_stage(n_dp, n_mp, counts, ga, gf, wq, wk, wv, wo, wg, wu, wd, x, cot):
     seq, d = x.shape
     chunk, hh = wq.shape
     ff = wg.shape[1]
@@ -786,13 +875,15 @@
         ((chunk, 2 * ff), BF),
         ((chunk, ff), BF),
         ((seq, d), BF),
+        ((2, chunk, 2 * ff * AHEAD // PIECES), BF),
     ]
     return pl.pallas_call(
         functools.partial(attn_kernel, n_dp, n_mp),
         out_shape=[jax.ShapeDtypeStruct(*s) for s in shapes],
-        in_specs=[pl.BlockSpec(memory_space=pltpu.SMEM), vm] + [hbm] * 9,
-        out_specs=[hbm, hbm, vm, hbm, vm, hbm, hbm, hbm],
+        in_specs=[pl.BlockSpec(memory_space=pltpu.SMEM), vm, vm] + [hbm] * 9,
+        out_specs=[hbm, hbm, vm, hbm, vm, hbm, hbm, hbm, hbm],
         scratch_shapes=[
+            pltpu.VMEM((8, chunk), F32),
             pltpu.VMEM((3, chunk, hh), F32),
             pltpu.VMEM((hh, chunk), F32),
             pltpu.VMEM((chunk, 4 * hh), BF),
@@ -809,12 +900,13 @@
             dma((5,)),
         ]
         + line_gather_scratch(n, 3)
-        + line_gather_scratch(n, 1) * 2,
+        + line_gather_scratch(n, 1) * 2
+        + [dma((2,))] * 2,
         compiler_params=pltpu.CompilerParams(
             collective_id=1, has_side_effects=True, vmem_limit_bytes=VMEM_LIMIT
         ),
         name="attn_stage",
-    )(counts, gains, wq, wk, wv, wo, wg, wu, wd, x, cot)
+    )(counts, ga, gf, wq, wk, wv, wo, wg, wu, wd, x, cot)
 
 
 def gate_kernel(
@@ -823,6 +915,8 @@
     att_ref,
     aw_hbm,
     sh_hbm,
+    gpre_hbm,
+    dnsh_hbm,
     x_hbm,
     gain_ref,
     gw_ref,
@@ -830,7 +924,9 @@
     hid_hbm,
     gu_ref,
     inner_ref,
+    dpre_ref,
     wo,
+    gp,
     sh,
     xs,
     hid,
@@ -839,6 +935,7 @@
     wbuf,
     gbuf,
     ibuf,
+    gp_s,
     load_s,
     wb_s,
     gb_s,
@@ -855,10 +952,12 @@
     chunk, wide = sh_hbm.shape
     pieces = sems[6].shape[0]
     width = wide // pieces
-    line = LineGather(at, pieces, cols_of(sh, width), rows_spot(gw_ref, chunk, width), sems)
+    line = LineGather(at, pieces, cols_of(sh, width), rows_spot(gw_ref, chunk, width), sems, AHEAD)
 
     load_sh = pltpu.make_async_copy(sh_hbm, sh, load_s.at[2])
     load_sh.start()
+    load_gp = pltpu.make_async_copy(gpre_hbm, gp, load_s.at[3])
+    load_gp.start()
     load = pltpu.make_async_copy(aw_hbm.at[:, pl.ds(3 * hh, hh)], wo, load_s.at[0])
     load.start()
     load_x = pltpu.make_async_copy(x_hbm.at[part_rows(at, part), :], xs, load_s.at[1])
@@ -866,6 +965,17 @@
     enter(at)
     load_sh.wait()
     line.start()
+    load_gp.wait()
+
+    def place(side, i):
+        b = at.dp + (2 if side == 0 else -2)
+        piece = gp.at[side, :, pl.ds(i * width, width)]
+        return pltpu.make_async_copy(piece, line.spot(b, i), gp_s.at[side, i])
+
+    for i in range(AHEAD):
+        line.early(i, *[gp.at[side, :, pl.ds(i * width, width)] for side in range(2)])
+        pl.when(at.has_above)(place(0, i).start)
+        pl.when(at.has_below)(place(1, i).start)
     load.wait()
 
     def terms(q):
@@ -905,6 +1015,14 @@
         line.stage(h)
     load.wait()
 
+    for i in range(AHEAD):
+        pl.when(at.has_above)(place(0, i).wait)
+        pl.when(at.has_below)(place(1, i).wait)
+    ahead = Presend(
+        at, dnsh_hbm.at[:, pl.ds(0, width // 2 * DOWN_AHEAD)], dpre_ref, rest[15:17]
+    )
+    ahead.start()
+
     pair = 2 * chunk
     near = jnp.where(2 * at.p < n, 0, 1)
     far = jnp.where(2 * at.p < n, n - 1, 0)
@@ -972,11 +1090,12 @@
         g_copy(i, i % 2).wait()
         i_copy(i, i % 2).wait()
     store_hid.wait()
+    ahead.finish()
     line.drain()
     quad.drain()
 
 
-def gate_stage(n_dp, n_mp, att, aw, shard, x, gain):
+def gate_stage(n_dp, n_mp, att, aw, shard, gpre, dnsh, x, gain):
     seq, hh = att.shape
     d = aw.shape[0]
     chunk, wide = shard.shape
@@ -993,11 +1112,13 @@
             jax.ShapeDtypeStruct((part, d), F32),
             jax.ShapeDtypeStruct((seq, wide), BF),
             jax.ShapeDtypeStruct((seq, wide // 2), BF),
+            jax.ShapeDtypeStruct((2, chunk, width // 2 * DOWN_AHEAD), BF),
         ],
-        in_specs=[vm, hbm, hbm, hbm, vm],
-        out_specs=[hbm] * 5,
+        in_specs=[vm, hbm, hbm, hbm, hbm, hbm, vm],
+        out_specs=[hbm] * 6,
         scratch_shapes=[
             pltpu.VMEM((d, hh), BF),
+            pltpu.VMEM((2, chunk, width * AHEAD), BF),
             pltpu.VMEM((chunk, wide), BF),
             pltpu.VMEM((part, d), BF),
             pltpu.VMEM((part, d), F32),
@@ -1006,19 +1127,21 @@
             pltpu.VMEM((2, d, width), BF),
             pltpu.VMEM((2, seq, width), BF),
             pltpu.VMEM((2, seq, width // 2), BF),
-            dma((3,)),
+            dma((2, AHEAD)),
+            dma((4,)),
             dma((2,)),
             dma((2,)),
             dma((2,)),
         ]
         + quad_sum_scratch(n_mp, part, d // 2)
         + quad_gather_scratch(n_mp, part, d // 2)
-        + line_gather_scratch(n, PIECES),
+        + line_gather_scratch(n, PIECES)
+        + [dma((2,))] * 2,
         compiler_params=pltpu.CompilerParams(
             collective_id=2, has_side_effects=True, vmem_limit_bytes=VMEM_LIMIT
         ),
         name="gate_stage",
-    )(att, aw, shard, x, gain)
+    )(att, aw, shard, gpre, dnsh, x, gain)
 
 
 def down_kernel(
@@ -1028,6 +1151,7 @@
     gu_hbm,
     cot_hbm,
     sh_hbm,
+    dpre_hbm,
     rs_ref,
     ft_ref,
     ggu_ref,
@@ -1038,6 +1162,7 @@
     acc,
     ftb,
     res,
+    dp_s,
     load_s,
     cot_s,
     in_s,
@@ -1054,7 +1179,7 @@
     chunk, ff = sh_hbm.shape
     pieces = sems[6].shape[0]
     width = ff // pieces
-    gather = LineGather(at, pieces, None, rows_spot(dn, chunk, width), sems)
+    gather = LineGather(at, pieces, None, rows_spot(dn, chunk, width), sems, DOWN_AHEAD)
     pair = 2 * chunk
     def cot_copy(k):
         cols = pl.ds(pl.multiple_of(order_of(k, at) * pair, pair), pair)
@@ -1069,6 +1194,15 @@
         sh_hbm, dn.at[pl.ds(pl.multiple_of(at.dp * chunk, chunk), chunk), :], dn_s.at[0]
     )
     own.start()
+
+    def pre_copy(side):
+        b = at.dp + (2 if side == 0 else -2)
+        rows = pl.ds(pl.multiple_of(b * chunk, chunk), chunk)
+        dst = dn.at[rows, pl.ds(0, width * DOWN_AHEAD)]
+        return pltpu.make_async_copy(dpre_hbm.at[side], dst, dp_s.at[side])
+
+    pl.when(at.has_above)(pre_copy(0).start)
+    pl.when(at.has_below)(pre_copy(1).start)
     cot_copy(0).start()
     for i in range(pieces):
         in_copy(i).start()
@@ -1078,6 +1212,10 @@
     enter(at)
     own.wait()
     gather.start()
+    pl.when(at.has_above)(pre_copy(0).wait)
+    pl.when(at.has_below)(pre_copy(1).wait)
+    for i in range(DOWN_AHEAD):
+        gather.early(i, gather.spot(at.dp + 2, i), gather.spot(at.dp - 2, i))
 
     def run(e):
         k, core = e // 2, e % 2
@@ -1146,8 +1284,7 @@
             gu[rs, gcols] = (u * sg * (1.0 + g * (1.0 - sg))).astype(BF)
             gu[rs, ucols] = (g * sg).astype(BF)
 
-    @pl.loop(1, n - 1)
-    def _(h):
+    for h in range(1, n - 1):
         gather.stage(h)
 
         @pl.when(p + h < n)
@@ -1207,7 +1344,7 @@
     gather.drain()
 
 
-def down_stage(n_dp, n_mp, inner, gu, cot, shard):
+def down_stage(n_dp, n_mp, inner, gu, cot, shard, dpre):
     seq, d = cot.shape
     chunk, ff = shard.shape
     n = n_dp // 2
@@ -1220,7 +1357,7 @@
             jax.ShapeDtypeStruct((seq, d), BF),
             jax.ShapeDtypeStruct((seq, 2 * ff), BF),
         ],
-        in_specs=[hbm] * 4,
+        in_specs=[hbm] * 5,
         out_specs=[hbm] * 3,
         scratch_shapes=[
             pltpu.VMEM((seq, ff), BF),
@@ -1230,6 +1367,7 @@
             pltpu.VMEM((seq, ff), F32),
             pltpu.VMEM((1, seq, 2 * chunk), BF),
             pltpu.VMEM((PIECES, chunk, ff // PIECES), BF),
+            dma((2,)),
             dma((1,)),
             dma((n,)),
             dma((PIECES,)),
@@ -1244,7 +1382,7 @@
             collective_id=3, has_side_effects=True, vmem_limit_bytes=VMEM_LIMIT
         ),
         name="down_stage",
-    )(inner, gu, cot, shard)
+    )(inner, gu, cot, shard, dpre)
 
 
 def mid_kernel(
@@ -1710,30 +1848,37 @@
     for b in range(1, len(bits)):
         fold_next(b)
     line.slot(0)
-    quad.arrive()
     load_x.wait()
     copies[6].wait()
     fold_next(len(bits))
-    @pl.loop(0, part // 32)
-    def _(b):
-        rs = pl.ds(pl.multiple_of(b * 32, 32), 32)
-        v = x[rs, :].astype(F32)
-        scale = lax.rsqrt(jnp.mean(v * v, axis=1, keepdims=True) + EPS)
-        g = jnp.concatenate([quad.total(0, rs), quad.total(1, rs)], axis=1)
-        unit = v * scale
-        weighted = g * gain_ref[0:1, :]
-        field = scale * (weighted - unit * jnp.mean(weighted * unit, axis=1, keepdims=True))
-        total = (gh[rs, :] + field).astype(BF)
-        gown[0, rs, :] = total[:, :half_cols]
-        gown[1, rs, :] = total[:, half_cols:]
-
-    for b in range(len(bits) + 1, len(devs) - 1):
-        fold_next(b)
-    gather.start()
+    step = part // gather.blocks
+
+    def norm(block):
+        @pl.loop(0, step // 32)
+        def _(b):
+            rs = pl.ds(pl.multiple_of(block * step + b * 32, 32), 32)
+            v = x[rs, :].astype(F32)
+            scale = lax.rsqrt(jnp.mean(v * v, axis=1, keepdims=True) + EPS)
+            g = jnp.concatenate([quad.total(0, rs), quad.total(1, rs)], axis=1)
+            unit = v * scale
+            weighted = g * gain_ref[0:1, :]
+            field = scale * (weighted - unit * jnp.mean(weighted * unit, axis=1, keepdims=True))
+            total = (gh[rs, :] + field).astype(BF)
+            gown[0, rs, :] = total[:, :half_cols]
+            gown[1, rs, :] = total[:, half_cols:]
+
+    for block in range(gather.blocks):
+        quad.arrive(block)
+        norm(block)
+        gather.start(block=block)
+        if block == 0:
+            for b in range(len(bits) + 1, len(devs) - 1):
+                fold_next(b)
     for s in range(1, n - 2):
         line.slot(s)
+    for block in range(gather.blocks):
+        gather.forward(block)
     fold_next(len(devs) - 1)
-    gather.forward()
     for i in range(2):
         for j in range(per_row):
             gsum[i, j * fold : (j + 1) * fold] = fold_out[len(devs), i * per_row + j]
@@ -1778,8 +1923,8 @@
             dma((7,)),
         ]
         + line_sum_scratch(n, 4, chunk, hh)
-        + quad_sum_scratch(n_mp, part, d // 2)
-        + quad_gather_scratch(n_mp, part, d // 2)
+        + quad_sum_scratch(n_mp, part, d // 2, None, 2)
+        + quad_gather_scratch(n_mp, part, d // 2, 2)
         + [
             pltpu.VMEM((8, d), F32),
             pltpu.VMEM((folds + 1, 8, d // 4), F32),
@@ -1881,15 +2026,26 @@
     w_down,
 ):
     n_dp, n_mp = lax.axis_size("dp"), lax.axis_size("mp")
-    gains = jnp.pad(jnp.stack([gain_attn, gain_ffn]), ((0, 6), (0, 0)))
-    gains = gains.astype(BF).astype(F32)
-    attn_w, qkv, attended, normed_in, gains, gu_shard, down_shard, grad_ffn = attn_stage(
-        n_dp, n_mp, counts, gains, w_query, w_key, w_value, w_output, w_gate, w_up, w_down, inputs, cotangent
+    attn_w, qkv, attended, normed_in, gains, gu_shard, down_shard, grad_ffn, gu_pre = attn_stage(
+        n_dp,
+        n_mp,
+        counts,
+        gain_attn,
+        gain_ffn,
+        w_query,
+        w_key,
+        w_value,
+        w_output,
+        w_gate,
+        w_up,
+        w_down,
+        inputs,
+        cotangent,
     )
-    gu_w, normed_mid, hidden, gu, inner = gate_stage(
-        n_dp, n_mp, attended, attn_w, gu_shard, inputs, gains
+    gu_w, normed_mid, hidden, gu, inner, down_pre = gate_stage(
+        n_dp, n_mp, attended, attn_w, gu_shard, gu_pre, down_shard, inputs, gains
     )
-    rs_down, ffn_terms, ggu = down_stage(n_dp, n_mp, inner, gu, grad_ffn, down_shard)
+    rs_down, ffn_terms, ggu = down_stage(n_dp, n_mp, inner, gu, grad_ffn, down_shard, down_pre)
     rs_gu, grad_low, layer_out, grad_hidden, g_gain_mid, dqkv = mid_stage(
         n_dp, n_mp, ggu, gu_w, normed_mid, ffn_terms, grad_ffn, qkv, attn_w, counts, hidden, gains
     )

time: 597 us -> 581 us (0.973)
  Pallas kernels: 583 us -> 570 us
    pallas_call x1, Pallas kernels: 151 us -> 141 us  [gate_stage(): pl.pallas_call(functools.partial(gate_kernel, n_dp, n_mp), out_shape=[jax...]
    pallas_call x1, Pallas kernels: 101 us -> 92.8 us  [down_stage(): pl.pallas_call(functools.partial(down_kernel, n_dp, n_mp), out_shape=[jax...]
    pallas_call x1, Pallas kernels: 81.3 us -> 89.1 us  [attn_stage(): pl.pallas_call(functools.partial(attn_kernel, n_dp, n_mp), out_shape=[jax...]
where the time goes in v8:
time: 581 us; the launch traced here: 572 us
  Pallas kernels  570 us (98%)
    pallas_call x1, Pallas kernels, mid_stage(): pl.pallas_call(functools.partial(mid_kernel, n_dp, n_mp), out_shape=[jax....  148 us
    pallas_call x1, Pallas kernels, gate_stage(): pl.pallas_call(functools.partial(gate_kernel, n_dp, n_mp), out_shape=[jax...  141 us
    pallas_call x1, Pallas kernels, down_stage(): pl.pallas_call(functools.partial(down_kernel, n_dp, n_mp), out_shape=[jax...  92.8 us
    pallas_call x1, Pallas kernels, attn_stage(): pl.pallas_call(functools.partial(attn_kernel, n_dp, n_mp), out_shape=[jax...  89.1 us
    pallas_call x1, Pallas kernels, last_stage(): pl.pallas_call(functools.partial(last_kernel, n_dp, n_mp), out_shape=[jax...  85.4 us
    pallas_call x1, Pallas kernels, finish_stage(): pl.pallas_call(finish_kernel, grid=(2 * steps,), in_specs=[row, row, two,...  13.9 us

profile of v8, /device:TPU:0, one launch (start us, length us, event | category | flops | bytes accessed | tf_op | source)
XLA Modules:
  0.0 571.7 jit_solution(2080666715589538078)
XLA Ops:
  1.3 89.1 %attn_stage.1 = (bf16[2048,2048]{1,0:T(8,128)(2,1)}, bf16[1024,1536]{1,0:T(8,128)(2,1)}, bf16[1024,512]{1,0:T(8,128)(2,1)}, bf16[1024,2048]{1,0:T(8,128)(2,1)}, ...) custom-call(s32[1]{0:T(128)S(6)} %copy.23.count_ref, ...), custom_call_target="tpu_custom_call" | custom-call | tf_op jit(solution)/shard_map/attn_stage/pallas_call | solution.py:880
  90.4 141.1 %gate_stage.1 = (bf16[2048,4096]{1,0:T(8,128)(2,1)}, bf16[1024,2048]{1,0:T(8,128)(2,1)}, f32[256,2048]{1,0:T(8,128)}, bf16[1024,4096]{1,0:T(8,128)(2,1)}, bf16[1...) custom-call(bf16[1024,512]{1,0:T(8,128)(2,1)} %get-tuple-element.49.att_ref.att_hbm, ...), custom_call_target="tpu_custom_call" | custom-call | tf_op jit(solution)/shard_map/gate_stage/pallas_call | solution.py:1107
  231.5 92.8 %down_stage.1 = (bf16[4,256,512]{2,1,0:T(8,128)(2,1)}, bf16[1024,2048]{1,0:T(8,128)(2,1)}, bf16[1024,4096]{1,0:T(8,128)(2,1)}) custom-call(bf16[1024,2048]{1,0:T(8,128)(2,1)} %get-tuple-element.55.inner_hbm, bf16[1024,4096]{1,0:T(8,128)(2,1)} %get-tuple-element.56.gu_hbm, bf16[1024,2048]{1,0:T(8,128)(2,1)} %get-tuple-element.57.cot_hbm, ...), custom_call_target="tpu_custom_call" | custom-call | tf_op jit(solution)/shard_map/down_stage/pallas_call | solution.py:1353
  324.3 147.6 %mid_stage.1 = (bf16[4,256,1024]{2,1,0:T(8,128)(2,1)}, bf16[1024,2048]{1,0:T(8,128)(2,1)}, bf16[1024,2048]{1,0:T(8,128)(2,1)}, f32[256,2048]{1,0:T(8,128)}, f32[...) custom-call(bf16[1024,4096]{1,0:T(8,128)(2,1)} %get-tuple-element.59.ggu_hbm, bf16[2048,4096]{1,0:T(8,128)(2,1)} %get-tuple-element.60.gw_hbm, ...), custom_call_target="tpu_custom_call" | custom-call | tf_op jit(solution)/shard_map/mid_stage/pallas_call | solution.py:1660
  471.9 85.4 %last_stage.1 = (bf16[4,256,512]{2,1,0:T(8,128)(2,1)}, bf16[1024,2048]{1,0:T(8,128)(2,1)}, f32[8,256]{1,0:T(8,128)}) custom-call(bf16[1024,1536]{1,0:T(8,128)(2,1)} %get-tuple-element.65.dqkv_hbm, bf16[2048,2048]{1,0:T(8,128)(2,1)} %get-tuple-element.50.aw_hbm, bf16[1024,2048]{1,0:T(8,128)(2,1)} %get-tuple-element.66.nin_hbm, ...), custom_call_target="tpu_custom_call" | custom-call | tf_op jit(solution)/shard_map/last_stage/pallas_call | solution.py:1904
  557.3 13.9 %finish_stage.1 = (bf16[1024,2048]{1,0:T(8,128)(2,1)}, f32[1024,2048]{1,0:T(8,128)}, f32[256,2048]{1,0:T(8,128)}, f32[256,2048]{1,0:T(8,128)}, f32[2048,256]{1,0...) custom-call(bf16[1024,2048]{1,0:T(8,128)(2,1)} %get-tuple-element.70, ...), custom_call_target="tpu_custom_call" | custom-call | tf_op jit(solution)/shard_map/finish_stage/pallas_call | solution.py:1991

commit v9 on v8

--- a/solution.py
+++ b/solution.py
@@ -117,8 +117,8 @@
 
 
 class LineSum:
-    def __init__(self, at, pout, own, din, uin, sems, paced=False):
-        self.paced = paced
+    def __init__(self, at, pout, own, din, uin, sems, paced=False, defer=False):
+        self.paced, self.defer = paced, defer
         self.at, self.pout, self.own, self.din, self.uin = at, pout, own, din, uin
         self.po_s, self.po_r, self.d_s, self.d_r, self.u_s, self.u_r = sems
         self.slots, self.pieces = pout.shape[0], own.shape[1]
@@ -194,13 +194,13 @@
             def _():
                 self.down_copy(sd, i).wait_recv()
                 self.add(self.own.at[sd, i], self.din.at[sd, i])
-                self.down_copy(sd, i).start()
+                pl.when((p > 1) if self.defer else True)(self.down_copy(sd, i).start)
 
             @pl.when((su >= 0) & (su < n - 1 - p) & at.has_below)
             def _():
                 self.up_copy(su, i).wait_recv()
                 self.add(self.own.at[n - 1 - su, i], self.uin.at[su, i])
-                self.up_copy(su, i).start()
+                pl.when((p < n - 2) if self.defer else True)(self.up_copy(su, i).start)
 
             if self.paced:
 
@@ -220,11 +220,13 @@
 
         @pl.loop(0, self.pieces)
         def _(i):
-            @pl.when(at.has_above)
+            inner = at.has_above & at.has_below
+
+            @pl.when(inner if self.defer else at.has_above)
             def _():
                 self.down_copy(p, i).wait_recv()
 
-            @pl.when(at.has_below)
+            @pl.when(inner if self.defer else at.has_below)
             def _():
                 self.up_copy(n - 1 - p, i).wait_recv()
 
@@ -245,11 +247,11 @@
 
             @pl.when(jnp.logical_not(at.has_below))
             def _():
-                close([down])
+                close([] if self.defer else [down])
 
             @pl.when(jnp.logical_not(at.has_above))
             def _():
-                close([up])
+                close([] if self.defer else [up])
 
             pltpu.make_async_copy(out.at[i], sink.at[i], sems.at[i]).start()
 
@@ -266,12 +268,14 @@
         for s in range(n - 1):
             done = self.paced and s < n - 2
 
-            @pl.when((s < p) & (at.has_above if done else at.has_below))
+            last = self.defer
+
+            @pl.when((s < p) & (p > 1 if last else at.has_above if done else at.has_below))
             def _():
                 for i in range(self.pieces):
                     self.down_copy(s, i).wait_send()
 
-            @pl.when((s < n - 1 - p) & (at.has_below if done else at.has_above))
+            @pl.when((s < n - 1 - p) & (p < n - 2 if last else at.has_below if done else at.has_above))
             def _():
                 for i in range(self.pieces):
                     self.up_copy(s, i).wait_send()
@@ -499,8 +503,8 @@
 
 
 class LineGather:
-    def __init__(self, at, pieces, shard, spot, sems, pre=0):
-        self.pre = pre
+    def __init__(self, at, pieces, shard, spot, sems, pre=0, wide=False):
+        self.pre, self.wide = pre, wide
         self.at, self.pieces, self.shard, self.spot = at, pieces, shard, spot
         self.d_s, self.d_r, self.u_s, self.u_r, self.c_s, self.c_r, self.here = sems
 
@@ -528,13 +532,14 @@
 
     def start(self):
         at = self.at
+        down, up = self.late()
         for i in range(self.pre, self.pieces):
 
-            @pl.when(at.has_below)
+            @pl.when(down)
             def _():
                 self.down_copy(0, i, True).start()
 
-            @pl.when(at.has_above)
+            @pl.when(up)
             def _():
                 self.up_copy(0, i, True).start()
 
@@ -543,6 +548,12 @@
             if self.shard:
                 self.keep(i).start()
 
+    def late(self):
+        at = self.at
+        if self.wide:
+            return at.p == 1, at.p == at.n - 2
+        return at.has_below, at.has_above
+
     def slot(self, h, i):
         at = self.at
         n, p = at.n, at.p
@@ -570,12 +581,30 @@
     def stage(self, h):
         @pl.loop(self.pre if h == 1 else 0, self.pieces)
         def _(i):
-            self.slot(h, i)
+            if h == 1 and self.wide:
+                self.slot_ends(i)
+            else:
+                self.slot(h, i)
+
+    def slot_ends(self, i):
+        at = self.at
+
+        @pl.when(at.p == 0)
+        def _():
+            self.down_copy(0, i).wait_recv()
+            self.core_copy(1, i).start()
+
+        @pl.when(at.p == at.n - 1)
+        def _():
+            self.up_copy(0, i).wait_recv()
+            self.core_copy(at.n - 2, i).start()
 
     def early(self, i, above, below):
         at = self.at
-
-        @pl.when(at.has_above)
+        both = at.has_above & at.has_below
+        everyone = i < self.pre
+
+        @pl.when(at.has_above if everyone else both)
         def _():
             b = 2 * at.p + 2 + at.c
             dst = self.spot(b, i)
@@ -587,7 +616,7 @@
             z = at.p + 1
             remote(above, dst, self.c_s.at[z, i], self.c_r.at[z, i], at.core).start()
 
-        @pl.when(at.has_below)
+        @pl.when(at.has_below if everyone else both)
         def _():
             b = 2 * at.p - 2 + at.c
             dst = self.spot(b, i)
@@ -606,19 +635,20 @@
         at = self.at
         n, p = at.n, at.p
 
+        down, up = self.late()
+
         @pl.loop(0, self.pieces)
         def _(i):
             for h in range(n):
-
-                sent = (i >= self.pre) if h == 0 else True
-
-                @pl.when((p + h < n) & at.has_below & sent)
+                own = h == 0
+
+                @pl.when((down & (i >= self.pre)) if own else ((p + h < n) & at.has_below))
                 def _():
-                    self.down_copy(h, i, h == 0).wait_send()
-
-                @pl.when((p - h >= 0) & at.has_above & sent)
+                    self.down_copy(h, i, own).wait_send()
+
+                @pl.when((up & (i >= self.pre)) if own else ((p - h >= 0) & at.has_above))
                 def _():
-                    self.up_copy(h, i, h == 0).wait_send()
+                    self.up_copy(h, i, own).wait_send()
 
             for z in range(n):
                 self.core_copy(z, i).wait_send()
@@ -642,21 +672,34 @@
 
 
 class Presend:
-    def __init__(self, at, src, got, sems):
+    def __init__(self, at, src, got, sems, narrow):
         s, r = sems
-        self.at = at
-        self.down = remote(src, got.at[0], s.at[0], r.at[0], at.below)
-        self.up = remote(src, got.at[1], s.at[1], r.at[1], at.above)
+        wide = src.shape[1]
+        n, p = at.n, at.p
+        self.sends, self.comes = [], []
+        for width in sorted({narrow, wide}):
+            cols = pl.ds(0, width)
+            down = remote(src.at[:, cols], got.at[0, :, cols], s.at[0], r.at[0], at.below)
+            up = remote(src.at[:, cols], got.at[1, :, cols], s.at[1], r.at[1], at.above)
+            if narrow == wide:
+                whens = at.has_below, at.has_above, at.has_above, at.has_below
+            elif width == narrow:
+                whens = p == 1, p == n - 2, p == 0, p == n - 1
+            else:
+                inner = at.has_above & at.has_below
+                whens = p > 1, p < n - 2, inner, inner
+            self.sends += [(whens[0], down), (whens[1], up)]
+            self.comes += [(whens[2], down), (whens[3], up)]
 
     def start(self):
-        pl.when(self.at.has_below)(self.down.start)
-        pl.when(self.at.has_above)(self.up.start)
+        for when, copy in self.sends:
+            pl.when(when)(copy.start)
 
     def finish(self):
-        pl.when(self.at.has_above)(self.down.wait_recv)
-        pl.when(self.at.has_below)(self.up.wait_recv)
-        pl.when(self.at.has_below)(self.down.wait_send)
-        pl.when(self.at.has_above)(self.up.wait_send)
+        for when, copy in self.comes:
+            pl.when(when)(copy.wait_recv)
+        for when, copy in self.sends:
+            pl.when(when)(copy.wait_send)
 
 
 def attend_rows(qkv, out, seq, hh, count, head):
@@ -833,7 +876,7 @@
     outs[-1].start()
     for h in range(2, n - 1):
         last.slot(h, 0)
-    ahead = Presend(at, gush.at[:, pl.ds(0, 2 * half * AHEAD)], gpre_ref, rest[21:23])
+    ahead = Presend(at, gush.at[:, pl.ds(0, 2 * half * AHEAD)], gpre_ref, rest[21:23], 2 * half * AHEAD)
     ahead.start()
     heads = hh // HD
 
@@ -1018,9 +1061,7 @@
     for i in range(AHEAD):
         pl.when(at.has_above)(place(0, i).wait)
         pl.when(at.has_below)(place(1, i).wait)
-    ahead = Presend(
-        at, dnsh_hbm.at[:, pl.ds(0, width // 2 * DOWN_AHEAD)], dpre_ref, rest[15:17]
-    )
+    ahead = Presend(at, dnsh_hbm, dpre_ref, rest[15:17], width // 2 * DOWN_AHEAD)
     ahead.start()
 
     pair = 2 * chunk
@@ -1112,7 +1153,7 @@
             jax.ShapeDtypeStruct((part, d), F32),
             jax.ShapeDtypeStruct((seq, wide), BF),
             jax.ShapeDtypeStruct((seq, wide // 2), BF),
-            jax.ShapeDtypeStruct((2, chunk, width // 2 * DOWN_AHEAD), BF),
+            jax.ShapeDtypeStruct((2, chunk, wide // 2), BF),
         ],
         in_specs=[vm, hbm, hbm, hbm, hbm, hbm, vm],
         out_specs=[hbm] * 6,
@@ -1155,6 +1196,7 @@
     rs_ref,
     ft_ref,
     ggu_ref,
+    pend_ref,
     inner,
     gu,
     cot,
@@ -1174,12 +1216,12 @@
 ):
     at = Place(n_dp, n_mp)
     n, p = at.n, at.p
-    line = LineSum(at, *rest[0:4], rest[4:10])
+    line = LineSum(at, *rest[0:4], rest[4:10], defer=True)
     sems = rest[10:17]
     chunk, ff = sh_hbm.shape
     pieces = sems[6].shape[0]
     width = ff // pieces
-    gather = LineGather(at, pieces, None, rows_spot(dn, chunk, width), sems, DOWN_AHEAD)
+    gather = LineGather(at, pieces, None, rows_spot(dn, chunk, width), sems, DOWN_AHEAD, True)
     pair = 2 * chunk
     def cot_copy(k):
         cols = pl.ds(pl.multiple_of(order_of(k, at) * pair, pair), pair)
@@ -1195,14 +1237,19 @@
     )
     own.start()
 
-    def pre_copy(side):
+    inside = at.has_above & at.has_below
+
+    def pre_copy(side, i):
         b = at.dp + (2 if side == 0 else -2)
-        rows = pl.ds(pl.multiple_of(b * chunk, chunk), chunk)
-        dst = dn.at[rows, pl.ds(0, width * DOWN_AHEAD)]
-        return pltpu.make_async_copy(dpre_hbm.at[side], dst, dp_s.at[side])
-
-    pl.when(at.has_above)(pre_copy(0).start)
-    pl.when(at.has_below)(pre_copy(1).start)
+        piece = dpre_hbm.at[side, :, pl.ds(i * width, width)]
+        return pltpu.make_async_copy(piece, gather.spot(b, i), dp_s.at[side, i])
+
+    def pre_whens(i):
+        return (at.has_above, at.has_below) if i < DOWN_AHEAD else (inside, inside)
+
+    for i in range(pieces):
+        for side in range(2):
+            pl.when(pre_whens(i)[side])(pre_copy(side, i).start)
     cot_copy(0).start()
     for i in range(pieces):
         in_copy(i).start()
@@ -1212,9 +1259,9 @@
     enter(at)
     own.wait()
     gather.start()
-    pl.when(at.has_above)(pre_copy(0).wait)
-    pl.when(at.has_below)(pre_copy(1).wait)
-    for i in range(DOWN_AHEAD):
+    for i in range(pieces):
+        for side in range(2):
+            pl.when(pre_whens(i)[side])(pre_copy(side, i).wait)
         gather.early(i, gather.spot(at.dp + 2, i), gather.spot(at.dp - 2, i))
 
     def run(e):
@@ -1261,8 +1308,23 @@
         ftb[0] = dot(inner[...], dn[rows_of(z), :], NT).astype(BF)
         ft_copy(z, 0).start()
 
+    def blocks(h):
+        @pl.when(p + h < n)
+        def _():
+            grads(p + h, False)
+            branch(p + h, False)
+
+        @pl.when(p - h >= 0)
+        def _():
+            grads(p - h, False)
+            branch(p - h, False)
+
+    gather.stage(1)
     grads(p, True)
     branch(p, True)
+    line.slot(0)
+    if n > 3:
+        gather.stage(2)
     load_gu.wait()
     half = width
 
@@ -1284,20 +1346,12 @@
             gu[rs, gcols] = (u * sg * (1.0 + g * (1.0 - sg))).astype(BF)
             gu[rs, ucols] = (g * sg).astype(BF)
 
-    for h in range(1, n - 1):
-        gather.stage(h)
-
-        @pl.when(p + h < n)
-        def _():
-            grads(p + h, False)
-            branch(p + h, False)
-
-        @pl.when(p - h >= 0)
-        def _():
-            grads(p - h, False)
-            branch(p - h, False)
-
+    blocks(1)
+    for h in range(2, n - 1):
         line.slot(h - 1)
+        if h + 1 < n - 1:
+            gather.stage(h + 1)
+        blocks(h)
 
     gather.stage(n - 1)
 
@@ -1335,6 +1389,11 @@
         branch(0, False)
 
     stores = line.final(res, rs_ref, rs_s)
+    keep_low = pltpu.make_async_copy(line.own.at[0], pend_ref, dn_s.at[0])
+    keep_high = pltpu.make_async_copy(line.own.at[n - 1], pend_ref, dn_s.at[0])
+    pl.when(p == 1)(keep_low.start)
+    pl.when(p == n - 2)(keep_high.start)
+    pl.when((p == 1) | (p == n - 2))(keep_low.wait)
     for i in range(pieces):
         gg_copy(i).wait()
     ft_copy(p, 0).wait()
@@ -1356,9 +1415,10 @@
             jax.ShapeDtypeStruct((PIECES, chunk, ff // PIECES), BF),
             jax.ShapeDtypeStruct((seq, d), BF),
             jax.ShapeDtypeStruct((seq, 2 * ff), BF),
+            jax.ShapeDtypeStruct((PIECES, chunk, ff // PIECES), BF),
         ],
         in_specs=[hbm] * 5,
-        out_specs=[hbm] * 3,
+        out_specs=[hbm] * 4,
         scratch_shapes=[
             pltpu.VMEM((seq, ff), BF),
             pltpu.VMEM((seq, 2 * ff), BF),
@@ -1367,7 +1427,7 @@
             pltpu.VMEM((seq, ff), F32),
             pltpu.VMEM((1, seq, 2 * chunk), BF),
             pltpu.VMEM((PIECES, chunk, ff // PIECES), BF),
-            dma((2,)),
+            dma((2, PIECES)),
             dma((1,)),
             dma((n,)),
             dma((PIECES,)),
@@ -1707,11 +1767,14 @@
     att_hbm,
     x_hbm,
     gh_hbm,
+    pend_hbm,
+    part_hbm,
     gain_ref,
     gmid_ref,
     rs_ref,
     grad_ref,
     gains_ref,
+    rsd_ref,
     rhs,
     aw,
     nin,
@@ -1721,6 +1784,9 @@
     gh,
     res,
     rs_s,
+    pbuf,
+    dbuf,
+    pd_s,
     loads,
     pout,
     own,
@@ -1762,6 +1828,7 @@
                 (low_hbm, low),
                 (x_hbm.at[part_rows(at, part), :], x),
                 (gh_hbm, gh),
+                (part_hbm, dbuf),
             ]
         )
     ]
@@ -1772,6 +1839,9 @@
     quad = QuadSum(at, t, r, (q1, q2))
     line = LineSum(at, pout, own, din, uin, (po_s, po_r, d_s, d_r, u_s, u_r), True)
     gather = QuadGather(at, gown, grad_ref, (g1, g2, g3))
+    n = at.n
+    low_end = remote(pend_hbm, pbuf, pd_s.at[0], pd_s.at[1], at.below)
+    high_end = remote(pend_hbm, pbuf, pd_s.at[0], pd_s.at[1], at.above)
     copies[0].wait()
     copies[1].wait()
 
@@ -1815,7 +1885,6 @@
         else:
             line.other(k, tile)
 
-    n = at.n
     devs = [at.core] + [at.fold(b) for b in bits] + [at.peer(b) for b in at.bits]
 
     def fold_copy(b):
@@ -1847,6 +1916,8 @@
     quad.turn()
     for b in range(1, len(bits)):
         fold_next(b)
+    pl.when(at.p == 1)(low_end.start)
+    pl.when(at.p == n - 2)(high_end.start)
     line.slot(0)
     load_x.wait()
     copies[6].wait()
@@ -1883,7 +1954,20 @@
         for j in range(per_row):
             gsum[i, j * fold : (j + 1) * fold] = fold_out[len(devs), i * per_row + j]
     gains_ref[...] = gsum[:, pl.ds(pl.multiple_of(at.dp * chunk, chunk), chunk)]
-    stores = line.final(res, rs_ref, rs_s)
+    copies[7].wait()
+
+    @pl.when((at.p == 0) | (at.p == n - 1))
+    def _():
+        low_end.wait_recv()
+
+        @pl.loop(0, 4)
+        def _(i):
+            dbuf[i] = (dbuf[i].astype(F32) + pbuf[i].astype(F32)).astype(BF)
+
+    store = pltpu.make_async_copy(dbuf, rsd_ref, pd_s.at[2])
+    store.start()
+    stores = line.final(res, rs_ref, rs_s) + [store]
+    pl.when((at.p == 1) | (at.p == n - 2))(low_end.wait_send)
     gather.finish()
     for cp in stores:
         cp.wait()
@@ -1893,7 +1977,7 @@
         fold_copy(b).wait_send()
 
 
-def last_stage(n_dp, n_mp, dqkv, aw, nin, low, att, x, gh, gain, gmid):
+def last_stage(n_dp, n_mp, dqkv, aw, nin, low, att, x, gh, pend, rs_down, gain, gmid):
     seq, hh = att.shape
     d = aw.shape[0]
     n, part, chunk = n_dp // 2, seq // n_mp, d // n_dp
@@ -1907,9 +1991,10 @@
             jax.ShapeDtypeStruct((4, chunk, hh), BF),
             jax.ShapeDtypeStruct((seq, d), BF),
             jax.ShapeDtypeStruct((8, chunk), F32),
+            jax.ShapeDtypeStruct(rs_down.shape, BF),
         ],
-        in_specs=[anyspace] * 7 + [vm] * 2,
-        out_specs=[anyspace, anyspace, vm],
+        in_specs=[anyspace] * 9 + [vm] * 2,
+        out_specs=[anyspace, anyspace, vm, anyspace],
         scratch_shapes=[
             pltpu.VMEM((seq, 4 * hh), BF),
             pltpu.VMEM((d, 3 * hh), BF),
@@ -1920,7 +2005,10 @@
             pltpu.VMEM((part, d), F32),
             pltpu.VMEM((4, chunk, hh), BF),
             dma((4,)),
-            dma((7,)),
+            pltpu.VMEM(rs_down.shape, BF),
+            pltpu.VMEM(rs_down.shape, BF),
+            dma((3,)),
+            dma((8,)),
         ]
         + line_sum_scratch(n, 4, chunk, hh)
         + quad_sum_scratch(n_mp, part, d // 2, None, 2)
@@ -1936,7 +2024,7 @@
             collective_id=5, has_side_effects=True, vmem_limit_bytes=VMEM_LIMIT
         ),
         name="last_stage",
-    )(dqkv, aw, nin, low, att, x, gh, gain, gmid)
+    )(dqkv, aw, nin, low, att, x, gh, pend, rs_down, gain, gmid)
 
 
 def finish_kernel(
@@ -2045,12 +2133,24 @@
     gu_w, normed_mid, hidden, gu, inner, down_pre = gate_stage(
         n_dp, n_mp, attended, attn_w, gu_shard, gu_pre, down_shard, inputs, gains
     )
-    rs_down, ffn_terms, ggu = down_stage(n_dp, n_mp, inner, gu, grad_ffn, down_shard, down_pre)
+    down_part, ffn_terms, ggu, down_pend = down_stage(n_dp, n_mp, inner, gu, grad_ffn, down_shard, down_pre)
     rs_gu, grad_low, layer_out, grad_hidden, g_gain_mid, dqkv = mid_stage(
         n_dp, n_mp, ggu, gu_w, normed_mid, ffn_terms, grad_ffn, qkv, attn_w, counts, hidden, gains
     )
-    rs_attn, grad_low_in, g_gains = last_stage(
-        n_dp, n_mp, dqkv, attn_w, normed_in, grad_low, attended, inputs, grad_hidden, gains, g_gain_mid
+    rs_attn, grad_low_in, g_gains, rs_down = last_stage(
+        n_dp,
+        n_mp,
+        dqkv,
+        attn_w,
+        normed_in,
+        grad_low,
+        attended,
+        inputs,
+        grad_hidden,
+        down_pend,
+        down_part,
+        gains,
+        g_gain_mid,
     )
     lay, grad_x, g_gate, g_up, g_down, g_q, g_k, g_v, g_o, g_attn, g_ffn = finish_stage(
         grad_low_in, layer_out, rs_gu, rs_down, rs_attn, g_gains

time: 581 us -> 570 us (0.981)
  Pallas kernels: 570 us -> 560 us
    pallas_call x1, Pallas kernels: 92.8 us -> 75.5 us  [down_stage(): pl.pallas_call(functools.partial(down_kernel, n_dp, n_mp), out_shape=[jax...]
    pallas_call x1, Pallas kernels: 85.4 us -> 92.8 us  [last_stage(): pl.pallas_call(functools.partial(last_kernel, n_dp, n_mp), out_shape=[jax...]
where the time goes in v9:
time: 570 us; the launch traced here: 562 us
  Pallas kernels  560 us (98%)
    pallas_call x1, Pallas kernels, mid_stage(): pl.pallas_call(functools.partial(mid_kernel, n_dp, n_mp), out_shape=[jax....  148 us
    pallas_call x1, Pallas kernels, gate_stage(): pl.pallas_call(functools.partial(gate_kernel, n_dp, n_mp), out_shape=[jax...  141 us
    pallas_call x1, Pallas kernels, last_stage(): pl.pallas_call(functools.partial(last_kernel, n_dp, n_mp), out_shape=[jax...  92.8 us
    pallas_call x1, Pallas kernels, attn_stage(): pl.pallas_call(functools.partial(attn_kernel, n_dp, n_mp), out_shape=[jax...  89.1 us
    pallas_call x1, Pallas kernels, down_stage(): pl.pallas_call(functools.partial(down_kernel, n_dp, n_mp), out_shape=[jax...  75.5 us
    pallas_call x1, Pallas kernels, finish_stage(): pl.pallas_call(finish_kernel, grid=(2 * steps,), in_specs=[row, row, two,...  13.9 us

profile of v9, /device:TPU:0, one launch (start us, length us, event | category | flops | bytes accessed | tf_op | source)
XLA Modules:
  0.0 562.3 jit_solution(16857857388086158932)
XLA Ops:
  1.3 89.1 %attn_stage.1 = (bf16[2048,2048]{1,0:T(8,128)(2,1)}, bf16[1024,1536]{1,0:T(8,128)(2,1)}, bf16[1024,512]{1,0:T(8,128)(2,1)}, bf16[1024,2048]{1,0:T(8,128)(2,1)}, ...) custom-call(s32[1]{0:T(128)S(6)} %copy.23.count_ref, ...), custom_call_target="tpu_custom_call" | custom-call | tf_op jit(solution)/shard_map/attn_stage/pallas_call | solution.py:923
  90.4 141.1 %gate_stage.1 = (bf16[2048,4096]{1,0:T(8,128)(2,1)}, bf16[1024,2048]{1,0:T(8,128)(2,1)}, f32[256,2048]{1,0:T(8,128)}, bf16[1024,4096]{1,0:T(8,128)(2,1)}, bf16[1...) custom-call(bf16[1024,512]{1,0:T(8,128)(2,1)} %get-tuple-element.51.att_ref.att_hbm, ...), custom_call_target="tpu_custom_call" | custom-call | tf_op jit(solution)/shard_map/gate_stage/pallas_call | solution.py:1148
  231.5 75.5 %down_stage.1 = (bf16[4,256,512]{2,1,0:T(8,128)(2,1)}, bf16[1024,2048]{1,0:T(8,128)(2,1)}, bf16[1024,4096]{1,0:T(8,128)(2,1)}, bf16[4,256,512]{2,1,0:T(8,128)(2,1)}) custom-call(bf16[1024,2048]{1,0:T(8,128)(2,1)} %get-tuple-element.57.inner_hbm, bf16[1024,4096]{1,0:T(8,128)(2,1)} %get-tuple-element.58.gu_hbm, bf16[1024,2048]{1,0:T(8,128)(2,1)} %get-tuple-element.59.cot_hbm, ...), custom_call_target="tpu_custom_call" | custom-call | tf_op jit(solution)/shard_map/down_stage/pallas_call | solution.py:1412
  307.0 148.1 %mid_stage.1 = (bf16[4,256,1024]{2,1,0:T(8,128)(2,1)}, bf16[1024,2048]{1,0:T(8,128)(2,1)}, bf16[1024,2048]{1,0:T(8,128)(2,1)}, f32[256,2048]{1,0:T(8,128)}, f32[...) custom-call(bf16[1024,4096]{1,0:T(8,128)(2,1)} %get-tuple-element.61.ggu_hbm, bf16[2048,4096]{1,0:T(8,128)(2,1)} %get-tuple-element.62.gw_hbm, ...), custom_call_target="tpu_custom_call" | custom-call | tf_op jit(solution)/shard_map/mid_stage/pallas_call | solution.py:1720
  455.1 92.8 %last_stage.1 = (bf16[4,256,512]{2,1,0:T(8,128)(2,1)}, bf16[1024,2048]{1,0:T(8,128)(2,1)}, f32[8,256]{1,0:T(8,128)}, bf16[4,256,512]{2,1,0:T(8,128)(2,1)}) custom-call(bf16[1024,1536]{1,0:T(8,128)(2,1)} %get-tuple-element.67.dqkv_hbm, bf16[2048,2048]{1,0:T(8,128)(2,1)} %get-tuple-element.52.aw_hbm, bf16[1024,2048]{1,0:T(8,128)(2,1)} %get-tuple-element.68.nin_hbm, ...), custom_call_target="tpu_custom_call" | custom-call | tf_op jit(solution)/shard_map/last_stage/pallas_call | solution.py:1988
  547.9 13.9 %finish_stage.1 = (bf16[1024,2048]{1,0:T(8,128)(2,1)}, f32[1024,2048]{1,0:T(8,128)}, f32[256,2048]{1,0:T(8,128)}, f32[256,2048]{1,0:T(8,128)}, f32[2048,256]{1,0...) custom-call(bf16[1024,2048]{1,0:T(8,128)(2,1)} %get-tuple-element.74, ...), custom_call_target="tpu_custom_call" | custom-call | tf_op jit(solution)/shard_map/finish_stage/pallas_call | solution.py:2079

commit v10 on v9

--- a/solution.py
+++ b/solution.py
@@ -182,13 +182,13 @@
             rs = pl.ds(pl.multiple_of(b * 64, 64), 64)
             dst[rs, :] = (dst[rs, :].astype(F32) + src[rs, :].astype(F32)).astype(BF)
 
-    def slot(self, t):
+    def slot(self, t, first=0, end=None):
         at = self.at
         n, p = at.n, at.p
         sd = t - (n - 2 - p)
         su = t - (p - 1)
 
-        @pl.loop(0, self.pieces)
+        @pl.loop(first, end or self.pieces)
         def _(i):
             @pl.when((sd >= 0) & (sd < p) & at.has_above)
             def _():
@@ -1572,7 +1572,9 @@
     for cp in lay.loads:
         cp.wait()
     lay.turn()
+    line.slot(0, 0, 2)
     terms(1)
+    line.slot(0, 2, 3)
     for e in range(4, 2 * n):
         run(e)
     lay.arrive()
@@ -1586,7 +1588,7 @@
             gather_lay.own[half, rs, :] = (h + lay.total(half, rs)).astype(BF)
 
     gather_lay.start([0])
-    line.slot(0)
+    line.slot(0, 3)
     per = half_cols // hh
     blocks_d = 2 * half_cols // part
     wo_spot = [(e // per // (n_mp // 2), e // per % (n_mp // 2), e % per) for e in range(blocks_d)]
@@ -1632,6 +1634,7 @@
         line.slot(s)
     gather_low.forward()
     gather_lay.start(range(1, gather_lay.levels))
+    gather_lay.forward()
     gather_low.finish()
     load_low = pltpu.make_async_copy(low_ref, space.at[:, pl.ds(0, 2 * half_cols)], load_s.at[3])
     load_low.start()
@@ -1686,9 +1689,7 @@
             wt[i // 2, :, at_cols((i % 2) * (wide // 2) + 2 * hh)] = dva[rows, :].astype(BF)
 
     heads = hh // HD
-    pl.loop(0, heads // 2)(back)
-    gather_lay.forward()
-    pl.loop(heads // 2, heads)(back)
+    pl.loop(0, heads)(back)
     stores = [
         pltpu.make_async_copy(
             wt.at[i // 2, :, pl.ds((i % 2) * (wide // 2), 3 * hh)],

time: 570 us -> 562 us (0.986)
  Pallas kernels: 560 us -> 552 us
    pallas_call x1, Pallas kernels: 92.8 us -> 84.6 us  [last_stage(): pl.pallas_call(functools.partial(last_kernel, n_dp, n_mp), out_shape=[jax...]
where the time goes in v10:
time: 562 us; the launch traced here: 554 us
  Pallas kernels  552 us (98%)
    pallas_call x1, Pallas kernels, mid_stage(): pl.pallas_call(functools.partial(mid_kernel, n_dp, n_mp), out_shape=[jax....  148 us
    pallas_call x1, Pallas kernels, gate_stage(): pl.pallas_call(functools.partial(gate_kernel, n_dp, n_mp), out_shape=[jax...  141 us
    pallas_call x1, Pallas kernels, attn_stage(): pl.pallas_call(functools.partial(attn_kernel, n_dp, n_mp), out_shape=[jax...  89.1 us
    pallas_call x1, Pallas kernels, last_stage(): pl.pallas_call(functools.partial(last_kernel, n_dp, n_mp), out_shape=[jax...  84.6 us
    pallas_call x1, Pallas kernels, down_stage(): pl.pallas_call(functools.partial(down_kernel, n_dp, n_mp), out_shape=[jax...  75.5 us
    pallas_call x1, Pallas kernels, finish_stage(): pl.pallas_call(finish_kernel, grid=(2 * steps,), in_specs=[row, row, two,...  13.9 us

profile of v10, /device:TPU:0, one launch (start us, length us, event | category | flops | bytes accessed | tf_op | source)
XLA Modules:
  0.0 554.1 jit_solution(15844150729649282861)
XLA Ops:
  1.3 89.1 %attn_stage.1 = (bf16[2048,2048]{1,0:T(8,128)(2,1)}, bf16[1024,1536]{1,0:T(8,128)(2,1)}, bf16[1024,512]{1,0:T(8,128)(2,1)}, bf16[1024,2048]{1,0:T(8,128)(2,1)}, ...) custom-call(s32[1]{0:T(128)S(6)} %copy.23.count_ref, ...), custom_call_target="tpu_custom_call" | custom-call | tf_op jit(solution)/shard_map/attn_stage/pallas_call | solution.py:923
  90.4 141.1 %gate_stage.1 = (bf16[2048,4096]{1,0:T(8,128)(2,1)}, bf16[1024,2048]{1,0:T(8,128)(2,1)}, f32[256,2048]{1,0:T(8,128)}, bf16[1024,4096]{1,0:T(8,128)(2,1)}, bf16[1...) custom-call(bf16[1024,512]{1,0:T(8,128)(2,1)} %get-tuple-element.51.att_ref.att_hbm, ...), custom_call_target="tpu_custom_call" | custom-call | tf_op jit(solution)/shard_map/gate_stage/pallas_call | solution.py:1148
  231.5 75.5 %down_stage.1 = (bf16[4,256,512]{2,1,0:T(8,128)(2,1)}, bf16[1024,2048]{1,0:T(8,128)(2,1)}, bf16[1024,4096]{1,0:T(8,128)(2,1)}, bf16[4,256,512]{2,1,0:T(8,128)(2,1)}) custom-call(bf16[1024,2048]{1,0:T(8,128)(2,1)} %get-tuple-element.57.inner_hbm, bf16[1024,4096]{1,0:T(8,128)(2,1)} %get-tuple-element.58.gu_hbm, bf16[1024,2048]{1,0:T(8,128)(2,1)} %get-tuple-element.59.cot_hbm, ...), custom_call_target="tpu_custom_call" | custom-call | tf_op jit(solution)/shard_map/down_stage/pallas_call | solution.py:1412
  307.0 148.1 %mid_stage.1 = (bf16[4,256,1024]{2,1,0:T(8,128)(2,1)}, bf16[1024,2048]{1,0:T(8,128)(2,1)}, bf16[1024,2048]{1,0:T(8,128)(2,1)}, f32[256,2048]{1,0:T(8,128)}, f32[...) custom-call(bf16[1024,4096]{1,0:T(8,128)(2,1)} %get-tuple-element.61.ggu_hbm, bf16[2048,4096]{1,0:T(8,128)(2,1)} %get-tuple-element.62.gw_hbm, ...), custom_call_target="tpu_custom_call" | custom-call | tf_op jit(solution)/shard_map/mid_stage/pallas_call | solution.py:1721
  455.1 84.6 %last_stage.1 = (bf16[4,256,512]{2,1,0:T(8,128)(2,1)}, bf16[1024,2048]{1,0:T(8,128)(2,1)}, f32[8,256]{1,0:T(8,128)}, bf16[4,256,512]{2,1,0:T(8,128)(2,1)}) custom-call(bf16[1024,1536]{1,0:T(8,128)(2,1)} %get-tuple-element.67.dqkv_hbm, bf16[2048,2048]{1,0:T(8,128)(2,1)} %get-tuple-element.52.aw_hbm, bf16[1024,2048]{1,0:T(8,128)(2,1)} %get-tuple-element.68.nin_hbm, ...), custom_call_target="tpu_custom_call" | custom-call | tf_op jit(solution)/shard_map/last_stage/pallas_call | solution.py:1989
  539.7 13.9 %finish_stage.1 = (bf16[1024,2048]{1,0:T(8,128)(2,1)}, f32[1024,2048]{1,0:T(8,128)}, f32[256,2048]{1,0:T(8,128)}, f32[256,2048]{1,0:T(8,128)}, f32[2048,256]{1,0...) custom-call(bf16[1024,2048]{1,0:T(8,128)(2,1)} %get-tuple-element.74, ...), custom_call_target="tpu_custom_call" | custom-call | tf_op jit(solution)/shard_map/finish_stage/pallas_call | solution.py:2080

commit v11 on v10

--- a/solution.py
+++ b/solution.py
@@ -1850,7 +1850,7 @@
     fold = fold_out.shape[2]
     per_row = d // fold
 
-    def terms(q):
+    def terms(q, gains=True):
         rs = pl.ds(pl.multiple_of(q * part, part), part)
         width = 512
 
@@ -1860,14 +1860,14 @@
                 d0 = pl.multiple_of(half * half_cols + i * width, width)
                 v = dot(rhs[rs, 0 : 3 * hh], aw[pl.ds(d0, width), :], NT)
                 t[half, q, :, pl.ds(pl.multiple_of(i * width, width), width)] = v.astype(BF)
-                u = v * nin[rs, pl.ds(d0, width)].astype(F32)
-                gsum[0:1, pl.ds(d0, width)] += jnp.sum(u, axis=0, keepdims=True)
-
-    gsum[...] = jnp.zeros_like(gsum)
+                if gains:
+                    u = v * nin[rs, pl.ds(d0, width)].astype(F32)
+                    gsum[0:1, pl.ds(d0, width)] += jnp.sum(u, axis=0, keepdims=True)
+
+    masks = quad.masks()
+    terms(at.quarter(masks[0]), False)
+    quad.offer(masks[0])
     copies[2].wait()
-    masks = quad.masks()
-    terms(at.quarter(masks[0]))
-    quad.offer(masks[0])
     for cp in copies[3:5]:
         cp.wait()
     load_x = copies[5]
@@ -1899,6 +1899,11 @@
 
     run(0, 0)
     run(0, 1)
+    first = pl.ds(pl.multiple_of(at.quarter(masks[0]) * part, part), part)
+    for half in range(2):
+        cols = slice(half * half_cols, (half + 1) * half_cols)
+        u = t[half, at.quarter(masks[0])].astype(F32) * nin[first, cols].astype(F32)
+        gsum[0:1, cols] = jnp.sum(u, axis=0, keepdims=True)
     for mask in masks[1:]:
         terms(at.quarter(mask))
         quad.offer(mask)
@@ -2052,13 +2057,9 @@
     half = gate_out.shape[1]
     gate_out[...] = gu_ref[0, :, :half].astype(F32)
     up_out[...] = gu_ref[0, :, half:].astype(F32)
-    step = pl.program_id(0)
-
-    @pl.when(lax.rem(step, 2) == 0)
-    def _():
-        down_out[...] = down_ref[0].T.astype(F32)
-
-    @pl.when(step == 0)
+    down_out[...] = down_ref[0].T.astype(F32)
+
+    @pl.when(pl.program_id(0) == 0)
     def _():
         for i, ref in enumerate((q_out, k_out, v_out)):
             ref[...] = attn_ref[i].astype(F32)
@@ -2071,17 +2072,16 @@
     seq, d = low.shape
     steps, chunk, wide = gu.shape
     width, hh = down.shape[2], attn.shape[2]
-    row = pl.BlockSpec((seq // (2 * steps), d), lambda i: (i, 0))
+    row = pl.BlockSpec((seq // steps, d), lambda i: (i, 0))
     fixed = lambda *shape: pl.BlockSpec(shape, lambda i: (0,) * len(shape))
-    two = pl.BlockSpec((1, chunk // 2, wide), lambda i: (i // 2, i % 2, 0))
-    piece = pl.BlockSpec((1, chunk, width), lambda i: (i // 2, 0, 0))
-    cols = pl.BlockSpec((chunk // 2, wide // 2), lambda i: (i % 2, i // 2))
+    piece = lambda w: pl.BlockSpec((1, chunk, w), lambda i: (i, 0, 0))
+    cols = pl.BlockSpec((chunk, wide // 2), lambda i: (0, i))
     f32 = lambda *shape: jax.ShapeDtypeStruct(shape, F32)
     return pl.pallas_call(
         finish_kernel,
-        grid=(2 * steps,),
-        in_specs=[row, row, two, piece, fixed(4, chunk, hh), fixed(*gains.shape)],
-        out_specs=[row, row, cols, cols, pl.BlockSpec((width, chunk), lambda i: (i // 2, 0))]
+        grid=(steps,),
+        in_specs=[row, row, piece(wide), piece(width), fixed(4, chunk, hh), fixed(*gains.shape)],
+        out_specs=[row, row, cols, cols, pl.BlockSpec((width, chunk), lambda i: (i, 0))]
         + [fixed(chunk, hh)] * 3
         + [fixed(hh, chunk)]
         + [fixed(chunk)] * 2,

time: 562 us -> 560 us (level)
  no operation moved by 1% of the time
where the time goes in v11:
time: 560 us; the launch traced here: 553 us
  Pallas kernels  551 us (98%)
    pallas_call x1, Pallas kernels, mid_stage(): pl.pallas_call(functools.partial(mid_kernel, n_dp, n_mp), out_shape=[jax....  148 us
    pallas_call x1, Pallas kernels, gate_stage(): pl.pallas_call(functools.partial(gate_kernel, n_dp, n_mp), out_shape=[jax...  141 us
    pallas_call x1, Pallas kernels, attn_stage(): pl.pallas_call(functools.partial(attn_kernel, n_dp, n_mp), out_shape=[jax...  89.1 us
    pallas_call x1, Pallas kernels, last_stage(): pl.pallas_call(functools.partial(last_kernel, n_dp, n_mp), out_shape=[jax...  84.1 us
    pallas_call x1, Pallas kernels, down_stage(): pl.pallas_call(functools.partial(down_kernel, n_dp, n_mp), out_shape=[jax...  75.5 us
    pallas_call x1, Pallas kernels, finish_stage(): pl.pallas_call(finish_kernel, grid=(steps,), in_specs=[row, row, piece(wi...  13.1 us

profile of v11, /device:TPU:0, one launch (start us, length us, event | category | flops | bytes accessed | tf_op | source)
XLA Modules:
  0.0 552.7 jit_solution(10717558654422558310)
XLA Ops:
  1.3 89.1 %attn_stage.1 = (bf16[2048,2048]{1,0:T(8,128)(2,1)}, bf16[1024,1536]{1,0:T(8,128)(2,1)}, bf16[1024,512]{1,0:T(8,128)(2,1)}, bf16[1024,2048]{1,0:T(8,128)(2,1)}, ...) custom-call(s32[1]{0:T(128)S(6)} %copy.23.count_ref, ...), custom_call_target="tpu_custom_call" | custom-call | tf_op jit(solution)/shard_map/attn_stage/pallas_call | solution.py:923
  90.4 141.1 %gate_stage.1 = (bf16[2048,4096]{1,0:T(8,128)(2,1)}, bf16[1024,2048]{1,0:T(8,128)(2,1)}, f32[256,2048]{1,0:T(8,128)}, bf16[1024,4096]{1,0:T(8,128)(2,1)}, bf16[1...) custom-call(bf16[1024,512]{1,0:T(8,128)(2,1)} %get-tuple-element.51.att_ref.att_hbm, ...), custom_call_target="tpu_custom_call" | custom-call | tf_op jit(solution)/shard_map/gate_stage/pallas_call | solution.py:1148
  231.5 75.5 %down_stage.1 = (bf16[4,256,512]{2,1,0:T(8,128)(2,1)}, bf16[1024,2048]{1,0:T(8,128)(2,1)}, bf16[1024,4096]{1,0:T(8,128)(2,1)}, bf16[4,256,512]{2,1,0:T(8,128)(2,1)}) custom-call(bf16[1024,2048]{1,0:T(8,128)(2,1)} %get-tuple-element.57.inner_hbm, bf16[1024,4096]{1,0:T(8,128)(2,1)} %get-tuple-element.58.gu_hbm, bf16[1024,2048]{1,0:T(8,128)(2,1)} %get-tuple-element.59.cot_hbm, ...), custom_call_target="tpu_custom_call" | custom-call | tf_op jit(solution)/shard_map/down_stage/pallas_call | solution.py:1412
  307.0 148.1 %mid_stage.1 = (bf16[4,256,1024]{2,1,0:T(8,128)(2,1)}, bf16[1024,2048]{1,0:T(8,128)(2,1)}, bf16[1024,2048]{1,0:T(8,128)(2,1)}, f32[256,2048]{1,0:T(8,128)}, f32[...) custom-call(bf16[1024,4096]{1,0:T(8,128)(2,1)} %get-tuple-element.61.ggu_hbm, bf16[2048,4096]{1,0:T(8,128)(2,1)} %get-tuple-element.62.gw_hbm, ...), custom_call_target="tpu_custom_call" | custom-call | tf_op jit(solution)/shard_map/mid_stage/pallas_call | solution.py:1721
  455.1 84.1 %last_stage.1 = (bf16[4,256,512]{2,1,0:T(8,128)(2,1)}, bf16[1024,2048]{1,0:T(8,128)(2,1)}, f32[8,256]{1,0:T(8,128)}, bf16[4,256,512]{2,1,0:T(8,128)(2,1)}) custom-call(bf16[1024,1536]{1,0:T(8,128)(2,1)} %get-tuple-element.67.dqkv_hbm, bf16[2048,2048]{1,0:T(8,128)(2,1)} %get-tuple-element.52.aw_hbm, bf16[1024,2048]{1,0:T(8,128)(2,1)} %get-tuple-element.68.nin_hbm, ...), custom_call_target="tpu_custom_call" | custom-call | tf_op jit(solution)/shard_map/last_stage/pallas_call | solution.py:1994
  539.2 13.1 %finish_stage.1 = (bf16[1024,2048]{1,0:T(8,128)(2,1)}, f32[1024,2048]{1,0:T(8,128)}, f32[256,2048]{1,0:T(8,128)}, f32[256,2048]{1,0:T(8,128)}, f32[2048,256]{1,0...) custom-call(bf16[1024,2048]{1,0:T(8,128)(2,1)} %get-tuple-element.74, ...), custom_call_target="tpu_custom_call" | custom-call | tf_op jit(solution)/shard_map/finish_stage/pallas_call | solution.py:2080
